TPU v7x, 32 devices: a whole 2x2x4 slice. The times are simulated.
32 devices in a mesh: ctx: 8 (over z, x), wt: 4 (over y, core).
Axes of the slice: x: 2, y: 2, z: 4, core: 2. Of those that a mesh axis runs over, the one named last changes fastest.
Arguments:
- tokens: bfloat16 [4, 1024, 768], P('wt', 'ctx'), may hold values from -6 to 6
- cotangent: bfloat16 [4, 1024, 768], P('wt', 'ctx'), may hold values from -6 to 6
- gain_attention: bfloat16 [768], P('wt'), may hold values from 0.5 to 1.5
- query_weight: bfloat16 [768, 768], P('wt'), may hold values from -0.21875 to 0.21875
- key_weight: bfloat16 [768, 768], P('wt'), may hold values from -0.21875 to 0.21875
- value_weight: bfloat16 [768, 768], P('wt'), may hold values from -0.21875 to 0.21875
- output_weight: bfloat16 [768, 768], P('wt'), may hold values from -0.875 to 0.875
- gain_mixer: bfloat16 [768], P('wt'), may hold values from 0.5 to 1.5
- router_weight: bfloat16 [768, 8], P('wt'), may hold values from -0.21875 to 0.21875
- shared_gate: bfloat16 [768, 2048], P('wt'), may hold values from -0.21875 to 0.21875
- shared_up: bfloat16 [768, 2048], P('wt'), may hold values from -0.21875 to 0.21875
- shared_down: bfloat16 [2048, 768], P('wt'), may hold values from -0.1875 to 0.1875
- expert_gate: bfloat16 [768, 16384], P('wt', 'ctx'), may hold values from -0.21875 to 0.21875
- expert_up: bfloat16 [768, 16384], P('wt', 'ctx'), may hold values from -0.21875 to 0.21875
- expert_down: bfloat16 [768, 16384], P('wt', 'ctx'), may hold values from -0.25 to 0.25
- routes: int32 [4, 1024, 2], P('wt', 'ctx'), may hold values from 0 to 7, all different within a row
- slot_order: int32 [4, 8, 256], P('wt', 'ctx'), may hold values from 0 to 255, each once within a row
- block_deal: int32 [8], replicated, may hold values from 0 to 7, each once
Outputs:
- output: bfloat16 [4, 1024, 768], P('wt', 'ctx')
- input_gradient: float32 [4, 1024, 768], P('wt', 'ctx')
- gain_attention_gradient: float32 [768], P('wt')
- query_gradient: float32 [768, 768], P('wt')
- key_gradient: float32 [768, 768], P('wt')
- value_gradient: float32 [768, 768], P('wt')
- output_weight_gradient: float32 [768, 768], P('wt')
- gain_mixer_gradient: float32 [768], P('wt')
- router_gradient: float32 [768, 8], P('wt')
- shared_gate_gradient: float32 [768, 2048], P('wt')
- shared_up_gradient: float32 [768, 2048], P('wt')
- shared_down_gradient: float32 [2048, 768], P('wt')
- expert_gate_gradient: float32 [768, 16384], P('wt', 'ctx')
- expert_up_gradient: float32 [768, 16384], P('wt', 'ctx')
- expert_down_gradient: float32 [768, 16384], P('wt', 'ctx')
Inputs may be any that keep to these rules, and one draw needn't show every extreme that they name: `routes`: each token names 2 different experts. `slot_order`: each row lists every pair index of a device once. `block_deal`: each rank's number appears once.
All inputs are finite; a program needn't handle non-finite values.
Results may differ from a plain program's by a relative error of at most 0.02.
Values may be sent and summed in bfloat16 or wider, within the bound.
A program may use at most 320 MiB of HBM per device.

v0:
```python
import jax
import jax.numpy as jnp
from jax import lax
from jax.sharding import PartitionSpec as P

HD = 64
BLK = 256


EPS = 1e-06
KEY_ROWS = 512
HIGH = lax.Precision.HIGHEST
MASKED = -1e30


def contract_product(left, right, left_dim, right_dim):
    return lax.dot_general(
        left, right, (((left_dim,), (right_dim,)), ((), ())), preferred_element_type=jnp.float32
    )


def contract_exact(left, right, left_dim, right_dim):
    return lax.dot_general(
        left,
        right,
        (((left_dim,), (right_dim,)), ((), ())),
        precision=HIGH,
        preferred_element_type=jnp.float32,
    )


def rms_norm(values, gain):
    norm_scale = lax.rsqrt(jnp.mean(values * values, axis=-1, keepdims=True) + EPS)
    return (values * norm_scale * gain, norm_scale)


def rms_back(values, norm_scale, gain, upstream):
    weighted = upstream * gain
    inner_mean = jnp.mean(weighted * values, axis=-1, keepdims=True)
    through = norm_scale * weighted - values * norm_scale * norm_scale * norm_scale * inner_mean
    return (through, jnp.sum(upstream * values * norm_scale, axis=0))


def silu_parts(gate_part):
    sigmoid = jax.nn.sigmoid(gate_part)
    return (gate_part * sigmoid, sigmoid * (1.0 + gate_part * (1.0 - sigmoid)))


def rotate(values, place, sign):
    half_size = HD // 2
    frequency = 10000.0 ** (-jnp.arange(half_size, dtype=jnp.float32) / half_size)
    angles = place.astype(jnp.float32)[:, None] * frequency[None, :]
    cosine = jnp.cos(angles)[:, None, :]
    sine_part = sign * jnp.sin(angles)[:, None, :]
    shaped = values.reshape(values.shape[0], values.shape[1] // HD, 2, half_size)
    first_half = shaped[:, :, 0, :]
    second_half = shaped[:, :, 1, :]
    turned = jnp.stack(
        [
            first_half * cosine - second_half * sine_part,
            second_half * cosine + first_half * sine_part,
        ],
        axis=2,
    )
    return turned.reshape(values.shape)


def places(first_row, row_count, block_deal, rows_dev):
    row_index = first_row + jnp.arange(row_count, dtype=jnp.int32)
    owner_rank = row_index // rows_dev
    inner_row = row_index % rows_dev
    ranks = block_deal.shape[0]
    matches = owner_rank[:, None] == jnp.arange(ranks, dtype=jnp.int32)[None, :]
    paired = jnp.sum(jnp.where(matches, block_deal[None, :], 0), axis=1)
    piece_size = rows_dev // 2
    unit_index = jnp.where(inner_row < piece_size, paired, 2 * ranks - 1 - paired)
    return unit_index * piece_size + inner_row % piece_size


def score_block(query_side, key_rows, key_place):
    query3, query_block = query_side
    key3 = key_rows.reshape(key_rows.shape[0], -1, HD)
    raw_scores = jnp.einsum("qhd,khd->hqk", query3, key3, preferred_element_type=jnp.float32)
    allowed = (key_place // BLK)[None, None, :] <= query_block[None, :, None]
    return (jnp.where(allowed, raw_scores * HD ** (-0.5), MASKED), allowed)


def absorb(running, key_rows, value_rows, key_place, query_side):
    largest, denom, accum = running
    scores, allowed = score_block(query_side, key_rows, key_place)
    new_largest = jnp.maximum(largest, jnp.max(scores, axis=2))
    factor = jnp.exp(largest - new_largest)
    raised = jnp.where(allowed, jnp.exp(scores - new_largest[:, :, None]), 0.0)
    denom = denom * factor + jnp.sum(raised, axis=2)
    value3 = value_rows.reshape(value_rows.shape[0], -1, HD)
    accum = accum * factor.T[:, :, None] + jnp.einsum(
        "hqk,khd->qhd", raised.astype(jnp.bfloat16), value3, preferred_element_type=jnp.float32
    )
    return (new_largest, denom, accum)


def fold_keys(running, key_piece, query_side, block_deal, rows_dev):
    key_all, value_all = key_piece
    row_count = key_all.shape[0]
    block_size = KEY_ROWS

    def key_step(current, offset):
        key_rows = lax.dynamic_slice_in_dim(key_all, offset, block_size, 0)
        value_rows = lax.dynamic_slice_in_dim(value_all, offset, block_size, 0)
        key_place = places(offset, block_size, block_deal, rows_dev)
        return (absorb(current, key_rows, value_rows, key_place, query_side), None)

    offsets = jnp.arange(row_count // block_size, dtype=jnp.int32) * block_size
    running, unused = lax.scan(key_step, running, offsets)
    return running


def differentiate(query_side, log_total, delta, grad_out3, key_rows, value_rows, key_place):
    scores, allowed = score_block(query_side, key_rows, key_place)
    probs_full = jnp.where(allowed, jnp.exp(scores - log_total[:, :, None]), 0.0)
    value3 = value_rows.reshape(value_rows.shape[0], -1, HD)
    grad_probs = jnp.einsum("qhd,khd->hqk", grad_out3, value3, preferred_element_type=jnp.float32)
    grad_scores = (probs_full * (grad_probs - delta[:, :, None]) * HD ** (-0.5)).astype(
        jnp.bfloat16
    )
    return (probs_full, grad_scores)


def assign_slots(route, order, experts, capacity):
    pair_count = order.shape[0]
    expert_ids = route.reshape(pair_count)
    ordered = expert_ids[order]
    onehot = (ordered[:, None] == jnp.arange(experts, dtype=jnp.int32)[None, :]).astype(jnp.int32)
    before = jnp.cumsum(onehot, axis=0) - onehot
    slot_turn = jnp.sum(before * onehot, axis=1)
    slot_index = jnp.zeros((pair_count,), jnp.int32).at[order].set(slot_turn)
    kept_pairs = slot_index < capacity
    target = jnp.where(kept_pairs, expert_ids * capacity + slot_index, experts * capacity)
    slot_table = (
        jnp.full((experts * capacity,), pair_count, jnp.int32)
        .at[target]
        .set(jnp.arange(pair_count, dtype=jnp.int32), mode="drop")
    )
    return (target, kept_pairs, slot_table)


def body(
    tokens,
    cotangent,
    gain_attention,
    query_weight,
    key_weight,
    value_weight,
    output_weight,
    gain_mixer,
    router_weight,
    shared_gate,
    shared_up,
    shared_down,
    expert_gate,
    expert_up,
    expert_down,
    routes,
    slot_order,
    block_deal,
):
    rows_dev = tokens.shape[1]
    width = tokens.shape[2]
    ranks = lax.axis_size("ctx")
    (
        gain_one,
        query_full,
        key_full,
        value_full,
        output_full,
        gain_two,
        router_full,
        sgate_full,
        sup_full,
        sdown_full,
        expert_gate_whole,
        expert_up_whole,
        edown_full,
    ) = (
        lax.all_gather(gain_attention, "wt", axis=0, tiled=True),
        lax.all_gather(query_weight, "wt", axis=0, tiled=True),
        lax.all_gather(key_weight, "wt", axis=0, tiled=True),
        lax.all_gather(value_weight, "wt", axis=0, tiled=True),
        lax.all_gather(output_weight, "wt", axis=0, tiled=True),
        lax.all_gather(gain_mixer, "wt", axis=0, tiled=True),
        lax.all_gather(router_weight, "wt", axis=0, tiled=True),
        lax.all_gather(shared_gate, "wt", axis=0, tiled=True),
        lax.all_gather(shared_up, "wt", axis=0, tiled=True),
        lax.all_gather(shared_down, "wt", axis=0, tiled=True),
        lax.all_gather(expert_gate, "wt", axis=0, tiled=True),
        lax.all_gather(expert_up, "wt", axis=0, tiled=True),
        lax.all_gather(expert_down, "wt", axis=0, tiled=True),
    )
    gain_first = gain_one.astype(jnp.float32)
    gain_second = gain_two.astype(jnp.float32)
    heads = width // HD
    inputs = tokens[0].astype(jnp.float32)
    here = places(lax.axis_index("ctx") * rows_dev, rows_dev, block_deal, rows_dev)
    query_side_block = here // BLK
    normed_f, scale_one = rms_norm(inputs, gain_first)
    normed = normed_f.astype(jnp.bfloat16)
    query_rot = rotate(
        jnp.dot(normed, query_full, preferred_element_type=jnp.float32), here, 1.0
    ).astype(jnp.bfloat16)
    key_rot = rotate(
        jnp.dot(normed, key_full, preferred_element_type=jnp.float32), here, 1.0
    ).astype(jnp.bfloat16)
    value_low = jnp.dot(normed, value_full, preferred_element_type=jnp.float32).astype(jnp.bfloat16)
    query3 = query_rot.reshape(rows_dev, heads, HD)
    query_side = (query3, query_side_block)
    start_state = (
        jnp.full((heads, rows_dev), MASKED, jnp.float32),
        jnp.zeros((heads, rows_dev), jnp.float32),
        jnp.zeros((rows_dev, heads, HD), jnp.float32),
    )
    largest, denom, accum = fold_keys(
        start_state,
        (
            lax.all_gather(key_rot, "ctx", axis=0, tiled=True),
            lax.all_gather(value_low, "ctx", axis=0, tiled=True),
        ),
        query_side,
        block_deal,
        rows_dev,
    )
    mixed3 = accum / denom.T[:, :, None]
    log_total = largest + jnp.log(denom)
    mixed_low = mixed3.reshape(rows_dev, width).astype(jnp.bfloat16)
    second = inputs + jnp.dot(mixed_low, output_full, preferred_element_type=jnp.float32)
    mixer_f, scale_two = rms_norm(second, gain_second)
    mixer = mixer_f.astype(jnp.bfloat16)
    experts = router_full.shape[1]
    logits = jnp.dot(mixer, router_full, preferred_element_type=jnp.float32)
    route = routes[0]
    top_count = route.shape[1]
    pair_count = rows_dev * top_count
    capacity = (5 * pair_count + 4 * experts - 1) // (4 * experts)
    split_count = ranks // experts
    expert_match = route[:, :, None] == jnp.arange(experts, dtype=jnp.int32)[None, None, :]
    chosen = jnp.sum(jnp.where(expert_match, logits[:, None, :], 0.0), axis=2)
    gates = jax.nn.softmax(chosen, axis=1)
    target, kept_pairs, slot_table = assign_slots(route, slot_order[0, 0], experts, capacity)
    valid = slot_table < pair_count
    pair_pick = jnp.minimum(slot_table, pair_count - 1)
    target_pick = jnp.minimum(target, experts * capacity - 1)
    send_rows = jnp.where(
        valid[:, None], mixer[pair_pick // top_count], jnp.zeros((), jnp.bfloat16)
    )
    send_rows = jnp.broadcast_to(
        send_rows.reshape(experts, 1, capacity, width), (experts, split_count, capacity, width)
    ).reshape(ranks, capacity, width)
    received = lax.all_to_all(send_rows, "ctx", split_axis=0, concat_axis=0, tiled=True)
    slot_count = received.shape[1]
    flattened_input = received.reshape(ranks * slot_count, width)
    gate_part = jnp.dot(flattened_input, expert_gate_whole, preferred_element_type=jnp.float32)
    up_projection_part = jnp.dot(
        flattened_input, expert_up_whole, preferred_element_type=jnp.float32
    )
    activated, unused = silu_parts(gate_part)
    hidden = (activated * up_projection_part).astype(jnp.bfloat16)
    partial_value = contract_product(hidden, edown_full, 1, 1).reshape(ranks, slot_count, width)
    back = lax.all_to_all(
        partial_value.astype(jnp.bfloat16), "ctx", split_axis=0, concat_axis=0, tiled=True
    ).astype(partial_value.dtype)
    expert_gate_part = gate_part.reshape(ranks, slot_count, -1)
    expert_up_part = up_projection_part.reshape(ranks, slot_count, -1)
    combined = jnp.sum(back.reshape(experts, split_count, capacity, width), axis=1).reshape(
        experts * capacity, width
    )
    pair_out = jnp.where(kept_pairs[:, None], combined[target_pick], 0.0).reshape(
        rows_dev, top_count, width
    )
    mixture = jnp.sum(gates[:, :, None] * pair_out, axis=1)
    sgate_part = jnp.dot(mixer, sgate_full, preferred_element_type=jnp.float32)
    sup_part = jnp.dot(mixer, sup_full, preferred_element_type=jnp.float32)
    shared_act, shared_slope = silu_parts(sgate_part)
    shared_hidden = (shared_act * sup_part).astype(jnp.bfloat16)
    shared_out = jnp.dot(shared_hidden, sdown_full, preferred_element_type=jnp.float32)
    result = (second + mixture + shared_out).astype(jnp.bfloat16)
    grad_final = cotangent[0].astype(jnp.float32)
    grad_low = grad_final.astype(jnp.bfloat16)
    sdown_grad = contract_product(shared_hidden, grad_low, 0, 0)
    grad_shared_hidden = contract_product(grad_low, sdown_full, 1, 1)
    grad_sgate = (grad_shared_hidden * sup_part * shared_slope).astype(jnp.bfloat16)
    grad_sup = (grad_shared_hidden * shared_act).astype(jnp.bfloat16)
    sgate_grad = contract_product(mixer, grad_sgate, 0, 0)
    sup_grad = contract_product(mixer, grad_sup, 0, 0)
    grad_mixer = contract_product(grad_sgate, sgate_full, 1, 1) + contract_product(
        grad_sup, sup_full, 1, 1
    )
    pair_grad = (
        (gates[:, :, None] * grad_final[:, None, :]).reshape(pair_count, width).astype(jnp.bfloat16)
    )
    grad_gates = jnp.sum(grad_final[:, None, :] * pair_out, axis=2)
    send_grad = jnp.where(valid[:, None], pair_grad[pair_pick], jnp.zeros((), jnp.bfloat16))
    send_grad = jnp.broadcast_to(
        send_grad.reshape(experts, 1, capacity, width), (experts, split_count, capacity, width)
    ).reshape(ranks, capacity, width)
    recv_grad = lax.all_to_all(send_grad, "ctx", split_axis=0, concat_axis=0, tiled=True)
    flattened_input = received.reshape(ranks * capacity, width)
    flat_grad = recv_grad.reshape(ranks * capacity, width)
    gate_flat = expert_gate_part.reshape(ranks * capacity, -1)
    up_flat = expert_up_part.reshape(ranks * capacity, -1)
    expert_activation, expert_slope = silu_parts(gate_flat)
    expert_hidden = (expert_activation * up_flat).astype(jnp.bfloat16)
    edown_grad = contract_product(flat_grad, expert_hidden, 0, 0)
    expert_hidden_grad = jnp.dot(flat_grad, edown_full, preferred_element_type=jnp.float32)
    expert_gate_grad_rows = (expert_hidden_grad * up_flat * expert_slope).astype(jnp.bfloat16)
    expert_up_grad_rows = (expert_hidden_grad * expert_activation).astype(jnp.bfloat16)
    egate_grad = contract_product(flattened_input, expert_gate_grad_rows, 0, 0)
    expert_up_weight_grad = contract_product(flattened_input, expert_up_grad_rows, 0, 0)
    input_back = (
        contract_product(expert_gate_grad_rows, expert_gate_whole, 1, 1)
        + contract_product(expert_up_grad_rows, expert_up_whole, 1, 1)
    ).reshape(ranks, capacity, width)
    back_grad = lax.all_to_all(
        input_back.astype(jnp.bfloat16), "ctx", split_axis=0, concat_axis=0, tiled=True
    ).astype(input_back.dtype)
    merged = jnp.sum(back_grad.reshape(experts, split_count, capacity, width), axis=1).reshape(
        experts * capacity, width
    )
    pair_back = jnp.where(kept_pairs[:, None], merged[target_pick], 0.0).reshape(
        rows_dev, top_count, width
    )
    grad_mixer = grad_mixer + jnp.sum(pair_back, axis=1)
    grad_chosen = gates * (grad_gates - jnp.sum(gates * grad_gates, axis=1, keepdims=True))
    grad_logits = jnp.sum(jnp.where(expert_match, grad_chosen[:, :, None], 0.0), axis=1)
    router_grad = contract_exact(mixer.astype(jnp.float32), grad_logits, 0, 0)
    grad_mixer = grad_mixer + contract_exact(grad_logits, router_full.astype(jnp.float32), 1, 1)
    through_two, gain_two_grad = rms_back(second, scale_two, gain_second, grad_mixer)
    grad_second = grad_final + through_two
    grad_attention = grad_second.astype(jnp.bfloat16)
    output_grad = contract_product(mixed_low, grad_attention, 0, 0)
    grad_mixed = contract_product(grad_attention, output_full, 1, 1).astype(jnp.bfloat16)
    grad_out3 = grad_mixed.reshape(rows_dev, heads, HD)
    delta = jnp.sum(grad_out3.astype(jnp.float32) * mixed3, axis=2).T
    all_keys, all_values = (
        lax.all_gather(key_rot, "ctx", axis=0, tiled=True),
        lax.all_gather(value_low, "ctx", axis=0, tiled=True),
    )
    total_rows = all_keys.shape[0]
    block_size = KEY_ROWS

    def query_step(grad_sum, offset):
        key_rows = lax.dynamic_slice_in_dim(all_keys, offset, block_size, 0)
        value_rows = lax.dynamic_slice_in_dim(all_values, offset, block_size, 0)
        key_place = places(offset, block_size, block_deal, rows_dev)
        unused, grad_scores = differentiate(
            query_side, log_total, delta, grad_out3, key_rows, value_rows, key_place
        )
        key3 = key_rows.reshape(block_size, heads, HD)
        return (
            grad_sum
            + jnp.einsum("hqk,khd->qhd", grad_scores, key3, preferred_element_type=jnp.float32),
            None,
        )

    offsets = jnp.arange(total_rows // block_size, dtype=jnp.int32) * block_size
    grad_query3, unused = lax.scan(
        query_step, jnp.zeros((rows_dev, heads, HD), jnp.float32), offsets
    )
    inner_size = KEY_ROWS

    def one_part(offset):
        key_rows = lax.dynamic_slice_in_dim(all_keys, offset, inner_size, 0)
        value_rows = lax.dynamic_slice_in_dim(all_values, offset, inner_size, 0)
        key_place = places(offset, inner_size, block_deal, rows_dev)
        probs_full, grad_scores = differentiate(
            query_side, log_total, delta, grad_out3, key_rows, value_rows, key_place
        )
        grad_value_rows = jnp.einsum(
            "hqk,qhd->khd",
            probs_full.astype(jnp.bfloat16),
            grad_out3,
            preferred_element_type=jnp.float32,
        )
        grad_key_rows = jnp.einsum(
            "hqk,qhd->khd", grad_scores, query3, preferred_element_type=jnp.float32
        )
        return jnp.concatenate(
            [grad_key_rows.reshape(inner_size, width), grad_value_rows.reshape(inner_size, width)],
            axis=1,
        )

    parts = lax.map(
        one_part,
        jnp.arange(lax.axis_size("ctx") * rows_dev // inner_size, dtype=jnp.int32) * inner_size,
    )
    key_value_grad = lax.psum_scatter(
        parts.reshape(lax.axis_size("ctx") * rows_dev, 2 * width),
        "ctx",
        scatter_dimension=0,
        tiled=True,
    )
    grad_key_pre = rotate(key_value_grad[:, :width], here, -1.0).astype(jnp.bfloat16)
    grad_value_low = key_value_grad[:, width:].astype(jnp.bfloat16)
    grad_query_pre = rotate(grad_query3.reshape(rows_dev, width), here, -1.0).astype(jnp.bfloat16)
    query_grad = contract_product(normed, grad_query_pre, 0, 0)
    key_grad = contract_product(normed, grad_key_pre, 0, 0)
    value_grad = contract_product(normed, grad_value_low, 0, 0)
    grad_normed = (
        contract_product(grad_query_pre, query_full, 1, 1)
        + contract_product(grad_key_pre, key_full, 1, 1)
        + contract_product(grad_value_low, value_full, 1, 1)
    )
    through_one, gain_one_grad = rms_back(inputs, scale_one, gain_first, grad_normed)
    grad_input = grad_second + through_one
    (
        gain_one_share,
        query_share,
        key_share,
        value_share,
        output_share,
        gain_two_share,
        router_share,
        sgate_share,
        sup_share,
        sdown_share,
        egate_share,
        expert_up_portion,
        edown_share,
    ) = (
        lax.psum_scatter(
            gain_one_grad.astype(jnp.bfloat16), "wt", scatter_dimension=0, tiled=True
        ).astype(jnp.float32),
        lax.psum_scatter(
            query_grad.astype(jnp.bfloat16), "wt", scatter_dimension=0, tiled=True
        ).astype(jnp.float32),
        lax.psum_scatter(
            key_grad.astype(jnp.bfloat16), "wt", scatter_dimension=0, tiled=True
        ).astype(jnp.float32),
        lax.psum_scatter(
            value_grad.astype(jnp.bfloat16), "wt", scatter_dimension=0, tiled=True
        ).astype(jnp.float32),
        lax.psum_scatter(
            output_grad.astype(jnp.bfloat16), "wt", scatter_dimension=0, tiled=True
        ).astype(jnp.float32),
        lax.psum_scatter(
            gain_two_grad.astype(jnp.bfloat16), "wt", scatter_dimension=0, tiled=True
        ).astype(jnp.float32),
        lax.psum_scatter(
            router_grad.astype(jnp.bfloat16), "wt", scatter_dimension=0, tiled=True
        ).astype(jnp.float32),
        lax.psum_scatter(
            sgate_grad.astype(jnp.bfloat16), "wt", scatter_dimension=0, tiled=True
        ).astype(jnp.float32),
        lax.psum_scatter(
            sup_grad.astype(jnp.bfloat16), "wt", scatter_dimension=0, tiled=True
        ).astype(jnp.float32),
        lax.psum_scatter(
            sdown_grad.astype(jnp.bfloat16), "wt", scatter_dimension=0, tiled=True
        ).astype(jnp.float32),
        lax.psum_scatter(
            egate_grad.astype(jnp.bfloat16), "wt", scatter_dimension=0, tiled=True
        ).astype(jnp.float32),
        lax.psum_scatter(
            expert_up_weight_grad.astype(jnp.bfloat16), "wt", scatter_dimension=0, tiled=True
        ).astype(jnp.float32),
        lax.psum_scatter(
            edown_grad.astype(jnp.bfloat16), "wt", scatter_dimension=0, tiled=True
        ).astype(jnp.float32),
    )
    (
        gain_one_sum,
        query_sum,
        key_sum,
        value_sum,
        output_sum,
        gain_two_sum,
        router_sum,
        sgate_sum,
        sup_sum,
        sdown_sum,
    ) = lax.psum(
        (
            gain_one_share,
            query_share,
            key_share,
            value_share,
            output_share,
            gain_two_share,
            router_share,
            sgate_share,
            sup_share,
            sdown_share,
        ),
        "ctx",
    )
    return (
        result[None],
        grad_input[None],
        gain_one_sum,
        query_sum,
        key_sum,
        value_sum,
        output_sum,
        gain_two_sum,
        router_sum,
        sgate_sum,
        sup_sum,
        sdown_sum,
        egate_share,
        expert_up_portion,
        edown_share,
    )


def solution(mesh):
    in_specs = (
        P("wt", "ctx", None),
        P("wt", "ctx", None),
        P("wt"),
        P("wt", None),
        P("wt", None),
        P("wt", None),
        P("wt", None),
        P("wt"),
        P("wt", None),
        P("wt", None),
        P("wt", None),
        P("wt", None),
        P("wt", "ctx"),
        P("wt", "ctx"),
        P("wt", "ctx"),
        P("wt", "ctx", None),
        P("wt", "ctx", None),
        P(),
    )
    out_specs = (
        P("wt", "ctx", None),
        P("wt", "ctx", None),
        P("wt"),
        P("wt", None),
        P("wt", None),
        P("wt", None),
        P("wt", None),
        P("wt"),
        P("wt", None),
        P("wt", None),
        P("wt", None),
        P("wt", None),
        P("wt", "ctx"),
        P("wt", "ctx"),
        P("wt", "ctx"),
    )
    return jax.shard_map(body, mesh=mesh, in_specs=in_specs, out_specs=out_specs, check_vma=False)
```

profile of v0, /device:TPU:0, one launch (start us, length us, event | category | flops | bytes accessed | tf_op | source)
XLA Modules:
  0.0 1216.4 jit_solution(2222060306107248217)
XLA Ops:
  13.1 8.3 all-reduce.6
  22.6 7.2 all-gather.20.cloned.1.call-done
  33.8 15.0 %all-gather.14.cloned.1.call-done = bf16[768,768]{1,0:T(8,128)(2,1)} async-done(((bf16[192,768]{1,0:T(8,128)(2,1)}), bf16[768,768]{1,0:T(8,128)(2,1)}) %all-gather.14.cloned.1.call-update) | async-done | bytes 1179664 | tf_op jit(solution)/shard_map/all_gather | solution.py:187
  50.4 17.5 %all-gather.18.cloned.1.call-done = bf16[768,768]{1,0:T(8,128)(2,1)} async-done(((bf16[192,768]{1,0:T(8,128)(2,1)}), bf16[768,768]{1,0:T(8,128)(2,1)}) %all-gather.18.cloned.1.call-update) | async-done | bytes 1179664 | tf_op jit(solution)/shard_map/all_gather | solution.py:186
  85.2 29.5 %all-gather.22.cloned.1.call-done = bf16[1024,768]{1,0:T(8,128)(2,1)} async-done(((bf16[128,768]{1,0:T(8,128)(2,1)}), bf16[1024,768]{1,0:T(8,128)(2,1)}) %all-gather.22.cloned.1.call-update) | async-done | bytes 1572880 | tf_op jit(solution)/shard_map/all_gather | solution.py:225
  117.3 44.0 %all-gather.16.cloned.1.call-done = bf16[1024,768]{0,1:T(8,128)(2,1)} async-done(((bf16[128,768]{0,1:T(8,128)(2,1)}), bf16[1024,768]{0,1:T(8,128)(2,1)}) %all-gather.16.cloned.1.call-update) | async-done | bytes 1572880 | tf_op jit(solution)/shard_map/all_gather | solution.py:224
  161.3 28.6 %while.46 = (s32[]{:T(128)}, f32[12,128]{1,0:T(8,128)S(1)}, f32[12,128]{1,0:T(8,128)}, f32[128,12,64]{0,2,1:T(8,128)}, s32[2]{0:T(128)}, /*index=5*/s32[8]{0:T(1...) while((s32[]{:T(128)}, f32[12,128]{1,0:T(8,128)S(1)}, ...), condition=%wide.region_6.7_spmd.clone, body=%wide.region_2.6_spmd.clone.sunk | while | flops 211961856 | bytes 16085843 | solution.py:114
  164.5 3.1 constant_dynamic-slice_fusion.10
  171.3 2.9 fusion.252
  178.8 3.0 constant_dynamic-slice_fusion.10
  185.4 3.1 fusion.252
  197.4 3.5 all-to-all-start
  201.5 7.1 all-gather.26.cloned.1.call-done
  208.5 5.9 all-to-all-done
  214.5 3.4 fusion.134
  217.9 20.8 %all-gather.28.cloned.1.call-done = bf16[768,2048]{1,0:T(8,128)(2,1)} async-done(((bf16[192,2048]{1,0:T(8,128)(2,1)}), bf16[768,2048]{1,0:T(8,128)(2,1)}) %all-gather.28.cloned.1.call-update) | async-done | bytes 3145744 | tf_op jit(solution)/shard_map/all_gather | solution.py:196
  238.7 5.1 multiply_convert_fusion.2
  243.8 25.1 %all-gather.30.cloned.1.call-done = bf16[768,2048]{1,0:T(8,128)(2,1)} async-done(((bf16[192,2048]{1,0:T(8,128)(2,1)}), bf16[768,2048]{1,0:T(8,128)(2,1)}) %all-gather.30.cloned.1.call-update) | async-done | bytes 3145744 | tf_op jit(solution)/shard_map/all_gather | solution.py:197
  268.9 4.3 convolution_convert_fusion.10
  273.2 5.6 all-to-all-start.1
  279.7 5.2 all-gather
  286.1 6.9 all-to-all-done.1
  298.8 3.6 all-to-all-start.2
  303.0 3.4 fusion.135
  306.5 22.6 %all-gather.34.cloned.1.call-done = bf16[768,2048]{1,0:T(8,128)(2,1)} async-done(((bf16[192,2048]{1,0:T(8,128)(2,1)}), bf16[768,2048]{1,0:T(8,128)(2,1)}) %all-gather.34.cloned.1.call-update) | async-done | bytes 3145744 | tf_op jit(solution)/shard_map/all_gather | solution.py:193
  329.1 3.4 fusion.136
  332.5 4.8 multiply_convert_fusion
  342.6 5.7 all-to-all-start.3
  348.5 10.6 all-gather.36.cloned.1.call-done
  359.1 4.7 multiply_convert_fusion.3
  373.6 2.6 gather.31
  376.3 4.2 select_reduce_fusion.3
  386.3 46.0 %while.45 = (s32[]{:T(128)}, f32[2,512,1536]{2,1,0:T(8,128)}, s32[2]{0:T(128)}, s32[8]{0:T(128)}, s32[128]{0:T(128)}, /*index=5*/bf16[1024,768]{0,1:T(8,128)(2,1...) while((s32[]{:T(128)}, f32[2,512,1536]{2,1,0:T(8,128)}, ...), condition=%wide.region_28.29_spmd, body=%wide.region_26.28_spmd.sunk | while | flops 413770752 | bytes 51371376 | solution.py:390
  389.5 2.8 constant_dynamic-slice_fusion.9
  396.4 4.1 fusion.243
  405.4 3.8 constant_dynamic-update-slice_fusion.2
  412.5 2.8 constant_dynamic-slice_fusion.9
  419.4 4.1 fusion.243
  428.4 3.9 constant_dynamic-update-slice_fusion.2
  435.9 2.8 convolution_convert_fusion.5
  438.7 2.6 convolution_convert_fusion.4
  441.5 2.7 convolution_convert_fusion.3
  444.2 4.8 convolution_convert_fusion
  450.1 4.9 convolution_convert_fusion.2
  455.0 4.8 convolution_convert_fusion.1
  460.5 29.5 %while.47 = (s32[]{:T(128)}, f32[128,12,64]{0,2,1:T(8,128)}, s32[2]{0:T(128)}, bf16[1024,768]{0,1:T(8,128)(2,1)S(1)}, s32[8]{0:T(128)}, /*index=5*/s32[128]{0:T(...) while((s32[]{:T(128)}, f32[128,12,64]{0,2,1:T(8,128)}, ...), condition=%wide.region_25.26_spmd.clone, body=%wide.region_23.25_spmd.clone.sunk | while | flops 308585472 | bytes 13132521 | solution.py:364
  470.8 4.5 fusion.259
  485.5 4.5 fusion.259
  490.0 60.4 %reduce-scatter.15.cloned.1.call-done = f32[128,1536]{1,0:T(8,128)} async-done(((f32[1024,1536]{1,0:T(8,128)}), f32[128,1536]{1,0:T(8,128)}) %reduce-scatter.15.cloned.1.call-update) | async-done | bytes 786448 | tf_op jit(solution)/shard_map/reduce_scatter | solution.py:394
  558.5 13.2 %reduce-scatter.37.cloned.1.call-done = bf16[192,8]{1,0:T(8,128)(2,1)} async-done(((bf16[768,8]{1,0:T(8,128)(2,1)}), bf16[192,8]{1,0:T(8,128)(2,1)}) %reduce-scatter.37.cloned.1.call-update) | async-done | bytes 3088
  572.5 3.2 fusion.76
  575.7 24.7 %reduce-scatter.23.cloned.1.call-done = bf16[192,768]{1,0:T(8,128)(2,1)} async-done(((bf16[768,768]{1,0:T(8,128)(2,1)}), bf16[192,768]{1,0:T(8,128)(2,1)}) %reduce-scatter.23.cloned.1.call-update) | async-done | bytes 294928 | tf_op jit(solution)/shard_map/reduce_scatter | solution.py:440
  600.4 40.6 %reduce-scatter.25.cloned.1.call-done = bf16[192,2048]{1,0:T(8,128)(2,1)} async-done(((bf16[768,2048]{1,0:T(8,128)(2,1)}), bf16[192,2048]{1,0:T(8,128)(2,1)}) %reduce-scatter.25.cloned.1.call-update) | async-done | bytes 786448 | tf_op jit(solution)/shard_map/reduce_scatter | solution.py:449
  640.9 40.4 %reduce-scatter.27.cloned.1.call-done = bf16[192,2048]{1,0:T(8,128)(2,1)} async-done(((bf16[768,2048]{1,0:T(8,128)(2,1)}), bf16[192,2048]{1,0:T(8,128)(2,1)}) %reduce-scatter.27.cloned.1.call-update) | async-done | bytes 786448 | tf_op jit(solution)/shard_map/reduce_scatter | solution.py:452
  681.3 40.6 %reduce-scatter.29.cloned.1.call-done = bf16[512,768]{1,0:T(8,128)(2,1)} async-done(((bf16[2048,768]{1,0:T(8,128)(2,1)}), bf16[512,768]{1,0:T(8,128)(2,1)}) %reduce-scatter.29.cloned.1.call-update) | async-done | bytes 786448 | tf_op jit(solution)/shard_map/reduce_scatter | solution.py:455
  721.9 40.5 %reduce-scatter.35.cloned.1.call-done = bf16[192,2048]{1,0:T(8,128)(2,1)} async-done(((bf16[768,2048]{1,0:T(8,128)(2,1)}), bf16[192,2048]{1,0:T(8,128)(2,1)}) %reduce-scatter.35.cloned.1.call-update) | async-done | bytes 786448 | tf_op jit(solution)/shard_map/reduce_scatter | solution.py:464
  764.8 38.1 %reduce-scatter.31.cloned.1.call-done = bf16[192,2048]{1,0:T(8,128)(2,1)} async-done(((bf16[768,2048]{1,0:T(8,128)(2,1)}), bf16[192,2048]{1,0:T(8,128)(2,1)}) %reduce-scatter.31.cloned.1.call-update) | async-done | bytes 786448 | tf_op jit(solution)/shard_map/reduce_scatter | solution.py:458
  805.4 38.1 %reduce-scatter.33.cloned.1.call-done = bf16[192,2048]{1,0:T(8,128)(2,1)} async-done(((bf16[768,2048]{1,0:T(8,128)(2,1)}), bf16[192,2048]{1,0:T(8,128)(2,1)}) %reduce-scatter.33.cloned.1.call-update) | async-done | bytes 786448 | tf_op jit(solution)/shard_map/reduce_scatter | solution.py:461
  843.4 2.6 convert_element_type.318
  847.8 5.8 all-reduce.5
  854.7 17.8 %reduce-scatter.19.cloned.1.call-done = bf16[192,768]{1,0:T(8,128)(2,1)} async-done(((bf16[768,768]{1,0:T(8,128)(2,1)}), bf16[192,768]{1,0:T(8,128)(2,1)}) %reduce-scatter.19.cloned.1.call-update) | async-done | bytes 294928 | tf_op jit(solution)/shard_map/reduce_scatter | solution.py:434
  872.5 28.9 %reduce-scatter.17.cloned.1.call-done = bf16[192,768]{1,0:T(8,128)(2,1)} async-done(((bf16[768,768]{1,0:T(8,128)(2,1)}), bf16[192,768]{1,0:T(8,128)(2,1)}) %reduce-scatter.17.cloned.1.call-update) | async-done | bytes 294928 | tf_op jit(solution)/shard_map/reduce_scatter | solution.py:431
  901.4 28.9 %reduce-scatter.21.cloned.1.call-done = bf16[192,768]{1,0:T(8,128)(2,1)} async-done(((bf16[768,768]{1,0:T(8,128)(2,1)}), bf16[192,768]{1,0:T(8,128)(2,1)}) %reduce-scatter.21.cloned.1.call-update) | async-done | bytes 294928 | tf_op jit(solution)/shard_map/reduce_scatter | solution.py:437
  930.3 278.8 %all-reduce.8 = (f32[192]{0:T(256)}, f32[192,768]{1,0:T(8,128)}, f32[192,768]{1,0:T(8,128)}, f32[192,768]{1,0:T(8,128)}, f32[192,768]{1,0:T(8,128)}, /*index=5*/...) all-reduce(f32[192]{0:T(256)S(1)} %dynamic-slice_convert_fusion.1, ...), channel_id=1, replica_groups=mesh['ctx'=8,'wt'=4] {'ctx'}, use_global_device_ids=true, to_apply=%region_33.34 | all-reduce | flops 1771392 | bytes 10629120 | tf_op jit(solution)/shard_map/psum | solution.py:479
  (405 shorter events, 139.4 us)
Async XLA Ops:
  7.2 22.6 %all-gather.20.cloned.1.call-start = ((), (), s32[]{:S(2)}) async-start(), calls=%async_computation.19 | async-start | bytes 1474560 | tf_op jit(solution)/shard_map/all_gather | solution.py:188
  7.9 40.9 %all-gather.14.cloned.1.call-start = ((), (), s32[]{:S(2)}) async-start(), calls=%async_computation.16 | async-start | bytes 1474560 | tf_op jit(solution)/shard_map/all_gather | solution.py:187
  8.7 59.2 %all-gather.18.cloned.1.call-start = ((), (), s32[]{:S(2)}) async-start(), calls=%async_computation.18 | async-start | bytes 1474560 | tf_op jit(solution)/shard_map/all_gather | solution.py:186
  9.4 105.3 %all-gather.22.cloned.1.call-start = ((), (), s32[]{:S(2)}) async-start(), calls=%async_computation.20 | async-start | bytes 1769472 | tf_op jit(solution)/shard_map/all_gather | solution.py:225
  21.5 48.5 %copy-start.50 = (f32[768]{0:T(1024)}, f32[768]{0:T(1024)S(1)}, u32[]{:S(2)}) copy-start(f32[768]{0:T(1024)S(1)} %convert_element_type.261) | copy-start | bytes 9220
  22.6 47.5 %copy-start.58 = (f32[128]{0:T(128)}, f32[128]{0:T(128)S(1)}, u32[]{:S(2)}) copy-start(f32[128]{0:T(128)S(1)} %add_rsqrt_fusion.1) | copy-start | bytes 1540
  22.6 46.9 %copy-start.3 = (bf16[1,128,768]{2,1,0:T(8,128)(2,1)S(1)}, bf16[1,128,768]{2,1,0:T(8,128)(2,1)}, u32[]{:S(2)}) copy-start(bf16[1,128,768]{2,1,0:T(8,128)(2,1)} %param.24) | copy-start | bytes 589828
  32.2 129.1 %all-gather.16.cloned.1.call-start = ((), (), s32[]{:S(2)}) async-start(), calls=%async_computation.17 | async-start | bytes 1769472 | tf_op jit(solution)/shard_map/all_gather | solution.py:224
  33.8 36.8 %copy-start.53 = (f32[128,32]{0,1:T(8,128)}, f32[128,32]{0,1:T(8,128)S(1)}, u32[]{:S(2)}) copy-start(f32[128,32]{0,1:T(8,128)S(1)} %get-tuple-element.875) | copy-start | bytes 49156
  71.5 119.5 %all-gather.24.cloned.1.call-start = ((), (), s32[]{:S(2)}) async-start(), calls=%async_computation.21 | async-start | bytes 1474560 | tf_op jit(solution)/shard_map/all_gather | solution.py:189
  72.0 136.5 %all-gather.26.cloned.1.call-start = ((), (), s32[]{:S(2)}) async-start(), calls=%async_computation.22 | async-start | bytes 3932160 | tf_op jit(solution)/shard_map/all_gather | solution.py:195
  72.8 165.9 %all-gather.28.cloned.1.call-start = ((), (), s32[]{:S(2)}) async-start(), calls=%async_computation.23 | async-start | bytes 3932160 | tf_op jit(solution)/shard_map/all_gather | solution.py:196
  73.5 195.3 %all-gather.30.cloned.1.call-start = ((), (), s32[]{:S(2)}) async-start(), calls=%async_computation.24 | async-start | bytes 3932160 | tf_op jit(solution)/shard_map/all_gather | solution.py:197
  74.3 228.8 %all-gather.32.cloned.1.call-start = ((), (), s32[]{:S(2)}) async-start(), calls=%async_computation.25 | async-start | bytes 3932160 | tf_op jit(solution)/shard_map/all_gather | solution.py:192
  74.9 254.2 %all-gather.34.cloned.1.call-start = ((), (), s32[]{:S(2)}) async-start(), calls=%async_computation.26 | async-start | bytes 3932160 | tf_op jit(solution)/shard_map/all_gather | solution.py:193
  197.4 17.1 %all-to-all-start = ((bf16[8,40,768]{2,1,0:T(8,128)(2,1)}), bf16[8,40,768]{2,1,0:T(8,128)(2,1)S(1)}, u32[]{:S(2)}, u32[]{:S(2)}) async-start(bf16[8,40,768]{2,1,0:T(8,128)(2,1)} %broadcast_select_fusion.1), calls=%async_computation | async-start | bytes 983040 | tf_op jit(solution)/shard_map/all_to_all | solution.py:257
  200.9 158.2 %all-gather.36.cloned.1.call-start = ((), (), s32[]{:S(2)}) async-start(), calls=%async_computation.27 | async-start | bytes 3932160 | tf_op jit(solution)/shard_map/all_gather | solution.py:194
  214.5 29.3 %copy-start.28 = (bf16[8,40,768]{2,1,0:T(8,128)(2,1)}, bf16[8,40,768]{2,1,0:T(8,128)(2,1)S(1)}, u32[]{:S(2)}) copy-start(bf16[8,40,768]{2,1,0:T(8,128)(2,1)S(1)} %all-to-all-done) | copy-start | bytes 1474564
  217.9 25.9 %copy-start.21 = (f32[320,2048]{1,0:T(8,128)}, f32[320,2048]{1,0:T(8,128)S(1)}, u32[]{:S(2)}) copy-start(f32[320,2048]{1,0:T(8,128)S(1)} %fusion.134) | copy-start | bytes 7864324
  268.9 10.0 copy-start.34
  273.2 6.5 copy-start.76
  273.2 11.9 copy-start.80
  273.2 12.7 %copy-start.77 = (s32[256]{0:T(256)S(1)}, s32[256]{0:T(256)}, u32[]{:S(2)}) copy-start(s32[256]{0:T(256)} %get-tuple-element.871) | copy-start | bytes 3076
  273.2 12.8 %copy-start.67 = (s32[1,128,2]{1,2,0:T(2,128)S(1)}, s32[1,128,2]{1,2,0:T(2,128)}, u32[]{:S(2)}) copy-start(s32[1,128,2]{1,2,0:T(2,128)} %param.39) | copy-start | bytes 3076
  273.2 19.8 %all-to-all-start.1 = ((bf16[8,40,768]{2,1,0:T(8,128)(2,1)}), bf16[8,40,768]{2,1,0:T(8,128)(2,1)S(1)}, u32[]{:S(2)}, u32[]{:S(2)}) async-start(bf16[8,40,768]{2,1,0:T(8,128)(2,1)} %bitcast.34), calls=%async_computation.1 | async-start | bytes 983040 | tf_op jit(solution)/shard_map/all_to_all | solution.py:267
  285.1 8.0 copy-start.55
  285.9 8.4 copy-start.68
  295.7 6.7 copy-start.47
  298.8 33.7 %all-to-all-start.2 = ((bf16[8,40,768]{2,1,0:T(8,128)(2,1)}), bf16[8,40,768]{2,1,0:T(8,128)(2,1)S(1)}, u32[]{:S(2)}, u32[]{:S(2)}) async-start(bf16[8,40,768]{2,1,0:T(8,128)(2,1)} %broadcast_select_fusion), calls=%async_computation.2 | async-start | bytes 983040 | tf_op jit(solution)/shard_map/all_to_all | solution.py:304
  306.5 26.0 %copy-start.22 = (f32[320,2048]{1,0:T(8,128)S(1)}, f32[320,2048]{1,0:T(8,128)}, u32[]{:S(2)}) copy-start(f32[320,2048]{1,0:T(8,128)} %copy-done.21) | copy-start | bytes 7864324
  342.6 27.9 %all-to-all-start.3 = ((bf16[8,40,768]{2,1,0:T(8,128)(2,1)}), bf16[8,40,768]{2,1,0:T(8,128)(2,1)}, u32[]{:S(2)}, u32[]{:S(2)}) async-start(bf16[8,40,768]{2,1,0:T(8,128)(2,1)} %bitcast.40), calls=%async_computation.3 | async-start | bytes 983040 | tf_op jit(solution)/shard_map/all_to_all | solution.py:321
  348.3 16.3 %copy-start.8 = (bf16[768,2048]{1,0:T(8,128)(2,1)S(1)}, bf16[768,2048]{1,0:T(8,128)(2,1)}, u32[]{:S(2)}) copy-start(bf16[768,2048]{1,0:T(8,128)(2,1)} %all-gather.32.cloned.1.call-done) | copy-start | bytes 9437188
  348.3 202.1 %reduce-scatter.15.cloned.1.call-start = ((), (), s32[]{:S(2)}) async-start(), calls=%async_computation.28 | async-start | bytes 7077888 | tf_op jit(solution)/shard_map/reduce_scatter | solution.py:394
  373.6 6.8 copy-start.7
  376.3 6.6 copy-start.10
  376.3 6.7 copy-start.56
  376.3 6.7 copy-start.57
  376.3 6.7 copy-start.74
  389.5 6.9 copy-start.69
  412.5 6.9 copy-start.69
  433.0 138.7 %reduce-scatter.37.cloned.1.call-start = ((), (), s32[]{:S(2)}) async-start(), calls=%async_computation.39 | async-start | bytes 245760
  434.0 166.3 %reduce-scatter.23.cloned.1.call-start = ((), (), s32[]{:S(2)}) async-start(), calls=%async_computation.32 | async-start | bytes 1474560 | tf_op jit(solution)/shard_map/reduce_scatter | solution.py:440
  435.8 205.1 %reduce-scatter.25.cloned.1.call-start = ((), (), s32[]{:S(2)}) async-start(), calls=%async_computation.33 | async-start | bytes 3932160 | tf_op jit(solution)/shard_map/reduce_scatter | solution.py:449
  438.7 242.6 %reduce-scatter.27.cloned.1.call-start = ((), (), s32[]{:S(2)}) async-start(), calls=%async_computation.34 | async-start | bytes 3932160 | tf_op jit(solution)/shard_map/reduce_scatter | solution.py:452
  441.4 280.5 %reduce-scatter.29.cloned.1.call-start = ((), (), s32[]{:S(2)}) async-start(), calls=%async_computation.35 | async-start | bytes 3932160 | tf_op jit(solution)/shard_map/reduce_scatter | solution.py:455
  444.2 318.2 %reduce-scatter.35.cloned.1.call-start = ((), (), s32[]{:S(2)}) async-start(), calls=%async_computation.38 | async-start | bytes 3932160 | tf_op jit(solution)/shard_map/reduce_scatter | solution.py:464
  449.1 353.9 %reduce-scatter.31.cloned.1.call-start = ((), (), s32[]{:S(2)}) async-start(), calls=%async_computation.36 | async-start | bytes 3932160 | tf_op jit(solution)/shard_map/reduce_scatter | solution.py:458
  454.9 388.5 %reduce-scatter.33.cloned.1.call-start = ((), (), s32[]{:S(2)}) async-start(), calls=%async_computation.37 | async-start | bytes 3932160 | tf_op jit(solution)/shard_map/reduce_scatter | solution.py:461
  459.8 412.7 %reduce-scatter.19.cloned.1.call-start = ((), (), s32[]{:S(2)}) async-start(), calls=%async_computation.30 | async-start | bytes 1474560 | tf_op jit(solution)/shard_map/reduce_scatter | solution.py:434
  460.5 91.1 %copy-start.54 = (f32[128,32]{0,1:T(8,128)S(1)}, f32[128,32]{0,1:T(8,128)}, u32[]{:S(2)}) copy-start(f32[128,32]{0,1:T(8,128)} %copy-done.53) | copy-start | bytes 49156
  490.0 62.8 %copy-start.4 = (bf16[1,128,768]{2,1,0:T(8,128)(2,1)S(1)}, bf16[1,128,768]{2,1,0:T(8,128)(2,1)}, u32[]{:S(2)}) copy-start(bf16[1,128,768]{2,1,0:T(8,128)(2,1)} %param.24) | copy-start | bytes 589828
  490.0 62.8 %copy-start.51 = (f32[768]{0:T(1024)S(1)}, f32[768]{0:T(1024)}, u32[]{:S(2)}) copy-start(f32[768]{0:T(1024)} %copy-done.50) | copy-start | bytes 9220
  490.0 62.8 %copy-start.59 = (f32[128]{0:T(128)S(1)}, f32[128]{0:T(128)}, u32[]{:S(2)}) copy-start(f32[128]{0:T(128)} %copy-done.58) | copy-start | bytes 1540
  554.5 18.0 %copy-start.11 = (f32[128,768]{1,0:T(8,128)S(1)}, f32[128,768]{1,0:T(8,128)}, u32[]{:S(2)}) copy-start(f32[128,768]{1,0:T(8,128)} %copy-done.9) | copy-start | bytes 1179652
  554.5 18.0 %copy-start.24 = (bf16[128,2048]{1,0:T(8,128)(2,1)S(1)}, bf16[128,2048]{1,0:T(8,128)(2,1)}, u32[]{:S(2)}) copy-start(bf16[128,2048]{1,0:T(8,128)(2,1)} %get-tuple-element.856) | copy-start | bytes 1572868
  554.5 18.0 %copy-start.37 = (f32[128,768]{1,0:T(8,128)S(1)}, f32[128,768]{1,0:T(8,128)}, u32[]{:S(2)}) copy-start(f32[128,768]{1,0:T(8,128)} %get-tuple-element.759) | copy-start | bytes 1179652
  554.5 346.9 %reduce-scatter.17.cloned.1.call-start = ((), (), s32[]{:S(2)}) async-start(), calls=%async_computation.29 | async-start | bytes 1474560 | tf_op jit(solution)/shard_map/reduce_scatter | solution.py:431
  556.2 374.1 %reduce-scatter.21.cloned.1.call-start = ((), (), s32[]{:S(2)}) async-start(), calls=%async_computation.31 | async-start | bytes 1474560 | tf_op jit(solution)/shard_map/reduce_scatter | solution.py:437
  575.7 270.4 %copy-start.17 = (bf16[768,768]{1,0:T(8,128)(2,1)S(1)}, bf16[768,768]{1,0:T(8,128)(2,1)}, u32[]{:S(2)}) copy-start(bf16[768,768]{1,0:T(8,128)(2,1)} %all-gather.18.cloned.1.call-done) | copy-start | bytes 3538948
  764.8 81.7 %copy-start.16 = (bf16[768,768]{1,0:T(8,128)(2,1)S(1)}, bf16[768,768]{1,0:T(8,128)(2,1)}, u32[]{:S(2)}) copy-start(bf16[768,768]{1,0:T(8,128)(2,1)} %all-gather.14.cloned.1.call-done) | copy-start | bytes 3538948
  846.0 7.7 copy-start.15
  846.6 83.7 %copy-start.42 = (bf16[192,2048]{1,0:T(8,128)(2,1)S(1)}, bf16[192,2048]{1,0:T(8,128)(2,1)}, u32[]{:S(2)}) copy-start(bf16[192,2048]{1,0:T(8,128)(2,1)} %reduce-scatter.25.cloned.1.call-done) | copy-start | bytes 2359300
  847.1 83.2 %copy-start.43 = (bf16[192,2048]{1,0:T(8,128)(2,1)S(1)}, bf16[192,2048]{1,0:T(8,128)(2,1)}, u32[]{:S(2)}) copy-start(bf16[192,2048]{1,0:T(8,128)(2,1)} %reduce-scatter.27.cloned.1.call-done) | copy-start | bytes 2359300
  847.1 83.2 %copy-start.52 = (bf16[192,768]{1,0:T(8,128)(2,1)S(1)}, bf16[192,768]{1,0:T(8,128)(2,1)}, u32[]{:S(2)}) copy-start(bf16[192,768]{1,0:T(8,128)(2,1)} %reduce-scatter.23.cloned.1.call-done) | copy-start | bytes 884740
  (57 other events, 162.3 us)
Sparse Core Ops, SparseCore 0:
  9.6 20.1 all-gather.19
  31.3 17.4 all-gather.13
  50.4 17.4 all-gather.17
  70.5 44.1 all-gather.21
  117.2 44.0 all-gather.15
  162.7 15.6 all-gather.23
  180.0 28.5 all-gather.25
  210.1 28.5 all-gather.27
  240.2 28.5 all-gather.29
  270.3 28.6 all-gather.31
  300.5 28.5 all-gather.33
  330.5 28.5 all-gather.35
  432.5 117.9 reduce-scatter.14
  552.7 18.8 reduce-scatter.36
  574.6 25.7 reduce-scatter.22
  602.9 37.9 reduce-scatter.24
  643.3 37.9 reduce-scatter.26
  683.9 37.9 reduce-scatter.28
  724.4 37.9 reduce-scatter.34
  764.9 37.9 reduce-scatter.30
  805.5 37.9 reduce-scatter.32
  846.7 25.7 reduce-scatter.18
  875.6 25.7 reduce-scatter.16
  904.6 25.7 reduce-scatter.20
where the time goes:
time: 1230 us; the launch traced here: 1220 us
  waiting for transfers between devices  630 us (51%)
  blocking collectives  298 us (24%)
  matrix products  113 us (9%)
  local copies, waits for them, and re-layouts  75.5 us (6%)
  other arithmetic  50 us (4%)
  starting transfers between devices  20.5 us (2%)
  between operations  17.2 us (1%)
    psum x1, blocking collectives, body(): lax.psum((gain_one_share, query_share, key_share, value_share, output_sha...  279 us
    reduce_scatter x1, waiting for transfers between devices, body(): lax.psum_scatter(parts.reshape(lax.axis_size('ctx') * rows_dev, 2 * width...  60.4 us
    dot_general x20, matrix products, contract_product(): lax.dot_general(left, right, (((left_dim,), (right_dim,)), ((), ())), pre...  47.8 us
    all_gather x1, waiting for transfers between devices, body(): lax.all_gather(key_rot, 'ctx', axis=0, tiled=True)  44 us
    reduce_scatter x1, waiting for transfers between devices, body(): lax.psum_scatter(sgate_grad.astype(jnp.bfloat16), 'wt', scatter_dimension...  40.6 us
    reduce_scatter x1, waiting for transfers between devices, body(): lax.psum_scatter(sdown_grad.astype(jnp.bfloat16), 'wt', scatter_dimension...  40.6 us
    reduce_scatter x1, waiting for transfers between devices, body(): lax.psum_scatter(edown_grad.astype(jnp.bfloat16), 'wt', scatter_dimension...  40.5 us
    reduce_scatter x1, waiting for transfers between devices, body(): lax.psum_scatter(sup_grad.astype(jnp.bfloat16), 'wt', scatter_dimension=0...  40.4 us
  transfers between devices with their start and end apart: 28, of which 24 were waited for; matrix products, arithmetic and copies ran while one was open for 14% of the time, Pallas kernels for 0%

commit v1 on v0

--- a/solution.py
+++ b/solution.py
@@ -1,6 +1,8 @@
 import jax
 import jax.numpy as jnp
 from jax import lax
+from jax.experimental import pallas as pl
+from jax.experimental.pallas import tpu as pltpu
 from jax.sharding import PartitionSpec as P
 
 HD = 64
@@ -11,6 +13,400 @@
 KEY_ROWS = 512
 HIGH = lax.Precision.HIGHEST
 MASKED = -1e30
+
+
+MESH = pl.DeviceIdType.MESH
+VMEM = pltpu.VMEM
+BF = jnp.bfloat16
+F32 = jnp.float32
+PAIR = 2 * HD
+
+
+class Spot:
+    def __init__(self, line_size):
+        self.k = lax.axis_index("ctx")
+        self.w = lax.axis_index("wt")
+        self.z, self.x = lax.div(self.k, 2), lax.rem(self.k, 2)
+        self.y, self.c = lax.div(self.w, 2), lax.rem(self.w, 2)
+        self.far = lax.div(self.z, 2)
+        self.mid = self.z + self.far * (3 - 2 * self.z)
+        step = 1 - 2 * self.far
+        self.core = (self.k, 2 * self.y + 1 - self.c)
+        self.across = (self.k, 2 * (1 - self.y) + self.c)
+        self.corner = (self.k, 2 * (1 - self.y) + 1 - self.c)
+        self.column = (2 * self.z + 1 - self.x, self.w)
+        self.inner = (2 * (self.z + step) + self.x, self.w)
+        self.outer = (2 * (self.z - step) + self.x, self.w)
+
+    def plane(self, step):
+        mirrored = (self.mid, 1 - self.mid, 2, 3)[step]
+        return mirrored + self.far * (3 - 2 * mirrored)
+
+
+class Sems:
+    def __init__(self, ref):
+        self.ref, self.used = ref, 0
+
+    def new(self):
+        self.used += 1
+        return self.ref.at[self.used - 1]
+
+
+def remote(src, dst, send, recv, to):
+    return pltpu.make_async_remote_copy(
+        src_ref=src, dst_ref=dst, send_sem=send, recv_sem=recv, device_id=to, device_id_type=MESH
+    )
+
+
+def greet(devices, middle=None):
+    barrier = pltpu.get_barrier_semaphore()
+    for to in devices:
+        pl.semaphore_signal(barrier, inc=1, device_id=to, device_id_type=MESH)
+    if middle is None:
+        pl.semaphore_wait(barrier, len(devices))
+        return
+
+    @pl.when(middle[0] == 1)
+    def _():
+        pl.semaphore_signal(barrier, inc=1, device_id=middle[1], device_id_type=MESH)
+
+    pl.semaphore_wait(barrier, len(devices) + middle[0])
+
+
+class Gather:
+    def __init__(self, spot, src, dst, sems):
+        self.spot, self.dst, self.sems = spot, dst, sems
+        self.rows = src.shape[0]
+        here = self.block(spot.w)
+        self.local = pltpu.make_async_copy(src, here, sems.new())
+        self.to_core = remote(src, here, sems.new(), sems.new(), spot.core)
+        self.to_across = remote(src, here, sems.new(), sems.new(), spot.across)
+        for copy in (self.to_across, self.to_core, self.local):
+            copy.start()
+
+    def block(self, w):
+        return self.dst.at[pl.ds(pl.multiple_of(self.rows * w, 64), self.rows)]
+
+    def forward(self):
+        self.to_across.wait_recv()
+        part = self.block(self.spot.across[1])
+        self.onward = remote(part, part, self.sems.new(), self.sems.new(), self.spot.core)
+        self.onward.start()
+
+    def finish(self):
+        self.local.wait()
+        self.to_core.wait_recv()
+        self.onward.wait_recv()
+
+    def drain(self):
+        self.to_core.wait_send()
+        self.to_across.wait_send()
+        self.onward.wait_send()
+
+
+class Spread:
+    def __init__(self, spot, pick, place, sems, local=True):
+        self.copies = []
+        for to in (spot.across, spot.corner, spot.core):
+            self.copies.append(remote(pick(to[1]), place(spot.w), sems.new(), sems.new(), to))
+        self.local = None
+        if local:
+            self.local = pltpu.make_async_copy(pick(spot.w), place(spot.w), sems.new())
+        for copy in self.copies:
+            copy.start()
+        if local:
+            self.local.start()
+
+    def finish(self):
+        for copy in self.copies:
+            copy.wait_recv()
+        if self.local is not None:
+            self.local.wait()
+
+    def drain(self):
+        for copy in self.copies:
+            copy.wait_send()
+
+
+def nt(left, right):
+    return lax.dot_general(left, right, (((1,), (1,)), ((), ())), preferred_element_type=F32)
+
+
+def nn(left, right):
+    return jnp.dot(left, right, preferred_element_type=F32)
+
+
+def tn(left, right):
+    return lax.dot_general(left, right, (((0,), (0,)), ((), ())), preferred_element_type=F32)
+
+
+def turn(values, cosine, sine):
+    wide = values.shape[1]
+    lane = lax.broadcasted_iota(jnp.int32, values.shape, 1)
+    first = lax.rem(lane, HD) < HD // 2
+    swapped = jnp.where(
+        first, pltpu.roll(values, wide - HD // 2, 1), pltpu.roll(values, HD // 2, 1)
+    )
+    copies = wide // PAIR
+    cosine = jnp.concatenate([cosine] * copies, axis=1)
+    sine = jnp.concatenate([sine] * copies, axis=1)
+    return values * cosine + swapped * sine
+
+
+def stack_pair(values):
+    lane = lax.broadcasted_iota(jnp.int32, values.shape, 1)
+    none = jnp.zeros_like(values)
+    return jnp.concatenate(
+        [jnp.where(lane < HD, values, none), jnp.where(lane < HD, none, values)], axis=0
+    )
+
+
+def unstack_pair(values):
+    rows = values.shape[0] // 2
+    lane = lax.broadcasted_iota(jnp.int32, (rows, PAIR), 1)
+    return jnp.where(lane < HD, values[:rows], values[rows:])
+
+
+class Ring:
+    def __init__(self, spot, blocks, recv, send):
+        self.spot, self.blocks, self.recv, self.send = spot, blocks, recv, send
+        self.used = 0
+        self.sent, self.sent_mid = [], []
+
+    def copy(self, slot, to):
+        self.used += 1
+        return remote(
+            self.blocks.at[slot],
+            self.blocks.at[slot],
+            self.send.at[self.used - 1],
+            self.recv.at[slot],
+            to,
+        )
+
+    def arrived(self, slot):
+        remote(
+            self.blocks.at[slot],
+            self.blocks.at[slot],
+            self.send.at[0],
+            self.recv.at[slot],
+            self.spot.column,
+        ).wait_recv()
+
+    def start(self):
+        spot = self.spot
+        own = self.copy(spot.k, spot.inner)
+        side = self.copy(spot.k, spot.column)
+        back = self.copy(spot.k, spot.outer)
+        own.start()
+
+        @pl.when(spot.mid == 1)
+        def _():
+            back.start()
+
+        side.start()
+        self.sent += [own, side]
+        self.sent_mid += [back]
+
+    def step(self, number):
+        spot = self.spot
+        plane = spot.plane(number)
+        if number > 0:
+            slot = 2 * plane + spot.x
+            self.arrived(slot)
+            along = self.copy(slot, spot.inner if number == 1 else spot.outer)
+
+            @pl.when(spot.mid == 1)
+            def _():
+                along.start()
+
+            side = self.copy(slot, spot.column)
+            side.start()
+            self.sent += [side]
+            self.sent_mid += [along]
+        return plane
+
+    def other(self, plane):
+        self.arrived(2 * plane + 1 - self.spot.x)
+
+    def drain(self):
+        for copy in self.sent:
+            copy.wait_send()
+
+        @pl.when(self.spot.mid == 1)
+        def _():
+            for copy in self.sent_mid:
+                copy.wait_send()
+
+
+def forward_kernel(
+    tok, pack, cosr, sinr, kb, qb, cot, wq, wk, wv, wo, sg, su, eg, eu,
+    q_out, kv_out, mixed_out, lse_out, second_out, mixer_out, normed_out, pack_out,
+    wfull_out, sg_out, su_out, eg_out, eu_out, cot_out,
+    wbuf, kv, packs, top, low, acc, sem, kv_recv, kv_send,
+):
+    spot = Spot(4)
+    sems = Sems(sem)
+    rows = tok.shape[0]
+    width = tok.shape[1]
+    pairs = width // PAIR
+    greet((spot.core, spot.across, spot.corner, spot.column, spot.inner), (spot.mid, spot.outer))
+    params = Spread(spot, lambda w: pack, lambda w: packs.at[w], sems)
+    key_w = Gather(spot, wk, wbuf.at[1], sems)
+    value_w = Gather(spot, wv, wbuf.at[2], sems)
+    query_w = Gather(spot, wq, wbuf.at[0], sems)
+    inputs = tok[...].astype(F32)
+    scale = lax.rsqrt(jnp.mean(inputs * inputs, axis=-1, keepdims=True) + EPS)
+    scaled = inputs * scale
+    params.finish()
+    pack_all = packs[0] + packs[1] + packs[2] + packs[3]
+    pack_out[...] = pack_all
+    normed = (scaled * pack_all[0:1]).astype(BF)
+    normed_out[...] = normed
+    cosine, sine = cosr[...], sinr[...]
+    key_w.forward()
+    value_w.forward()
+    key_w.finish()
+    kv[spot.k, :, 0:width] = turn(nn(normed, wbuf[1]), cosine, sine).astype(BF)
+    value_w.finish()
+    kv[spot.k, :, width : 2 * width] = nn(normed, wbuf[2]).astype(BF)
+    ring = Ring(spot, kv, kv_recv, kv_send)
+    ring.start()
+    query_w.forward()
+    out_w = Gather(spot, wo, wbuf.at[3], sems)
+    sg_w = Spread(
+        spot,
+        lambda w: sg.at[:, pl.ds(pl.multiple_of(512 * w, 512), 512)],
+        lambda w: sg_out.at[pl.ds(pl.multiple_of(192 * w, 64), 192)],
+        sems,
+    )
+    su_w = Spread(
+        spot,
+        lambda w: su.at[:, pl.ds(pl.multiple_of(512 * w, 512), 512)],
+        lambda w: su_out.at[pl.ds(pl.multiple_of(192 * w, 64), 192)],
+        sems,
+    )
+    cot_w = Spread(spot, lambda w: cot, lambda w: cot_out.at[w], sems)
+    gate_w = Gather(spot, eg, eg_out, sems)
+    up_w = Gather(spot, eu, eu_out, sems)
+    query_w.finish()
+    query = turn(nn(normed, wbuf[0]), cosine, sine).astype(BF) * jnp.asarray(HD**-0.5, BF)
+    for j in range(pairs):
+        q_out[j] = stack_pair(query[:, PAIR * j : PAIR * (j + 1)])
+    top[...] = jnp.full_like(top, MASKED)
+    low[...] = jnp.zeros_like(low)
+    acc[...] = jnp.zeros_like(acc)
+    q_block = qb[...]
+
+    def chunk(plane):
+        k_block = kb[:, pl.ds(pl.multiple_of(2 * rows * plane, 2 * rows), 2 * rows)]
+        allowed = k_block <= q_block
+
+        def one_pair(j, carry):
+            lane = pl.multiple_of(PAIR * j, PAIR)
+            key = kv[pl.ds(2 * plane, 2), :, pl.ds(lane, PAIR)].reshape(2 * rows, PAIR)
+            value = kv[pl.ds(2 * plane, 2), :, pl.ds(width + lane, PAIR)].reshape(2 * rows, PAIR)
+            scores = jnp.where(allowed, nt(q_out[j], key), MASKED)
+            old = top[j]
+            new = jnp.maximum(old, jnp.max(scores, axis=1, keepdims=True))
+            raised = jnp.where(allowed, jnp.exp(scores - new[:, 0:1]), 0.0)
+            factor = jnp.exp(old - new)
+            top[j] = new
+            low[j] = low[j] * factor + jnp.sum(raised, axis=1, keepdims=True)
+            acc[j] = acc[j] * factor + nn(raised.astype(BF), value)
+            return carry
+
+        lax.fori_loop(0, pairs, one_pair, 0)
+
+    for number in range(4):
+        plane = ring.step(number)
+        ring.other(plane)
+        chunk(plane)
+    saves = [pltpu.make_async_copy(kv, kv_out, sems.new())]
+    saves[0].start()
+    out_w.forward()
+    for j in range(pairs):
+        mixed_out[:, PAIR * j : PAIR * (j + 1)] = unstack_pair(acc[j] / low[j])
+        lse_out[j] = top[j] + jnp.log(low[j])
+    out_w.finish()
+    saves.append(pltpu.make_async_copy(wbuf, wfull_out, sems.new()))
+    saves[1].start()
+    second = inputs + nn(mixed_out[...].astype(BF), wbuf[3])
+    second_out[...] = second
+    scale_two = lax.rsqrt(jnp.mean(second * second, axis=-1, keepdims=True) + EPS)
+    mixer_out[...] = (second * scale_two * pack_all[1:2]).astype(BF)
+    gate_w.forward()
+    up_w.forward()
+    for part in (sg_w, su_w, cot_w, gate_w, up_w):
+        part.finish()
+    for part in (params, key_w, value_w, query_w, out_w, sg_w, su_w, cot_w, gate_w, up_w, ring):
+        part.drain()
+    for copy in saves:
+        copy.wait()
+
+
+def run_forward(tok, pack, cosr, sinr, kb, qb, cot, wq, wk, wv, wo, sg, su, eg, eu):
+    rows, width = tok.shape
+    pairs = width // PAIR
+    ranks = 8
+    any_, vm = pl.BlockSpec(memory_space=pl.ANY), pl.BlockSpec(memory_space=VMEM)
+    shape = jax.ShapeDtypeStruct
+    hidden = eg.shape[1]
+    part = sg.shape[1] // 4
+    return pl.pallas_call(
+        forward_kernel,
+        out_shape=(
+            shape((pairs, 2 * rows, PAIR), BF),
+            shape((ranks, rows, 2 * width), BF),
+            shape((rows, width), F32),
+            shape((pairs, 2 * rows, PAIR), F32),
+            shape((rows, width), F32),
+            shape((rows, width), BF),
+            shape((rows, width), BF),
+            shape(pack.shape, F32),
+            shape((4, width, width), BF),
+            shape((width, part), BF),
+            shape((width, part), BF),
+            shape((width, hidden), BF),
+            shape((width, hidden), BF),
+            shape((4, rows, width), BF),
+        ),
+        in_specs=[vm] * 6 + [any_] * 9,
+        out_specs=(vm, any_, vm, vm, vm, vm, vm, vm, any_, any_, any_, any_, any_, any_),
+        scratch_shapes=[
+            VMEM((4, width, width), BF),
+            VMEM((ranks, rows, 2 * width), BF),
+            VMEM((4,) + pack.shape, F32),
+            VMEM((pairs, 2 * rows, PAIR), F32),
+            VMEM((pairs, 2 * rows, PAIR), F32),
+            VMEM((pairs, 2 * rows, PAIR), F32),
+            pltpu.SemaphoreType.DMA((96,)),
+            pltpu.SemaphoreType.DMA((ranks,)),
+            pltpu.SemaphoreType.DMA((16,)),
+        ],
+        compiler_params=pltpu.CompilerParams(
+            collective_id=1, has_side_effects=True, vmem_limit_bytes=48 * 2**20
+        ),
+    )(tok, pack, cosr, sinr, kb, qb, cot, wq, wk, wv, wo, sg, su, eg, eu)
+
+
+def angles_of(block_deal, rows_dev):
+    here = places(lax.axis_index("ctx") * rows_dev, rows_dev, block_deal, rows_dev)
+    half_size = HD // 2
+    frequency = 10000.0 ** (-jnp.arange(half_size, dtype=F32) / half_size)
+    angles = here.astype(F32)[:, None] * frequency[None, :]
+    cosine, sine = jnp.cos(angles), jnp.sin(angles)
+    cosr = jnp.concatenate([cosine] * 4, axis=1)
+    sinr = jnp.concatenate([-sine, sine, -sine, sine], axis=1)
+    return here, cosr, sinr
+
+
+def pack_params(gain_one, gain_two, router):
+    width = 4 * gain_one.shape[0]
+    shard = jnp.concatenate(
+        [gain_one[None], gain_two[None], router.T, jnp.zeros((6, gain_one.shape[0]), BF)], axis=0
+    ).astype(F32)
+    start = lax.axis_index("wt") * gain_one.shape[0]
+    return lax.dynamic_update_slice(jnp.zeros((16, width), F32), shard, (0, start))
 
 
 def contract_product(left, right, left_dim, right_dim):
@@ -510,6 +906,330 @@
     )
 
 
+def fast_body(
+    tokens,
+    cotangent,
+    gain_attention,
+    query_weight,
+    key_weight,
+    value_weight,
+    output_weight,
+    gain_mixer,
+    router_weight,
+    shared_gate,
+    shared_up,
+    shared_down,
+    expert_gate,
+    expert_up,
+    expert_down,
+    routes,
+    slot_order,
+    block_deal,
+):
+    rows_dev = tokens.shape[1]
+    width = tokens.shape[2]
+    ranks = lax.axis_size("ctx")
+    heads = width // HD
+    inputs = tokens[0].astype(jnp.float32)
+    here, cosr, sinr = angles_of(block_deal, rows_dev)
+    query_side_block = here // BLK
+    kb = (places(0, ranks * rows_dev, block_deal, rows_dev) // BLK)[None, :]
+    qb = jnp.concatenate([query_side_block, query_side_block])[:, None]
+    pack = pack_params(gain_attention, gain_mixer, router_weight)
+    (q_st, kv_all, mixed_f, lse, second, mixer, normed, pack_all, wfull, sg_sl, su_sl, expert_gate_whole, expert_up_whole, cot4) = run_forward(
+        tokens[0], pack, cosr, sinr, kb, qb, cotangent[0], query_weight, key_weight, value_weight, output_weight, shared_gate, shared_up, expert_gate, expert_up)
+    gain_first, gain_second = pack_all[0], pack_all[1]
+    router_full = pack_all[2:10].T.astype(jnp.bfloat16)
+    query_full, key_full, value_full, output_full = wfull[0], wfull[1], wfull[2], wfull[3]
+    sgate_full = lax.all_gather(shared_gate, "wt", axis=0, tiled=True)
+    sup_full = lax.all_gather(shared_up, "wt", axis=0, tiled=True)
+    sdown_full = lax.all_gather(shared_down, "wt", axis=0, tiled=True)
+    edown_full = lax.all_gather(expert_down, "wt", axis=0, tiled=True)
+    query_rot = (8.0 * (q_st[:, :rows_dev] + q_st[:, rows_dev:])).astype(jnp.bfloat16).transpose(1, 0, 2).reshape(rows_dev, width)
+    query3 = query_rot.reshape(rows_dev, heads, HD)
+    query_side = (query3, query_side_block)
+    log_total = lse[:, :, 0].reshape(heads, rows_dev)
+    mixed3 = mixed_f.reshape(rows_dev, heads, HD)
+    scale_one = lax.rsqrt(jnp.mean(inputs * inputs, axis=-1, keepdims=True) + EPS)
+    scale_two = lax.rsqrt(jnp.mean(second * second, axis=-1, keepdims=True) + EPS)
+    key_rot = kv_all[lax.axis_index("ctx"), :, :width]
+    mixed_low = mixed3.reshape(rows_dev, width).astype(jnp.bfloat16)
+    experts = router_full.shape[1]
+    logits = jnp.dot(mixer, router_full, preferred_element_type=jnp.float32)
+    route = routes[0]
+    top_count = route.shape[1]
+    pair_count = rows_dev * top_count
+    capacity = (5 * pair_count + 4 * experts - 1) // (4 * experts)
+    split_count = ranks // experts
+    expert_match = route[:, :, None] == jnp.arange(experts, dtype=jnp.int32)[None, None, :]
+    chosen = jnp.sum(jnp.where(expert_match, logits[:, None, :], 0.0), axis=2)
+    gates = jax.nn.softmax(chosen, axis=1)
+    target, kept_pairs, slot_table = assign_slots(route, slot_order[0, 0], experts, capacity)
+    valid = slot_table < pair_count
+    pair_pick = jnp.minimum(slot_table, pair_count - 1)
+    target_pick = jnp.minimum(target, experts * capacity - 1)
+    send_rows = jnp.where(
+        valid[:, None], mixer[pair_pick // top_count], jnp.zeros((), jnp.bfloat16)
+    )
+    send_rows = jnp.broadcast_to(
+        send_rows.reshape(experts, 1, capacity, width), (experts, split_count, capacity, width)
+    ).reshape(ranks, capacity, width)
+    received = lax.all_to_all(send_rows, "ctx", split_axis=0, concat_axis=0, tiled=True)
+    slot_count = received.shape[1]
+    flattened_input = received.reshape(ranks * slot_count, width)
+    gate_part = jnp.dot(flattened_input, expert_gate_whole, preferred_element_type=jnp.float32)
+    up_projection_part = jnp.dot(
+        flattened_input, expert_up_whole, preferred_element_type=jnp.float32
+    )
+    activated, unused = silu_parts(gate_part)
+    hidden = (activated * up_projection_part).astype(jnp.bfloat16)
+    partial_value = contract_product(hidden, edown_full, 1, 1).reshape(ranks, slot_count, width)
+    back = lax.all_to_all(
+        partial_value.astype(jnp.bfloat16), "ctx", split_axis=0, concat_axis=0, tiled=True
+    ).astype(partial_value.dtype)
+    expert_gate_part = gate_part.reshape(ranks, slot_count, -1)
+    expert_up_part = up_projection_part.reshape(ranks, slot_count, -1)
+    combined = jnp.sum(back.reshape(experts, split_count, capacity, width), axis=1).reshape(
+        experts * capacity, width
+    )
+    pair_out = jnp.where(kept_pairs[:, None], combined[target_pick], 0.0).reshape(
+        rows_dev, top_count, width
+    )
+    mixture = jnp.sum(gates[:, :, None] * pair_out, axis=1)
+    sgate_part = jnp.dot(mixer, sgate_full, preferred_element_type=jnp.float32)
+    sup_part = jnp.dot(mixer, sup_full, preferred_element_type=jnp.float32)
+    shared_act, shared_slope = silu_parts(sgate_part)
+    shared_hidden = (shared_act * sup_part).astype(jnp.bfloat16)
+    shared_out = jnp.dot(shared_hidden, sdown_full, preferred_element_type=jnp.float32)
+    result = (second + mixture + shared_out).astype(jnp.bfloat16)
+    grad_final = cotangent[0].astype(jnp.float32)
+    grad_low = grad_final.astype(jnp.bfloat16)
+    sdown_grad = contract_product(shared_hidden, grad_low, 0, 0)
+    grad_shared_hidden = contract_product(grad_low, sdown_full, 1, 1)
+    grad_sgate = (grad_shared_hidden * sup_part * shared_slope).astype(jnp.bfloat16)
+    grad_sup = (grad_shared_hidden * shared_act).astype(jnp.bfloat16)
+    sgate_grad = contract_product(mixer, grad_sgate, 0, 0)
+    sup_grad = contract_product(mixer, grad_sup, 0, 0)
+    grad_mixer = contract_product(grad_sgate, sgate_full, 1, 1) + contract_product(
+        grad_sup, sup_full, 1, 1
+    )
+    pair_grad = (
+        (gates[:, :, None] * grad_final[:, None, :]).reshape(pair_count, width).astype(jnp.bfloat16)
+    )
+    grad_gates = jnp.sum(grad_final[:, None, :] * pair_out, axis=2)
+    send_grad = jnp.where(valid[:, None], pair_grad[pair_pick], jnp.zeros((), jnp.bfloat16))
+    send_grad = jnp.broadcast_to(
+        send_grad.reshape(experts, 1, capacity, width), (experts, split_count, capacity, width)
+    ).reshape(ranks, capacity, width)
+    recv_grad = lax.all_to_all(send_grad, "ctx", split_axis=0, concat_axis=0, tiled=True)
+    flattened_input = received.reshape(ranks * capacity, width)
+    flat_grad = recv_grad.reshape(ranks * capacity, width)
+    gate_flat = expert_gate_part.reshape(ranks * capacity, -1)
+    up_flat = expert_up_part.reshape(ranks * capacity, -1)
+    expert_activation, expert_slope = silu_parts(gate_flat)
+    expert_hidden = (expert_activation * up_flat).astype(jnp.bfloat16)
+    edown_grad = contract_product(flat_grad, expert_hidden, 0, 0)
+    expert_hidden_grad = jnp.dot(flat_grad, edown_full, preferred_element_type=jnp.float32)
+    expert_gate_grad_rows = (expert_hidden_grad * up_flat * expert_slope).astype(jnp.bfloat16)
+    expert_up_grad_rows = (expert_hidden_grad * expert_activation).astype(jnp.bfloat16)
+    egate_grad = contract_product(flattened_input, expert_gate_grad_rows, 0, 0)
+    expert_up_weight_grad = contract_product(flattened_input, expert_up_grad_rows, 0, 0)
+    input_back = (
+        contract_product(expert_gate_grad_rows, expert_gate_whole, 1, 1)
+        + contract_product(expert_up_grad_rows, expert_up_whole, 1, 1)
+    ).reshape(ranks, capacity, width)
+    back_grad = lax.all_to_all(
+        input_back.astype(jnp.bfloat16), "ctx", split_axis=0, concat_axis=0, tiled=True
+    ).astype(input_back.dtype)
+    merged = jnp.sum(back_grad.reshape(experts, split_count, capacity, width), axis=1).reshape(
+        experts * capacity, width
+    )
+    pair_back = jnp.where(kept_pairs[:, None], merged[target_pick], 0.0).reshape(
+        rows_dev, top_count, width
+    )
+    grad_mixer = grad_mixer + jnp.sum(pair_back, axis=1)
+    grad_chosen = gates * (grad_gates - jnp.sum(gates * grad_gates, axis=1, keepdims=True))
+    grad_logits = jnp.sum(jnp.where(expert_match, grad_chosen[:, :, None], 0.0), axis=1)
+    router_grad = contract_exact(mixer.astype(jnp.float32), grad_logits, 0, 0)
+    grad_mixer = grad_mixer + contract_exact(grad_logits, router_full.astype(jnp.float32), 1, 1)
+    through_two, gain_two_grad = rms_back(second, scale_two, gain_second, grad_mixer)
+    grad_second = grad_final + through_two
+    grad_attention = grad_second.astype(jnp.bfloat16)
+    output_grad = contract_product(mixed_low, grad_attention, 0, 0)
+    grad_mixed = contract_product(grad_attention, output_full, 1, 1).astype(jnp.bfloat16)
+    grad_out3 = grad_mixed.reshape(rows_dev, heads, HD)
+    delta = jnp.sum(grad_out3.astype(jnp.float32) * mixed3, axis=2).T
+    all_keys, all_values = (
+        kv_all[:, :, :width].reshape(ranks * rows_dev, width),
+        kv_all[:, :, width:].reshape(ranks * rows_dev, width),
+    )
+    total_rows = all_keys.shape[0]
+    block_size = KEY_ROWS
+
+    def query_step(grad_sum, offset):
+        key_rows = lax.dynamic_slice_in_dim(all_keys, offset, block_size, 0)
+        value_rows = lax.dynamic_slice_in_dim(all_values, offset, block_size, 0)
+        key_place = places(offset, block_size, block_deal, rows_dev)
+        unused, grad_scores = differentiate(
+            query_side, log_total, delta, grad_out3, key_rows, value_rows, key_place
+        )
+        key3 = key_rows.reshape(block_size, heads, HD)
+        return (
+            grad_sum
+            + jnp.einsum("hqk,khd->qhd", grad_scores, key3, preferred_element_type=jnp.float32),
+            None,
+        )
+
+    offsets = jnp.arange(total_rows // block_size, dtype=jnp.int32) * block_size
+    grad_query3, unused = lax.scan(
+        query_step, jnp.zeros((rows_dev, heads, HD), jnp.float32), offsets
+    )
+    inner_size = KEY_ROWS
+
+    def one_part(offset):
+        key_rows = lax.dynamic_slice_in_dim(all_keys, offset, inner_size, 0)
+        value_rows = lax.dynamic_slice_in_dim(all_values, offset, inner_size, 0)
+        key_place = places(offset, inner_size, block_deal, rows_dev)
+        probs_full, grad_scores = differentiate(
+            query_side, log_total, delta, grad_out3, key_rows, value_rows, key_place
+        )
+        grad_value_rows = jnp.einsum(
+            "hqk,qhd->khd",
+            probs_full.astype(jnp.bfloat16),
+            grad_out3,
+            preferred_element_type=jnp.float32,
+        )
+        grad_key_rows = jnp.einsum(
+            "hqk,qhd->khd", grad_scores, query3, preferred_element_type=jnp.float32
+        )
+        return jnp.concatenate(
+            [grad_key_rows.reshape(inner_size, width), grad_value_rows.reshape(inner_size, width)],
+            axis=1,
+        )
+
+    parts = lax.map(
+        one_part,
+        jnp.arange(lax.axis_size("ctx") * rows_dev // inner_size, dtype=jnp.int32) * inner_size,
+    )
+    key_value_grad = lax.psum_scatter(
+        parts.reshape(lax.axis_size("ctx") * rows_dev, 2 * width),
+        "ctx",
+        scatter_dimension=0,
+        tiled=True,
+    )
+    grad_key_pre = rotate(key_value_grad[:, :width], here, -1.0).astype(jnp.bfloat16)
+    grad_value_low = key_value_grad[:, width:].astype(jnp.bfloat16)
+    grad_query_pre = rotate(grad_query3.reshape(rows_dev, width), here, -1.0).astype(jnp.bfloat16)
+    query_grad = contract_product(normed, grad_query_pre, 0, 0)
+    key_grad = contract_product(normed, grad_key_pre, 0, 0)
+    value_grad = contract_product(normed, grad_value_low, 0, 0)
+    grad_normed = (
+        contract_product(grad_query_pre, query_full, 1, 1)
+        + contract_product(grad_key_pre, key_full, 1, 1)
+        + contract_product(grad_value_low, value_full, 1, 1)
+    )
+    through_one, gain_one_grad = rms_back(inputs, scale_one, gain_first, grad_normed)
+    grad_input = grad_second + through_one
+    (
+        gain_one_share,
+        query_share,
+        key_share,
+        value_share,
+        output_share,
+        gain_two_share,
+        router_share,
+        sgate_share,
+        sup_share,
+        sdown_share,
+        egate_share,
+        expert_up_portion,
+        edown_share,
+    ) = (
+        lax.psum_scatter(
+            gain_one_grad.astype(jnp.bfloat16), "wt", scatter_dimension=0, tiled=True
+        ).astype(jnp.float32),
+        lax.psum_scatter(
+            query_grad.astype(jnp.bfloat16), "wt", scatter_dimension=0, tiled=True
+        ).astype(jnp.float32),
+        lax.psum_scatter(
+            key_grad.astype(jnp.bfloat16), "wt", scatter_dimension=0, tiled=True
+        ).astype(jnp.float32),
+        lax.psum_scatter(
+            value_grad.astype(jnp.bfloat16), "wt", scatter_dimension=0, tiled=True
+        ).astype(jnp.float32),
+        lax.psum_scatter(
+            output_grad.astype(jnp.bfloat16), "wt", scatter_dimension=0, tiled=True
+        ).astype(jnp.float32),
+        lax.psum_scatter(
+            gain_two_grad.astype(jnp.bfloat16), "wt", scatter_dimension=0, tiled=True
+        ).astype(jnp.float32),
+        lax.psum_scatter(
+            router_grad.astype(jnp.bfloat16), "wt", scatter_dimension=0, tiled=True
+        ).astype(jnp.float32),
+        lax.psum_scatter(
+            sgate_grad.astype(jnp.bfloat16), "wt", scatter_dimension=0, tiled=True
+        ).astype(jnp.float32),
+        lax.psum_scatter(
+            sup_grad.astype(jnp.bfloat16), "wt", scatter_dimension=0, tiled=True
+        ).astype(jnp.float32),
+        lax.psum_scatter(
+            sdown_grad.astype(jnp.bfloat16), "wt", scatter_dimension=0, tiled=True
+        ).astype(jnp.float32),
+        lax.psum_scatter(
+            egate_grad.astype(jnp.bfloat16), "wt", scatter_dimension=0, tiled=True
+        ).astype(jnp.float32),
+        lax.psum_scatter(
+            expert_up_weight_grad.astype(jnp.bfloat16), "wt", scatter_dimension=0, tiled=True
+        ).astype(jnp.float32),
+        lax.psum_scatter(
+            edown_grad.astype(jnp.bfloat16), "wt", scatter_dimension=0, tiled=True
+        ).astype(jnp.float32),
+    )
+    (
+        gain_one_sum,
+        query_sum,
+        key_sum,
+        value_sum,
+        output_sum,
+        gain_two_sum,
+        router_sum,
+        sgate_sum,
+        sup_sum,
+        sdown_sum,
+    ) = lax.psum(
+        (
+            gain_one_share,
+            query_share,
+            key_share,
+            value_share,
+            output_share,
+            gain_two_share,
+            router_share,
+            sgate_share,
+            sup_share,
+            sdown_share,
+        ),
+        "ctx",
+    )
+    return (
+        result[None],
+        grad_input[None],
+        gain_one_sum,
+        query_sum,
+        key_sum,
+        value_sum,
+        output_sum,
+        gain_two_sum,
+        router_sum,
+        sgate_sum,
+        sup_sum,
+        sdown_sum,
+        egate_share,
+        expert_up_portion,
+        edown_share,
+    )
+
+
 def solution(mesh):
     in_specs = (
         P("wt", "ctx", None),
@@ -548,4 +1268,5 @@
         P("wt", "ctx"),
         P("wt", "ctx"),
     )
-    return jax.shard_map(body, mesh=mesh, in_specs=in_specs, out_specs=out_specs, check_vma=False)
+    chosen = fast_body if (mesh.shape["ctx"], mesh.shape["wt"]) == (8, 4) else body
+    return jax.shard_map(chosen, mesh=mesh, in_specs=in_specs, out_specs=out_specs, check_vma=False)

time: 1230 us -> 1140 us (0.927)
  waiting for transfers between devices: 630 us -> 429 us
  Pallas kernels: 0 us -> 140 us
  blocking collectives: 298 us -> 285 us
    all_gather x12 -> x4, waiting for transfers between devices: 199 us -> 0.02 us  [the longest x1 0.02 us: fast_body(): sdown_full = lax.all_gather(shared_down, 'wt', axis=0, tiled=True)]
    pallas_call x0 -> x1, Pallas kernels: none -> 140 us  [run_forward(): pl.pallas_call(forward_kernel, out_shape=(shape((pairs, 2 * rows, PAIR),...]
    unnamed x25 -> x17, waiting for transfers between devices: 19.3 us -> 2.33 us
    dot_general x13 -> x7, matrix products: 34.8 us -> 22.5 us  [the longest x1 5.58 us: fast_body(): jnp.dot(flat_grad, edown_full, preferred_element_type=jnp.float32)]
  transfers between devices with their start and end apart: 28 -> 20, of which waited for: 24 -> 14; matrix products, arithmetic and copies ran while one was open for 14% -> 14% of each run, Pallas kernels for 0% -> 12%
where the time goes in v1:
time: 1140 us; the launch traced here: 1130 us
  waiting for transfers between devices  429 us (38%)
  blocking collectives  285 us (25%)
  Pallas kernels  140 us (12%)
  matrix products  116 us (10%)
  local copies, waits for them, and re-layouts  80.8 us (7%)
  other arithmetic  38.3 us (3%)
  starting transfers between devices  21.2 us (2%)
  between operations  15.9 us (1%)
    psum x1, blocking collectives, fast_body(): lax.psum((gain_one_share, query_share, key_share, value_share, output_sha...  279 us
    pallas_call x1, Pallas kernels, run_forward(): pl.pallas_call(forward_kernel, out_shape=(shape((pairs, 2 * rows, PAIR),...  140 us
    reduce_scatter x1, waiting for transfers between devices, fast_body(): lax.psum_scatter(parts.reshape(lax.axis_size('ctx') * rows_dev, 2 * width...  84.7 us
    dot_general x20, matrix products, contract_product(): lax.dot_general(left, right, (((left_dim,), (right_dim,)), ((), ())), pre...  57.4 us
    reduce_scatter x1, waiting for transfers between devices, fast_body(): lax.psum_scatter(sgate_grad.astype(jnp.bfloat16), 'wt', scatter_dimension...  40.7 us
    reduce_scatter x1, waiting for transfers between devices, fast_body(): lax.psum_scatter(sup_grad.astype(jnp.bfloat16), 'wt', scatter_dimension=0...  40.5 us
    reduce_scatter x1, waiting for transfers between devices, fast_body(): lax.psum_scatter(edown_grad.astype(jnp.bfloat16), 'wt', scatter_dimension...  40.5 us
    reduce_scatter x1, waiting for transfers between devices, fast_body(): lax.psum_scatter(sdown_grad.astype(jnp.bfloat16), 'wt', scatter_dimension...  40.5 us
  transfers between devices with their start and end apart: 20, of which 14 were waited for; matrix products, arithmetic and copies ran while one was open for 14% of the time, Pallas kernels for 12%

profile of v1, /device:TPU:0, one launch (start us, length us, event | category | flops | bytes accessed | tf_op | source)
XLA Modules:
  0.0 1133.6 jit_solution(12420269607899317326)
XLA Ops:
  23.9 140.1 %shard_map.289 = (bf16[6,256,128]{2,1,0:T(8,128)(2,1)S(1)}, bf16[8,128,1536]{2,1,0:T(8,128)(2,1)}, f32[128,768]{1,0:T(8,128)S(1)}, f32[6,256,128]{2,1,0:T(8,128)...) custom-call(bf16[128,768]{1,0:T(8,128)(2,1)S(1)} %bitcast.285, ...), custom_call_target="tpu_custom_call" | custom-call | tf_op jit(solution)/shard_map/pallas_call | solution.py:355
  168.2 5.8 all-to-all-start
  177.5 2.6 mul.446
  182.7 4.1 fusion.105
  186.7 2.6 copy.140
  189.3 2.6 copy.142
  192.1 3.3 fusion.108
  196.9 3.4 multiply_convert_fusion.2
  200.3 4.3 convolution_convert_fusion.10
  204.7 6.0 all-to-all-start.1
  211.5 12.9 %all-to-all-done.1 = bf16[8,40,768]{2,1,0:T(8,128)(2,1)S(1)} async-done(((bf16[8,40,768]{2,1,0:T(8,128)(2,1)}), bf16[8,40,768]{2,1,0:T(8,128)(2,1)S(1)}, u32[]{:S(2)}, u32[]{:S(2)}) %all-to-all-start.1) | async-done | bytes 491552 | tf_op jit(solution)/shard_map/all_to_all | solution.py:987
  232.9 3.6 all-to-all-start.2
  237.1 3.4 fusion.109
  240.5 3.4 fusion.110
  244.0 6.6 all-to-all-done.2
  250.5 5.6 multiply_convert_fusion
  261.0 4.1 all-to-all-start.3
  265.4 4.7 multiply_convert_fusion.3
  274.7 4.0 all-to-all-done.3
  283.4 4.0 select_reduce_fusion.2
  287.4 3.1 fusion.49
  296.3 54.3 %while.29 = (s32[]{:T(128)}, f32[2,512,1536]{2,1,0:T(8,128)}, s32[2]{0:T(128)}, s32[8]{0:T(128)S(1)}, s32[128]{0:T(128)S(1)}, /*index=5*/bf16[1024,768]{0,1:T(8,...) while((s32[]{:T(128)}, f32[2,512,1536]{2,1,0:T(8,128)}, ...), condition=%wide.wide.region_24.25_spmd, body=%wide.wide.region_22.24_spmd.sunk | while | flops 413770752 | bytes 43506976 | solution.py:1110
  299.5 2.8 constant_dynamic-slice_fusion.8
  306.1 5.2 fusion.212
  311.3 3.0 fusion.211
  316.2 3.5 copy.173
  319.7 3.7 constant_dynamic-update-slice_fusion.3
  326.6 2.8 constant_dynamic-slice_fusion.8
  333.2 5.2 fusion.212
  338.3 3.0 fusion.211
  343.3 3.5 copy.173
  346.8 3.8 constant_dynamic-update-slice_fusion.3
  352.4 2.5 convolution_convert_fusion.6
  355.1 3.7 convolution_convert_fusion.5
  358.9 3.7 convolution_convert_fusion.4
  362.7 2.7 convolution_convert_fusion.3
  366.4 4.8 convolution_convert_fusion
  372.3 4.9 convolution_convert_fusion.2
  377.3 4.8 convolution_convert_fusion.1
  383.1 84.7 %reduce-scatter.15.cloned.1.call-done = f32[128,1536]{1,0:T(8,128)} async-done(((f32[1024,1536]{1,0:T(8,128)}), f32[128,1536]{1,0:T(8,128)}) %reduce-scatter.15.cloned.1.call-update) | async-done | bytes 786448 | tf_op jit(solution)/shard_map/reduce_scatter | solution.py:1114
  467.8 2.5 convolution_convert_fusion.7
  470.6 27.8 %while.30 = (s32[]{:T(128)}, f32[128,12,64]{0,2,1:T(8,128)}, s32[2]{0:T(128)S(1)}, bf16[1024,768]{0,1:T(8,128)(2,1)S(1)}, s32[8]{0:T(128)S(1)}, /*index=5*/s32[1...) while((s32[]{:T(128)}, f32[128,12,64]{0,2,1:T(8,128)}, ...), condition=%wide.wide.region_21.22_spmd.clone, body=%wide.wide.region_19.21_spmd.clone.sunk | while | flops 308585472 | bytes 13132529 | solution.py:1084
  473.2 2.8 constant_dynamic-slice_fusion.9
  476.0 2.3 fusion.218
  479.9 4.7 fusion.219
  487.1 2.8 constant_dynamic-slice_fusion.9
  489.9 2.3 fusion.218
  493.7 4.7 fusion.219
  506.3 3.2 fusion.64
  509.5 8.4 reduce-scatter.23.cloned.1.call-done
  517.9 40.7 %reduce-scatter.25.cloned.1.call-done = bf16[192,2048]{1,0:T(8,128)(2,1)} async-done(((bf16[768,2048]{1,0:T(8,128)(2,1)}), bf16[192,2048]{1,0:T(8,128)(2,1)}) %reduce-scatter.25.cloned.1.call-update) | async-done | bytes 786448 | tf_op jit(solution)/shard_map/reduce_scatter | solution.py:1169
  558.6 40.5 %reduce-scatter.27.cloned.1.call-done = bf16[192,2048]{1,0:T(8,128)(2,1)} async-done(((bf16[768,2048]{1,0:T(8,128)(2,1)}), bf16[192,2048]{1,0:T(8,128)(2,1)}) %reduce-scatter.27.cloned.1.call-update) | async-done | bytes 786448 | tf_op jit(solution)/shard_map/reduce_scatter | solution.py:1172
  599.1 40.5 %reduce-scatter.29.cloned.1.call-done = bf16[512,768]{1,0:T(8,128)(2,1)} async-done(((bf16[2048,768]{1,0:T(8,128)(2,1)}), bf16[512,768]{1,0:T(8,128)(2,1)}) %reduce-scatter.29.cloned.1.call-update) | async-done | bytes 786448 | tf_op jit(solution)/shard_map/reduce_scatter | solution.py:1175
  639.6 40.5 %reduce-scatter.35.cloned.1.call-done = bf16[192,2048]{1,0:T(8,128)(2,1)} async-done(((bf16[768,2048]{1,0:T(8,128)(2,1)}), bf16[192,2048]{1,0:T(8,128)(2,1)}) %reduce-scatter.35.cloned.1.call-update) | async-done | bytes 786448 | tf_op jit(solution)/shard_map/reduce_scatter | solution.py:1184
  680.2 2.5 convert_element_type.262
  682.6 38.1 %reduce-scatter.31.cloned.1.call-done = bf16[192,2048]{1,0:T(8,128)(2,1)} async-done(((bf16[768,2048]{1,0:T(8,128)(2,1)}), bf16[192,2048]{1,0:T(8,128)(2,1)}) %reduce-scatter.31.cloned.1.call-update) | async-done | bytes 786448 | tf_op jit(solution)/shard_map/reduce_scatter | solution.py:1178
  720.7 2.5 convert_element_type.258
  723.2 38.1 %reduce-scatter.33.cloned.1.call-done = bf16[192,2048]{1,0:T(8,128)(2,1)} async-done(((bf16[768,2048]{1,0:T(8,128)(2,1)}), bf16[192,2048]{1,0:T(8,128)(2,1)}) %reduce-scatter.33.cloned.1.call-update) | async-done | bytes 786448 | tf_op jit(solution)/shard_map/reduce_scatter | solution.py:1181
  761.2 2.5 convert_element_type.260
  769.4 5.8 all-reduce.3
  776.2 13.9 %reduce-scatter.21.cloned.1.call-done = bf16[192,768]{1,0:T(8,128)(2,1)} async-done(((bf16[768,768]{1,0:T(8,128)(2,1)}), bf16[192,768]{1,0:T(8,128)(2,1)}) %reduce-scatter.21.cloned.1.call-update) | async-done | bytes 294928 | tf_op jit(solution)/shard_map/reduce_scatter | solution.py:1157
  790.1 28.7 %reduce-scatter.19.cloned.1.call-done = bf16[192,768]{1,0:T(8,128)(2,1)} async-done(((bf16[768,768]{1,0:T(8,128)(2,1)}), bf16[192,768]{1,0:T(8,128)(2,1)}) %reduce-scatter.19.cloned.1.call-update) | async-done | bytes 294928 | tf_op jit(solution)/shard_map/reduce_scatter | solution.py:1154
  818.9 28.9 %reduce-scatter.17.cloned.1.call-done = bf16[192,768]{1,0:T(8,128)(2,1)} async-done(((bf16[768,768]{1,0:T(8,128)(2,1)}), bf16[192,768]{1,0:T(8,128)(2,1)}) %reduce-scatter.17.cloned.1.call-update) | async-done | bytes 294928 | tf_op jit(solution)/shard_map/reduce_scatter | solution.py:1151
  847.8 278.8 %all-reduce.5 = (f32[192]{0:T(256)}, f32[192,768]{1,0:T(8,128)}, f32[192,768]{1,0:T(8,128)}, f32[192,768]{1,0:T(8,128)}, f32[192,768]{1,0:T(8,128)}, /*index=5*/...) all-reduce(f32[192]{0:T(256)S(1)} %dynamic-slice_convert_fusion.1, ...), channel_id=1, replica_groups=mesh['ctx'=8,'wt'=4] {'ctx'}, use_global_device_ids=true, to_apply=%region_29.30 | all-reduce | flops 1771392 | bytes 10629120 | tf_op jit(solution)/shard_map/psum | solution.py:1199
  (291 shorter events, 95.9 us)
Async XLA Ops:
  7.2 13.1 %copy-start.34 = (s32[8]{0:T(128)S(1)}, s32[8]{0:T(128)}, u32[]{:S(2)}) copy-start(s32[8]{0:T(128)} %param.39) | copy-start | bytes 100
  7.2 12.7 %copy-start.46 = (bf16[192,8]{0,1:T(8,128)(2,1)S(1)}, bf16[192,8]{0,1:T(8,128)(2,1)}, u32[]{:S(2)}) copy-start(bf16[192,8]{0,1:T(8,128)(2,1)} %param.30) | copy-start | bytes 9220
  7.2 14.7 %copy-start = (bf16[1,128,768]{2,1,0:T(8,128)(2,1)S(1)}, bf16[1,128,768]{2,1,0:T(8,128)(2,1)}, u32[]{:S(2)}) copy-start(bf16[1,128,768]{2,1,0:T(8,128)(2,1)} %param.22) | copy-start | bytes 589828
  7.2 14.7 %copy-start.1 = (bf16[1,128,768]{2,1,0:T(8,128)(2,1)S(1)}, bf16[1,128,768]{2,1,0:T(8,128)(2,1)}, u32[]{:S(2)}) copy-start(bf16[1,128,768]{2,1,0:T(8,128)(2,1)} %param.23) | copy-start | bytes 589828
  7.2 14.7 %copy-start.2 = (bf16[192,768]{1,0:T(8,128)(2,1)S(1)}, bf16[192,768]{1,0:T(8,128)(2,1)}, u32[]{:S(2)}) copy-start(bf16[192,768]{1,0:T(8,128)(2,1)} %wq.1) | copy-start | bytes 884740
  7.2 14.7 %copy-start.3 = (bf16[192,768]{1,0:T(8,128)(2,1)S(1)}, bf16[192,768]{1,0:T(8,128)(2,1)}, u32[]{:S(2)}) copy-start(bf16[192,768]{1,0:T(8,128)(2,1)} %wk.1) | copy-start | bytes 884740
  7.2 193.1 %all-gather.5.cloned.1.call-start = ((), (), s32[]{:S(2)}) async-start(), calls=%async_computation.16 | async-start | bytes 3932160 | tf_op jit(solution)/shard_map/all_gather | solution.py:947
  8.0 229.1 %all-gather.7.cloned.1.call-start = ((), (), s32[]{:S(2)}) async-start(), calls=%async_computation.17 | async-start | bytes 3932160 | tf_op jit(solution)/shard_map/all_gather | solution.py:944
  8.7 231.8 %all-gather.9.cloned.1.call-start = ((), (), s32[]{:S(2)}) async-start(), calls=%async_computation.18 | async-start | bytes 3932160 | tf_op jit(solution)/shard_map/all_gather | solution.py:945
  17.7 2.6 copy-start.50
  19.8 147.5 %copy-start.43 = (pred[8,40]{1,0:T(8,128)(4,1)}, pred[8,40]{1,0:T(8,128)(4,1)S(1)}, u32[]{:S(2)}) copy-start(pred[8,40]{1,0:T(8,128)(4,1)S(1)} %broadcast_in_dim.298) | copy-start | bytes 964
  167.3 12.7 %copy-start.51 = (s32[256]{0:T(256)S(1)}, s32[256]{0:T(256)}, u32[]{:S(2)}) copy-start(s32[256]{0:T(256)} %copy-done.50) | copy-start | bytes 3076
  168.2 23.9 %all-to-all-start = ((bf16[8,40,768]{2,1,0:T(8,128)(2,1)}), bf16[8,40,768]{2,1,0:T(8,128)(2,1)S(1)}, u32[]{:S(2)}, u32[]{:S(2)}) async-start(bf16[8,40,768]{2,1,0:T(8,128)(2,1)} %broadcast_select_fusion.1), calls=%async_computation | async-start | bytes 983040 | tf_op jit(solution)/shard_map/all_to_all | solution.py:977
  174.0 91.4 %all-gather.11.cloned.1.call-start = ((), (), s32[]{:S(2)}) async-start(), calls=%async_computation.19 | async-start | bytes 3932160 | tf_op jit(solution)/shard_map/all_gather | solution.py:946
  180.0 6.7 copy-start.47
  182.0 4.7 copy-start.31
  192.1 8.2 copy-start.20
  192.1 4.8 copy-start.52
  200.3 10.3 copy-start.7
  200.3 10.5 copy-start.38
  200.3 11.0 copy-start.45
  204.7 19.7 %all-to-all-start.1 = ((bf16[8,40,768]{2,1,0:T(8,128)(2,1)}), bf16[8,40,768]{2,1,0:T(8,128)(2,1)S(1)}, u32[]{:S(2)}, u32[]{:S(2)}) async-start(bf16[8,40,768]{2,1,0:T(8,128)(2,1)} %bitcast.23), calls=%async_computation.1 | async-start | bytes 983040 | tf_op jit(solution)/shard_map/all_to_all | solution.py:987
  224.5 2.0 copy-start.48
  224.5 5.3 copy-start.37
  228.1 3.9 copy-start.44
  232.9 17.6 %all-to-all-start.2 = ((bf16[8,40,768]{2,1,0:T(8,128)(2,1)}), bf16[8,40,768]{2,1,0:T(8,128)(2,1)S(1)}, u32[]{:S(2)}, u32[]{:S(2)}) async-start(bf16[8,40,768]{2,1,0:T(8,128)(2,1)} %broadcast_select_fusion), calls=%async_computation.2 | async-start | bytes 983040 | tf_op jit(solution)/shard_map/all_to_all | solution.py:1024
  250.5 5.6 copy-start.27
  250.5 5.6 copy-start.14
  256.2 2.8 copy-start.53
  261.0 17.8 %all-to-all-start.3 = ((bf16[8,40,768]{2,1,0:T(8,128)(2,1)}), bf16[8,40,768]{2,1,0:T(8,128)(2,1)}, u32[]{:S(2)}, u32[]{:S(2)}) async-start(bf16[8,40,768]{2,1,0:T(8,128)(2,1)} %bitcast.28), calls=%async_computation.3 | async-start | bytes 983040 | tf_op jit(solution)/shard_map/all_to_all | solution.py:1041
  265.1 202.7 %reduce-scatter.15.cloned.1.call-start = ((), (), s32[]{:S(2)}) async-start(), calls=%async_computation.20 | async-start | bytes 7077888 | tf_op jit(solution)/shard_map/reduce_scatter | solution.py:1114
  265.4 5.5 copy-start.10
  270.0 17.4 %copy-start.18 = (bf16[128,2048]{1,0:T(8,128)(2,1)}, bf16[128,2048]{1,0:T(8,128)(2,1)S(1)}, u32[]{:S(2)}) copy-start(bf16[128,2048]{1,0:T(8,128)(2,1)S(1)} %get-tuple-element.649) | copy-start | bytes 1572868
  270.0 2.7 copy-start.11
  279.8 3.6 copy-start.33
  283.4 7.1 copy-start.35
  283.4 7.1 copy-start.49
  290.6 5.8 copy-start.8
  299.4 6.6 copy-start.42
  311.3 3.0 copy-start.9
  326.6 6.6 copy-start.42
  338.3 3.0 copy-start.9
  351.2 154.3 %reduce-scatter.37.cloned.1.call-start = ((), (), s32[]{:S(2)}) async-start(), calls=%async_computation.31 | async-start | bytes 245760
  352.3 165.6 %reduce-scatter.23.cloned.1.call-start = ((), (), s32[]{:S(2)}) async-start(), calls=%async_computation.24 | async-start | bytes 1474560 | tf_op jit(solution)/shard_map/reduce_scatter | solution.py:1160
  354.9 203.7 %reduce-scatter.25.cloned.1.call-start = ((), (), s32[]{:S(2)}) async-start(), calls=%async_computation.25 | async-start | bytes 3932160 | tf_op jit(solution)/shard_map/reduce_scatter | solution.py:1169
  358.8 3.9 copy-start.16
  358.8 240.3 %reduce-scatter.27.cloned.1.call-start = ((), (), s32[]{:S(2)}) async-start(), calls=%async_computation.26 | async-start | bytes 3932160 | tf_op jit(solution)/shard_map/reduce_scatter | solution.py:1172
  362.6 277.0 %reduce-scatter.29.cloned.1.call-start = ((), (), s32[]{:S(2)}) async-start(), calls=%async_computation.27 | async-start | bytes 3932160 | tf_op jit(solution)/shard_map/reduce_scatter | solution.py:1175
  365.4 314.7 %reduce-scatter.35.cloned.1.call-start = ((), (), s32[]{:S(2)}) async-start(), calls=%async_computation.30 | async-start | bytes 3932160 | tf_op jit(solution)/shard_map/reduce_scatter | solution.py:1184
  371.3 349.4 %reduce-scatter.31.cloned.1.call-start = ((), (), s32[]{:S(2)}) async-start(), calls=%async_computation.28 | async-start | bytes 3932160 | tf_op jit(solution)/shard_map/reduce_scatter | solution.py:1178
  377.2 384.0 %reduce-scatter.33.cloned.1.call-start = ((), (), s32[]{:S(2)}) async-start(), calls=%async_computation.29 | async-start | bytes 3932160 | tf_op jit(solution)/shard_map/reduce_scatter | solution.py:1181
  382.1 88.5 %copy-start.40 = (f32[12,128]{1,0:T(8,128)S(1)}, f32[12,128]{1,0:T(8,128)}, u32[]{:S(2)}) copy-start(f32[12,128]{1,0:T(8,128)} %copy-done.39) | copy-start | bytes 18436
  382.1 88.5 %copy-start.55 = (s32[2]{0:T(128)S(1)}, s32[2]{0:T(128)}, u32[]{:S(2)}) copy-start(s32[2]{0:T(128)} %get-tuple-element.1085) | copy-start | bytes 28
  382.1 408.0 %reduce-scatter.21.cloned.1.call-start = ((), (), s32[]{:S(2)}) async-start(), calls=%async_computation.23 | async-start | bytes 1474560 | tf_op jit(solution)/shard_map/reduce_scatter | solution.py:1157
  470.3 348.6 %reduce-scatter.19.cloned.1.call-start = ((), (), s32[]{:S(2)}) async-start(), calls=%async_computation.22 | async-start | bytes 1474560 | tf_op jit(solution)/shard_map/reduce_scatter | solution.py:1154
  500.9 3.2 copy-start.54
  500.9 5.4 copy-start.17
  500.9 5.4 copy-start.23
  502.5 345.3 %reduce-scatter.17.cloned.1.call-start = ((), (), s32[]{:S(2)}) async-start(), calls=%async_computation.21 | async-start | bytes 1474560 | tf_op jit(solution)/shard_map/reduce_scatter | solution.py:1151
  723.2 44.3 %copy-start.22 = (f32[128,1536]{1,0:T(8,128)S(1)}, f32[128,1536]{1,0:T(8,128)}, u32[]{:S(2)}) copy-start(f32[128,1536]{1,0:T(8,128)} %reduce-scatter.15.cloned.1.call-done) | copy-start | bytes 2359300
  763.7 5.7 copy-start.41
  763.7 11.6 %copy-start.13 = (f32[128,768]{1,0:T(8,128)S(1)}, f32[128,768]{1,0:T(8,128)}, u32[]{:S(2)}) copy-start(f32[128,768]{1,0:T(8,128)} %copy-done.12) | copy-start | bytes 1179652
  765.5 82.3 %copy-start.24 = (bf16[192,2048]{1,0:T(8,128)(2,1)S(1)}, bf16[192,2048]{1,0:T(8,128)(2,1)}, u32[]{:S(2)}) copy-start(bf16[192,2048]{1,0:T(8,128)(2,1)} %reduce-scatter.25.cloned.1.call-done) | copy-start | bytes 2359300
  765.5 82.3 %copy-start.29 = (bf16[192,768]{1,0:T(8,128)(2,1)S(1)}, bf16[192,768]{1,0:T(8,128)(2,1)}, u32[]{:S(2)}) copy-start(bf16[192,768]{1,0:T(8,128)(2,1)} %reduce-scatter.23.cloned.1.call-done) | copy-start | bytes 884740
  (16 other events, 14.8 us)
Sparse Core Ops, SparseCore 0:
  9.6 41.6 all-gather.4
  52.9 45.7 all-gather.6
  100.2 45.9 all-gather.8
  176.1 29.9 all-gather.10
  350.7 117.0 reduce-scatter.14
  470.1 18.8 reduce-scatter.36
  492.1 25.7 reduce-scatter.22
  520.6 37.9 reduce-scatter.24
  561.1 37.9 reduce-scatter.26
  601.6 37.9 reduce-scatter.28
  642.2 37.9 reduce-scatter.34
  682.7 37.9 reduce-scatter.30
  723.2 37.9 reduce-scatter.32
  764.4 25.7 reduce-scatter.20
  793.1 25.7 reduce-scatter.18
  822.0 25.6 reduce-scatter.16

commit v2 on v1

--- a/solution.py
+++ b/solution.py
@@ -407,6 +407,320 @@
     ).astype(F32)
     start = lax.axis_index("wt") * gain_one.shape[0]
     return lax.dynamic_update_slice(jnp.zeros((16, width), F32), shard, (0, start))
+
+
+def swish(values):
+    sigmoid = 1.0 / (1.0 + jnp.exp(-values))
+    return values * sigmoid, sigmoid * (1.0 + values * (1.0 - sigmoid))
+
+
+class Exchange:
+    def __init__(self, spot, out, back, send, recv):
+        self.spot, self.out, self.back = spot, out, back
+        self.send, self.recv, self.ranks = send, recv, out.shape[0]
+        self.copies = []
+
+    def start(self):
+        spot = self.spot
+        for offset in range(1, self.ranks):
+            peer = lax.rem(spot.k + offset, self.ranks)
+            self.copies.append(
+                remote(
+                    self.out.at[peer],
+                    self.back.at[spot.k],
+                    self.send.at[offset],
+                    self.recv.at[spot.k],
+                    (peer, spot.w),
+                )
+            )
+            self.copies[-1].start()
+        self.back[spot.k] = self.out[spot.k]
+
+    def finish(self):
+        spot = self.spot
+        for offset in range(1, self.ranks):
+            peer = lax.rem(spot.k + offset, self.ranks)
+            remote(
+                self.out.at[peer],
+                self.back.at[peer],
+                self.send.at[offset],
+                self.recv.at[peer],
+                (peer, spot.w),
+            ).wait_recv()
+
+    def drain(self):
+        for copy in self.copies:
+            copy.wait_send()
+
+
+def fold_rows(values, ref):
+    ranks = ref.shape[0]
+    slots = values.shape[0] // ranks
+    for e in range(ranks):
+        part = values[slots * e : slots * (e + 1)]
+        tiles = [part[:, 128 * t : 128 * (t + 1)] for t in range(values.shape[1] // 128)]
+        ref[e] = jnp.concatenate(tiles, axis=0).astype(BF)
+
+
+def unfold_rows(ref, slots):
+    parts = []
+    for e in range(ref.shape[0]):
+        part = ref[e].astype(F32)
+        tiles = [part[slots * t : slots * (t + 1)] for t in range(part.shape[0] // slots)]
+        parts.append(jnp.concatenate(tiles, axis=1))
+    return jnp.concatenate(parts, axis=0).astype(BF)
+
+
+def split_three(values):
+    high = values.astype(BF)
+    rest = values - high.astype(F32)
+    middle = rest.astype(BF)
+    return high, middle, (rest - middle.astype(F32)).astype(BF)
+
+
+def slot_maps(e_row, e_col, o_row, o_col, slots, experts):
+    pairs = e_row.shape[1]
+    down = lax.broadcasted_iota(jnp.int32, (pairs, pairs), 0)
+    along = lax.broadcasted_iota(jnp.int32, (pairs, pairs), 1)
+    turn_row = jnp.sum(jnp.where(o_col == along, down.astype(F32), 0.0), axis=0, keepdims=True)
+    turn_col = jnp.sum(jnp.where(o_row == down, along.astype(F32), 0.0), axis=1, keepdims=True)
+    same = e_col == e_row
+    slot_row = jnp.sum(
+        jnp.where(same & (turn_col < turn_row), 1.0, 0.0), axis=0, keepdims=True
+    ).astype(jnp.int32)
+    slot_col = jnp.sum(
+        jnp.where(same & (turn_row < turn_col), 1.0, 0.0), axis=1, keepdims=True
+    ).astype(jnp.int32)
+    target_row = jnp.where(slot_row < slots, e_row * slots + slot_row, -1)
+    target_col = jnp.where(slot_col < slots, e_col * slots + slot_col, -1)
+    total = experts * slots
+    place = lax.broadcasted_iota(jnp.int32, (total, pairs), 0)
+    to_slots = jnp.where(place == target_row, 1.0, 0.0).astype(BF)
+    place = lax.broadcasted_iota(jnp.int32, (pairs, total), 1)
+    to_pairs = jnp.where(place == target_col, 1.0, 0.0).astype(BF)
+    return to_slots, to_pairs
+
+
+def experts_kernel(
+    second_ref, mixer_ref, pack_ref, cot_ref, route_ref, e_row, e_col, o_row, o_col,
+    sd_ref, sg_ref, su_ref, cot4_ref, eg_ref, eu_ref, ed_ref,
+    result_out, grad_second_out, pack_grad_out, dsg_out, dsu_out, dsd_out,
+    dg_out, du_out, dd_out,
+    wg, wu, wd, m4, sh_send, sh_recv, gm_send, gm_recv,
+    xs, xr, gs, gr, os, orr, bs, br, x_s, g_s, sum_s,
+    gate_s, up_s, hid_s, dgate_s, dup_s, sem, a2a_send, a2a_recv,
+):
+    spot = Spot(4)
+    sems = Sems(sem)
+    rows, width = mixer_ref.shape
+    ranks = xs.shape[0]
+    slots = xs.shape[1] * 128 // width
+    hidden = wg.shape[1]
+    loads = [
+        pltpu.make_async_copy(eg_ref, wg, sems.new()),
+        pltpu.make_async_copy(eu_ref, wu, sems.new()),
+    ]
+    for copy in loads:
+        copy.start()
+    others = [(lax.rem(spot.k + o, ranks), spot.w) for o in range(1, ranks)]
+    greet([spot.core, spot.across, spot.corner] + others)
+    mixer = mixer_ref[...]
+    to_slots, to_pairs = slot_maps(
+        e_row[...], e_col[...], o_row[...], o_col[...], slots, ranks
+    )
+    fold_rows(nn(to_slots[:, :rows] + to_slots[:, rows:], mixer), xs)
+    rows_out = Exchange(spot, xs, xr, a2a_send.at[0], a2a_recv.at[0])
+    rows_out.start()
+    mixers = Spread(spot, lambda w: mixer_ref, lambda w: m4.at[w], sems)
+    down_w = Gather(spot, ed_ref, wd, sems)
+    pack = pack_ref[...]
+    router = pack[2:16].astype(BF)
+    router = jnp.concatenate([router, jnp.zeros((2, width), BF)], axis=0)
+    logits = nt(mixer, router)
+    lane = lax.broadcasted_iota(jnp.int32, logits.shape, 1)
+    matches = [lane == route_ref[:, j : j + 1] for j in range(2)]
+    chosen = [jnp.sum(jnp.where(m, logits, 0.0), axis=1, keepdims=True) for m in matches]
+    largest = jnp.maximum(chosen[0], chosen[1])
+    raised = [jnp.exp(c - largest) for c in chosen]
+    gates = [r / (raised[0] + raised[1]) for r in raised]
+    grad = cot_ref[...].astype(F32)
+    pair_grad = jnp.concatenate([(g * grad).astype(BF) for g in gates], axis=0)
+    fold_rows(nn(to_slots, pair_grad), gs)
+    grads_out = Exchange(spot, gs, gr, a2a_send.at[1], a2a_recv.at[1])
+    grads_out.start()
+
+    mixers.finish()
+    rows_all = m4[...].reshape(4 * rows, width)
+    grad_all = cot4_ref[...].reshape(4 * rows, width)
+    gate_part, up_part = nn(rows_all, sg_ref[...]), nn(rows_all, su_ref[...])
+    act, slope = swish(gate_part)
+    shared_hidden = (act * up_part).astype(BF)
+    sh_send[...] = nn(shared_hidden, sd_ref[...]).astype(BF).reshape(4, rows, width)
+    shared_out = Spread(spot, lambda w: sh_send.at[w], lambda w: sh_recv.at[w], sems)
+    hid_grad = nt(grad_all, sd_ref[...])
+    grad_gate = (hid_grad * up_part * slope).astype(BF)
+    grad_up = (hid_grad * act).astype(BF)
+    back = nt(grad_gate, sg_ref[...]) + nt(grad_up, su_ref[...])
+    gm_send[...] = back.astype(BF).reshape(4, rows, width)
+    shared_back = Spread(spot, lambda w: gm_send.at[w], lambda w: gm_recv.at[w], sems)
+    down_w.forward()
+    for copy in loads:
+        copy.wait()
+
+    rows_out.finish()
+    x_s[...] = unfold_rows(xr, slots)
+    block = 512
+
+    def parts(i):
+        return pl.ds(pl.multiple_of(block * i, block), block)
+
+    def up_step(i, carry):
+        at = parts(i)
+        gate = nn(x_s[...], wg[:, at])
+        up = nn(x_s[...], wu[:, at])
+        act, slope = swish(gate)
+        hid_s[:, at] = (act * up).astype(BF)
+        gate_s[:, at] = up * slope
+        up_s[:, at] = act
+        return carry
+
+    lax.fori_loop(0, hidden // block, up_step, 0)
+    down_w.finish()
+    sum_s[...] = nt(hid_s[...], wd[...])
+    fold_rows(sum_s[...], os)
+    outs = Exchange(spot, os, orr, a2a_send.at[2], a2a_recv.at[2])
+    outs.start()
+    grads_out.finish()
+    g_s[...] = unfold_rows(gr, slots)
+
+    def down_step(i, carry):
+        at = parts(i)
+        grad_hidden = nn(g_s[...], wd[:, at])
+        dgate_s[:, at] = (grad_hidden * gate_s[:, at]).astype(BF)
+        dup_s[:, at] = (grad_hidden * up_s[:, at]).astype(BF)
+        return carry
+
+    lax.fori_loop(0, hidden // block, down_step, 0)
+    sum_s[...] = nt(dgate_s[...], wg[...]) + nt(dup_s[...], wu[...])
+    fold_rows(sum_s[...], bs)
+    backs = Exchange(spot, bs, br, a2a_send.at[3], a2a_recv.at[3])
+    backs.start()
+
+    down_w.drain()
+
+    def grad_step(i, carry):
+        at = parts(i)
+        wg[:, at] = tn(x_s[...], dgate_s[:, at]).astype(BF)
+        wu[:, at] = tn(x_s[...], dup_s[:, at]).astype(BF)
+        wd[:, at] = tn(g_s[...], hid_s[:, at]).astype(BF)
+        return carry
+
+    lax.fori_loop(0, hidden // block, grad_step, 0)
+    saves = [
+        pltpu.make_async_copy(src, dst, sems.new())
+        for src, dst in ((wg, dg_out), (wu, du_out), (wd, dd_out))
+    ]
+    for copy in saves:
+        copy.start()
+    dsg_out[...] = tn(rows_all, grad_gate).astype(BF)
+    dsu_out[...] = tn(rows_all, grad_up).astype(BF)
+    dsd_out[...] = tn(shared_hidden, grad_all).astype(BF)
+
+    second = second_ref[...]
+    shared_out.finish()
+    total = second
+    for w in range(4):
+        total = total + sh_recv[w].astype(F32)
+    outs.finish()
+    pair_out = nn(to_pairs, unfold_rows(orr, slots))
+    pair_out = [pair_out[:rows], pair_out[rows:]]
+    result_out[...] = (total + gates[0] * pair_out[0] + gates[1] * pair_out[1]).astype(BF)
+    grad_gates = [jnp.sum(grad * p, axis=1, keepdims=True) for p in pair_out]
+    inner = gates[0] * grad_gates[0] + gates[1] * grad_gates[1]
+    grad_logits = jnp.zeros_like(logits)
+    for j in range(2):
+        grad_logits += jnp.where(matches[j], gates[j] * (grad_gates[j] - inner), 0.0)
+    pieces = split_three(grad_logits)
+    router_grad = sum(tn(piece, mixer) for piece in pieces)
+    grad_mixer = sum(nn(piece, router) for piece in pieces)
+    shared_back.finish()
+    for w in range(4):
+        grad_mixer = grad_mixer + gm_recv[w].astype(F32)
+    backs.finish()
+    grad_mixer = grad_mixer + nn(to_pairs[:rows] + to_pairs[rows:], unfold_rows(br, slots))
+    scale = lax.rsqrt(jnp.mean(second * second, axis=-1, keepdims=True) + EPS)
+    weighted = grad_mixer * pack[1:2]
+    mean = jnp.mean(weighted * second, axis=-1, keepdims=True)
+    grad_second_out[...] = grad + scale * weighted - second * (scale * scale * scale * mean)
+    gain_grad = jnp.sum(grad_mixer * second * scale, axis=0, keepdims=True)
+    pack_grad_out[...] = jnp.concatenate(
+        [jnp.zeros_like(gain_grad), gain_grad, router_grad[:14]], axis=0
+    )
+    for part in (rows_out, grads_out, outs, backs, mixers, shared_out, shared_back):
+        part.drain()
+    for copy in saves:
+        copy.wait()
+
+
+def run_experts(
+    second, mixer, pack, cot, route, e_row, e_col, o_row, o_col, sd, sg, su, cot4, eg, eu, ed
+):
+    rows, width = mixer.shape
+    ranks, slots = 8, 40
+    hidden = eg.shape[1]
+    part = sg.shape[1]
+    total = ranks * slots
+    folded = (ranks, slots * width // 128, 128)
+    any_, vm = pl.BlockSpec(memory_space=pl.ANY), pl.BlockSpec(memory_space=VMEM)
+    shape = jax.ShapeDtypeStruct
+    return pl.pallas_call(
+        experts_kernel,
+        out_shape=(
+            shape((rows, width), BF),
+            shape((rows, width), F32),
+            shape(pack.shape, F32),
+            shape((width, part), BF),
+            shape((width, part), BF),
+            shape((part, width), BF),
+            shape((width, hidden), BF),
+            shape((width, hidden), BF),
+            shape((width, hidden), BF),
+        ),
+        in_specs=[vm] * 13 + [any_] * 3,
+        out_specs=tuple([vm] * 6 + [any_] * 3),
+        scratch_shapes=[
+            VMEM((width, hidden), BF),
+            VMEM((width, hidden), BF),
+            VMEM((width, hidden), BF),
+            VMEM((4, rows, width), BF),
+            VMEM((4, rows, width), BF),
+            VMEM((4, rows, width), BF),
+            VMEM((4, rows, width), BF),
+            VMEM((4, rows, width), BF),
+            VMEM(folded, BF),
+            VMEM(folded, BF),
+            VMEM(folded, BF),
+            VMEM(folded, BF),
+            VMEM(folded, BF),
+            VMEM(folded, BF),
+            VMEM(folded, BF),
+            VMEM(folded, BF),
+            VMEM((total, width), BF),
+            VMEM((total, width), BF),
+            VMEM((total, width), F32),
+            VMEM((total, hidden), F32),
+            VMEM((total, hidden), F32),
+            VMEM((total, hidden), BF),
+            VMEM((total, hidden), BF),
+            VMEM((total, hidden), BF),
+            pltpu.SemaphoreType.DMA((48,)),
+            pltpu.SemaphoreType.DMA((4, ranks)),
+            pltpu.SemaphoreType.DMA((4, ranks)),
+        ],
+        compiler_params=pltpu.CompilerParams(
+            collective_id=2, has_side_effects=True, vmem_limit_bytes=56 * 2**20
+        ),
+    )(second, mixer, pack, cot, route, e_row, e_col, o_row, o_col, sd, sg, su, cot4, eg, eu, ed)
 
 
 def contract_product(left, right, left_dim, right_dim):
@@ -936,124 +1250,28 @@
     kb = (places(0, ranks * rows_dev, block_deal, rows_dev) // BLK)[None, :]
     qb = jnp.concatenate([query_side_block, query_side_block])[:, None]
     pack = pack_params(gain_attention, gain_mixer, router_weight)
-    (q_st, kv_all, mixed_f, lse, second, mixer, normed, pack_all, wfull, sg_sl, su_sl, expert_gate_whole, expert_up_whole, cot4) = run_forward(
+    (q_st, kv_all, mixed_f, lse, second, mixer, normed, pack_all, wfull, sg_sl, su_sl, eg_full, eu_full, cot4) = run_forward(
         tokens[0], pack, cosr, sinr, kb, qb, cotangent[0], query_weight, key_weight, value_weight, output_weight, shared_gate, shared_up, expert_gate, expert_up)
     gain_first, gain_second = pack_all[0], pack_all[1]
-    router_full = pack_all[2:10].T.astype(jnp.bfloat16)
     query_full, key_full, value_full, output_full = wfull[0], wfull[1], wfull[2], wfull[3]
-    sgate_full = lax.all_gather(shared_gate, "wt", axis=0, tiled=True)
-    sup_full = lax.all_gather(shared_up, "wt", axis=0, tiled=True)
-    sdown_full = lax.all_gather(shared_down, "wt", axis=0, tiled=True)
-    edown_full = lax.all_gather(expert_down, "wt", axis=0, tiled=True)
+    route = routes[0]
+    top_count = route.shape[1]
+    by_choice = route.T.reshape(1, rows_dev * top_count)
+    turns = slot_order[0, 0]
+    turns = lax.rem(turns, top_count) * rows_dev + lax.div(turns, top_count)
+    (result, grad_second, pack_grad, dsg, dsu, dsd, egate_grad, expert_up_weight_grad, edown_grad) = run_experts(
+        second, mixer, pack_all, cotangent[0], route, by_choice, by_choice.reshape(-1, 1), turns[None, :], turns[:, None],
+        shared_down, sg_sl, su_sl, cot4, eg_full, eu_full, expert_down)
     query_rot = (8.0 * (q_st[:, :rows_dev] + q_st[:, rows_dev:])).astype(jnp.bfloat16).transpose(1, 0, 2).reshape(rows_dev, width)
     query3 = query_rot.reshape(rows_dev, heads, HD)
     query_side = (query3, query_side_block)
     log_total = lse[:, :, 0].reshape(heads, rows_dev)
     mixed3 = mixed_f.reshape(rows_dev, heads, HD)
     scale_one = lax.rsqrt(jnp.mean(inputs * inputs, axis=-1, keepdims=True) + EPS)
-    scale_two = lax.rsqrt(jnp.mean(second * second, axis=-1, keepdims=True) + EPS)
-    key_rot = kv_all[lax.axis_index("ctx"), :, :width]
+    gain_two_grad = pack_grad[1]
+    router_grad = pack_grad[2:10].T
+    sgate_grad, sup_grad, sdown_grad = dsg, dsu, dsd
     mixed_low = mixed3.reshape(rows_dev, width).astype(jnp.bfloat16)
-    experts = router_full.shape[1]
-    logits = jnp.dot(mixer, router_full, preferred_element_type=jnp.float32)
-    route = routes[0]
-    top_count = route.shape[1]
-    pair_count = rows_dev * top_count
-    capacity = (5 * pair_count + 4 * experts - 1) // (4 * experts)
-    split_count = ranks // experts
-    expert_match = route[:, :, None] == jnp.arange(experts, dtype=jnp.int32)[None, None, :]
-    chosen = jnp.sum(jnp.where(expert_match, logits[:, None, :], 0.0), axis=2)
-    gates = jax.nn.softmax(chosen, axis=1)
-    target, kept_pairs, slot_table = assign_slots(route, slot_order[0, 0], experts, capacity)
-    valid = slot_table < pair_count
-    pair_pick = jnp.minimum(slot_table, pair_count - 1)
-    target_pick = jnp.minimum(target, experts * capacity - 1)
-    send_rows = jnp.where(
-        valid[:, None], mixer[pair_pick // top_count], jnp.zeros((), jnp.bfloat16)
-    )
-    send_rows = jnp.broadcast_to(
-        send_rows.reshape(experts, 1, capacity, width), (experts, split_count, capacity, width)
-    ).reshape(ranks, capacity, width)
-    received = lax.all_to_all(send_rows, "ctx", split_axis=0, concat_axis=0, tiled=True)
-    slot_count = received.shape[1]
-    flattened_input = received.reshape(ranks * slot_count, width)
-    gate_part = jnp.dot(flattened_input, expert_gate_whole, preferred_element_type=jnp.float32)
-    up_projection_part = jnp.dot(
-        flattened_input, expert_up_whole, preferred_element_type=jnp.float32
-    )
-    activated, unused = silu_parts(gate_part)
-    hidden = (activated * up_projection_part).astype(jnp.bfloat16)
-    partial_value = contract_product(hidden, edown_full, 1, 1).reshape(ranks, slot_count, width)
-    back = lax.all_to_all(
-        partial_value.astype(jnp.bfloat16), "ctx", split_axis=0, concat_axis=0, tiled=True
-    ).astype(partial_value.dtype)
-    expert_gate_part = gate_part.reshape(ranks, slot_count, -1)
-    expert_up_part = up_projection_part.reshape(ranks, slot_count, -1)
-    combined = jnp.sum(back.reshape(experts, split_count, capacity, width), axis=1).reshape(
-        experts * capacity, width
-    )
-    pair_out = jnp.where(kept_pairs[:, None], combined[target_pick], 0.0).reshape(
-        rows_dev, top_count, width
-    )
-    mixture = jnp.sum(gates[:, :, None] * pair_out, axis=1)
-    sgate_part = jnp.dot(mixer, sgate_full, preferred_element_type=jnp.float32)
-    sup_part = jnp.dot(mixer, sup_full, preferred_element_type=jnp.float32)
-    shared_act, shared_slope = silu_parts(sgate_part)
-    shared_hidden = (shared_act * sup_part).astype(jnp.bfloat16)
-    shared_out = jnp.dot(shared_hidden, sdown_full, preferred_element_type=jnp.float32)
-    result = (second + mixture + shared_out).astype(jnp.bfloat16)
-    grad_final = cotangent[0].astype(jnp.float32)
-    grad_low = grad_final.astype(jnp.bfloat16)
-    sdown_grad = contract_product(shared_hidden, grad_low, 0, 0)
-    grad_shared_hidden = contract_product(grad_low, sdown_full, 1, 1)
-    grad_sgate = (grad_shared_hidden * sup_part * shared_slope).astype(jnp.bfloat16)
-    grad_sup = (grad_shared_hidden * shared_act).astype(jnp.bfloat16)
-    sgate_grad = contract_product(mixer, grad_sgate, 0, 0)
-    sup_grad = contract_product(mixer, grad_sup, 0, 0)
-    grad_mixer = contract_product(grad_sgate, sgate_full, 1, 1) + contract_product(
-        grad_sup, sup_full, 1, 1
-    )
-    pair_grad = (
-        (gates[:, :, None] * grad_final[:, None, :]).reshape(pair_count, width).astype(jnp.bfloat16)
-    )
-    grad_gates = jnp.sum(grad_final[:, None, :] * pair_out, axis=2)
-    send_grad = jnp.where(valid[:, None], pair_grad[pair_pick], jnp.zeros((), jnp.bfloat16))
-    send_grad = jnp.broadcast_to(
-        send_grad.reshape(experts, 1, capacity, width), (experts, split_count, capacity, width)
-    ).reshape(ranks, capacity, width)
-    recv_grad = lax.all_to_all(send_grad, "ctx", split_axis=0, concat_axis=0, tiled=True)
-    flattened_input = received.reshape(ranks * capacity, width)
-    flat_grad = recv_grad.reshape(ranks * capacity, width)
-    gate_flat = expert_gate_part.reshape(ranks * capacity, -1)
-    up_flat = expert_up_part.reshape(ranks * capacity, -1)
-    expert_activation, expert_slope = silu_parts(gate_flat)
-    expert_hidden = (expert_activation * up_flat).astype(jnp.bfloat16)
-    edown_grad = contract_product(flat_grad, expert_hidden, 0, 0)
-    expert_hidden_grad = jnp.dot(flat_grad, edown_full, preferred_element_type=jnp.float32)
-    expert_gate_grad_rows = (expert_hidden_grad * up_flat * expert_slope).astype(jnp.bfloat16)
-    expert_up_grad_rows = (expert_hidden_grad * expert_activation).astype(jnp.bfloat16)
-    egate_grad = contract_product(flattened_input, expert_gate_grad_rows, 0, 0)
-    expert_up_weight_grad = contract_product(flattened_input, expert_up_grad_rows, 0, 0)
-    input_back = (
-        contract_product(expert_gate_grad_rows, expert_gate_whole, 1, 1)
-        + contract_product(expert_up_grad_rows, expert_up_whole, 1, 1)
-    ).reshape(ranks, capacity, width)
-    back_grad = lax.all_to_all(
-        input_back.astype(jnp.bfloat16), "ctx", split_axis=0, concat_axis=0, tiled=True
-    ).astype(input_back.dtype)
-    merged = jnp.sum(back_grad.reshape(experts, split_count, capacity, width), axis=1).reshape(
-        experts * capacity, width
-    )
-    pair_back = jnp.where(kept_pairs[:, None], merged[target_pick], 0.0).reshape(
-        rows_dev, top_count, width
-    )
-    grad_mixer = grad_mixer + jnp.sum(pair_back, axis=1)
-    grad_chosen = gates * (grad_gates - jnp.sum(gates * grad_gates, axis=1, keepdims=True))
-    grad_logits = jnp.sum(jnp.where(expert_match, grad_chosen[:, :, None], 0.0), axis=1)
-    router_grad = contract_exact(mixer.astype(jnp.float32), grad_logits, 0, 0)
-    grad_mixer = grad_mixer + contract_exact(grad_logits, router_full.astype(jnp.float32), 1, 1)
-    through_two, gain_two_grad = rms_back(second, scale_two, gain_second, grad_mixer)
-    grad_second = grad_final + through_two
     grad_attention = grad_second.astype(jnp.bfloat16)
     output_grad = contract_product(mixed_low, grad_attention, 0, 0)
     grad_mixed = contract_product(grad_attention, output_full, 1, 1).astype(jnp.bfloat16)
@@ -1166,15 +1384,9 @@
         lax.psum_scatter(
             router_grad.astype(jnp.bfloat16), "wt", scatter_dimension=0, tiled=True
         ).astype(jnp.float32),
-        lax.psum_scatter(
-            sgate_grad.astype(jnp.bfloat16), "wt", scatter_dimension=0, tiled=True
-        ).astype(jnp.float32),
-        lax.psum_scatter(
-            sup_grad.astype(jnp.bfloat16), "wt", scatter_dimension=0, tiled=True
-        ).astype(jnp.float32),
-        lax.psum_scatter(
-            sdown_grad.astype(jnp.bfloat16), "wt", scatter_dimension=0, tiled=True
-        ).astype(jnp.float32),
+        lax.all_to_all(sgate_grad, "wt", split_axis=0, concat_axis=1, tiled=True).astype(jnp.float32),
+        lax.all_to_all(sup_grad, "wt", split_axis=0, concat_axis=1, tiled=True).astype(jnp.float32),
+        sdown_grad.astype(jnp.float32),
         lax.psum_scatter(
             egate_grad.astype(jnp.bfloat16), "wt", scatter_dimension=0, tiled=True
         ).astype(jnp.float32),

time: 1140 us -> 842 us (0.74)
  waiting for transfers between devices: 429 us -> 304 us
  matrix products: 116 us -> 38.1 us
  blocking collectives: 285 us -> 213 us
  starting transfers between devices: 21.2 us -> 3.85 us
  Pallas kernels: 140 us -> 157 us
  local copies, waits for them, and re-layouts: 80.8 us -> 66.5 us
    reduce_scatter x3 -> x0, waiting for transfers between devices: 122 us -> none  [the longest x1 40.7 us: fast_body(): lax.psum_scatter(sgate_grad.astype(jnp.bfloat16), 'wt', scatter_dimension...]
    psum x1, blocking collectives: 279 us -> 192 us  [fast_body(): lax.psum((gain_one_share, query_share, key_share, value_share, output_sha...]
    pallas_call x0 -> x1, Pallas kernels: none -> 61.1 us  [run_experts(): pl.pallas_call(experts_kernel, out_shape=(shape((rows, width), BF), shape...]
    pallas_call x1, Pallas kernels: 140 us -> 96.2 us  [run_forward(): pl.pallas_call(forward_kernel, out_shape=(shape((pairs, 2 * rows, PAIR),...]
    dot_general x20 -> x8, matrix products: 57.4 us -> 13.8 us  [contract_product(): lax.dot_general(left, right, (((left_dim,), (right_dim,)), ((), ())), pre...]
    dot_general x9 -> x0, matrix products: 23.7 us -> none  [the longest x1 5.58 us: fast_body(): jnp.dot(flat_grad, edown_full, preferred_element_type=jnp.float32)]
    all_to_all x4 -> x1, starting transfers between devices: 19.5 us -> 3.49 us  [fast_body(): lax.all_to_all(sup_grad, 'wt', split_axis=0, concat_axis=1, tiled=True)]
    all_to_all x0 -> x1, blocking collectives: none -> 15.3 us  [fast_body(): lax.all_to_all(sgate_grad, 'wt', split_axis=0, concat_axis=1, tiled=True)]
  transfers between devices with their start and end apart: 20 -> 11, of which waited for: 14 -> 10; matrix products, arithmetic and copies ran while one was open for 14% -> 7% of each run, Pallas kernels for 12% -> 0%
where the time goes in v2:
time: 842 us; the launch traced here: 840 us
  waiting for transfers between devices  304 us (36%)
  blocking collectives  213 us (25%)
  Pallas kernels  157 us (19%)
  local copies, waits for them, and re-layouts  66.5 us (8%)
  matrix products  38.1 us (5%)
  other arithmetic  34.2 us (4%)
  between operations  15.3 us (2%)
    psum x1, blocking collectives, fast_body(): lax.psum((gain_one_share, query_share, key_share, value_share, output_sha...  192 us
    pallas_call x1, Pallas kernels, run_forward(): pl.pallas_call(forward_kernel, out_shape=(shape((pairs, 2 * rows, PAIR),...  96.2 us
    reduce_scatter x1, waiting for transfers between devices, fast_body(): lax.psum_scatter(parts.reshape(lax.axis_size('ctx') * rows_dev, 2 * width...  84.7 us
    pallas_call x1, Pallas kernels, run_experts(): pl.pallas_call(experts_kernel, out_shape=(shape((rows, width), BF), shape...  61.1 us
    reduce_scatter x1, waiting for transfers between devices, fast_body(): lax.psum_scatter(egate_grad.astype(jnp.bfloat16), 'wt', scatter_dimension...  40.5 us
    reduce_scatter x1, waiting for transfers between devices, fast_body(): lax.psum_scatter(edown_grad.astype(jnp.bfloat16), 'wt', scatter_dimension...  38.1 us
    reduce_scatter x1, waiting for transfers between devices, fast_body(): lax.psum_scatter(expert_up_weight_grad.astype(jnp.bfloat16), 'wt', scatte...  37.9 us
    reduce_scatter x1, waiting for transfers between devices, fast_body(): lax.psum_scatter(key_grad.astype(jnp.bfloat16), 'wt', scatter_dimension=0...  28.5 us
  transfers between devices with their start and end apart: 11, of which 10 were waited for; matrix products, arithmetic and copies ran while one was open for 7% of the time, Pallas kernels for 0%

profile of v2, /device:TPU:0, one launch (start us, length us, event | category | flops | bytes accessed | tf_op | source)
XLA Modules:
  0.0 840.3 jit_solution(7406496349630555990)
XLA Ops:
  12.6 1.2 fusion.82.o_row
  19.5 1.0 copy-done.6
  20.5 1.0 copy-done.7
  21.4 1.0 copy-done.8
  22.4 1.0 copy-done.9
  23.4 96.2 %shard_map.289 = (bf16[6,256,128]{2,1,0:T(8,128)(2,1)S(1)}, bf16[8,128,1536]{2,1,0:T(8,128)(2,1)}, f32[128,768]{1,0:T(8,128)S(1)}, f32[6,256,128]{2,1,0:T(8,128)...) custom-call(bf16[128,768]{1,0:T(8,128)(2,1)S(1)} %bitcast.239, ...), custom_call_target="tpu_custom_call" | custom-call | tf_op jit(solution)/shard_map/pallas_call | solution.py:355
  119.6 4.0 fusion.86
  123.7 1.6 copy.167
  125.8 2.6 copy.169
  128.4 61.1 %shard_map.290 = (bf16[128,768]{1,0:T(8,128)(2,1)}, f32[128,768]{1,0:T(8,128)}, f32[16,768]{1,0:T(8,128)}, bf16[768,512]{1,0:T(8,128)(2,1)}, bf16[768,512]{1,0:T...) custom-call(f32[128,768]{1,0:T(8,128)} %copy-done.5, ...), custom_call_target="tpu_custom_call" | custom-call | tf_op jit(solution)/shard_map/pallas_call | solution.py:676
  189.6 1.9 fusion.57
  192.5 1.0 multiply_reduce_fusion
  193.5 51.8 %while.29 = (s32[]{:T(128)}, f32[2,512,1536]{2,1,0:T(8,128)}, s32[2]{0:T(128)}, s32[8]{0:T(128)}, s32[128]{0:T(128)S(1)}, /*index=5*/bf16[1024,768]{0,1:T(8,128)...) while((s32[]{:T(128)}, f32[2,512,1536]{2,1,0:T(8,128)}, ...), condition=%wide.wide.region_9.10_spmd, body=%wide.wide.region_7.9_spmd.sunk | while | flops 413770752 | bytes 49773324 | solution.py:1328
  193.5 1.2 dynamic_slice.59
  196.7 2.2 constant_dynamic-slice_fusion.8
  201.9 2.0 fusion.149
  203.8 4.9 fusion.150
  208.8 3.4 maximum_bitcast_fusion.3
  212.2 3.6 copy.194
  215.7 3.7 constant_dynamic-update-slice_fusion.3
  219.5 1.2 dynamic_slice.59
  222.7 2.1 constant_dynamic-slice_fusion.8
  227.7 2.0 fusion.149
  229.7 4.9 fusion.150
  234.6 3.4 maximum_bitcast_fusion.3
  238.0 3.6 copy.194
  241.6 3.8 constant_dynamic-update-slice_fusion.3
  247.1 1.5 convolution_convert_fusion
  252.4 29.2 %while.30 = (s32[]{:T(128)}, f32[128,12,64]{0,2,1:T(8,128)}, s32[2]{0:T(128)}, bf16[1024,768]{0,1:T(8,128)(2,1)}, s32[8]{0:T(128)}, /*index=5*/s32[128]{0:T(128)...) while((s32[]{:T(128)}, f32[128,12,64]{0,2,1:T(8,128)}, ...), condition=%wide.wide.region_6.7_spmd.clone, body=%wide.wide.region_4.6_spmd.clone.sunk | while | flops 308585472 | bytes 16280369 | solution.py:1302
  252.4 1.3 dynamic_slice.61
  255.6 3.1 constant_dynamic-slice_fusion.9
  263.1 3.9 fusion.157
  267.0 1.2 dynamic_slice.61
  270.2 3.0 constant_dynamic-slice_fusion.9
  277.6 4.1 fusion.157
  281.6 84.7 %reduce-scatter.12.cloned.1.call-done = f32[128,1536]{1,0:T(8,128)} async-done(((f32[1024,1536]{1,0:T(8,128)}), f32[128,1536]{1,0:T(8,128)}) %reduce-scatter.12.cloned.1.call-update) | async-done | bytes 786448 | tf_op jit(solution)/shard_map/reduce_scatter | solution.py:1332
  366.3 1.0 slice.77
  367.5 1.2 multiply_subtract_fusion
  368.7 1.5 convolution_convert_fusion.3
  370.3 1.5 convolution_convert_fusion.2
  371.9 1.6 convolution_convert_fusion.1
  373.6 15.3 %all_to_all.26 = bf16[4,192,512]{2,1,0:T(8,128)(2,1)S(1)} all-to-all(bf16[4,192,512]{2,1,0:T(8,128)(2,1)S(1)} %bitcast.263), channel_id=1, replica_groups=mesh['ctx'=8,'wt'=4] {'wt'}, dimensions={0} | all-to-all | bytes 1572864 | tf_op jit(solution)/shard_map/all_to_all | solution.py:1387
  388.8 3.5 all-to-all-start.1
  392.6 1.3 copy.190
  393.9 10.0 %all-to-all-done.1 = bf16[4,192,512]{2,1,0:T(8,128)(2,1)S(1)} async-done(((bf16[4,192,512]{2,1,0:T(8,128)(2,1)}), bf16[4,192,512]{2,1,0:T(8,128)(2,1)S(1)}, u32[]{:S(2)}, u32[]{:S(2)}) %all-to-all-start.1) | async-done | bytes 786464 | tf_op jit(solution)/shard_map/all_to_all | solution.py:1388
  404.2 1.3 copy.191
  409.3 8.0 reduce-scatter.20.cloned.1.call-done
  417.2 40.5 %reduce-scatter.22.cloned.1.call-done = bf16[192,2048]{1,0:T(8,128)(2,1)} async-done(((bf16[768,2048]{1,0:T(8,128)(2,1)}), bf16[192,2048]{1,0:T(8,128)(2,1)}) %reduce-scatter.22.cloned.1.call-update) | async-done | bytes 786448 | tf_op jit(solution)/shard_map/reduce_scatter | solution.py:1390
  457.7 2.5 convert_element_type.181
  460.2 37.9 %reduce-scatter.24.cloned.1.call-done = bf16[192,2048]{1,0:T(8,128)(2,1)} async-done(((bf16[768,2048]{1,0:T(8,128)(2,1)}), bf16[192,2048]{1,0:T(8,128)(2,1)}) %reduce-scatter.24.cloned.1.call-update) | async-done | bytes 786448 | tf_op jit(solution)/shard_map/reduce_scatter | solution.py:1393
  498.1 2.5 convert_element_type.182
  500.6 38.1 %reduce-scatter.26.cloned.1.call-done = bf16[192,2048]{1,0:T(8,128)(2,1)} async-done(((bf16[768,2048]{1,0:T(8,128)(2,1)}), bf16[192,2048]{1,0:T(8,128)(2,1)}) %reduce-scatter.26.cloned.1.call-update) | async-done | bytes 786448 | tf_op jit(solution)/shard_map/reduce_scatter | solution.py:1396
  538.7 2.5 convert_element_type.183
  541.1 1.8 fusion.49
  543.0 1.9 convolution_add_fusion.1
  544.8 2.0 fusion.69
  546.9 5.8 all-reduce.4
  553.7 13.9 %reduce-scatter.14.cloned.1.call-done = bf16[192,768]{1,0:T(8,128)(2,1)} async-done(((bf16[768,768]{1,0:T(8,128)(2,1)}), bf16[192,768]{1,0:T(8,128)(2,1)}) %reduce-scatter.14.cloned.1.call-update) | async-done | bytes 294928 | tf_op jit(solution)/shard_map/reduce_scatter | solution.py:1369
  567.6 28.5 %reduce-scatter.16.cloned.1.call-done = bf16[192,768]{1,0:T(8,128)(2,1)} async-done(((bf16[768,768]{1,0:T(8,128)(2,1)}), bf16[192,768]{1,0:T(8,128)(2,1)}) %reduce-scatter.16.cloned.1.call-update) | async-done | bytes 294928 | tf_op jit(solution)/shard_map/reduce_scatter | solution.py:1372
  596.1 28.4 %reduce-scatter.18.cloned.1.call-done = bf16[192,768]{1,0:T(8,128)(2,1)} async-done(((bf16[768,768]{1,0:T(8,128)(2,1)}), bf16[192,768]{1,0:T(8,128)(2,1)}) %reduce-scatter.18.cloned.1.call-update) | async-done | bytes 294928 | tf_op jit(solution)/shard_map/reduce_scatter | solution.py:1375
  624.4 192.3 %all-reduce.9 = (f32[192]{0:T(256)}, f32[192,768]{1,0:T(8,128)}, f32[192,768]{1,0:T(8,128)}, f32[192,768]{1,0:T(8,128)}, f32[192,768]{1,0:T(8,128)}, /*index=5*/...) all-reduce(f32[192]{0:T(256)S(1)} %dynamic-slice_convert_fusion.1, ...), channel_id=1, replica_groups=mesh['ctx'=8,'wt'=4] {'ctx'}, use_global_device_ids=true, to_apply=%region_14.15 | all-reduce | flops 984960 | bytes 5910528 | tf_op jit(solution)/shard_map/psum | solution.py:1411
  816.7 12.2 %all-reduce.8.cloned.1.call-done = (f32[192,2048]{1,0:T(8,128)}, f32[192,2048]{1,0:T(8,128)}) async-done(((f32[192,2048]{1,0:T(8,128)}, f32[192,2048]{1,0:T(8,128)}), (f32[192,2048]{1,0:T(8,128)}, f32[192,2048]{1,0:T(8,128)})) %all-reduce.8.cloned.1.call-update) | async-done | bytes 3145744 | tf_op jit(solution)/shard_map/psum | solution.py:1411
  829.6 2.7 copy.227
  832.3 1.1 copy.228
  (170 shorter events, 38.1 us)
Async XLA Ops:
  7.2 359.1 %reduce-scatter.12.cloned.1.call-start = ((), (), s32[]{:S(2)}) async-start(), calls=%async_computation.11 | async-start | bytes 7077888 | tf_op jit(solution)/shard_map/reduce_scatter | solution.py:1332
  11.7 6.0 copy-start.20
  11.7 111.9 %copy-start.33 = (s32[2,128]{1,0:T(2,128)}, s32[2,128]{1,0:T(2,128)S(1)}, u32[]{:S(2)}) copy-start(s32[2,128]{1,0:T(2,128)S(1)} %copy.158) | copy-start | bytes 3076
  16.4 1.3 copy-start.21
  17.7 0.9 copy-start
  18.6 0.9 copy-start.4
  19.5 1.0 copy-start.6
  20.5 1.0 copy-start.7
  21.4 1.0 copy-start.8
  22.4 1.0 copy-start.9
  119.5 4.1 copy-start.2
  119.6 4.1 copy-start.3
  119.6 4.1 copy-start.5
  119.6 4.1 copy-start.10
  119.6 4.1 copy-start.11
  125.8 66.7 %copy-start.26 = (f32[6,256,1]{1,0,2:T(8,128)}, f32[6,256,1]{1,0,2:T(8,128)S(1)}, u32[]{:S(2)}) copy-start(f32[6,256,1]{1,0,2:T(8,128)S(1)} %copy.168) | copy-start | bytes 18436
  199.6 2.3 copy-start.12
  225.4 2.3 copy-start.12
  245.3 0.5 copy-start.30
  245.3 0.6 copy-start.34
  245.3 0.8 copy-start.32
  245.3 1.7 copy-start.14
  245.9 162.5 %reduce-scatter.28.cloned.1.call-start = ((), (), s32[]{:S(2)}) async-start(), calls=%async_computation.19 | async-start | bytes 245760
  246.1 3.0 copy-start.29
  247.0 170.2 %reduce-scatter.20.cloned.1.call-start = ((), (), s32[]{:S(2)}) async-start(), calls=%async_computation.15 | async-start | bytes 1474560 | tf_op jit(solution)/shard_map/reduce_scatter | solution.py:1378
  248.6 209.2 %reduce-scatter.22.cloned.1.call-start = ((), (), s32[]{:S(2)}) async-start(), calls=%async_computation.16 | async-start | bytes 3932160 | tf_op jit(solution)/shard_map/reduce_scatter | solution.py:1390
  249.2 248.9 %reduce-scatter.24.cloned.1.call-start = ((), (), s32[]{:S(2)}) async-start(), calls=%async_computation.17 | async-start | bytes 3932160 | tf_op jit(solution)/shard_map/reduce_scatter | solution.py:1393
  249.2 1.2 copy-start.22
  249.2 1.8 copy-start.27
  249.3 2.4 copy-start.24
  249.8 288.9 %reduce-scatter.26.cloned.1.call-start = ((), (), s32[]{:S(2)}) async-start(), calls=%async_computation.18 | async-start | bytes 3932160 | tf_op jit(solution)/shard_map/reduce_scatter | solution.py:1396
  250.3 317.2 %reduce-scatter.14.cloned.1.call-start = ((), (), s32[]{:S(2)}) async-start(), calls=%async_computation.12 | async-start | bytes 1474560 | tf_op jit(solution)/shard_map/reduce_scatter | solution.py:1369
  252.4 115.2 %copy-start.28 = (f32[128,32]{0,1:T(8,128)S(1)}, f32[128,32]{0,1:T(8,128)}, u32[]{:S(2)}) copy-start(f32[128,32]{0,1:T(8,128)} %copy.170) | copy-start | bytes 49156
  255.6 6.8 copy-start.31
  258.7 0.9 copy-start.13
  270.2 6.6 copy-start.31
  273.2 0.9 copy-start.13
  368.7 3.3 copy-start.16
  370.3 3.3 copy-start.19
  370.3 225.8 %reduce-scatter.16.cloned.1.call-start = ((), (), s32[]{:S(2)}) async-start(), calls=%async_computation.13 | async-start | bytes 1474560 | tf_op jit(solution)/shard_map/reduce_scatter | solution.py:1372
  371.9 252.5 %reduce-scatter.18.cloned.1.call-start = ((), (), s32[]{:S(2)}) async-start(), calls=%async_computation.14 | async-start | bytes 1474560 | tf_op jit(solution)/shard_map/reduce_scatter | solution.py:1375
  388.8 15.1 %all-to-all-start.1 = ((bf16[4,192,512]{2,1,0:T(8,128)(2,1)}), bf16[4,192,512]{2,1,0:T(8,128)(2,1)S(1)}, u32[]{:S(2)}, u32[]{:S(2)}) async-start(bf16[4,192,512]{2,1,0:T(8,128)(2,1)} %bitcast.262), calls=%async_computation.6 | async-start | bytes 1572864 | tf_op jit(solution)/shard_map/all_to_all | solution.py:1388
  392.3 436.6 %all-reduce.8.cloned.1.call-start = ((), (), s32[]{:S(2)}) async-start(), calls=%async_computation.20 | async-start | bytes 6291456 | tf_op jit(solution)/shard_map/psum | solution.py:1411
  404.1 1.4 copy-start.35
  404.2 4.1 copy-start.1
  541.1 11.7 %copy-start.15 = (f32[128,768]{1,0:T(8,128)S(1)}, f32[128,768]{1,0:T(8,128)}, u32[]{:S(2)}) copy-start(f32[128,768]{1,0:T(8,128)} %get-tuple-element.413) | copy-start | bytes 1179652
  543.0 81.5 %copy-start.23 = (bf16[192,768]{1,0:T(8,128)(2,1)S(1)}, bf16[192,768]{1,0:T(8,128)(2,1)}, u32[]{:S(2)}) copy-start(bf16[192,768]{1,0:T(8,128)(2,1)} %reduce-scatter.20.cloned.1.call-done) | copy-start | bytes 884740
  544.8 79.6 %copy-start.18 = (bf16[512,768]{1,0:T(8,128)(2,1)S(1)}, bf16[512,768]{1,0:T(8,128)(2,1)}, u32[]{:S(2)}) copy-start(bf16[512,768]{1,0:T(8,128)(2,1)} %get-tuple-element.425) | copy-start | bytes 2359300
  544.8 284.1 %copy-start.25 = (bf16[128,768]{1,0:T(8,128)(2,1)S(1)}, bf16[128,768]{1,0:T(8,128)(2,1)}, u32[]{:S(2)}) copy-start(bf16[128,768]{1,0:T(8,128)(2,1)} %get-tuple-element.412) | copy-start | bytes 589828
  828.9 3.4 copy-start.17
Sparse Core Ops, SparseCore 0:
  245.5 120.7 reduce-scatter.11
  369.3 19.8 reduce-scatter.27
  392.4 24.7 reduce-scatter.19
  419.8 37.9 reduce-scatter.21
  460.1 37.9 reduce-scatter.23
  500.7 37.9 reduce-scatter.25
  541.8 25.7 reduce-scatter.13
  570.3 25.7 reduce-scatter.15
  598.7 25.7 reduce-scatter.17
  628.9 199.8 all-reduce.7

commit v3 on v2

--- a/solution.py
+++ b/solution.py
@@ -504,11 +504,11 @@
 def experts_kernel(
     second_ref, mixer_ref, pack_ref, cot_ref, route_ref, e_row, e_col, o_row, o_col,
     sd_ref, sg_ref, su_ref, cot4_ref, eg_ref, eu_ref, ed_ref,
-    result_out, grad_second_out, pack_grad_out, dsg_out, dsu_out, dsd_out,
+    result_out, grad_second_out, pack_grad_out, dsh_out,
     dg_out, du_out, dd_out,
     wg, wu, wd, m4, sh_send, sh_recv, gm_send, gm_recv,
     xs, xr, gs, gr, os, orr, bs, br, x_s, g_s, sum_s,
-    gate_s, up_s, hid_s, dgate_s, dup_s, sem, a2a_send, a2a_recv,
+    gate_s, up_s, hid_s, dgate_s, dup_s, dsh, dsh_x, sem, a2a_send, a2a_recv, sem_sh,
 ):
     spot = Spot(4)
     sems = Sems(sem)
@@ -563,6 +563,26 @@
     back = nt(grad_gate, sg_ref[...]) + nt(grad_up, su_ref[...])
     gm_send[...] = back.astype(BF).reshape(4, rows, width)
     shared_back = Spread(spot, lambda w: gm_send.at[w], lambda w: gm_recv.at[w], sems)
+    shard = width // 4
+    half = shard // 2
+    for at, values in ((0, tn(rows_all, grad_gate)), (half, tn(rows_all, grad_up))):
+        values = values.astype(BF)
+        for r in range(ranks):
+            top, left = half * (r // 4), 128 * (r % 4)
+            for w in range(4):
+                dsh[r, shard * w + at : shard * w + at + half] = values[
+                    shard * w + top : shard * w + top + half, left : left + 128
+                ]
+    values = tn(shared_hidden, grad_all).astype(BF)
+    deep = values.shape[0] // ranks
+    for r in range(ranks):
+        for t in range(width // 128):
+            dsh[r, width + deep * t : width + deep * (t + 1)] = values[
+                deep * r : deep * (r + 1), 128 * t : 128 * (t + 1)
+            ]
+    shared_grad = Reduce(spot, dsh, dsh_x, None, None, sem_sh)
+    for number in (3, 2, 1, 0):
+        shared_grad.side(number)
     down_w.forward()
     for copy in loads:
         copy.wait()
@@ -622,9 +642,11 @@
     ]
     for copy in saves:
         copy.start()
-    dsg_out[...] = tn(rows_all, grad_gate).astype(BF)
-    dsu_out[...] = tn(rows_all, grad_up).astype(BF)
-    dsd_out[...] = tn(shared_hidden, grad_all).astype(BF)
+
+    for number in (3, 2, 1, 0):
+        shared_grad.meet(number)
+        plane = spot.plane(number)
+        dsh_out[plane] = dsh[2 * plane + spot.x]
 
     second = second_ref[...]
     shared_out.finish()
@@ -658,6 +680,8 @@
     )
     for part in (rows_out, grads_out, outs, backs, mixers, shared_out, shared_back):
         part.drain()
+    for copy in shared_grad.sent:
+        copy.wait_send()
     for copy in saves:
         copy.wait()
 
@@ -670,6 +694,7 @@
     hidden = eg.shape[1]
     part = sg.shape[1]
     total = ranks * slots
+    tall = width + part * width // (128 * ranks)
     folded = (ranks, slots * width // 128, 128)
     any_, vm = pl.BlockSpec(memory_space=pl.ANY), pl.BlockSpec(memory_space=VMEM)
     shape = jax.ShapeDtypeStruct
@@ -679,15 +704,13 @@
             shape((rows, width), BF),
             shape((rows, width), F32),
             shape(pack.shape, F32),
-            shape((width, part), BF),
-            shape((width, part), BF),
-            shape((part, width), BF),
+            shape((4, tall, 128), BF),
             shape((width, hidden), BF),
             shape((width, hidden), BF),
             shape((width, hidden), BF),
         ),
         in_specs=[vm] * 13 + [any_] * 3,
-        out_specs=tuple([vm] * 6 + [any_] * 3),
+        out_specs=tuple([vm] * 4 + [any_] * 3),
         scratch_shapes=[
             VMEM((width, hidden), BF),
             VMEM((width, hidden), BF),
@@ -713,14 +736,469 @@
             VMEM((total, hidden), BF),
             VMEM((total, hidden), BF),
             VMEM((total, hidden), BF),
+            VMEM((ranks, tall, 128), BF),
+            VMEM((4, tall, 128), BF),
             pltpu.SemaphoreType.DMA((48,)),
             pltpu.SemaphoreType.DMA((4, ranks)),
             pltpu.SemaphoreType.DMA((4, ranks)),
+            pltpu.SemaphoreType.DMA((5, 4)),
         ],
         compiler_params=pltpu.CompilerParams(
             collective_id=2, has_side_effects=True, vmem_limit_bytes=56 * 2**20
         ),
     )(second, mixer, pack, cot, route, e_row, e_col, o_row, o_col, sd, sg, su, cot4, eg, eu, ed)
+
+
+class Reduce:
+    def __init__(self, spot, part, sides, zo, zi, sems, folded=False):
+        self.spot, self.part, self.sides, self.zo, self.zi = spot, part, sides, zo, zi
+        self.x_send, self.x_recv, self.z_send, self.zo_recv, self.zi_recv = (
+            sems.at[i] for i in range(5)
+        )
+        self.folded = folded
+        self.sent, self.sent_end, self.sent_mid = [], [], []
+
+    def own(self, plane):
+        return self.part.at[plane if self.folded else 2 * plane + self.spot.x]
+
+    def wait(self, land, recv, plane):
+        remote(
+            land.at[plane], land.at[plane], self.z_send.at[plane], recv.at[plane], self.spot.column
+        ).wait_recv()
+
+    def side(self, number):
+        spot = self.spot
+        plane = spot.plane(number)
+        copy = remote(
+            self.part.at[2 * plane + 1 - spot.x],
+            self.sides.at[plane],
+            self.x_send.at[plane],
+            self.x_recv.at[plane],
+            spot.column,
+        )
+        copy.start()
+        self.sent.append(copy)
+
+    def meet(self, number):
+        plane = self.spot.plane(number)
+        self.wait(self.sides, self.x_recv, plane)
+        own = self.own(plane)
+        own[...] = (own[...].astype(F32) + self.sides[plane].astype(F32)).astype(BF)
+
+    def launch(self, number):
+        plane = self.spot.plane(number)
+        copy = remote(
+            self.own(plane),
+            self.zo.at[plane],
+            self.z_send.at[plane],
+            self.zo_recv.at[plane],
+            self.spot.inner,
+        )
+
+        @pl.when(self.spot.mid == 0)
+        def _():
+            copy.start()
+
+        self.sent_end.append(copy)
+
+    def relay(self, number):
+        plane = self.spot.plane(number)
+        land, recv = (self.zi, self.zi_recv) if number == 1 else (self.zo, self.zo_recv)
+        own = self.own(plane)
+        copy = remote(
+            own,
+            self.zi.at[plane],
+            self.z_send.at[plane],
+            self.zi_recv.at[plane],
+            self.spot.outer if number == 1 else self.spot.inner,
+        )
+
+        @pl.when(self.spot.mid == 1)
+        def _():
+            self.wait(land, recv, plane)
+            own[...] = (own[...].astype(F32) + land[plane].astype(F32)).astype(BF)
+            copy.start()
+
+        self.sent_mid.append(copy)
+
+    def last(self, result):
+        plane = self.spot.plane(0)
+        self.wait(self.zi, self.zi_recv, plane)
+        result[...] = self.own(plane)[...].astype(F32) + self.zi[plane].astype(F32)
+
+        @pl.when(self.spot.mid == 1)
+        def _():
+            self.wait(self.zo, self.zo_recv, plane)
+            result[...] += self.zo[plane].astype(F32)
+
+    def drain(self):
+        for copy in self.sent:
+            copy.wait_send()
+
+        @pl.when(self.spot.mid == 0)
+        def _():
+            for copy in self.sent_end:
+                copy.wait_send()
+
+        @pl.when(self.spot.mid == 1)
+        def _():
+            for copy in self.sent_mid:
+                copy.wait_send()
+
+
+def backward_kernel(
+    grad_second_ref, tok, pack_ref, pack_grad_ref, normed_ref, mixed_ref, q_ref, lse_ref,
+    cosr, sinr, kb, qb, dsh_ref, kv_ref, wfull_ref, dg_ref, du_ref, dd_ref,
+    grad_input_out, pack_out, att1_out, att2_out, sh_out, keep_out, other_out,
+    wbuf, kv, kvb, kv_x, kv_zo, kv_zi, kv_sum, gst, delta_s, dq,
+    ga, ga4, gq, gq4, gkv, gkv4, n_t, m_t, n_all, m_all, pk, pk4,
+    a1, a1_x, a1_zo, a1_zi, a1_sum, a2, a2_x, a2_zo, a2_zi, a2_sum, r1, r2,
+    sh, sh_zo, sh_zi, sh_sum, sh_chunk, sh_land, r3, po, cb,
+    sem, sem_kv, sem_a1, sem_a2, sem_sh, ring_recv, ring_send,
+):
+    spot = Spot(4)
+    sems = Sems(sem)
+    rows, width = tok.shape
+    pairs = width // PAIR
+    shard = width // 4
+    loads = [pltpu.make_async_copy(wfull_ref.at[i], wbuf.at[i], sems.new()) for i in (3, 0, 1, 2)]
+    loads.insert(1, pltpu.make_async_copy(kv_ref, kv, sems.new()))
+    loads.append(pltpu.make_async_copy(dsh_ref, sh, sems.new()))
+    for copy in loads:
+        copy.start()
+    grads = (dg_ref, du_ref, dd_ref)
+
+    def block(ref, w):
+        return ref.at[pl.ds(pl.multiple_of(shard * w, 64), shard)]
+
+    mine = []
+    for a in range(3):
+        for row in range(2):
+            mine.append(
+                pltpu.make_async_copy(block(grads[a], 2 * row + spot.c), po.at[a, row], sems.new())
+            )
+            mine[-1].start()
+    greet((spot.core, spot.across, spot.corner, spot.column, spot.inner), (spot.mid, spot.outer))
+    grad_second = grad_second_ref[...]
+    ga[...] = grad_second.astype(BF)
+    grads_w = Spread(spot, lambda w: ga, lambda w: ga4.at[w], sems)
+    swaps = []
+    for a in range(3):
+        for row in range(2):
+            swaps.append(
+                remote(
+                    block(grads[a], 2 * row + 1 - spot.c),
+                    cb.at[a, row],
+                    sems.new(),
+                    sems.new(),
+                    spot.core,
+                )
+            )
+            swaps[-1].start()
+    loads[-1].wait()
+    shared = Reduce(spot, sh, None, sh_zo, sh_zi, sem_sh, folded=True)
+    for number in (3, 2, 1):
+        shared.launch(number)
+    mixed = mixed_ref[...]
+    n_t[...] = normed_ref[...].T
+    m_t[...] = mixed.astype(BF).T
+
+    def columns(ref):
+        return lambda w: ref.at[:, pl.ds(pl.multiple_of(rows * w, 128), rows)]
+
+    normed_w = Spread(spot, lambda w: block(n_t, w), columns(n_all), sems)
+    mixed_w = Spread(spot, lambda w: block(m_t, w), columns(m_all), sems)
+    loads[0].wait()
+    grad_mixed = nt(ga[...], wbuf[3]).astype(BF)
+    product = grad_mixed.astype(F32) * mixed
+    for j in range(pairs):
+        lanes = slice(PAIR * j, PAIR * (j + 1))
+        gst[j] = stack_pair(grad_mixed[:, lanes])
+        delta_s[j] = jnp.broadcast_to(
+            jnp.sum(stack_pair(product[:, lanes]), axis=1, keepdims=True), (2 * rows, PAIR)
+        )
+    dq[...] = jnp.zeros_like(dq)
+    loads[1].wait()
+    q_block = qb[...]
+
+    def chunk(number):
+        plane = spot.plane(number)
+        k_block = kb[:, pl.ds(pl.multiple_of(2 * rows * plane, 2 * rows), 2 * rows)]
+        allowed = k_block <= q_block
+
+        def one_pair(j, carry):
+            lane = pl.multiple_of(PAIR * j, PAIR)
+            both = pl.ds(2 * plane, 2)
+            key = kv[both, :, pl.ds(lane, PAIR)].reshape(2 * rows, PAIR)
+            value = kv[both, :, pl.ds(width + lane, PAIR)].reshape(2 * rows, PAIR)
+            query, grad = q_ref[j], gst[j]
+            scores = nt(query, key)
+            probs = jnp.where(allowed, jnp.exp(scores - lse_ref[j][:, 0:1]), 0.0)
+            inner = nt(grad, value) - delta_s[j][:, 0:1]
+            grad_scores = (probs * inner * HD**-0.5).astype(BF)
+            dq[j] += nn(grad_scores, key)
+            grad_key = tn(grad_scores, query) * HD**0.5
+            grad_value = tn(probs.astype(BF), grad)
+            kvb[both, :, pl.ds(lane, PAIR)] = grad_key.astype(BF).reshape(2, rows, PAIR)
+            kvb[both, :, pl.ds(width + lane, PAIR)] = grad_value.astype(BF).reshape(2, rows, PAIR)
+            return carry
+
+        lax.fori_loop(0, pairs, one_pair, 0)
+
+    kv_grad = Reduce(spot, kvb, kv_x, kv_zo, kv_zi, sem_kv)
+    chunk(3)
+    kv_grad.side(3)
+
+    for copy in mine:
+        copy.wait()
+    across = []
+    for a in range(3):
+        for row in range(2):
+            swaps[2 * a + row].wait_recv()
+
+        def add(i, carry):
+            at = pl.ds(pl.multiple_of(16 * i, 16), 16)
+            for row in range(2):
+                total = po[a, row, at].astype(F32) + cb[a, row, at].astype(F32)
+                po[a, row, at] = total.astype(BF)
+            return carry
+
+        lax.fori_loop(0, shard // 16, add, 0)
+        across.append(
+            remote(po.at[a, 1 - spot.y], other_out.at[a], sems.new(), sems.new(), spot.across)
+        )
+        across[-1].start()
+    keeps = [
+        pltpu.make_async_copy(po.at[a, spot.y], keep_out.at[a], sems.new()) for a in range(3)
+    ]
+    for copy in keeps:
+        copy.start()
+
+    shared.relay(3)
+    chunk(2)
+    kv_grad.side(2)
+    kv_grad.meet(3)
+    kv_grad.launch(3)
+    shared.relay(2)
+    chunk(1)
+    kv_grad.side(1)
+    kv_grad.meet(2)
+    kv_grad.launch(2)
+    kv_grad.relay(3)
+    shared.relay(1)
+    chunk(0)
+    kv_grad.side(0)
+    cosine, sine = cosr[...], sinr[...]
+    gq[...] = turn(
+        jnp.concatenate([unstack_pair(dq[j]) for j in range(pairs)], axis=1), cosine, -sine
+    ).astype(BF)
+    query_w = Spread(spot, lambda w: gq, lambda w: gq4.at[w], sems)
+    shared.last(sh_sum)
+    sh_chunk[...] = sh_sum[...].astype(BF)
+    part = 2 * shard // 2
+
+    def piece(w):
+        return sh_chunk.at[pl.ds(pl.multiple_of(part * w, 64), part)]
+
+    def place(w):
+        return r3.at[spot.k, pl.ds(pl.multiple_of(part * w, 64), part)]
+
+    shared_w = Spread(spot, piece, place, sems)
+    rest = sh_chunk.shape[0] - 4 * part
+    r3[spot.k, pl.ds(4 * part, rest)] = sh_chunk[pl.ds(4 * part, rest)]
+    kv_grad.meet(1)
+    kv_grad.launch(1)
+    kv_grad.relay(2)
+    for part_w in (grads_w, normed_w, mixed_w):
+        part_w.finish()
+    out_grad = nn(m_all[...], ga4[...].reshape(4 * rows, width))
+    kv_grad.meet(0)
+    kv_grad.relay(1)
+    query_w.finish()
+    query_grad = nn(n_all[...], gq4[...].reshape(4 * rows, width))
+    half = jnp.concatenate([out_grad, query_grad], axis=0).astype(BF)
+    a1[...] = half.reshape(a1.shape)
+    first = Reduce(spot, a1, a1_x, a1_zo, a1_zi, sem_a1)
+    for number in (3, 2, 1, 0):
+        first.side(number)
+    shared_w.finish()
+    ring3 = Ring(spot, r3, ring_recv.at[2], ring_send.at[2])
+    ring3.start()
+    kv_grad.last(kv_sum)
+    gkv[:, 0:width] = turn(kv_sum[:, 0:width], cosine, -sine).astype(BF)
+    gkv[:, width : 2 * width] = kv_sum[:, width : 2 * width].astype(BF)
+    kv_w = Spread(spot, lambda w: gkv, lambda w: gkv4.at[w], sems)
+    for copy in loads[2:5]:
+        copy.wait()
+    grad_normed = nt(gq[...], wbuf[0]) + nt(gkv[:, 0:width], wbuf[1])
+    grad_normed = grad_normed + nt(gkv[:, width : 2 * width], wbuf[2])
+    inputs = tok[...].astype(F32)
+    scale = lax.rsqrt(jnp.mean(inputs * inputs, axis=-1, keepdims=True) + EPS)
+    weighted = grad_normed * pack_ref[0:1]
+    mean = jnp.mean(weighted * inputs, axis=-1, keepdims=True)
+    grad_input_out[...] = (
+        grad_second + scale * weighted - inputs * (scale * scale * scale * mean)
+    )
+    gain_grad = jnp.sum(grad_normed * inputs * scale, axis=0, keepdims=True)
+    pk[...] = jnp.concatenate([gain_grad, pack_grad_ref[1:16]], axis=0)
+    pack_w = Spread(spot, lambda w: pk, lambda w: pk4.at[w], sems)
+    for number in (3, 2, 1):
+        first.meet(number)
+        first.launch(number)
+    first.meet(0)
+    first.relay(3)
+    ring3.step(1)
+    first.relay(2)
+    first.relay(1)
+    kv_w.finish()
+    pack_w.finish()
+    grad_kv = gkv4[...].reshape(4 * rows, 2 * width)
+    both = nn(n_all[...], grad_kv)
+    both = jnp.concatenate([both[:, 0:width], both[:, width : 2 * width]], axis=0).astype(BF)
+    size = both.shape[0] // 8
+    extra = (pk4[0] + pk4[1] + pk4[2] + pk4[3]).astype(BF)
+    for r in range(8):
+        a2[r, 0:size] = both[size * r : size * (r + 1)]
+        a2[r, size : size + 16] = extra
+    second = Reduce(spot, a2, a2_x, a2_zo, a2_zi, sem_a2)
+    for number in (3, 2, 1, 0):
+        second.side(number)
+    first.last(a1_sum)
+    r1[spot.k] = a1_sum[...].astype(BF)
+    ring1 = Ring(spot, r1, ring_recv.at[0], ring_send.at[0])
+    ring1.start()
+    for number in (3, 2, 1):
+        second.meet(number)
+        second.launch(number)
+    second.meet(0)
+    ring3.step(2)
+    second.relay(3)
+    second.relay(2)
+    second.relay(1)
+    ring3.step(3)
+    ring1.step(1)
+    second.last(a2_sum)
+    r2[spot.k] = a2_sum[0:size].astype(BF)
+    ring2 = Ring(spot, r2, ring_recv.at[1], ring_send.at[1])
+    ring2.start()
+    pack_out[...] = a2_sum[size : size + 16]
+    for number in (2, 3):
+        ring1.step(number)
+    for number in (1, 2, 3):
+        ring2.step(number)
+    for ring in (ring3, ring1, ring2):
+        for number in range(4):
+            ring.other(spot.plane(number))
+    saves = [
+        pltpu.make_async_copy(src, dst, sems.new())
+        for src, dst in ((r3, sh_out), (r1, att1_out), (r2, att2_out))
+    ]
+    for copy in saves:
+        copy.start()
+    for copy in across:
+        copy.wait_recv()
+    for copy in swaps + across:
+        copy.wait_send()
+    for part_w in (grads_w, normed_w, mixed_w, query_w, shared_w, kv_w, pack_w):
+        part_w.drain()
+    for part_w in (shared, kv_grad, first, second, ring1, ring2, ring3):
+        part_w.drain()
+    for copy in saves + keeps:
+        copy.wait()
+
+
+def run_backward(
+    grad_second, tok, pack, pack_grad, normed, mixed, q, lse, cosr, sinr, kb, qb, dsh, kv, wfull,
+    dg, du, dd,
+):
+    rows, width = tok.shape
+    pairs = width // PAIR
+    ranks = 8
+    shard, hidden = width // 4, dg.shape[1]
+    size = 2 * shard // ranks
+    tall = dsh.shape[1]
+    any_, vm = pl.BlockSpec(memory_space=pl.ANY), pl.BlockSpec(memory_space=VMEM)
+    shape = jax.ShapeDtypeStruct
+
+    def low(*dims):
+        return VMEM(dims, BF)
+
+    def full(*dims):
+        return VMEM(dims, F32)
+
+    dma = pltpu.SemaphoreType.DMA
+    return pl.pallas_call(
+        backward_kernel,
+        out_shape=(
+            shape((rows, width), F32),
+            shape(pack.shape, F32),
+            shape((ranks, size, width), BF),
+            shape((ranks, size, width), BF),
+            shape((ranks, tall, 128), BF),
+            shape((3, shard, hidden), BF),
+            shape((3, shard, hidden), BF),
+        ),
+        in_specs=[vm] * 12 + [any_] * 6,
+        out_specs=(vm, vm, any_, any_, any_, any_, any_),
+        scratch_shapes=[
+            low(4, width, width),
+            low(ranks, rows, 2 * width),
+            low(ranks, rows, 2 * width),
+            low(4, rows, 2 * width),
+            low(4, rows, 2 * width),
+            low(4, rows, 2 * width),
+            full(rows, 2 * width),
+            low(pairs, 2 * rows, PAIR),
+            full(pairs, 2 * rows, PAIR),
+            full(pairs, 2 * rows, PAIR),
+            low(rows, width),
+            low(4, rows, width),
+            low(rows, width),
+            low(4, rows, width),
+            low(rows, 2 * width),
+            low(4, rows, 2 * width),
+            low(width, rows),
+            low(width, rows),
+            low(shard, 4 * rows),
+            low(shard, 4 * rows),
+            full(16, width),
+            full(4, 16, width),
+            low(ranks, size, width),
+            low(4, size, width),
+            low(4, size, width),
+            low(4, size, width),
+            full(size, width),
+            low(ranks, size + 16, width),
+            low(4, size + 16, width),
+            low(4, size + 16, width),
+            low(4, size + 16, width),
+            full(size + 16, width),
+            low(ranks, size, width),
+            low(ranks, size, width),
+            low(4, tall, 128),
+            low(4, tall, 128),
+            low(4, tall, 128),
+            full(tall, 128),
+            low(tall, 128),
+            low(16, 128),
+            low(ranks, tall, 128),
+            low(3, 2, shard, hidden),
+            low(3, 2, shard, hidden),
+            dma((112,)),
+            dma((5, 4)),
+            dma((5, 4)),
+            dma((5, 4)),
+            dma((5, 4)),
+            dma((3, ranks)),
+            dma((3, 16)),
+        ],
+        compiler_params=pltpu.CompilerParams(
+            collective_id=3, has_side_effects=True, vmem_limit_bytes=58 * 2**20
+        ),
+    )(
+        grad_second, tok, pack, pack_grad, normed, mixed, q, lse, cosr, sinr, kb, qb, dsh, kv,
+        wfull, dg, du, dd,
+    )
 
 
 def contract_product(left, right, left_dim, right_dim):
@@ -1240,205 +1718,60 @@
     slot_order,
     block_deal,
 ):
-    rows_dev = tokens.shape[1]
-    width = tokens.shape[2]
+    rows_dev, width = tokens.shape[1:]
     ranks = lax.axis_size("ctx")
-    heads = width // HD
-    inputs = tokens[0].astype(jnp.float32)
+    shard = width // 4
     here, cosr, sinr = angles_of(block_deal, rows_dev)
-    query_side_block = here // BLK
     kb = (places(0, ranks * rows_dev, block_deal, rows_dev) // BLK)[None, :]
-    qb = jnp.concatenate([query_side_block, query_side_block])[:, None]
+    qb = jnp.concatenate([here // BLK] * 2)[:, None]
     pack = pack_params(gain_attention, gain_mixer, router_weight)
-    (q_st, kv_all, mixed_f, lse, second, mixer, normed, pack_all, wfull, sg_sl, su_sl, eg_full, eu_full, cot4) = run_forward(
-        tokens[0], pack, cosr, sinr, kb, qb, cotangent[0], query_weight, key_weight, value_weight, output_weight, shared_gate, shared_up, expert_gate, expert_up)
-    gain_first, gain_second = pack_all[0], pack_all[1]
-    query_full, key_full, value_full, output_full = wfull[0], wfull[1], wfull[2], wfull[3]
+    (
+        q_st, kv_all, mixed, lse, second, mixer, normed, pack_all, wfull, sg_part, su_part,
+        eg_full, eu_full, cot4,
+    ) = run_forward(
+        tokens[0], pack, cosr, sinr, kb, qb, cotangent[0], query_weight, key_weight,
+        value_weight, output_weight, shared_gate, shared_up, expert_gate, expert_up,
+    )
     route = routes[0]
     top_count = route.shape[1]
     by_choice = route.T.reshape(1, rows_dev * top_count)
     turns = slot_order[0, 0]
     turns = lax.rem(turns, top_count) * rows_dev + lax.div(turns, top_count)
-    (result, grad_second, pack_grad, dsg, dsu, dsd, egate_grad, expert_up_weight_grad, edown_grad) = run_experts(
-        second, mixer, pack_all, cotangent[0], route, by_choice, by_choice.reshape(-1, 1), turns[None, :], turns[:, None],
-        shared_down, sg_sl, su_sl, cot4, eg_full, eu_full, expert_down)
-    query_rot = (8.0 * (q_st[:, :rows_dev] + q_st[:, rows_dev:])).astype(jnp.bfloat16).transpose(1, 0, 2).reshape(rows_dev, width)
-    query3 = query_rot.reshape(rows_dev, heads, HD)
-    query_side = (query3, query_side_block)
-    log_total = lse[:, :, 0].reshape(heads, rows_dev)
-    mixed3 = mixed_f.reshape(rows_dev, heads, HD)
-    scale_one = lax.rsqrt(jnp.mean(inputs * inputs, axis=-1, keepdims=True) + EPS)
-    gain_two_grad = pack_grad[1]
-    router_grad = pack_grad[2:10].T
-    sgate_grad, sup_grad, sdown_grad = dsg, dsu, dsd
-    mixed_low = mixed3.reshape(rows_dev, width).astype(jnp.bfloat16)
-    grad_attention = grad_second.astype(jnp.bfloat16)
-    output_grad = contract_product(mixed_low, grad_attention, 0, 0)
-    grad_mixed = contract_product(grad_attention, output_full, 1, 1).astype(jnp.bfloat16)
-    grad_out3 = grad_mixed.reshape(rows_dev, heads, HD)
-    delta = jnp.sum(grad_out3.astype(jnp.float32) * mixed3, axis=2).T
-    all_keys, all_values = (
-        kv_all[:, :, :width].reshape(ranks * rows_dev, width),
-        kv_all[:, :, width:].reshape(ranks * rows_dev, width),
-    )
-    total_rows = all_keys.shape[0]
-    block_size = KEY_ROWS
-
-    def query_step(grad_sum, offset):
-        key_rows = lax.dynamic_slice_in_dim(all_keys, offset, block_size, 0)
-        value_rows = lax.dynamic_slice_in_dim(all_values, offset, block_size, 0)
-        key_place = places(offset, block_size, block_deal, rows_dev)
-        unused, grad_scores = differentiate(
-            query_side, log_total, delta, grad_out3, key_rows, value_rows, key_place
-        )
-        key3 = key_rows.reshape(block_size, heads, HD)
-        return (
-            grad_sum
-            + jnp.einsum("hqk,khd->qhd", grad_scores, key3, preferred_element_type=jnp.float32),
-            None,
-        )
-
-    offsets = jnp.arange(total_rows // block_size, dtype=jnp.int32) * block_size
-    grad_query3, unused = lax.scan(
-        query_step, jnp.zeros((rows_dev, heads, HD), jnp.float32), offsets
-    )
-    inner_size = KEY_ROWS
-
-    def one_part(offset):
-        key_rows = lax.dynamic_slice_in_dim(all_keys, offset, inner_size, 0)
-        value_rows = lax.dynamic_slice_in_dim(all_values, offset, inner_size, 0)
-        key_place = places(offset, inner_size, block_deal, rows_dev)
-        probs_full, grad_scores = differentiate(
-            query_side, log_total, delta, grad_out3, key_rows, value_rows, key_place
-        )
-        grad_value_rows = jnp.einsum(
-            "hqk,qhd->khd",
-            probs_full.astype(jnp.bfloat16),
-            grad_out3,
-            preferred_element_type=jnp.float32,
-        )
-        grad_key_rows = jnp.einsum(
-            "hqk,qhd->khd", grad_scores, query3, preferred_element_type=jnp.float32
-        )
-        return jnp.concatenate(
-            [grad_key_rows.reshape(inner_size, width), grad_value_rows.reshape(inner_size, width)],
-            axis=1,
-        )
-
-    parts = lax.map(
-        one_part,
-        jnp.arange(lax.axis_size("ctx") * rows_dev // inner_size, dtype=jnp.int32) * inner_size,
-    )
-    key_value_grad = lax.psum_scatter(
-        parts.reshape(lax.axis_size("ctx") * rows_dev, 2 * width),
-        "ctx",
-        scatter_dimension=0,
-        tiled=True,
-    )
-    grad_key_pre = rotate(key_value_grad[:, :width], here, -1.0).astype(jnp.bfloat16)
-    grad_value_low = key_value_grad[:, width:].astype(jnp.bfloat16)
-    grad_query_pre = rotate(grad_query3.reshape(rows_dev, width), here, -1.0).astype(jnp.bfloat16)
-    query_grad = contract_product(normed, grad_query_pre, 0, 0)
-    key_grad = contract_product(normed, grad_key_pre, 0, 0)
-    value_grad = contract_product(normed, grad_value_low, 0, 0)
-    grad_normed = (
-        contract_product(grad_query_pre, query_full, 1, 1)
-        + contract_product(grad_key_pre, key_full, 1, 1)
-        + contract_product(grad_value_low, value_full, 1, 1)
-    )
-    through_one, gain_one_grad = rms_back(inputs, scale_one, gain_first, grad_normed)
-    grad_input = grad_second + through_one
-    (
-        gain_one_share,
-        query_share,
-        key_share,
-        value_share,
-        output_share,
-        gain_two_share,
-        router_share,
-        sgate_share,
-        sup_share,
-        sdown_share,
-        egate_share,
-        expert_up_portion,
-        edown_share,
-    ) = (
-        lax.psum_scatter(
-            gain_one_grad.astype(jnp.bfloat16), "wt", scatter_dimension=0, tiled=True
-        ).astype(jnp.float32),
-        lax.psum_scatter(
-            query_grad.astype(jnp.bfloat16), "wt", scatter_dimension=0, tiled=True
-        ).astype(jnp.float32),
-        lax.psum_scatter(
-            key_grad.astype(jnp.bfloat16), "wt", scatter_dimension=0, tiled=True
-        ).astype(jnp.float32),
-        lax.psum_scatter(
-            value_grad.astype(jnp.bfloat16), "wt", scatter_dimension=0, tiled=True
-        ).astype(jnp.float32),
-        lax.psum_scatter(
-            output_grad.astype(jnp.bfloat16), "wt", scatter_dimension=0, tiled=True
-        ).astype(jnp.float32),
-        lax.psum_scatter(
-            gain_two_grad.astype(jnp.bfloat16), "wt", scatter_dimension=0, tiled=True
-        ).astype(jnp.float32),
-        lax.psum_scatter(
-            router_grad.astype(jnp.bfloat16), "wt", scatter_dimension=0, tiled=True
-        ).astype(jnp.float32),
-        lax.all_to_all(sgate_grad, "wt", split_axis=0, concat_axis=1, tiled=True).astype(jnp.float32),
-        lax.all_to_all(sup_grad, "wt", split_axis=0, concat_axis=1, tiled=True).astype(jnp.float32),
-        sdown_grad.astype(jnp.float32),
-        lax.psum_scatter(
-            egate_grad.astype(jnp.bfloat16), "wt", scatter_dimension=0, tiled=True
-        ).astype(jnp.float32),
-        lax.psum_scatter(
-            expert_up_weight_grad.astype(jnp.bfloat16), "wt", scatter_dimension=0, tiled=True
-        ).astype(jnp.float32),
-        lax.psum_scatter(
-            edown_grad.astype(jnp.bfloat16), "wt", scatter_dimension=0, tiled=True
-        ).astype(jnp.float32),
-    )
-    (
-        gain_one_sum,
-        query_sum,
-        key_sum,
-        value_sum,
-        output_sum,
-        gain_two_sum,
-        router_sum,
-        sgate_sum,
-        sup_sum,
-        sdown_sum,
-    ) = lax.psum(
-        (
-            gain_one_share,
-            query_share,
-            key_share,
-            value_share,
-            output_share,
-            gain_two_share,
-            router_share,
-            sgate_share,
-            sup_share,
-            sdown_share,
-        ),
-        "ctx",
-    )
+    result, grad_second, pack_grad, dsh, dg, du, dd = run_experts(
+        second, mixer, pack_all, cotangent[0], route, by_choice, by_choice.reshape(-1, 1),
+        turns[None, :], turns[:, None], shared_down, sg_part, su_part, cot4, eg_full, eu_full,
+        expert_down,
+    )
+    grad_input, pack_sum, att1, att2, sh, keep, other = run_backward(
+        grad_second, tokens[0], pack_all, pack_grad, normed, mixed, q_st, lse, cosr, sinr, kb, qb,
+        dsh, kv_all, wfull, dg, du, dd,
+    )
+    att1 = att1.reshape(2 * shard, width).astype(F32)
+    att2 = att2.reshape(2 * shard, width).astype(F32)
+    mine = lax.dynamic_slice(
+        pack_sum, (0, lax.axis_index("wt") * shard), (pack_sum.shape[0], shard)
+    )
+    both = sh[:, :width].reshape(2, 4, 4, 2, shard // 2, 128)
+    both = both.transpose(3, 0, 4, 2, 1, 5).reshape(2, shard, shared_gate.shape[1]).astype(F32)
+    down = sh[:, width:].reshape(ranks, width // 128, -1, 128).transpose(0, 2, 1, 3)
+    down = down.reshape(shared_down.shape).astype(F32)
+    sums = [keep[a].astype(F32) + other[a].astype(F32) for a in range(3)]
     return (
         result[None],
         grad_input[None],
-        gain_one_sum,
-        query_sum,
-        key_sum,
-        value_sum,
-        output_sum,
-        gain_two_sum,
-        router_sum,
-        sgate_sum,
-        sup_sum,
-        sdown_sum,
-        egate_share,
-        expert_up_portion,
-        edown_share,
+        mine[0],
+        att1[shard:],
+        att2[:shard],
+        att2[shard:],
+        att1[:shard],
+        mine[1],
+        mine[2 : 2 + router_weight.shape[1]].T,
+        both[0],
+        both[1],
+        down,
+        sums[0],
+        sums[1],
+        sums[2],
     )
 
 

time: 842 us -> 354 us (0.42)
  waiting for transfers between devices: 304 us -> 0 us
  blocking collectives: 213 us -> 0 us
  Pallas kernels: 157 us -> 311 us
  matrix products: 38.1 us -> 0 us
  local copies, waits for them, and re-layouts: 66.5 us -> 31.2 us
  other arithmetic: 34.2 us -> 9.47 us
  between operations: 15.3 us -> 0.94 us
    reduce_scatter x8 -> x0, waiting for transfers between devices: 280 us -> none  [the longest x1 84.7 us: fast_body(): lax.psum_scatter(parts.reshape(lax.axis_size('ctx') * rows_dev, 2 * width...]
    psum x1 -> x0, blocking collectives: 192 us -> none  [fast_body(): lax.psum((gain_one_share, query_share, key_share, value_share, output_sha...]
    pallas_call x0 -> x1, Pallas kernels: none -> 151 us  [run_backward(): pl.pallas_call(backward_kernel, out_shape=(shape((rows, width), F32), sha...]
    dot_general x18 -> x0, matrix products: 38.1 us -> none  [the longest x8 13.8 us: contract_product(): lax.dot_general(left, right, (((left_dim,), (right_dim,)), ((), ())), pre...]
    dynamic_slice x8 -> x0, local copies, waits for them, and re-layouts: 15.4 us -> none  [the longest x2 6.12 us: query_step(): value_rows = lax.dynamic_slice_in_dim(all_values, offset, block_size, 0)]
    all_to_all x1 -> x0, blocking collectives: 15.3 us -> none  [fast_body(): lax.all_to_all(sgate_grad, 'wt', split_axis=0, concat_axis=1, tiled=True)]
    dynamic_update_slice x4 -> x0, local copies, waits for them, and re-layouts: 14.6 us -> none  [fast_body(): lax.map(one_part, jnp.arange(lax.axis_size('ctx') * rows_dev // inner_siz...]
    psum x1 -> x0, waiting for transfers between devices: 12.2 us -> none  [fast_body(): lax.psum((gain_one_share, query_share, key_share, value_share, output_sha...]
  transfers between devices with their start and end apart: 11 -> 0, of which waited for: 10 -> 0; matrix products, arithmetic and copies ran while one was open for 7% -> 0% of each run, Pallas kernels for 0% -> 0%
where the time goes in v3:
time: 354 us; the launch traced here: 353 us
  Pallas kernels  311 us (88%)
  local copies, waits for them, and re-layouts  31.2 us (9%)
  other arithmetic  9.47 us (3%)
    pallas_call x1, Pallas kernels, run_backward(): pl.pallas_call(backward_kernel, out_shape=(shape((rows, width), F32), sha...  151 us
    pallas_call x1, Pallas kernels, run_forward(): pl.pallas_call(forward_kernel, out_shape=(shape((pairs, 2 * rows, PAIR),...  96.2 us
    pallas_call x1, Pallas kernels, run_experts(): pl.pallas_call(experts_kernel, out_shape=(shape((rows, width), BF), shape...  64.4 us
    unnamed x60, local copies, waits for them, and re-layouts  15.7 us

profile of v3, /device:TPU:0, one launch (start us, length us, event | category | flops | bytes accessed | tf_op | source)
XLA Modules:
  0.0 352.9 jit_solution(6872381599858972917)
XLA Ops:
  0.7 0.7 select_reduce_fusion.1
  1.5 0.3 fusion.2
  1.8 0.2 pad_maximum_fusion
  2.0 0.0 copy-start.6
  2.0 0.0 copy-start.7
  2.0 0.7 broadcast_in_dim.57
  2.7 0.7 broadcast_in_dim.58
  3.3 0.1 pad.13.clone
  3.4 0.8 maximum_convert_fusion
  4.2 0.3 dynamic_update_slice.3.pack
  4.5 0.1 copy.64.qb
  4.7 0.0 copy-start
  4.7 0.8 select_reduce_fusion
  5.5 0.0 copy-start.18
  5.5 0.0 copy-start.1
  5.5 0.9 copy-done.1
  6.5 0.9 copy-done.5
  7.4 1.0 copy-done.11
  8.4 1.0 copy-done.12
  9.3 1.0 copy-done.13
  10.3 1.0 copy-done.14
  11.2 96.2 %shard_map.289 = (bf16[6,256,128]{2,1,0:T(8,128)(2,1)S(1)}, bf16[8,128,1536]{2,1,0:T(8,128)(2,1)}, f32[128,768]{1,0:T(8,128)S(1)}, f32[6,256,128]{2,1,0:T(8,128)...) custom-call(bf16[128,768]{1,0:T(8,128)(2,1)S(1)} %bitcast.48, ...), custom_call_target="tpu_custom_call" | custom-call | tf_op jit(solution)/shard_map/pallas_call | solution.py:355
  107.4 0.0 copy-done.6
  107.4 0.0 copy-done.7
  107.4 0.0 copy-done
  107.4 0.0 copy-done.18
  107.5 0.0 copy-start.2
  107.5 0.9 copy-done.2
  108.3 0.9 copy-done.3
  109.2 0.9 copy-done.4
  110.1 0.7 copy-done.8
  110.8 0.7 copy-done.9
  111.6 0.7 copy-done.10
  112.3 0.7 copy-done.15
  113.0 0.7 copy-done.16
  113.7 0.6 copy-done.17
  114.3 0.0 copy-done.27
  114.3 0.1 copy.65
  114.4 0.1 copy.66
  114.5 0.8 copy.71.e_col
  115.3 0.0 copy-done.26
  115.3 0.1 copy.68
  115.5 0.7 fusion.1.o_col
  116.2 0.6 fusion.8.o_row
  116.7 64.4 %shard_map.290 = (bf16[128,768]{1,0:T(8,128)(2,1)}, f32[128,768]{1,0:T(8,128)}, f32[16,768]{1,0:T(8,128)}, bf16[4,1152,128]{2,1,0:T(8,128)(2,1)}, bf16[768,2048]...) custom-call(f32[128,768]{1,0:T(8,128)} %copy-done.8, bf16[128,768]{1,0:T(8,128)(2,1)} %copy-done.16, ...), custom_call_target="tpu_custom_call" | custom-call | tf_op jit(solution)/shard_map/pallas_call | solution.py:701
  181.2 150.7 %shard_map.291 = (f32[128,768]{1,0:T(8,128)}, f32[16,768]{1,0:T(8,128)}, bf16[8,48,768]{2,1,0:T(8,128)(2,1)}, bf16[8,48,768]{2,1,0:T(8,128)(2,1)}, bf16[8,1152,1...) custom-call(f32[128,768]{1,0:T(8,128)} %get-tuple-element.52.grad_second_ref, ...), custom_call_target="tpu_custom_call" | custom-call | tf_op jit(solution)/shard_map/pallas_call | solution.py:1130
  331.9 4.9 %add_bitcast_fusion = (f32[192,2048]{1,0:T(8,128)}, f32[192,2048]{1,0:T(8,128)}, f32[192,2048]{1,0:T(8,128)}) fusion(bf16[3,192,2048]{2,1,0:T(8,128)(2,1)} %get-tuple-element.70, bf16[3,192,2048]{2,1,0:T(8,128)(2,1)} %get-tuple-element.69), kind=kLoop, calls=%fused_computation.2 | loop fusion | flops 3538944 | bytes 9437184 | tf_op jit(solution)/shard_map/add | solution.py:1758
  336.8 0.1 slice.76
  336.9 0.4 convert_bitcast_fusion
  337.3 0.2 fusion.12
  337.6 1.0 copy.73
  338.6 1.8 squeeze.41
  340.4 1.0 copy.74
  341.4 1.8 squeeze.42
  343.1 1.2 slice.79
  344.3 0.5 copy.75
  344.8 1.5 copy.78
  346.3 1.1 fusion.13
  347.4 0.1 copy-done.20
  347.5 1.1 fusion.14
  348.6 1.4 dynamic-slice_bitcast_fusion
  350.1 1.4 fusion.15
  351.5 0.7 copy.82
  352.2 0.7 copy.83
  (37 shorter events, 0.2 us)
Async XLA Ops:
  2.0 105.5 %copy-start.6 = (f32[128,128]{1,0:T(8,128)}, f32[128,128]{1,0:T(8,128)S(1)}, u32[]{:S(2)}) copy-start(f32[128,128]{1,0:T(8,128)S(1)} %get-tuple-element.87.cosr) | copy-start | bytes 196612
  2.0 105.5 %copy-start.7 = (f32[128,128]{1,0:T(8,128)}, f32[128,128]{1,0:T(8,128)S(1)}, u32[]{:S(2)}) copy-start(f32[128,128]{1,0:T(8,128)S(1)} %get-tuple-element.88.sinr) | copy-start | bytes 196612
  4.7 102.8 %copy-start = (s32[256,1]{1,0:T(8,128)}, s32[256,1]{1,0:T(8,128)S(1)}, u32[]{:S(2)}) copy-start(s32[256,1]{1,0:T(8,128)S(1)} %copy.64.qb) | copy-start | bytes 3076
  5.5 101.9 %copy-start.18 = (s32[1,1024]{1,0:T(1,128)}, s32[1,1024]{1,0:T(1,128)S(1)}, u32[]{:S(2)}) copy-start(s32[1,1024]{1,0:T(1,128)S(1)} %and_select_fusion.kb) | copy-start | bytes 12292
  5.5 0.9 copy-start.1
  6.5 0.9 copy-start.5
  7.4 1.0 copy-start.11
  8.3 1.0 copy-start.12
  9.3 1.0 copy-start.13
  10.3 1.0 copy-start.14
  11.2 103.1 %copy-start.27 = (s32[1,128,2]{1,2,0:T(2,128)S(1)}, s32[1,128,2]{1,2,0:T(2,128)}, u32[]{:S(2)}) copy-start(s32[1,128,2]{1,2,0:T(2,128)} %param.33) | copy-start | bytes 3076
  11.2 104.1 %copy-start.26 = (s32[1,1,256]{2,1,0:T(1,128)S(1)}, s32[1,1,256]{2,1,0:T(1,128)}, u32[]{:S(2)}) copy-start(s32[1,1,256]{2,1,0:T(1,128)} %param.34) | copy-start | bytes 3076
  107.5 0.9 copy-start.2
  108.3 0.9 copy-start.3
  109.2 0.9 copy-start.4
  110.1 0.7 copy-start.8
  110.8 0.7 copy-start.9
  111.6 0.7 copy-start.10
  112.3 0.7 copy-start.15
  113.0 0.7 copy-start.16
  113.7 0.6 copy-start.17
  114.4 2.3 copy-start.22
  114.5 2.3 copy-start.25
  331.9 5.0 %copy-start.19 = (bf16[8,1152,128]{2,1,0:T(8,128)(2,1)S(1)}, bf16[8,1152,128]{2,1,0:T(8,128)(2,1)}, u32[]{:S(2)}) copy-start(bf16[8,1152,128]{2,1,0:T(8,128)(2,1)} %get-tuple-element.68) | copy-start | bytes 7077892
  344.8 1.5 copy-start.21
  346.3 1.2 copy-start.20
  347.4 4.0 %copy-start.24 = (bf16[128,768]{1,0:T(8,128)(2,1)S(1)}, bf16[128,768]{1,0:T(8,128)(2,1)}, u32[]{:S(2)}) copy-start(bf16[128,768]{1,0:T(8,128)(2,1)} %get-tuple-element.51) | copy-start | bytes 589828
  347.4 4.7 %copy-start.23 = (f32[128,768]{1,0:T(8,128)S(1)}, f32[128,768]{1,0:T(8,128)}, u32[]{:S(2)}) copy-start(f32[128,768]{1,0:T(8,128)} %get-tuple-element.64) | copy-start | bytes 1179652

commit v4 on v3

--- a/solution.py
+++ b/solution.py
@@ -20,6 +20,7 @@
 BF = jnp.bfloat16
 F32 = jnp.float32
 PAIR = 2 * HD
+VMEM_BYTES = 63 * 2**20
 
 
 class Spot:
@@ -104,6 +105,53 @@
         self.onward.wait_send()
 
 
+class Share:
+    def __init__(self, spot, src, dst, sems):
+        self.spot, self.dst, self.sems = spot, dst, sems
+        self.rows = src.shape[0]
+        self.half = self.rows // 2
+        here = self.block(spot.w)
+        half = pl.ds(pl.multiple_of(self.half * spot.x, 32), self.half)
+        self.local = pltpu.make_async_copy(src, here, sems.new())
+        self.to_core = remote(src, here, sems.new(), sems.new(), spot.core)
+        self.to_across = remote(
+            src.at[half], self.part(spot.w, spot.x), sems.new(), sems.new(), spot.across
+        )
+        for copy in (self.to_across, self.to_core, self.local):
+            copy.start()
+
+    def block(self, w):
+        return self.dst.at[pl.ds(pl.multiple_of(self.rows * w, 64), self.rows)]
+
+    def part(self, w, x):
+        return self.dst.at[pl.ds(pl.multiple_of(self.rows * w + self.half * x, 32), self.half)]
+
+    def forward(self):
+        spot = self.spot
+        self.to_across.wait_recv()
+        part = self.part(spot.across[1], spot.x)
+        self.aside = remote(part, part, self.sems.new(), self.sems.new(), spot.column)
+        self.onward = remote(part, part, self.sems.new(), self.sems.new(), spot.core)
+        self.aside.start()
+        self.onward.start()
+
+    def second(self):
+        self.aside.wait_recv()
+        part = self.part(self.spot.across[1], 1 - self.spot.x)
+        self.rest = remote(part, part, self.sems.new(), self.sems.new(), self.spot.core)
+        self.rest.start()
+
+    def finish(self):
+        self.local.wait()
+        self.to_core.wait_recv()
+        self.onward.wait_recv()
+        self.rest.wait_recv()
+
+    def drain(self):
+        for copy in (self.to_core, self.to_across, self.aside, self.onward, self.rest):
+            copy.wait_send()
+
+
 class Spread:
     def __init__(self, spot, pick, place, sems, local=True):
         self.copies = []
@@ -168,65 +216,67 @@
 
 
 class Ring:
-    def __init__(self, spot, blocks, recv, send):
-        self.spot, self.blocks, self.recv, self.send = spot, blocks, recv, send
+    def __init__(self, spot, blocks, recv, send, parts=1):
+        self.spot, self.blocks, self.recv, self.send, self.parts = spot, blocks, recv, send, parts
+        self.ranks = blocks.shape[0]
         self.used = 0
         self.sent, self.sent_mid = [], []
 
-    def copy(self, slot, to):
+    def piece(self, slot, part):
+        rows = self.blocks.shape[1] // self.parts
+        return self.blocks.at[slot, pl.ds(rows * part, rows)]
+
+    def copy(self, slot, part, to):
         self.used += 1
         return remote(
-            self.blocks.at[slot],
-            self.blocks.at[slot],
+            self.piece(slot, part),
+            self.piece(slot, part),
             self.send.at[self.used - 1],
-            self.recv.at[slot],
+            self.recv.at[slot + self.ranks * part],
             to,
         )
 
-    def arrived(self, slot):
+    def arrived(self, slot, part):
         remote(
-            self.blocks.at[slot],
-            self.blocks.at[slot],
+            self.piece(slot, part),
+            self.piece(slot, part),
             self.send.at[0],
-            self.recv.at[slot],
+            self.recv.at[slot + self.ranks * part],
             self.spot.column,
         ).wait_recv()
 
     def start(self):
         spot = self.spot
-        own = self.copy(spot.k, spot.inner)
-        side = self.copy(spot.k, spot.column)
-        back = self.copy(spot.k, spot.outer)
-        own.start()
-
-        @pl.when(spot.mid == 1)
+        for part in range(self.parts):
+            own = self.copy(spot.k, part, spot.inner)
+            side = self.copy(spot.k, part, spot.column)
+            back = self.copy(spot.k, part, spot.outer)
+            own.start()
+            self.middle(back)
+            side.start()
+            self.sent += [own, side]
+            self.sent_mid += [back]
+
+    def middle(self, copy):
+        @pl.when(self.spot.mid == 1)
         def _():
-            back.start()
-
-        side.start()
-        self.sent += [own, side]
-        self.sent_mid += [back]
+            copy.start()
 
     def step(self, number):
         spot = self.spot
-        plane = spot.plane(number)
-        if number > 0:
-            slot = 2 * plane + spot.x
-            self.arrived(slot)
-            along = self.copy(slot, spot.inner if number == 1 else spot.outer)
-
-            @pl.when(spot.mid == 1)
-            def _():
-                along.start()
-
-            side = self.copy(slot, spot.column)
+        slot = 2 * spot.plane(number) + spot.x
+        for part in range(self.parts):
+            self.arrived(slot, part)
+            along = self.copy(slot, part, spot.inner if number == 1 else spot.outer)
+            self.middle(along)
+            side = self.copy(slot, part, spot.column)
             side.start()
             self.sent += [side]
             self.sent_mid += [along]
-        return plane
-
-    def other(self, plane):
-        self.arrived(2 * plane + 1 - self.spot.x)
+
+    def other(self, number):
+        for part in range(self.parts):
+            self.arrived(2 * self.spot.plane(number) + 1 - self.spot.x, part)
 
     def drain(self):
         for copy in self.sent:
@@ -238,175 +288,127 @@
                 copy.wait_send()
 
 
-def forward_kernel(
-    tok, pack, cosr, sinr, kb, qb, cot, wq, wk, wv, wo, sg, su, eg, eu,
-    q_out, kv_out, mixed_out, lse_out, second_out, mixer_out, normed_out, pack_out,
-    wfull_out, sg_out, su_out, eg_out, eu_out, cot_out,
-    wbuf, kv, packs, top, low, acc, sem, kv_recv, kv_send,
-):
-    spot = Spot(4)
-    sems = Sems(sem)
-    rows = tok.shape[0]
-    width = tok.shape[1]
-    pairs = width // PAIR
-    greet((spot.core, spot.across, spot.corner, spot.column, spot.inner), (spot.mid, spot.outer))
-    params = Spread(spot, lambda w: pack, lambda w: packs.at[w], sems)
-    key_w = Gather(spot, wk, wbuf.at[1], sems)
-    value_w = Gather(spot, wv, wbuf.at[2], sems)
-    query_w = Gather(spot, wq, wbuf.at[0], sems)
-    inputs = tok[...].astype(F32)
-    scale = lax.rsqrt(jnp.mean(inputs * inputs, axis=-1, keepdims=True) + EPS)
-    scaled = inputs * scale
-    params.finish()
-    pack_all = packs[0] + packs[1] + packs[2] + packs[3]
-    pack_out[...] = pack_all
-    normed = (scaled * pack_all[0:1]).astype(BF)
-    normed_out[...] = normed
-    cosine, sine = cosr[...], sinr[...]
-    key_w.forward()
-    value_w.forward()
-    key_w.finish()
-    kv[spot.k, :, 0:width] = turn(nn(normed, wbuf[1]), cosine, sine).astype(BF)
-    value_w.finish()
-    kv[spot.k, :, width : 2 * width] = nn(normed, wbuf[2]).astype(BF)
-    ring = Ring(spot, kv, kv_recv, kv_send)
-    ring.start()
-    query_w.forward()
-    out_w = Gather(spot, wo, wbuf.at[3], sems)
-    sg_w = Spread(
-        spot,
-        lambda w: sg.at[:, pl.ds(pl.multiple_of(512 * w, 512), 512)],
-        lambda w: sg_out.at[pl.ds(pl.multiple_of(192 * w, 64), 192)],
-        sems,
-    )
-    su_w = Spread(
-        spot,
-        lambda w: su.at[:, pl.ds(pl.multiple_of(512 * w, 512), 512)],
-        lambda w: su_out.at[pl.ds(pl.multiple_of(192 * w, 64), 192)],
-        sems,
-    )
-    cot_w = Spread(spot, lambda w: cot, lambda w: cot_out.at[w], sems)
-    gate_w = Gather(spot, eg, eg_out, sems)
-    up_w = Gather(spot, eu, eu_out, sems)
-    query_w.finish()
-    query = turn(nn(normed, wbuf[0]), cosine, sine).astype(BF) * jnp.asarray(HD**-0.5, BF)
-    for j in range(pairs):
-        q_out[j] = stack_pair(query[:, PAIR * j : PAIR * (j + 1)])
-    top[...] = jnp.full_like(top, MASKED)
-    low[...] = jnp.zeros_like(low)
-    acc[...] = jnp.zeros_like(acc)
-    q_block = qb[...]
-
-    def chunk(plane):
-        k_block = kb[:, pl.ds(pl.multiple_of(2 * rows * plane, 2 * rows), 2 * rows)]
-        allowed = k_block <= q_block
-
-        def one_pair(j, carry):
-            lane = pl.multiple_of(PAIR * j, PAIR)
-            key = kv[pl.ds(2 * plane, 2), :, pl.ds(lane, PAIR)].reshape(2 * rows, PAIR)
-            value = kv[pl.ds(2 * plane, 2), :, pl.ds(width + lane, PAIR)].reshape(2 * rows, PAIR)
-            scores = jnp.where(allowed, nt(q_out[j], key), MASKED)
-            old = top[j]
-            new = jnp.maximum(old, jnp.max(scores, axis=1, keepdims=True))
-            raised = jnp.where(allowed, jnp.exp(scores - new[:, 0:1]), 0.0)
-            factor = jnp.exp(old - new)
-            top[j] = new
-            low[j] = low[j] * factor + jnp.sum(raised, axis=1, keepdims=True)
-            acc[j] = acc[j] * factor + nn(raised.astype(BF), value)
-            return carry
-
-        lax.fori_loop(0, pairs, one_pair, 0)
-
-    for number in range(4):
-        plane = ring.step(number)
-        ring.other(plane)
-        chunk(plane)
-    saves = [pltpu.make_async_copy(kv, kv_out, sems.new())]
-    saves[0].start()
-    out_w.forward()
-    for j in range(pairs):
-        mixed_out[:, PAIR * j : PAIR * (j + 1)] = unstack_pair(acc[j] / low[j])
-        lse_out[j] = top[j] + jnp.log(low[j])
-    out_w.finish()
-    saves.append(pltpu.make_async_copy(wbuf, wfull_out, sems.new()))
-    saves[1].start()
-    second = inputs + nn(mixed_out[...].astype(BF), wbuf[3])
-    second_out[...] = second
-    scale_two = lax.rsqrt(jnp.mean(second * second, axis=-1, keepdims=True) + EPS)
-    mixer_out[...] = (second * scale_two * pack_all[1:2]).astype(BF)
-    gate_w.forward()
-    up_w.forward()
-    for part in (sg_w, su_w, cot_w, gate_w, up_w):
-        part.finish()
-    for part in (params, key_w, value_w, query_w, out_w, sg_w, su_w, cot_w, gate_w, up_w, ring):
-        part.drain()
-    for copy in saves:
-        copy.wait()
-
-
-def run_forward(tok, pack, cosr, sinr, kb, qb, cot, wq, wk, wv, wo, sg, su, eg, eu):
-    rows, width = tok.shape
-    pairs = width // PAIR
-    ranks = 8
-    any_, vm = pl.BlockSpec(memory_space=pl.ANY), pl.BlockSpec(memory_space=VMEM)
-    shape = jax.ShapeDtypeStruct
-    hidden = eg.shape[1]
-    part = sg.shape[1] // 4
-    return pl.pallas_call(
-        forward_kernel,
-        out_shape=(
-            shape((pairs, 2 * rows, PAIR), BF),
-            shape((ranks, rows, 2 * width), BF),
-            shape((rows, width), F32),
-            shape((pairs, 2 * rows, PAIR), F32),
-            shape((rows, width), F32),
-            shape((rows, width), BF),
-            shape((rows, width), BF),
-            shape(pack.shape, F32),
-            shape((4, width, width), BF),
-            shape((width, part), BF),
-            shape((width, part), BF),
-            shape((width, hidden), BF),
-            shape((width, hidden), BF),
-            shape((4, rows, width), BF),
-        ),
-        in_specs=[vm] * 6 + [any_] * 9,
-        out_specs=(vm, any_, vm, vm, vm, vm, vm, vm, any_, any_, any_, any_, any_, any_),
-        scratch_shapes=[
-            VMEM((4, width, width), BF),
-            VMEM((ranks, rows, 2 * width), BF),
-            VMEM((4,) + pack.shape, F32),
-            VMEM((pairs, 2 * rows, PAIR), F32),
-            VMEM((pairs, 2 * rows, PAIR), F32),
-            VMEM((pairs, 2 * rows, PAIR), F32),
-            pltpu.SemaphoreType.DMA((96,)),
-            pltpu.SemaphoreType.DMA((ranks,)),
-            pltpu.SemaphoreType.DMA((16,)),
-        ],
-        compiler_params=pltpu.CompilerParams(
-            collective_id=1, has_side_effects=True, vmem_limit_bytes=48 * 2**20
-        ),
-    )(tok, pack, cosr, sinr, kb, qb, cot, wq, wk, wv, wo, sg, su, eg, eu)
-
-
-def angles_of(block_deal, rows_dev):
-    here = places(lax.axis_index("ctx") * rows_dev, rows_dev, block_deal, rows_dev)
-    half_size = HD // 2
-    frequency = 10000.0 ** (-jnp.arange(half_size, dtype=F32) / half_size)
-    angles = here.astype(F32)[:, None] * frequency[None, :]
-    cosine, sine = jnp.cos(angles), jnp.sin(angles)
-    cosr = jnp.concatenate([cosine] * 4, axis=1)
-    sinr = jnp.concatenate([-sine, sine, -sine, sine], axis=1)
-    return here, cosr, sinr
-
-
-def pack_params(gain_one, gain_two, router):
-    width = 4 * gain_one.shape[0]
-    shard = jnp.concatenate(
-        [gain_one[None], gain_two[None], router.T, jnp.zeros((6, gain_one.shape[0]), BF)], axis=0
-    ).astype(F32)
-    start = lax.axis_index("wt") * gain_one.shape[0]
-    return lax.dynamic_update_slice(jnp.zeros((16, width), F32), shard, (0, start))
+class Reduce:
+    def __init__(self, spot, part, sides, zo, zi, sems, folded=False, parts=1):
+        self.spot, self.part, self.sides, self.zo, self.zi = spot, part, sides, zo, zi
+        self.x_send, self.x_recv, self.z_send, self.zo_recv, self.zi_recv = (
+            sems.at[i] for i in range(5)
+        )
+        self.folded, self.parts = folded, parts
+        self.rows = part.shape[1] // parts
+        self.sent, self.sent_end, self.sent_mid = [], [], []
+
+    def cut(self, ref, index, h):
+        return ref.at[index, pl.ds(self.rows * h, self.rows)]
+
+    def own(self, plane, h):
+        return self.cut(self.part, plane if self.folded else 2 * plane + self.spot.x, h)
+
+    def wait(self, land, recv, plane, h):
+        piece = self.cut(land, plane, h)
+        at = plane + 4 * h
+        remote(piece, piece, self.z_send.at[at], recv.at[at], self.spot.column).wait_recv()
+
+    def side(self, number):
+        spot = self.spot
+        plane = spot.plane(number)
+        for h in range(self.parts):
+            at = plane + 4 * h
+            copy = remote(
+                self.cut(self.part, 2 * plane + 1 - spot.x, h),
+                self.cut(self.sides, plane, h),
+                self.x_send.at[at],
+                self.x_recv.at[at],
+                spot.column,
+            )
+            copy.start()
+            self.sent.append(copy)
+
+    def add(self, ref, land):
+        ref[...] = (ref[...].astype(F32) + land[...].astype(F32)).astype(BF)
+
+    def meet(self, number):
+        plane = self.spot.plane(number)
+        for h in range(self.parts):
+            self.wait(self.sides, self.x_recv, plane, h)
+            self.add(self.own(plane, h), self.cut(self.sides, plane, h))
+            if number > 0 and self.zo is not None:
+                self.launch_part(number, h)
+
+    def launch(self, number):
+        for h in range(self.parts):
+            self.launch_part(number, h)
+
+    def launch_part(self, number, h):
+        plane = self.spot.plane(number)
+        at = plane + 4 * h
+        copy = remote(
+            self.own(plane, h),
+            self.cut(self.zo, plane, h),
+            self.z_send.at[at],
+            self.zo_recv.at[at],
+            self.spot.inner,
+        )
+
+        @pl.when(self.spot.mid == 0)
+        def _():
+            copy.start()
+
+        self.sent_end.append(copy)
+
+    def relay(self, number):
+        plane = self.spot.plane(number)
+        land, recv = (self.zi, self.zi_recv) if number == 1 else (self.zo, self.zo_recv)
+        copies = []
+        for h in range(self.parts):
+            at = plane + 4 * h
+            copies.append(
+                remote(
+                    self.own(plane, h),
+                    self.cut(self.zi, plane, h),
+                    self.z_send.at[at],
+                    self.zi_recv.at[at],
+                    self.spot.outer if number == 1 else self.spot.inner,
+                )
+            )
+
+        @pl.when(self.spot.mid == 1)
+        def _():
+            for h, copy in enumerate(copies):
+                self.wait(land, recv, plane, h)
+                self.add(self.own(plane, h), self.cut(land, plane, h))
+                copy.start()
+
+        self.sent_mid += copies
+
+    def last(self, result):
+        plane = self.spot.plane(0)
+        for h in range(self.parts):
+            self.wait(self.zi, self.zi_recv, plane, h)
+            rows = pl.ds(self.rows * h, self.rows)
+            total = self.own(plane, h)[...].astype(F32)
+            result[rows] = total + self.cut(self.zi, plane, h)[...].astype(F32)
+
+        @pl.when(self.spot.mid == 1)
+        def _():
+            for h in range(self.parts):
+                self.wait(self.zo, self.zo_recv, plane, h)
+                rows = pl.ds(self.rows * h, self.rows)
+                result[rows] += self.cut(self.zo, plane, h)[...].astype(F32)
+
+    def drain(self):
+        for copy in self.sent:
+            copy.wait_send()
+
+        @pl.when(self.spot.mid == 0)
+        def _():
+            for copy in self.sent_end:
+                copy.wait_send()
+
+        @pl.when(self.spot.mid == 1)
+        def _():
+            for copy in self.sent_mid:
+                copy.wait_send()
 
 
 def swish(values):
@@ -478,8 +480,23 @@
     return high, middle, (rest - middle.astype(F32)).astype(BF)
 
 
-def slot_maps(e_row, e_col, o_row, o_col, slots, experts):
-    pairs = e_row.shape[1]
+def diagonal(values, axis):
+    size = max(values.shape)
+    down = lax.broadcasted_iota(jnp.int32, (size, size), 0)
+    along = lax.broadcasted_iota(jnp.int32, (size, size), 1)
+    return jnp.sum(
+        jnp.where(down == along, values.astype(F32), 0.0), axis=axis, keepdims=True
+    ).astype(jnp.int32)
+
+
+def slot_maps(routes, order, slots, experts):
+    rows, top = routes.shape
+    pairs = rows * top
+    columns = [routes[:, j : j + 1] for j in range(top)]
+    e_col = jnp.concatenate(columns, axis=0)
+    e_row = jnp.concatenate([diagonal(column, 0) for column in columns], axis=1)
+    o_row = lax.rem(order, top) * rows + lax.div(order, top)
+    o_col = diagonal(o_row, 1)
     down = lax.broadcasted_iota(jnp.int32, (pairs, pairs), 0)
     along = lax.broadcasted_iota(jnp.int32, (pairs, pairs), 1)
     turn_row = jnp.sum(jnp.where(o_col == along, down.astype(F32), 0.0), axis=0, keepdims=True)
@@ -501,77 +518,167 @@
     return to_slots, to_pairs
 
 
-def experts_kernel(
-    second_ref, mixer_ref, pack_ref, cot_ref, route_ref, e_row, e_col, o_row, o_col,
-    sd_ref, sg_ref, su_ref, cot4_ref, eg_ref, eu_ref, ed_ref,
-    result_out, grad_second_out, pack_grad_out, dsh_out,
-    dg_out, du_out, dd_out,
-    wg, wu, wd, m4, sh_send, sh_recv, gm_send, gm_recv,
-    xs, xr, gs, gr, os, orr, bs, br, x_s, g_s, sum_s,
-    gate_s, up_s, hid_s, dgate_s, dup_s, dsh, dsh_x, sem, a2a_send, a2a_recv, sem_sh,
+def forward_kernel(
+    tok, pack, cosr, sinr, kb, qb, cot, routes, order, sd,
+    wq, wk, wv, wo, sg, su, eg, eu, ed,
+    q_out, mixed_out, lse_out, normed_out, pack_out, result_out, grad_second_out, pack_grad_out,
+    dsh_out, kv_out, wfull_out, keep_out, give_out, other_out,
+    wbuf, kv, packs, top, low, acc, sg_all, su_all, wg, wu, wd, mix, m4, cot4,
+    sh_send, sh_recv, gm_send, gm_recv, xs, xr, gs, gr, os, orr, bs, br,
+    x_s, g_s, sum_s, gate_s, up_s, hid_s, dgate_s, dup_s, dsh, dsh_x, slot_s, pair_s, cb,
+    sem, kv_recv, kv_send, a2a_send, a2a_recv, sem_sh,
 ):
     spot = Spot(4)
     sems = Sems(sem)
-    rows, width = mixer_ref.shape
+    rows, width = tok.shape
+    pairs = width // PAIR
     ranks = xs.shape[0]
     slots = xs.shape[1] * 128 // width
     hidden = wg.shape[1]
-    loads = [
-        pltpu.make_async_copy(eg_ref, wg, sems.new()),
-        pltpu.make_async_copy(eu_ref, wu, sems.new()),
-    ]
-    for copy in loads:
-        copy.start()
-    others = [(lax.rem(spot.k + o, ranks), spot.w) for o in range(1, ranks)]
-    greet([spot.core, spot.across, spot.corner] + others)
-    mixer = mixer_ref[...]
-    to_slots, to_pairs = slot_maps(
-        e_row[...], e_col[...], o_row[...], o_col[...], slots, ranks
-    )
-    fold_rows(nn(to_slots[:, :rows] + to_slots[:, rows:], mixer), xs)
+    shard = width // 4
+    part = sg_all.shape[1]
+    peers = [(lax.rem(spot.k + o, ranks), spot.w) for o in range(1, ranks)]
+    greet([spot.core, spot.across, spot.corner] + peers)
+    params = Spread(spot, lambda w: pack, lambda w: packs.at[w], sems)
+    key_w = Share(spot, wk, wbuf.at[1], sems)
+    value_w = Share(spot, wv, wbuf.at[2], sems)
+    query_w = Share(spot, wq, wbuf.at[0], sems)
+    inputs = tok[...].astype(F32)
+    scale = lax.rsqrt(jnp.mean(inputs * inputs, axis=-1, keepdims=True) + EPS)
+    scaled = inputs * scale
+    params.finish()
+    pack_all = packs[0] + packs[1] + packs[2] + packs[3]
+    pack_out[...] = pack_all
+    normed = (scaled * pack_all[0:1]).astype(BF)
+    normed_out[...] = normed
+    cosine, sine = cosr[...], sinr[...]
+    key_w.forward()
+    to_slots, to_pairs = slot_maps(routes[...], order[...], slots, ranks)
+    slot_s[...] = to_slots
+    pair_s[...] = to_pairs
+    value_w.forward()
+    key_w.second()
+    query_w.forward()
+    key_w.finish()
+    kv[spot.k, :, 0:width] = turn(nn(normed, wbuf[1]), cosine, sine).astype(BF)
+    value_w.second()
+    value_w.finish()
+    kv[spot.k, :, width : 2 * width] = nn(normed, wbuf[2]).astype(BF)
+    ring = Ring(spot, kv, kv_recv, kv_send, parts=2)
+    ring.start()
+    query_w.second()
+    out_w = Gather(spot, wo, wbuf.at[3], sems)
+
+    def columns(ref):
+        return lambda w: ref.at[:, pl.ds(pl.multiple_of(part * w, part), part)]
+
+    def stripe(ref):
+        return lambda w: ref.at[pl.ds(pl.multiple_of(shard * w, 64), shard)]
+
+    gate_w = Gather(spot, eg, wg, sems)
+    query_w.finish()
+    query = turn(nn(normed, wbuf[0]), cosine, sine).astype(BF) * jnp.asarray(HD**-0.5, BF)
+    for j in range(pairs):
+        q_out[j] = stack_pair(query[:, PAIR * j : PAIR * (j + 1)])
+    top[...] = jnp.full_like(top, MASKED)
+    low[...] = jnp.zeros_like(low)
+    acc[...] = jnp.zeros_like(acc)
+    q_block = qb[...]
+
+    def chunk(plane):
+        k_block = kb[:, pl.ds(pl.multiple_of(2 * rows * plane, 2 * rows), 2 * rows)]
+        allowed = k_block <= q_block
+
+        def one_pair(j, carry):
+            lane = pl.multiple_of(PAIR * j, PAIR)
+            key = kv[pl.ds(2 * plane, 2), :, pl.ds(lane, PAIR)].reshape(2 * rows, PAIR)
+            value = kv[pl.ds(2 * plane, 2), :, pl.ds(width + lane, PAIR)].reshape(2 * rows, PAIR)
+            scores = jnp.where(allowed, nt(q_out[j], key), MASKED)
+            old = top[j]
+            new = jnp.maximum(old, jnp.max(scores, axis=1, keepdims=True))
+            raised = jnp.where(allowed, jnp.exp(scores - new[:, 0:1]), 0.0)
+            factor = jnp.exp(old - new)
+            top[j] = new
+            low[j] = low[j] * factor + jnp.sum(raised, axis=1, keepdims=True)
+            acc[j] = acc[j] * factor + nn(raised.astype(BF), value)
+            return carry
+
+        lax.fori_loop(0, pairs, one_pair, 0)
+
+    ring.step(1)
+    ring.step(2)
+    sg_w = Spread(spot, columns(sg), stripe(sg_all), sems)
+    su_w = Spread(spot, columns(su), stripe(su_all), sems)
+    cot_w = Spread(spot, lambda w: cot, lambda w: cot4.at[w], sems)
+    ring.other(0)
+    chunk(spot.plane(0))
+    ring.step(3)
+    ring.other(1)
+    chunk(spot.plane(1))
+    out_w.forward()
+    gate_w.forward()
+    up_w = Gather(spot, eu, wu, sems)
+    ring.other(2)
+    chunk(spot.plane(2))
+    ring.other(3)
+    chunk(spot.plane(3))
+    saves = [pltpu.make_async_copy(kv, kv_out, sems.new())]
+    saves[0].start()
+    for j in range(pairs):
+        mixed_out[:, PAIR * j : PAIR * (j + 1)] = unstack_pair(acc[j] / low[j])
+        lse_out[j] = top[j] + jnp.log(low[j])
+    out_w.finish()
+    saves.append(pltpu.make_async_copy(wbuf, wfull_out, sems.new()))
+    saves[1].start()
+    second = inputs + nn(mixed_out[...].astype(BF), wbuf[3])
+    scale = lax.rsqrt(jnp.mean(second * second, axis=-1, keepdims=True) + EPS)
+    mixer = (second * scale * pack_all[1:2]).astype(BF)
+    mix[...] = mixer
+
+    mixers = Spread(spot, lambda w: mix, lambda w: m4.at[w], sems)
+    fold_rows(nn(slot_s[:, :rows] + slot_s[:, rows:], mixer), xs)
     rows_out = Exchange(spot, xs, xr, a2a_send.at[0], a2a_recv.at[0])
     rows_out.start()
-    mixers = Spread(spot, lambda w: mixer_ref, lambda w: m4.at[w], sems)
-    down_w = Gather(spot, ed_ref, wd, sems)
-    pack = pack_ref[...]
-    router = pack[2:16].astype(BF)
+    router = pack_all[2:16].astype(BF)
     router = jnp.concatenate([router, jnp.zeros((2, width), BF)], axis=0)
     logits = nt(mixer, router)
     lane = lax.broadcasted_iota(jnp.int32, logits.shape, 1)
-    matches = [lane == route_ref[:, j : j + 1] for j in range(2)]
+    matches = [lane == routes[:, j : j + 1] for j in range(2)]
     chosen = [jnp.sum(jnp.where(m, logits, 0.0), axis=1, keepdims=True) for m in matches]
     largest = jnp.maximum(chosen[0], chosen[1])
     raised = [jnp.exp(c - largest) for c in chosen]
     gates = [r / (raised[0] + raised[1]) for r in raised]
-    grad = cot_ref[...].astype(F32)
+    grad = cot[...].astype(F32)
     pair_grad = jnp.concatenate([(g * grad).astype(BF) for g in gates], axis=0)
-    fold_rows(nn(to_slots, pair_grad), gs)
+    fold_rows(nn(slot_s[...], pair_grad), gs)
     grads_out = Exchange(spot, gs, gr, a2a_send.at[1], a2a_recv.at[1])
     grads_out.start()
-
-    mixers.finish()
+    up_w.forward()
+    down_w = Gather(spot, ed, wd, sems)
+
+    for part_w in (sg_w, su_w, cot_w, mixers):
+        part_w.finish()
     rows_all = m4[...].reshape(4 * rows, width)
-    grad_all = cot4_ref[...].reshape(4 * rows, width)
-    gate_part, up_part = nn(rows_all, sg_ref[...]), nn(rows_all, su_ref[...])
+    grad_all = cot4[...].reshape(4 * rows, width)
+    gate_part, up_part = nn(rows_all, sg_all[...]), nn(rows_all, su_all[...])
     act, slope = swish(gate_part)
     shared_hidden = (act * up_part).astype(BF)
-    sh_send[...] = nn(shared_hidden, sd_ref[...]).astype(BF).reshape(4, rows, width)
+    sh_send[...] = nn(shared_hidden, sd[...]).astype(BF).reshape(4, rows, width)
     shared_out = Spread(spot, lambda w: sh_send.at[w], lambda w: sh_recv.at[w], sems)
-    hid_grad = nt(grad_all, sd_ref[...])
+    hid_grad = nt(grad_all, sd[...])
     grad_gate = (hid_grad * up_part * slope).astype(BF)
     grad_up = (hid_grad * act).astype(BF)
-    back = nt(grad_gate, sg_ref[...]) + nt(grad_up, su_ref[...])
+    back = nt(grad_gate, sg_all[...]) + nt(grad_up, su_all[...])
     gm_send[...] = back.astype(BF).reshape(4, rows, width)
     shared_back = Spread(spot, lambda w: gm_send.at[w], lambda w: gm_recv.at[w], sems)
-    shard = width // 4
     half = shard // 2
     for at, values in ((0, tn(rows_all, grad_gate)), (half, tn(rows_all, grad_up))):
         values = values.astype(BF)
         for r in range(ranks):
-            top, left = half * (r // 4), 128 * (r % 4)
+            down, left = half * (r // 4), 128 * (r % 4)
             for w in range(4):
                 dsh[r, shard * w + at : shard * w + at + half] = values[
-                    shard * w + top : shard * w + top + half, left : left + 128
+                    shard * w + down : shard * w + down + half, left : left + 128
                 ]
     values = tn(shared_hidden, grad_all).astype(BF)
     deep = values.shape[0] // ranks
@@ -583,10 +690,9 @@
     shared_grad = Reduce(spot, dsh, dsh_x, None, None, sem_sh)
     for number in (3, 2, 1, 0):
         shared_grad.side(number)
-    down_w.forward()
-    for copy in loads:
-        copy.wait()
-
+
+    for part_w in (gate_w, up_w):
+        part_w.finish()
     rows_out.finish()
     x_s[...] = unfold_rows(xr, slots)
     block = 512
@@ -605,13 +711,10 @@
         return carry
 
     lax.fori_loop(0, hidden // block, up_step, 0)
-    down_w.finish()
-    sum_s[...] = nt(hid_s[...], wd[...])
-    fold_rows(sum_s[...], os)
-    outs = Exchange(spot, os, orr, a2a_send.at[2], a2a_recv.at[2])
-    outs.start()
     grads_out.finish()
     g_s[...] = unfold_rows(gr, slots)
+    down_w.forward()
+    down_w.finish()
 
     def down_step(i, carry):
         at = parts(i)
@@ -625,36 +728,66 @@
     fold_rows(sum_s[...], bs)
     backs = Exchange(spot, bs, br, a2a_send.at[3], a2a_recv.at[3])
     backs.start()
-
-    down_w.drain()
-
-    def grad_step(i, carry):
-        at = parts(i)
-        wg[:, at] = tn(x_s[...], dgate_s[:, at]).astype(BF)
-        wu[:, at] = tn(x_s[...], dup_s[:, at]).astype(BF)
-        wd[:, at] = tn(g_s[...], hid_s[:, at]).astype(BF)
-        return carry
-
-    lax.fori_loop(0, hidden // block, grad_step, 0)
-    saves = [
-        pltpu.make_async_copy(src, dst, sems.new())
-        for src, dst in ((wg, dg_out), (wu, du_out), (wd, dd_out))
-    ]
-    for copy in saves:
-        copy.start()
-
+    sum_s[...] = nt(hid_s[...], wd[...])
+    fold_rows(sum_s[...], os)
+    outs = Exchange(spot, os, orr, a2a_send.at[2], a2a_recv.at[2])
+    outs.start()
+
+    for part_w in (gate_w, up_w, down_w):
+        part_w.drain()
+    swaps = []
+    for a, (ref, left, right) in enumerate(
+        ((wg, x_s, dgate_s), (wu, x_s, dup_s), (wd, g_s, hid_s))
+    ):
+
+        def grad_step(i, carry, ref=ref, left=left, right=right):
+            at = parts(i)
+            ref[:, at] = tn(left[...], right[:, at]).astype(BF)
+            return carry
+
+        lax.fori_loop(0, hidden // block, grad_step, 0)
+        for row in range(2):
+            src = ref.at[pl.ds(pl.multiple_of(shard * (2 * row + 1 - spot.c), 64), shard)]
+            swaps.append(remote(src, cb.at[a, row], sems.new(), sems.new(), spot.core))
+            swaps[-1].start()
+    across = []
+    for a, ref in enumerate((wg, wu, wd)):
+        for row in range(2):
+            swaps[2 * a + row].wait_recv()
+
+        def add(i, carry, a=a, ref=ref):
+            for row in range(2):
+                at = pl.ds(pl.multiple_of(shard * (2 * row + spot.c) + 16 * i, 16), 16)
+                own = ref[at].astype(F32)
+                ref[at] = (own + cb[a, row, pl.ds(16 * i, 16)].astype(F32)).astype(BF)
+            return carry
+
+        lax.fori_loop(0, shard // 16, add, 0)
+        give = ref.at[pl.ds(pl.multiple_of(shard * spot.across[1], 64), shard)]
+        keep = ref.at[pl.ds(pl.multiple_of(shard * spot.w, 64), shard)]
+        saves.append(pltpu.make_async_copy(keep, keep_out.at[a], sems.new()))
+        saves[-1].start()
+        if a == 0:
+            across.append(remote(give, other_out, sems.new(), sems.new(), spot.across))
+            across[-1].start()
+        else:
+            saves.append(pltpu.make_async_copy(give, give_out.at[a - 1], sems.new()))
+            saves[-1].start()
     for number in (3, 2, 1, 0):
         shared_grad.meet(number)
         plane = spot.plane(number)
         dsh_out[plane] = dsh[2 * plane + spot.x]
 
-    second = second_ref[...]
     shared_out.finish()
     total = second
     for w in range(4):
         total = total + sh_recv[w].astype(F32)
+    shared_back.finish()
+    grad_mixer = gm_recv[0].astype(F32)
+    for w in range(1, 4):
+        grad_mixer = grad_mixer + gm_recv[w].astype(F32)
     outs.finish()
-    pair_out = nn(to_pairs, unfold_rows(orr, slots))
+    pair_out = nn(pair_s[...], unfold_rows(orr, slots))
     pair_out = [pair_out[:rows], pair_out[rows:]]
     result_out[...] = (total + gates[0] * pair_out[0] + gates[1] * pair_out[1]).astype(BF)
     grad_gates = [jnp.sum(grad * p, axis=1, keepdims=True) for p in pair_out]
@@ -664,196 +797,124 @@
         grad_logits += jnp.where(matches[j], gates[j] * (grad_gates[j] - inner), 0.0)
     pieces = split_three(grad_logits)
     router_grad = sum(tn(piece, mixer) for piece in pieces)
-    grad_mixer = sum(nn(piece, router) for piece in pieces)
-    shared_back.finish()
-    for w in range(4):
-        grad_mixer = grad_mixer + gm_recv[w].astype(F32)
+    grad_mixer = grad_mixer + sum(nn(piece, router) for piece in pieces)
     backs.finish()
-    grad_mixer = grad_mixer + nn(to_pairs[:rows] + to_pairs[rows:], unfold_rows(br, slots))
-    scale = lax.rsqrt(jnp.mean(second * second, axis=-1, keepdims=True) + EPS)
-    weighted = grad_mixer * pack[1:2]
+    grad_mixer = grad_mixer + nn(pair_s[:rows] + pair_s[rows:], unfold_rows(br, slots))
+    weighted = grad_mixer * pack_all[1:2]
     mean = jnp.mean(weighted * second, axis=-1, keepdims=True)
     grad_second_out[...] = grad + scale * weighted - second * (scale * scale * scale * mean)
     gain_grad = jnp.sum(grad_mixer * second * scale, axis=0, keepdims=True)
     pack_grad_out[...] = jnp.concatenate(
         [jnp.zeros_like(gain_grad), gain_grad, router_grad[:14]], axis=0
     )
-    for part in (rows_out, grads_out, outs, backs, mixers, shared_out, shared_back):
-        part.drain()
-    for copy in shared_grad.sent:
+    for copy in across:
+        copy.wait_recv()
+    for part_w in (params, key_w, value_w, query_w, out_w, sg_w, su_w, cot_w, ring, mixers):
+        part_w.drain()
+    for part_w in (rows_out, grads_out, outs, backs, shared_out, shared_back):
+        part_w.drain()
+    for copy in shared_grad.sent + swaps + across:
         copy.wait_send()
     for copy in saves:
         copy.wait()
 
 
-def run_experts(
-    second, mixer, pack, cot, route, e_row, e_col, o_row, o_col, sd, sg, su, cot4, eg, eu, ed
+def run_forward(
+    tok, pack, cosr, sinr, kb, qb, cot, routes, order, sd, wq, wk, wv, wo, sg, su, eg, eu, ed
 ):
-    rows, width = mixer.shape
+    rows, width = tok.shape
+    pairs = width // PAIR
     ranks, slots = 8, 40
     hidden = eg.shape[1]
-    part = sg.shape[1]
+    part = sg.shape[1] // 4
+    shard = width // 4
     total = ranks * slots
     tall = width + part * width // (128 * ranks)
-    folded = (ranks, slots * width // 128, 128)
     any_, vm = pl.BlockSpec(memory_space=pl.ANY), pl.BlockSpec(memory_space=VMEM)
     shape = jax.ShapeDtypeStruct
+
+    def low(*dims):
+        return VMEM(dims, BF)
+
+    def full(*dims):
+        return VMEM(dims, F32)
+
+    dma = pltpu.SemaphoreType.DMA
+    folded = low(ranks, slots * width // 128, 128)
     return pl.pallas_call(
-        experts_kernel,
+        forward_kernel,
         out_shape=(
+            shape((pairs, 2 * rows, PAIR), BF),
+            shape((rows, width), F32),
+            shape((pairs, 2 * rows, PAIR), F32),
+            shape((rows, width), BF),
+            shape(pack.shape, F32),
             shape((rows, width), BF),
             shape((rows, width), F32),
             shape(pack.shape, F32),
             shape((4, tall, 128), BF),
-            shape((width, hidden), BF),
-            shape((width, hidden), BF),
-            shape((width, hidden), BF),
+            shape((ranks, rows, 2 * width), BF),
+            shape((4, width, width), BF),
+            shape((3, shard, hidden), BF),
+            shape((2, shard, hidden), BF),
+            shape((shard, hidden), BF),
         ),
-        in_specs=[vm] * 13 + [any_] * 3,
-        out_specs=tuple([vm] * 4 + [any_] * 3),
+        in_specs=[vm] * 10 + [any_] * 9,
+        out_specs=tuple([vm] * 9 + [any_] * 5),
         scratch_shapes=[
-            VMEM((width, hidden), BF),
-            VMEM((width, hidden), BF),
-            VMEM((width, hidden), BF),
-            VMEM((4, rows, width), BF),
-            VMEM((4, rows, width), BF),
-            VMEM((4, rows, width), BF),
-            VMEM((4, rows, width), BF),
-            VMEM((4, rows, width), BF),
-            VMEM(folded, BF),
-            VMEM(folded, BF),
-            VMEM(folded, BF),
-            VMEM(folded, BF),
-            VMEM(folded, BF),
-            VMEM(folded, BF),
-            VMEM(folded, BF),
-            VMEM(folded, BF),
-            VMEM((total, width), BF),
-            VMEM((total, width), BF),
-            VMEM((total, width), F32),
-            VMEM((total, hidden), F32),
-            VMEM((total, hidden), F32),
-            VMEM((total, hidden), BF),
-            VMEM((total, hidden), BF),
-            VMEM((total, hidden), BF),
-            VMEM((ranks, tall, 128), BF),
-            VMEM((4, tall, 128), BF),
-            pltpu.SemaphoreType.DMA((48,)),
-            pltpu.SemaphoreType.DMA((4, ranks)),
-            pltpu.SemaphoreType.DMA((4, ranks)),
-            pltpu.SemaphoreType.DMA((5, 4)),
+            low(4, width, width),
+            low(ranks, rows, 2 * width),
+            full(4, *pack.shape),
+            full(pairs, 2 * rows, PAIR),
+            full(pairs, 2 * rows, PAIR),
+            full(pairs, 2 * rows, PAIR),
+            low(width, part),
+            low(width, part),
+            low(width, hidden),
+            low(width, hidden),
+            low(width, hidden),
+            low(rows, width),
+            low(4, rows, width),
+            low(4, rows, width),
+            low(4, rows, width),
+            low(4, rows, width),
+            low(4, rows, width),
+            low(4, rows, width),
+            *[folded] * 8,
+            low(total, width),
+            low(total, width),
+            full(total, width),
+            full(total, hidden),
+            full(total, hidden),
+            low(total, hidden),
+            low(total, hidden),
+            low(total, hidden),
+            low(ranks, tall, 128),
+            low(4, tall, 128),
+            low(total, 2 * rows),
+            low(2 * rows, total),
+            low(3, 2, shard, hidden),
+            dma((144,)),
+            dma((2 * ranks,)),
+            dma((32,)),
+            dma((4, ranks)),
+            dma((4, ranks)),
+            dma((5, 8)),
         ],
         compiler_params=pltpu.CompilerParams(
-            collective_id=2, has_side_effects=True, vmem_limit_bytes=56 * 2**20
+            collective_id=1, has_side_effects=True, vmem_limit_bytes=VMEM_BYTES
         ),
-    )(second, mixer, pack, cot, route, e_row, e_col, o_row, o_col, sd, sg, su, cot4, eg, eu, ed)
-
-
-class Reduce:
-    def __init__(self, spot, part, sides, zo, zi, sems, folded=False):
-        self.spot, self.part, self.sides, self.zo, self.zi = spot, part, sides, zo, zi
-        self.x_send, self.x_recv, self.z_send, self.zo_recv, self.zi_recv = (
-            sems.at[i] for i in range(5)
-        )
-        self.folded = folded
-        self.sent, self.sent_end, self.sent_mid = [], [], []
-
-    def own(self, plane):
-        return self.part.at[plane if self.folded else 2 * plane + self.spot.x]
-
-    def wait(self, land, recv, plane):
-        remote(
-            land.at[plane], land.at[plane], self.z_send.at[plane], recv.at[plane], self.spot.column
-        ).wait_recv()
-
-    def side(self, number):
-        spot = self.spot
-        plane = spot.plane(number)
-        copy = remote(
-            self.part.at[2 * plane + 1 - spot.x],
-            self.sides.at[plane],
-            self.x_send.at[plane],
-            self.x_recv.at[plane],
-            spot.column,
-        )
-        copy.start()
-        self.sent.append(copy)
-
-    def meet(self, number):
-        plane = self.spot.plane(number)
-        self.wait(self.sides, self.x_recv, plane)
-        own = self.own(plane)
-        own[...] = (own[...].astype(F32) + self.sides[plane].astype(F32)).astype(BF)
-
-    def launch(self, number):
-        plane = self.spot.plane(number)
-        copy = remote(
-            self.own(plane),
-            self.zo.at[plane],
-            self.z_send.at[plane],
-            self.zo_recv.at[plane],
-            self.spot.inner,
-        )
-
-        @pl.when(self.spot.mid == 0)
-        def _():
-            copy.start()
-
-        self.sent_end.append(copy)
-
-    def relay(self, number):
-        plane = self.spot.plane(number)
-        land, recv = (self.zi, self.zi_recv) if number == 1 else (self.zo, self.zo_recv)
-        own = self.own(plane)
-        copy = remote(
-            own,
-            self.zi.at[plane],
-            self.z_send.at[plane],
-            self.zi_recv.at[plane],
-            self.spot.outer if number == 1 else self.spot.inner,
-        )
-
-        @pl.when(self.spot.mid == 1)
-        def _():
-            self.wait(land, recv, plane)
-            own[...] = (own[...].astype(F32) + land[plane].astype(F32)).astype(BF)
-            copy.start()
-
-        self.sent_mid.append(copy)
-
-    def last(self, result):
-        plane = self.spot.plane(0)
-        self.wait(self.zi, self.zi_recv, plane)
-        result[...] = self.own(plane)[...].astype(F32) + self.zi[plane].astype(F32)
-
-        @pl.when(self.spot.mid == 1)
-        def _():
-            self.wait(self.zo, self.zo_recv, plane)
-            result[...] += self.zo[plane].astype(F32)
-
-    def drain(self):
-        for copy in self.sent:
-            copy.wait_send()
-
-        @pl.when(self.spot.mid == 0)
-        def _():
-            for copy in self.sent_end:
-                copy.wait_send()
-
-        @pl.when(self.spot.mid == 1)
-        def _():
-            for copy in self.sent_mid:
-                copy.wait_send()
+    )(tok, pack, cosr, sinr, kb, qb, cot, routes, order, sd, wq, wk, wv, wo, sg, su, eg, eu, ed)
 
 
 def backward_kernel(
     grad_second_ref, tok, pack_ref, pack_grad_ref, normed_ref, mixed_ref, q_ref, lse_ref,
-    cosr, sinr, kb, qb, dsh_ref, kv_ref, wfull_ref, dg_ref, du_ref, dd_ref,
-    grad_input_out, pack_out, att1_out, att2_out, sh_out, keep_out, other_out,
+    cosr, sinr, kb, qb, dsh_ref, kv_ref, wfull_ref, give_ref,
+    grad_input_out, pack_out, att1_out, att2_out, sh_out, other_out,
     wbuf, kv, kvb, kv_x, kv_zo, kv_zi, kv_sum, gst, delta_s, dq,
     ga, ga4, gq, gq4, gkv, gkv4, n_t, m_t, n_all, m_all, pk, pk4,
     a1, a1_x, a1_zo, a1_zi, a1_sum, a2, a2_x, a2_zo, a2_zi, a2_sum, r1, r2,
-    sh, sh_zo, sh_zi, sh_sum, sh_chunk, sh_land, r3, po, cb,
+    sh, sh_zo, sh_zi, sh_sum, sh_chunk, r3,
     sem, sem_kv, sem_a1, sem_a2, sem_sh, ring_recv, ring_send,
 ):
     spot = Spot(4)
@@ -866,35 +927,14 @@
     loads.append(pltpu.make_async_copy(dsh_ref, sh, sems.new()))
     for copy in loads:
         copy.start()
-    grads = (dg_ref, du_ref, dd_ref)
 
     def block(ref, w):
         return ref.at[pl.ds(pl.multiple_of(shard * w, 64), shard)]
 
-    mine = []
-    for a in range(3):
-        for row in range(2):
-            mine.append(
-                pltpu.make_async_copy(block(grads[a], 2 * row + spot.c), po.at[a, row], sems.new())
-            )
-            mine[-1].start()
     greet((spot.core, spot.across, spot.corner, spot.column, spot.inner), (spot.mid, spot.outer))
     grad_second = grad_second_ref[...]
     ga[...] = grad_second.astype(BF)
     grads_w = Spread(spot, lambda w: ga, lambda w: ga4.at[w], sems)
-    swaps = []
-    for a in range(3):
-        for row in range(2):
-            swaps.append(
-                remote(
-                    block(grads[a], 2 * row + 1 - spot.c),
-                    cb.at[a, row],
-                    sems.new(),
-                    sems.new(),
-                    spot.core,
-                )
-            )
-            swaps[-1].start()
     loads[-1].wait()
     shared = Reduce(spot, sh, None, sh_zo, sh_zi, sem_sh, folded=True)
     for number in (3, 2, 1):
@@ -908,6 +948,12 @@
 
     normed_w = Spread(spot, lambda w: block(n_t, w), columns(n_all), sems)
     mixed_w = Spread(spot, lambda w: block(m_t, w), columns(m_all), sems)
+    across = []
+    for a in range(2):
+        across.append(
+            remote(give_ref.at[a], other_out.at[a], sems.new(), sems.new(), spot.across)
+        )
+        across[-1].start()
     loads[0].wait()
     grad_mixed = nt(ga[...], wbuf[3]).astype(BF)
     product = grad_mixed.astype(F32) * mixed
@@ -945,47 +991,16 @@
 
         lax.fori_loop(0, pairs, one_pair, 0)
 
-    kv_grad = Reduce(spot, kvb, kv_x, kv_zo, kv_zi, sem_kv)
+    kv_grad = Reduce(spot, kvb, kv_x, kv_zo, kv_zi, sem_kv, parts=2)
     chunk(3)
     kv_grad.side(3)
-
-    for copy in mine:
-        copy.wait()
-    across = []
-    for a in range(3):
-        for row in range(2):
-            swaps[2 * a + row].wait_recv()
-
-        def add(i, carry):
-            at = pl.ds(pl.multiple_of(16 * i, 16), 16)
-            for row in range(2):
-                total = po[a, row, at].astype(F32) + cb[a, row, at].astype(F32)
-                po[a, row, at] = total.astype(BF)
-            return carry
-
-        lax.fori_loop(0, shard // 16, add, 0)
-        across.append(
-            remote(po.at[a, 1 - spot.y], other_out.at[a], sems.new(), sems.new(), spot.across)
-        )
-        across[-1].start()
-    keeps = [
-        pltpu.make_async_copy(po.at[a, spot.y], keep_out.at[a], sems.new()) for a in range(3)
-    ]
-    for copy in keeps:
-        copy.start()
-
-    shared.relay(3)
     chunk(2)
     kv_grad.side(2)
-    kv_grad.meet(3)
-    kv_grad.launch(3)
-    shared.relay(2)
+    shared.relay(3)
     chunk(1)
     kv_grad.side(1)
-    kv_grad.meet(2)
-    kv_grad.launch(2)
-    kv_grad.relay(3)
-    shared.relay(1)
+    kv_grad.meet(3)
+    shared.relay(2)
     chunk(0)
     kv_grad.side(0)
     cosine, sine = cosr[...], sinr[...]
@@ -993,6 +1008,12 @@
         jnp.concatenate([unstack_pair(dq[j]) for j in range(pairs)], axis=1), cosine, -sine
     ).astype(BF)
     query_w = Spread(spot, lambda w: gq, lambda w: gq4.at[w], sems)
+    for part_w in (grads_w, normed_w, mixed_w):
+        part_w.finish()
+    out_grad = nn(m_all[...], ga4[...].reshape(4 * rows, width))
+    kv_grad.meet(2)
+    kv_grad.relay(3)
+    shared.relay(1)
     shared.last(sh_sum)
     sh_chunk[...] = sh_sum[...].astype(BF)
     part = 2 * shard // 2
@@ -1007,12 +1028,7 @@
     rest = sh_chunk.shape[0] - 4 * part
     r3[spot.k, pl.ds(4 * part, rest)] = sh_chunk[pl.ds(4 * part, rest)]
     kv_grad.meet(1)
-    kv_grad.launch(1)
     kv_grad.relay(2)
-    for part_w in (grads_w, normed_w, mixed_w):
-        part_w.finish()
-    out_grad = nn(m_all[...], ga4[...].reshape(4 * rows, width))
-    kv_grad.meet(0)
     kv_grad.relay(1)
     query_w.finish()
     query_grad = nn(n_all[...], gq4[...].reshape(4 * rows, width))
@@ -1021,13 +1037,14 @@
     first = Reduce(spot, a1, a1_x, a1_zo, a1_zi, sem_a1)
     for number in (3, 2, 1, 0):
         first.side(number)
-    shared_w.finish()
-    ring3 = Ring(spot, r3, ring_recv.at[2], ring_send.at[2])
-    ring3.start()
+    kv_grad.meet(0)
     kv_grad.last(kv_sum)
     gkv[:, 0:width] = turn(kv_sum[:, 0:width], cosine, -sine).astype(BF)
     gkv[:, width : 2 * width] = kv_sum[:, width : 2 * width].astype(BF)
     kv_w = Spread(spot, lambda w: gkv, lambda w: gkv4.at[w], sems)
+    shared_w.finish()
+    ring3 = Ring(spot, r3, ring_recv.at[2], ring_send.at[2], parts=2)
+    ring3.start()
     for copy in loads[2:5]:
         copy.wait()
     grad_normed = nt(gq[...], wbuf[0]) + nt(gkv[:, 0:width], wbuf[1])
@@ -1042,14 +1059,10 @@
     gain_grad = jnp.sum(grad_normed * inputs * scale, axis=0, keepdims=True)
     pk[...] = jnp.concatenate([gain_grad, pack_grad_ref[1:16]], axis=0)
     pack_w = Spread(spot, lambda w: pk, lambda w: pk4.at[w], sems)
-    for number in (3, 2, 1):
+    for number in (3, 2, 1, 0):
         first.meet(number)
-        first.launch(number)
-    first.meet(0)
     first.relay(3)
-    ring3.step(1)
     first.relay(2)
-    first.relay(1)
     kv_w.finish()
     pack_w.finish()
     grad_kv = gkv4[...].reshape(4 * rows, 2 * width)
@@ -1063,58 +1076,54 @@
     second = Reduce(spot, a2, a2_x, a2_zo, a2_zi, sem_a2)
     for number in (3, 2, 1, 0):
         second.side(number)
+    first.relay(1)
+    ring3.step(1)
     first.last(a1_sum)
     r1[spot.k] = a1_sum[...].astype(BF)
     ring1 = Ring(spot, r1, ring_recv.at[0], ring_send.at[0])
     ring1.start()
-    for number in (3, 2, 1):
+    ring3.step(2)
+    for number in (3, 2, 1, 0):
         second.meet(number)
-        second.launch(number)
-    second.meet(0)
-    ring3.step(2)
+    ring1.step(1)
+    ring3.step(3)
     second.relay(3)
     second.relay(2)
     second.relay(1)
-    ring3.step(3)
-    ring1.step(1)
+    ring1.step(2)
     second.last(a2_sum)
     r2[spot.k] = a2_sum[0:size].astype(BF)
     ring2 = Ring(spot, r2, ring_recv.at[1], ring_send.at[1])
     ring2.start()
     pack_out[...] = a2_sum[size : size + 16]
-    for number in (2, 3):
-        ring1.step(number)
+    ring1.step(3)
     for number in (1, 2, 3):
         ring2.step(number)
-    for ring in (ring3, ring1, ring2):
+    saves = []
+    for ring, src, dst in ((ring3, r3, sh_out), (ring1, r1, att1_out), (ring2, r2, att2_out)):
         for number in range(4):
-            ring.other(spot.plane(number))
-    saves = [
-        pltpu.make_async_copy(src, dst, sems.new())
-        for src, dst in ((r3, sh_out), (r1, att1_out), (r2, att2_out))
-    ]
-    for copy in saves:
-        copy.start()
+            ring.other(number)
+        saves.append(pltpu.make_async_copy(src, dst, sems.new()))
+        saves[-1].start()
     for copy in across:
         copy.wait_recv()
-    for copy in swaps + across:
         copy.wait_send()
     for part_w in (grads_w, normed_w, mixed_w, query_w, shared_w, kv_w, pack_w):
         part_w.drain()
     for part_w in (shared, kv_grad, first, second, ring1, ring2, ring3):
         part_w.drain()
-    for copy in saves + keeps:
+    for copy in saves:
         copy.wait()
 
 
 def run_backward(
     grad_second, tok, pack, pack_grad, normed, mixed, q, lse, cosr, sinr, kb, qb, dsh, kv, wfull,
-    dg, du, dd,
+    give,
 ):
     rows, width = tok.shape
     pairs = width // PAIR
     ranks = 8
-    shard, hidden = width // 4, dg.shape[1]
+    shard, hidden = width // 4, give.shape[2]
     size = 2 * shard // ranks
     tall = dsh.shape[1]
     any_, vm = pl.BlockSpec(memory_space=pl.ANY), pl.BlockSpec(memory_space=VMEM)
@@ -1135,11 +1144,10 @@
             shape((ranks, size, width), BF),
             shape((ranks, size, width), BF),
             shape((ranks, tall, 128), BF),
-            shape((3, shard, hidden), BF),
-            shape((3, shard, hidden), BF),
+            shape((2, shard, hidden), BF),
         ),
-        in_specs=[vm] * 12 + [any_] * 6,
-        out_specs=(vm, vm, any_, any_, any_, any_, any_),
+        in_specs=[vm] * 12 + [any_] * 4,
+        out_specs=(vm, vm, any_, any_, any_, any_),
         scratch_shapes=[
             low(4, width, width),
             low(ranks, rows, 2 * width),
@@ -1180,25 +1188,137 @@
             low(4, tall, 128),
             full(tall, 128),
             low(tall, 128),
-            low(16, 128),
             low(ranks, tall, 128),
-            low(3, 2, shard, hidden),
-            low(3, 2, shard, hidden),
             dma((112,)),
-            dma((5, 4)),
-            dma((5, 4)),
-            dma((5, 4)),
-            dma((5, 4)),
-            dma((3, ranks)),
-            dma((3, 16)),
+            dma((5, 8)),
+            dma((5, 8)),
+            dma((5, 8)),
+            dma((5, 8)),
+            dma((3, 2 * ranks)),
+            dma((3, 32)),
         ],
         compiler_params=pltpu.CompilerParams(
-            collective_id=3, has_side_effects=True, vmem_limit_bytes=58 * 2**20
+            collective_id=3, has_side_effects=True, vmem_limit_bytes=VMEM_BYTES
         ),
     )(
         grad_second, tok, pack, pack_grad, normed, mixed, q, lse, cosr, sinr, kb, qb, dsh, kv,
-        wfull, dg, du, dd,
-    )
+        wfull, give,
+    )
+
+
+def unpack_kernel(
+    result, grad_input, pack, att1, att2, sh, keep, other0, other,
+    result_out, grad_input_out, gain_one, gain_two, router,
+    query, key, value, output, gate, up, down, eg, eu, ed,
+):
+    i = pl.program_id(0)
+    result_out[...] = result[...]
+    grad_input_out[...] = grad_input[...]
+    output[...] = att1[0, 0].astype(F32)
+    query[...] = att1[1, 0].astype(F32)
+    key[...] = att2[0, 0].astype(F32)
+    value[...] = att2[1, 0].astype(F32)
+    eg[...] = keep[0].astype(F32) + other0[...].astype(F32)
+    eu[...] = keep[1].astype(F32) + other[0].astype(F32)
+    ed[...] = keep[2].astype(F32) + other[1].astype(F32)
+    size = gate.shape[0]
+    shard = 4 * size
+    width = 4 * shard
+    row, within = lax.div(i, 2), lax.rem(i, 2) * size
+    for c in range(4):
+        for w in range(4):
+            lanes = slice(512 * w + 128 * c, 512 * w + 128 * (c + 1))
+            start = pl.multiple_of(shard * w + within, 16)
+            gate[:, lanes] = sh[4 * row + c, pl.ds(start, size)].astype(F32)
+            start = pl.multiple_of(shard * w + shard // 2 + within, 16)
+            up[:, lanes] = sh[4 * row + c, pl.ds(start, size)].astype(F32)
+    deep = down.shape[0] // 2
+    for r in range(2):
+        for t in range(width // 128):
+            at = slice(width + deep * t, width + deep * (t + 1))
+            down[deep * r : deep * (r + 1), 128 * t : 128 * (t + 1)] = sh[2 * i + r, at].astype(F32)
+
+    @pl.when(i == 0)
+    def _():
+        back = lax.rem(4 - lax.axis_index("wt"), 4) * shard
+        mine = pltpu.roll(pack[...], back, 1)[:, 0:256]
+        gain_one[...] = mine[0:1, 0:shard]
+        gain_two[...] = mine[1:2, 0:shard]
+        router[...] = mine.T[0:shard, 2 : 2 + router.shape[1]]
+
+
+def run_unpack(result, grad_input, pack, att1, att2, sh, keep, other0, other, experts):
+    rows, width = result.shape
+    shard, hidden = other0.shape
+    steps = 4
+    shape = jax.ShapeDtypeStruct
+    size = shard // steps
+    att1 = att1.reshape(2, 4, size, width)
+    att2 = att2.reshape(2, 4, size, width)
+    shared_hidden = sh.shape[0] * (sh.shape[1] - width) * 128 // width
+    shared = 4 * shared_hidden
+    by_rows = lambda r, c: pl.BlockSpec((r, c), lambda i: (i, 0))
+    whole = lambda *dims: pl.BlockSpec(dims, lambda i: (0,) * len(dims))
+    stack = lambda n, r, c: pl.BlockSpec((n, r, c), lambda i: (0, i, 0))
+    att = pl.BlockSpec((2, 1, size, width), lambda i: (0, i, 0, 0))
+    return pl.pallas_call(
+        unpack_kernel,
+        grid=(steps,),
+        out_shape=(
+            shape((rows, width), BF),
+            shape((rows, width), F32),
+            shape((1, shard), F32),
+            shape((1, shard), F32),
+            shape((shard, experts), F32),
+            *[shape((shard, width), F32)] * 4,
+            *[shape((shard, shared), F32)] * 2,
+            shape((shared_hidden, width), F32),
+            *[shape((shard, hidden), F32)] * 3,
+        ),
+        in_specs=[
+            by_rows(rows // steps, width),
+            by_rows(rows // steps, width),
+            whole(*pack.shape),
+            att,
+            att,
+            whole(*sh.shape),
+            stack(3, size, hidden),
+            by_rows(size, hidden),
+            stack(2, size, hidden),
+        ],
+        out_specs=(
+            by_rows(rows // steps, width),
+            by_rows(rows // steps, width),
+            whole(1, shard),
+            whole(1, shard),
+            whole(shard, experts),
+            *[by_rows(size, width)] * 4,
+            *[by_rows(size, shared)] * 2,
+            by_rows(shared_hidden // steps, width),
+            *[by_rows(size, hidden)] * 3,
+        ),
+        compiler_params=pltpu.CompilerParams(vmem_limit_bytes=VMEM_BYTES),
+    )(result, grad_input, pack, att1, att2, sh, keep, other0, other)
+
+
+def angles_of(block_deal, rows_dev):
+    here = places(lax.axis_index("ctx") * rows_dev, rows_dev, block_deal, rows_dev)
+    half_size = HD // 2
+    frequency = 10000.0 ** (-jnp.arange(half_size, dtype=F32) / half_size)
+    angles = here.astype(F32)[:, None] * frequency[None, :]
+    cosine, sine = jnp.cos(angles), jnp.sin(angles)
+    cosr = jnp.concatenate([cosine] * 4, axis=1)
+    sinr = jnp.concatenate([-sine, sine, -sine, sine], axis=1)
+    return here, cosr, sinr
+
+
+def pack_params(gain_one, gain_two, router):
+    width = 4 * gain_one.shape[0]
+    shard = jnp.concatenate(
+        [gain_one[None], gain_two[None], router.T, jnp.zeros((6, gain_one.shape[0]), BF)], axis=0
+    ).astype(F32)
+    start = lax.axis_index("wt") * gain_one.shape[0]
+    return lax.dynamic_update_slice(jnp.zeros((16, width), F32), shard, (0, start))
 
 
 def contract_product(left, right, left_dim, right_dim):
@@ -1718,60 +1838,33 @@
     slot_order,
     block_deal,
 ):
-    rows_dev, width = tokens.shape[1:]
+    rows_dev = tokens.shape[1]
     ranks = lax.axis_size("ctx")
-    shard = width // 4
     here, cosr, sinr = angles_of(block_deal, rows_dev)
     kb = (places(0, ranks * rows_dev, block_deal, rows_dev) // BLK)[None, :]
     qb = jnp.concatenate([here // BLK] * 2)[:, None]
     pack = pack_params(gain_attention, gain_mixer, router_weight)
     (
-        q_st, kv_all, mixed, lse, second, mixer, normed, pack_all, wfull, sg_part, su_part,
-        eg_full, eu_full, cot4,
+        q_st, mixed, lse, normed, pack_all, result, grad_second, pack_grad, dsh, kv_all, wfull,
+        keep, give, other0,
     ) = run_forward(
-        tokens[0], pack, cosr, sinr, kb, qb, cotangent[0], query_weight, key_weight,
-        value_weight, output_weight, shared_gate, shared_up, expert_gate, expert_up,
-    )
-    route = routes[0]
-    top_count = route.shape[1]
-    by_choice = route.T.reshape(1, rows_dev * top_count)
-    turns = slot_order[0, 0]
-    turns = lax.rem(turns, top_count) * rows_dev + lax.div(turns, top_count)
-    result, grad_second, pack_grad, dsh, dg, du, dd = run_experts(
-        second, mixer, pack_all, cotangent[0], route, by_choice, by_choice.reshape(-1, 1),
-        turns[None, :], turns[:, None], shared_down, sg_part, su_part, cot4, eg_full, eu_full,
-        expert_down,
-    )
-    grad_input, pack_sum, att1, att2, sh, keep, other = run_backward(
+        tokens[0], pack, cosr, sinr, kb, qb, cotangent[0], routes[0], slot_order[0], shared_down,
+        query_weight, key_weight, value_weight, output_weight, shared_gate, shared_up,
+        expert_gate, expert_up, expert_down,
+    )
+    grad_input, pack_sum, att1, att2, sh, other = run_backward(
         grad_second, tokens[0], pack_all, pack_grad, normed, mixed, q_st, lse, cosr, sinr, kb, qb,
-        dsh, kv_all, wfull, dg, du, dd,
-    )
-    att1 = att1.reshape(2 * shard, width).astype(F32)
-    att2 = att2.reshape(2 * shard, width).astype(F32)
-    mine = lax.dynamic_slice(
-        pack_sum, (0, lax.axis_index("wt") * shard), (pack_sum.shape[0], shard)
-    )
-    both = sh[:, :width].reshape(2, 4, 4, 2, shard // 2, 128)
-    both = both.transpose(3, 0, 4, 2, 1, 5).reshape(2, shard, shared_gate.shape[1]).astype(F32)
-    down = sh[:, width:].reshape(ranks, width // 128, -1, 128).transpose(0, 2, 1, 3)
-    down = down.reshape(shared_down.shape).astype(F32)
-    sums = [keep[a].astype(F32) + other[a].astype(F32) for a in range(3)]
+        dsh, kv_all, wfull, give,
+    )
+    (
+        result, grad_input, gain_one, gain_two, router, query, key, value, output, gate, up, down,
+        eg, eu, ed,
+    ) = run_unpack(
+        result, grad_input, pack_sum, att1, att2, sh, keep, other0, other, router_weight.shape[1]
+    )
     return (
-        result[None],
-        grad_input[None],
-        mine[0],
-        att1[shard:],
-        att2[:shard],
-        att2[shard:],
-        att1[:shard],
-        mine[1],
-        mine[2 : 2 + router_weight.shape[1]].T,
-        both[0],
-        both[1],
-        down,
-        sums[0],
-        sums[1],
-        sums[2],
+        result[None], grad_input[None], gain_one.reshape(-1), query, key, value, output,
+        gain_two.reshape(-1), router, gate, up, down, eg, eu, ed,
     )
 
 

time: 354 us -> 306 us (0.86)
  local copies, waits for them, and re-layouts: 31.2 us -> 5.52 us
  Pallas kernels: 311 us -> 296 us
  other arithmetic: 9.47 us -> 4.05 us
    pallas_call x1, Pallas kernels: 96.2 us -> 156 us  [run_forward(): pl.pallas_call(forward_kernel, out_shape=(shape((pairs, 2 * rows, PAIR),...]
    pallas_call x1, Pallas kernels: 64.4 us -> 9.08 us  [run_unpack(): pl.pallas_call(unpack_kernel, grid=(steps,), out_shape=(shape((rows, widt...]
    pallas_call x1, Pallas kernels: 151 us -> 130 us  [run_backward(): pl.pallas_call(backward_kernel, out_shape=(shape((rows, width), F32), sha...]
    unnamed x60 -> x4, local copies, waits for them, and re-layouts: 15.7 us -> 3 us
    slice x8 -> x0, local copies, waits for them, and re-layouts: 7.16 us -> none  [the longest x1 1.42 us: fast_body(): mine[1]]
    add x3 -> x0, other arithmetic: 6.23 us -> none  [the longest x1 4.94 us: fast_body(): sums = [keep[a].astype(F32) + other[a].astype(F32) for a in range(3)]]
    squeeze x3 -> x0, local copies, waits for them, and re-layouts: 3.68 us -> none  [the longest x1 1.77 us: fast_body(): both[1]]
where the time goes in v4:
time: 306 us
  Pallas kernels  296 us (97%)
  local copies, waits for them, and re-layouts  5.52 us (2%)
  other arithmetic  4.05 us (1%)
    pallas_call x1, Pallas kernels, run_forward(): pl.pallas_call(forward_kernel, out_shape=(shape((pairs, 2 * rows, PAIR),...  156 us
    pallas_call x1, Pallas kernels, run_backward(): pl.pallas_call(backward_kernel, out_shape=(shape((rows, width), F32), sha...  130 us
    pallas_call x1, Pallas kernels, run_unpack(): pl.pallas_call(unpack_kernel, grid=(steps,), out_shape=(shape((rows, widt...  9.08 us

profile of v4, /device:TPU:0, one launch (start us, length us, event | category | flops | bytes accessed | tf_op | source)
XLA Modules:
  0.0 306.0 jit_solution(17187327333701999446)
XLA Ops:
  0.7 0.1 pad.13.clone
  0.8 0.7 select_reduce_fusion.1
  1.6 0.7 broadcast_in_dim.55
  2.2 0.7 broadcast_in_dim.56
  2.9 0.7 select_reduce_fusion
  3.6 0.6 and_select_fusion.kb
  4.2 0.8 maximum_convert_fusion
  5.0 0.3 dynamic_update_slice.3.pack
  5.3 0.0 copy-start
  5.3 1.4 copy.44
  6.8 0.8 copy.45.qb
  7.6 0.3 fusion
  7.9 0.8 pad_maximum_fusion
  8.7 0.0 copy-done
  8.7 156.3 %shard_map.289 = (bf16[6,256,128]{2,1,0:T(8,128)(2,1)}, f32[128,768]{1,0:T(8,128)}, f32[6,256,128]{2,1,0:T(8,128)}, bf16[128,768]{1,0:T(8,128)(2,1)}, f32[16,768...) custom-call(bf16[128,768]{1,0:T(8,128)(2,1)} %bitcast.13, ...), custom_call_target="tpu_custom_call" | custom-call | tf_op jit(solution)/shard_map/pallas_call | solution.py:844
  165.0 130.3 %shard_map.290 = (f32[128,768]{1,0:T(8,128)}, f32[16,768]{1,0:T(8,128)}, bf16[8,48,768]{2,1,0:T(8,128)(2,1)}, bf16[8,48,768]{2,1,0:T(8,128)(2,1)}, bf16[8,1152,1...) custom-call(f32[128,768]{1,0:T(8,128)} %get-tuple-element.51.grad_second_ref, bf16[128,768]{1,0:T(8,128)(2,1)} %bitcast.14, ...), custom_call_target="tpu_custom_call" | custom-call | tf_op jit(solution)/shard_map/pallas_call | solution.py:1139
  295.3 9.1 %shard_map.291 = (bf16[128,768]{1,0:T(8,128)(2,1)}, f32[128,768]{1,0:T(8,128)}, f32[1,192]{1,0:T(1,128)}, f32[1,192]{1,0:T(1,128)}, f32[192,8]{1,0:T(8,128)}, /*...) custom-call(bf16[128,768]{1,0:T(8,128)(2,1)} %get-tuple-element.50.r, ...), custom_call_target="tpu_custom_call" | custom-call | tf_op jit(solution)/shard_map/pallas_call | solution.py:1264
  304.4 1.6 copy.47
  (8 shorter events, 0.1 us)
Async XLA Ops:
  5.3 3.4 %copy-start = (f32[16,768]{1,0:T(8,128)}, f32[16,768]{1,0:T(8,128)S(1)}, u32[]{:S(2)}) copy-start(f32[16,768]{1,0:T(8,128)S(1)} %dynamic_update_slice.3.pack) | copy-start | bytes 147460

commit v5 on v4

--- a/solution.py
+++ b/solution.py
@@ -36,6 +36,8 @@
         self.across = (self.k, 2 * (1 - self.y) + self.c)
         self.corner = (self.k, 2 * (1 - self.y) + 1 - self.c)
         self.column = (2 * self.z + 1 - self.x, self.w)
+        self.odd = lax.rem(self.z, 2)
+        self.line = (2 * (self.z + 1 - 2 * self.odd) + self.x, self.w)
         self.inner = (2 * (self.z + step) + self.x, self.w)
         self.outer = (2 * (self.z - step) + self.x, self.w)
 
@@ -75,69 +77,64 @@
 
 
 class Gather:
-    def __init__(self, spot, src, dst, sems):
-        self.spot, self.dst, self.sems = spot, dst, sems
-        self.rows = src.shape[0]
-        here = self.block(spot.w)
-        self.local = pltpu.make_async_copy(src, here, sems.new())
+    def __init__(self, spot, src, place, sems, local=True):
+        self.spot, self.place, self.sems = spot, place, sems
+        here = place(spot.w)
+        self.local = pltpu.make_async_copy(src, here, sems.new()) if local else None
         self.to_core = remote(src, here, sems.new(), sems.new(), spot.core)
         self.to_across = remote(src, here, sems.new(), sems.new(), spot.across)
-        for copy in (self.to_across, self.to_core, self.local):
-            copy.start()
-
-    def block(self, w):
-        return self.dst.at[pl.ds(pl.multiple_of(self.rows * w, 64), self.rows)]
+        self.to_across.start()
+        self.to_core.start()
+        if local:
+            self.local.start()
 
     def forward(self):
         self.to_across.wait_recv()
-        part = self.block(self.spot.across[1])
+        part = self.place(self.spot.across[1])
         self.onward = remote(part, part, self.sems.new(), self.sems.new(), self.spot.core)
         self.onward.start()
 
     def finish(self):
-        self.local.wait()
+        if self.local is not None:
+            self.local.wait()
         self.to_core.wait_recv()
         self.onward.wait_recv()
 
     def drain(self):
-        self.to_core.wait_send()
-        self.to_across.wait_send()
-        self.onward.wait_send()
+        for copy in (self.to_core, self.to_across, self.onward):
+            copy.wait_send()
 
 
 class Share:
-    def __init__(self, spot, src, dst, sems):
-        self.spot, self.dst, self.sems = spot, dst, sems
+    def __init__(self, spot, src, dst, sems, mate, bit):
+        self.spot, self.dst, self.sems, self.mate, self.bit = spot, dst, sems, mate, bit
         self.rows = src.shape[0]
         self.half = self.rows // 2
-        here = self.block(spot.w)
-        half = pl.ds(pl.multiple_of(self.half * spot.x, 32), self.half)
+        here = dst.at[pl.ds(pl.multiple_of(self.rows * spot.w, 64), self.rows)]
+        half = pl.ds(pl.multiple_of(self.half * bit, 32), self.half)
         self.local = pltpu.make_async_copy(src, here, sems.new())
         self.to_core = remote(src, here, sems.new(), sems.new(), spot.core)
         self.to_across = remote(
-            src.at[half], self.part(spot.w, spot.x), sems.new(), sems.new(), spot.across
+            src.at[half], self.part(spot.w, bit), sems.new(), sems.new(), spot.across
         )
         for copy in (self.to_across, self.to_core, self.local):
             copy.start()
 
-    def block(self, w):
-        return self.dst.at[pl.ds(pl.multiple_of(self.rows * w, 64), self.rows)]
-
-    def part(self, w, x):
-        return self.dst.at[pl.ds(pl.multiple_of(self.rows * w + self.half * x, 32), self.half)]
+    def part(self, w, bit):
+        return self.dst.at[pl.ds(pl.multiple_of(self.rows * w + self.half * bit, 32), self.half)]
 
     def forward(self):
         spot = self.spot
         self.to_across.wait_recv()
-        part = self.part(spot.across[1], spot.x)
-        self.aside = remote(part, part, self.sems.new(), self.sems.new(), spot.column)
+        part = self.part(spot.across[1], self.bit)
+        self.aside = remote(part, part, self.sems.new(), self.sems.new(), self.mate)
         self.onward = remote(part, part, self.sems.new(), self.sems.new(), spot.core)
         self.aside.start()
         self.onward.start()
 
     def second(self):
         self.aside.wait_recv()
-        part = self.part(self.spot.across[1], 1 - self.spot.x)
+        part = self.part(self.spot.across[1], 1 - self.bit)
         self.rest = remote(part, part, self.sems.new(), self.sems.new(), self.spot.core)
         self.rest.start()
 
@@ -152,24 +149,100 @@
             copy.wait_send()
 
 
+class ShareColumns:
+    def __init__(self, spot, src, dst, sems, mate, bit):
+        self.spot, self.dst, self.sems, self.mate, self.bit = spot, dst, sems, mate, bit
+        self.rows, self.part_cols = src.shape[0], dst.shape[1]
+        self.half = self.rows // 2
+        half = pl.ds(pl.multiple_of(self.half * bit, 32), self.half)
+
+        def columns(to):
+            return pl.ds(pl.multiple_of(self.part_cols * to, self.part_cols), self.part_cols)
+
+        here = dst.at[pl.ds(pl.multiple_of(self.rows * spot.w, 64), self.rows)]
+        self.halves = [
+            remote(
+                src.at[half, columns(to[1])],
+                self.part(spot.w, bit),
+                sems.new(),
+                sems.new(),
+                to,
+            )
+            for to in (spot.across, spot.corner)
+        ]
+        self.to_core = remote(
+            src.at[:, columns(spot.core[1])], here, sems.new(), sems.new(), spot.core
+        )
+        self.local = pltpu.make_async_copy(src.at[:, columns(spot.w)], here, sems.new())
+        for copy in self.halves + [self.to_core, self.local]:
+            copy.start()
+
+    def part(self, w, bit):
+        return self.dst.at[pl.ds(pl.multiple_of(self.rows * w + self.half * bit, 32), self.half)]
+
+    def forward(self):
+        self.aside = []
+        for copy, source in zip(self.halves, (self.spot.across, self.spot.corner)):
+            copy.wait_recv()
+            part = self.part(source[1], self.bit)
+            self.aside.append(remote(part, part, self.sems.new(), self.sems.new(), self.mate))
+            self.aside[-1].start()
+
+    def finish(self):
+        self.local.wait()
+        self.to_core.wait_recv()
+        for copy in self.aside:
+            copy.wait_recv()
+
+    def drain(self):
+        for copy in self.halves + self.aside + [self.to_core]:
+            copy.wait_send()
+
+
+class Merge:
+    def __init__(self, spot, send, land, sems):
+        self.spot, self.send, self.land = spot, send, land
+        self.far = remote(
+            send.at[spot.corner[1]], land.at[0], sems.new(), sems.new(), spot.core
+        )
+        self.near = remote(send.at[spot.core[1]], land.at[1], sems.new(), sems.new(), spot.core)
+        self.over = remote(
+            send.at[spot.across[1]], land.at[2], sems.new(), sems.new(), spot.across
+        )
+        self.far.start()
+        self.near.start()
+
+    def forward(self):
+        self.far.wait_recv()
+        block = self.send.at[self.spot.across[1]]
+        block[...] = (block[...].astype(F32) + self.land[0].astype(F32)).astype(BF)
+        self.over.start()
+
+    def finish(self):
+        self.near.wait_recv()
+        self.over.wait_recv()
+        own = self.send[self.spot.w].astype(F32)
+        return own + self.land[1].astype(F32) + self.land[2].astype(F32)
+
+    def drain(self):
+        for copy in (self.far, self.near, self.over):
+            copy.wait_send()
+
+
 class Spread:
-    def __init__(self, spot, pick, place, sems, local=True):
+    def __init__(self, spot, pick, place, sems):
         self.copies = []
         for to in (spot.across, spot.corner, spot.core):
             self.copies.append(remote(pick(to[1]), place(spot.w), sems.new(), sems.new(), to))
-        self.local = None
-        if local:
-            self.local = pltpu.make_async_copy(pick(spot.w), place(spot.w), sems.new())
+        self.local = pltpu.make_async_copy(pick(spot.w), place(spot.w), sems.new())
         for copy in self.copies:
             copy.start()
-        if local:
-            self.local.start()
+        self.local.start()
 
     def finish(self):
         for copy in self.copies:
             copy.wait_recv()
-        if self.local is not None:
-            self.local.wait()
+        self.local.wait()
 
     def drain(self):
         for copy in self.copies:
@@ -220,7 +293,7 @@
         self.spot, self.blocks, self.recv, self.send, self.parts = spot, blocks, recv, send, parts
         self.ranks = blocks.shape[0]
         self.used = 0
-        self.sent, self.sent_mid = [], []
+        self.sent, self.sent_mid, self.sent_end = [], [], []
 
     def piece(self, slot, part):
         rows = self.blocks.shape[1] // self.parts
@@ -262,17 +335,36 @@
         def _():
             copy.start()
 
-    def step(self, number):
+    def step(self, number, only=None):
         spot = self.spot
         slot = 2 * spot.plane(number) + spot.x
+        onward = spot.inner if number == 1 else spot.outer
+        pieces = []
         for part in range(self.parts):
-            self.arrived(slot, part)
-            along = self.copy(slot, part, spot.inner if number == 1 else spot.outer)
-            self.middle(along)
-            side = self.copy(slot, part, spot.column)
-            side.start()
-            self.sent += [side]
-            self.sent_mid += [along]
+            along = self.copy(slot, part, onward) if only != 0 else None
+            pieces.append((along, self.copy(slot, part, spot.column)))
+        if only != 0:
+
+            @pl.when(spot.mid == 1)
+            def _():
+                for part, (along, side) in enumerate(pieces):
+                    self.arrived(slot, part)
+                    along.start()
+                    side.start()
+
+        if only != 1:
+
+            @pl.when(spot.mid == 0)
+            def _():
+                for part, (along, side) in enumerate(pieces):
+                    self.arrived(slot, part)
+                    side.start()
+
+        if only != 0:
+            self.sent_mid += [along for along, _ in pieces]
+            self.sent_mid += [side for _, side in pieces]
+        if only != 1:
+            self.sent_end += [side for _, side in pieces]
 
     def other(self, number):
         for part in range(self.parts):
@@ -281,11 +373,12 @@
     def drain(self):
         for copy in self.sent:
             copy.wait_send()
-
-        @pl.when(self.spot.mid == 1)
-        def _():
-            for copy in self.sent_mid:
-                copy.wait_send()
+        for role, copies in ((0, self.sent_end), (1, self.sent_mid)):
+
+            @pl.when(self.spot.mid == role)
+            def _(copies=copies):
+                for copy in copies:
+                    copy.wait_send()
 
 
 class Reduce:
@@ -519,11 +612,11 @@
 
 
 def forward_kernel(
-    tok, pack, cosr, sinr, kb, qb, cot, routes, order, sd,
+    tok, gain_one, gain_two, router_ref, freq, deal, cot, routes, order, sd,
     wq, wk, wv, wo, sg, su, eg, eu, ed,
-    q_out, mixed_out, lse_out, normed_out, pack_out, result_out, grad_second_out, pack_grad_out,
+    cosr, sinr, kb, qb, q_out, mixed_out, lse_out, normed_out, pack_out, result_out, grad_second_out, pack_grad_out,
     dsh_out, kv_out, wfull_out, keep_out, give_out, other_out,
-    wbuf, kv, packs, top, low, acc, sg_all, su_all, wg, wu, wd, mix, m4, cot4,
+    wbuf, kv, pack, packs, top, low, acc, sg_all, su_all, wg, wu, wd, mix, m4, cot4,
     sh_send, sh_recv, gm_send, gm_recv, xs, xr, gs, gr, os, orr, bs, br,
     x_s, g_s, sum_s, gate_s, up_s, hid_s, dgate_s, dup_s, dsh, dsh_x, slot_s, pair_s, cb,
     sem, kv_recv, kv_send, a2a_send, a2a_recv, sem_sh,
@@ -539,15 +632,43 @@
     part = sg_all.shape[1]
     peers = [(lax.rem(spot.k + o, ranks), spot.w) for o in range(1, ranks)]
     greet([spot.core, spot.across, spot.corner] + peers)
-    params = Spread(spot, lambda w: pack, lambda w: packs.at[w], sems)
-    key_w = Share(spot, wk, wbuf.at[1], sems)
-    value_w = Share(spot, wv, wbuf.at[2], sems)
-    query_w = Share(spot, wq, wbuf.at[0], sems)
+    column = (spot.column, spot.x)
+    key_w = Share(spot, wk, wbuf.at[1], sems, *column)
+    value_w = Share(spot, wv, wbuf.at[2], sems, *column)
+    shards = jnp.concatenate(
+        [
+            jnp.concatenate([gain_one[...], gain_two[...]], axis=0).astype(F32),
+            router_ref[...].astype(F32).T,
+            jnp.zeros((16 - 2 - router_ref.shape[1], shard), F32),
+        ],
+        axis=0,
+    )
+    shards = jnp.concatenate([shards, jnp.zeros((16, width - shard), F32)], axis=1)
+    pack[...] = pltpu.roll(shards, shard * spot.w, 1).astype(BF)
+    params = Gather(spot, pack, lambda w: packs.at[w], sems)
+    query_w = Share(spot, wq, wbuf.at[0], sems, *column)
     inputs = tok[...].astype(F32)
     scale = lax.rsqrt(jnp.mean(inputs * inputs, axis=-1, keepdims=True) + EPS)
     scaled = inputs * scale
+    piece = rows // 2
+    inner = lax.broadcasted_iota(jnp.int32, (rows, 1), 0)
+    paired = deal[spot.k]
+    unit = jnp.where(inner < piece, paired, 2 * ranks - 1 - paired)
+    place = unit * piece + lax.rem(inner, piece)
+    qb[...] = jnp.concatenate([lax.div(place, BLK)] * 2, axis=0)
+    along = lax.broadcasted_iota(jnp.int32, (1, rows), 1)
+    for r in range(ranks):
+        unit = jnp.where(along < piece, deal[r], 2 * ranks - 1 - deal[r])
+        kb[:, rows * r : rows * (r + 1)] = lax.div(unit * piece + lax.rem(along, piece), BLK)
+    angles = place.astype(F32) * freq[...]
+    cosr[...] = jnp.cos(angles)
+    lane = lax.broadcasted_iota(jnp.int32, angles.shape, 1)
+    sinr[...] = jnp.sin(angles) * jnp.where(lax.rem(lane, HD) < HD // 2, -1.0, 1.0)
+    params.forward()
     params.finish()
-    pack_all = packs[0] + packs[1] + packs[2] + packs[3]
+    pack_all = (packs[0].astype(F32) + packs[1].astype(F32)) + (
+        packs[2].astype(F32) + packs[3].astype(F32)
+    )
     pack_out[...] = pack_all
     normed = (scaled * pack_all[0:1]).astype(BF)
     normed_out[...] = normed
@@ -567,15 +688,17 @@
     ring = Ring(spot, kv, kv_recv, kv_send, parts=2)
     ring.start()
     query_w.second()
-    out_w = Gather(spot, wo, wbuf.at[3], sems)
-
-    def columns(ref):
-        return lambda w: ref.at[:, pl.ds(pl.multiple_of(part * w, part), part)]
 
     def stripe(ref):
         return lambda w: ref.at[pl.ds(pl.multiple_of(shard * w, 64), shard)]
 
-    gate_w = Gather(spot, eg, wg, sems)
+    line = (spot.line, spot.odd)
+    gate_w = Gather(spot, eg, stripe(wg), sems)
+    out_w = Share(spot, wo, wbuf.at[3], sems, *line)
+    cot_w = Gather(spot, cot, lambda w: cot4.at[w], sems)
+    sg_w = ShareColumns(spot, sg, sg_all, sems, *line)
+    su_w = ShareColumns(spot, su, su_all, sems, *line)
+    up_w = Gather(spot, eu, stripe(wu), sems)
     query_w.finish()
     query = turn(nn(normed, wbuf[0]), cosine, sine).astype(BF) * jnp.asarray(HD**-0.5, BF)
     for j in range(pairs):
@@ -606,20 +729,19 @@
         lax.fori_loop(0, pairs, one_pair, 0)
 
     ring.step(1)
-    ring.step(2)
-    sg_w = Spread(spot, columns(sg), stripe(sg_all), sems)
-    su_w = Spread(spot, columns(su), stripe(su_all), sems)
-    cot_w = Spread(spot, lambda w: cot, lambda w: cot4.at[w], sems)
+    ring.step(2, only=1)
     ring.other(0)
     chunk(spot.plane(0))
-    ring.step(3)
+    ring.step(2, only=0)
+    ring.step(3, only=1)
     ring.other(1)
     chunk(spot.plane(1))
+    ring.step(3, only=0)
     out_w.forward()
-    gate_w.forward()
-    up_w = Gather(spot, eu, wu, sems)
     ring.other(2)
     chunk(spot.plane(2))
+    out_w.second()
+    cot_w.forward()
     ring.other(3)
     chunk(spot.plane(3))
     saves = [pltpu.make_async_copy(kv, kv_out, sems.new())]
@@ -635,7 +757,8 @@
     mixer = (second * scale * pack_all[1:2]).astype(BF)
     mix[...] = mixer
 
-    mixers = Spread(spot, lambda w: mix, lambda w: m4.at[w], sems)
+    mixers = Gather(spot, mix, lambda w: m4.at[w], sems)
+    down_w = Gather(spot, ed, stripe(wd), sems)
     fold_rows(nn(slot_s[:, :rows] + slot_s[:, rows:], mixer), xs)
     rows_out = Exchange(spot, xs, xr, a2a_send.at[0], a2a_recv.at[0])
     rows_out.start()
@@ -653,8 +776,11 @@
     fold_rows(nn(slot_s[...], pair_grad), gs)
     grads_out = Exchange(spot, gs, gr, a2a_send.at[1], a2a_recv.at[1])
     grads_out.start()
+    sg_w.forward()
+    su_w.forward()
+    gate_w.forward()
     up_w.forward()
-    down_w = Gather(spot, ed, wd, sems)
+    mixers.forward()
 
     for part_w in (sg_w, su_w, cot_w, mixers):
         part_w.finish()
@@ -664,13 +790,14 @@
     act, slope = swish(gate_part)
     shared_hidden = (act * up_part).astype(BF)
     sh_send[...] = nn(shared_hidden, sd[...]).astype(BF).reshape(4, rows, width)
-    shared_out = Spread(spot, lambda w: sh_send.at[w], lambda w: sh_recv.at[w], sems)
+    shared_out = Merge(spot, sh_send, sh_recv, sems)
     hid_grad = nt(grad_all, sd[...])
     grad_gate = (hid_grad * up_part * slope).astype(BF)
     grad_up = (hid_grad * act).astype(BF)
     back = nt(grad_gate, sg_all[...]) + nt(grad_up, su_all[...])
     gm_send[...] = back.astype(BF).reshape(4, rows, width)
-    shared_back = Spread(spot, lambda w: gm_send.at[w], lambda w: gm_recv.at[w], sems)
+    shared_out.forward()
+    shared_back = Merge(spot, gm_send, gm_recv, sems)
     half = shard // 2
     for at, values in ((0, tn(rows_all, grad_gate)), (half, tn(rows_all, grad_up))):
         values = values.astype(BF)
@@ -687,6 +814,7 @@
             dsh[r, width + deep * t : width + deep * (t + 1)] = values[
                 deep * r : deep * (r + 1), 128 * t : 128 * (t + 1)
             ]
+    shared_back.forward()
     shared_grad = Reduce(spot, dsh, dsh_x, None, None, sem_sh)
     for number in (3, 2, 1, 0):
         shared_grad.side(number)
@@ -735,12 +863,14 @@
 
     for part_w in (gate_w, up_w, down_w):
         part_w.drain()
-    swaps = []
-    for a, (ref, left, right) in enumerate(
-        ((wg, x_s, dgate_s), (wu, x_s, dup_s), (wd, g_s, hid_s))
-    ):
-
-        def grad_step(i, carry, ref=ref, left=left, right=right):
+    swaps, across = [], []
+    first = 2 * shard // 3
+    sources = ((wg, x_s, dgate_s), (wu, x_s, dup_s), (wd, g_s, hid_s))
+
+    def grads_of(a):
+        ref, left, right = sources[a]
+
+        def grad_step(i, carry):
             at = parts(i)
             ref[:, at] = tn(left[...], right[:, at]).astype(BF)
             return carry
@@ -750,42 +880,51 @@
             src = ref.at[pl.ds(pl.multiple_of(shard * (2 * row + 1 - spot.c), 64), shard)]
             swaps.append(remote(src, cb.at[a, row], sems.new(), sems.new(), spot.core))
             swaps[-1].start()
-    across = []
-    for a, ref in enumerate((wg, wu, wd)):
+
+    def add_mate(a):
+        ref = sources[a][0]
         for row in range(2):
             swaps[2 * a + row].wait_recv()
 
-        def add(i, carry, a=a, ref=ref):
+        def add(i, carry):
             for row in range(2):
                 at = pl.ds(pl.multiple_of(shard * (2 * row + spot.c) + 16 * i, 16), 16)
-                own = ref[at].astype(F32)
-                ref[at] = (own + cb[a, row, pl.ds(16 * i, 16)].astype(F32)).astype(BF)
+                mate = cb[a, row, pl.ds(pl.multiple_of(16 * i, 16), 16)].astype(F32)
+                ref[at] = (ref[at].astype(F32) + mate).astype(BF)
             return carry
 
         lax.fori_loop(0, shard // 16, add, 0)
-        give = ref.at[pl.ds(pl.multiple_of(shard * spot.across[1], 64), shard)]
+        start = pl.multiple_of(shard * spot.across[1], 64)
         keep = ref.at[pl.ds(pl.multiple_of(shard * spot.w, 64), shard)]
         saves.append(pltpu.make_async_copy(keep, keep_out.at[a], sems.new()))
-        saves[-1].start()
         if a == 0:
-            across.append(remote(give, other_out, sems.new(), sems.new(), spot.across))
+            across.append(
+                remote(ref.at[pl.ds(start, first)], other_out, sems.new(), sems.new(), spot.across)
+            )
             across[-1].start()
+            give = ref.at[pl.ds(pl.multiple_of(start + first, 64), shard - first)]
+            saves.append(
+                pltpu.make_async_copy(give, give_out.at[0, pl.ds(first, shard - first)], sems.new())
+            )
         else:
-            saves.append(pltpu.make_async_copy(give, give_out.at[a - 1], sems.new()))
-            saves[-1].start()
+            give = ref.at[pl.ds(start, shard)]
+            saves.append(pltpu.make_async_copy(give, give_out.at[a], sems.new()))
+        for copy in saves[-2:]:
+            copy.start()
+
+    grads_of(0)
+    grads_of(1)
+    add_mate(0)
+    grads_of(2)
+    add_mate(1)
+    add_mate(2)
     for number in (3, 2, 1, 0):
         shared_grad.meet(number)
         plane = spot.plane(number)
         dsh_out[plane] = dsh[2 * plane + spot.x]
 
-    shared_out.finish()
-    total = second
-    for w in range(4):
-        total = total + sh_recv[w].astype(F32)
-    shared_back.finish()
-    grad_mixer = gm_recv[0].astype(F32)
-    for w in range(1, 4):
-        grad_mixer = grad_mixer + gm_recv[w].astype(F32)
+    total = second + shared_out.finish()
+    grad_mixer = shared_back.finish()
     outs.finish()
     pair_out = nn(pair_s[...], unfold_rows(orr, slots))
     pair_out = [pair_out[:rows], pair_out[rows:]]
@@ -820,7 +959,8 @@
 
 
 def run_forward(
-    tok, pack, cosr, sinr, kb, qb, cot, routes, order, sd, wq, wk, wv, wo, sg, su, eg, eu, ed
+    tok, gain_one, gain_two, router, freq, deal, cot, routes, order, sd,
+    wq, wk, wv, wo, sg, su, eg, eu, ed,
 ):
     rows, width = tok.shape
     pairs = width // PAIR
@@ -844,27 +984,32 @@
     return pl.pallas_call(
         forward_kernel,
         out_shape=(
+            shape((rows, PAIR), F32),
+            shape((rows, PAIR), F32),
+            shape((1, ranks * rows), jnp.int32),
+            shape((2 * rows, 1), jnp.int32),
             shape((pairs, 2 * rows, PAIR), BF),
             shape((rows, width), F32),
             shape((pairs, 2 * rows, PAIR), F32),
             shape((rows, width), BF),
-            shape(pack.shape, F32),
+            shape((16, width), F32),
             shape((rows, width), BF),
             shape((rows, width), F32),
-            shape(pack.shape, F32),
+            shape((16, width), F32),
             shape((4, tall, 128), BF),
             shape((ranks, rows, 2 * width), BF),
             shape((4, width, width), BF),
             shape((3, shard, hidden), BF),
-            shape((2, shard, hidden), BF),
-            shape((shard, hidden), BF),
+            shape((3, shard, hidden), BF),
+            shape((2 * shard // 3, hidden), BF),
         ),
-        in_specs=[vm] * 10 + [any_] * 9,
-        out_specs=tuple([vm] * 9 + [any_] * 5),
+        in_specs=[vm] * 5 + [pl.BlockSpec(memory_space=pltpu.SMEM)] + [vm] * 4 + [any_] * 9,
+        out_specs=tuple([vm] * 13 + [any_] * 5),
         scratch_shapes=[
             low(4, width, width),
             low(ranks, rows, 2 * width),
-            full(4, *pack.shape),
+            low(16, width),
+            low(4, 16, width),
             full(pairs, 2 * rows, PAIR),
             full(pairs, 2 * rows, PAIR),
             full(pairs, 2 * rows, PAIR),
@@ -877,9 +1022,9 @@
             low(4, rows, width),
             low(4, rows, width),
             low(4, rows, width),
+            low(3, rows, width),
             low(4, rows, width),
-            low(4, rows, width),
-            low(4, rows, width),
+            low(3, rows, width),
             *[folded] * 8,
             low(total, width),
             low(total, width),
@@ -904,12 +1049,15 @@
         compiler_params=pltpu.CompilerParams(
             collective_id=1, has_side_effects=True, vmem_limit_bytes=VMEM_BYTES
         ),
-    )(tok, pack, cosr, sinr, kb, qb, cot, routes, order, sd, wq, wk, wv, wo, sg, su, eg, eu, ed)
+    )(
+        tok, gain_one, gain_two, router, freq, deal, cot, routes, order, sd,
+        wq, wk, wv, wo, sg, su, eg, eu, ed,
+    )
 
 
 def backward_kernel(
     grad_second_ref, tok, pack_ref, pack_grad_ref, normed_ref, mixed_ref, q_ref, lse_ref,
-    cosr, sinr, kb, qb, dsh_ref, kv_ref, wfull_ref, give_ref,
+    cosr, sinr, kb, qb, dsh_ref, kv_ref, wfull_ref, give_ref, other_ref,
     grad_input_out, pack_out, att1_out, att2_out, sh_out, other_out,
     wbuf, kv, kvb, kv_x, kv_zo, kv_zi, kv_sum, gst, delta_s, dq,
     ga, ga4, gq, gq4, gkv, gkv4, n_t, m_t, n_all, m_all, pk, pk4,
@@ -934,7 +1082,7 @@
     greet((spot.core, spot.across, spot.corner, spot.column, spot.inner), (spot.mid, spot.outer))
     grad_second = grad_second_ref[...]
     ga[...] = grad_second.astype(BF)
-    grads_w = Spread(spot, lambda w: ga, lambda w: ga4.at[w], sems)
+    grads_w = Gather(spot, ga, lambda w: ga4.at[w], sems)
     loads[-1].wait()
     shared = Reduce(spot, sh, None, sh_zo, sh_zi, sem_sh, folded=True)
     for number in (3, 2, 1):
@@ -949,11 +1097,17 @@
     normed_w = Spread(spot, lambda w: block(n_t, w), columns(n_all), sems)
     mixed_w = Spread(spot, lambda w: block(m_t, w), columns(m_all), sems)
     across = []
-    for a in range(2):
-        across.append(
-            remote(give_ref.at[a], other_out.at[a], sems.new(), sems.new(), spot.across)
-        )
+
+    def send_across(src, dst):
+        across.append(remote(src, dst, sems.new(), sems.new(), spot.across))
         across[-1].start()
+
+    done = other_ref.shape[0]
+    loads.append(pltpu.make_async_copy(other_ref, other_out.at[0, pl.ds(0, done)], sems.new()))
+    loads[-1].start()
+    left = pl.ds(done, shard - done)
+    send_across(give_ref.at[0, left], other_out.at[0, left])
+    send_across(give_ref.at[1], other_out.at[1])
     loads[0].wait()
     grad_mixed = nt(ga[...], wbuf[3]).astype(BF)
     product = grad_mixed.astype(F32) * mixed
@@ -999,21 +1153,22 @@
     shared.relay(3)
     chunk(1)
     kv_grad.side(1)
+    shared.relay(2)
     kv_grad.meet(3)
-    shared.relay(2)
     chunk(0)
     kv_grad.side(0)
     cosine, sine = cosr[...], sinr[...]
     gq[...] = turn(
         jnp.concatenate([unstack_pair(dq[j]) for j in range(pairs)], axis=1), cosine, -sine
     ).astype(BF)
-    query_w = Spread(spot, lambda w: gq, lambda w: gq4.at[w], sems)
+    query_w = Gather(spot, gq, lambda w: gq4.at[w], sems)
+    shared.relay(1)
+    kv_grad.meet(2)
+    kv_grad.relay(3)
+    grads_w.forward()
     for part_w in (grads_w, normed_w, mixed_w):
         part_w.finish()
     out_grad = nn(m_all[...], ga4[...].reshape(4 * rows, width))
-    kv_grad.meet(2)
-    kv_grad.relay(3)
-    shared.relay(1)
     shared.last(sh_sum)
     sh_chunk[...] = sh_sum[...].astype(BF)
     part = 2 * shard // 2
@@ -1030,6 +1185,7 @@
     kv_grad.meet(1)
     kv_grad.relay(2)
     kv_grad.relay(1)
+    query_w.forward()
     query_w.finish()
     query_grad = nn(n_all[...], gq4[...].reshape(4 * rows, width))
     half = jnp.concatenate([out_grad, query_grad], axis=0).astype(BF)
@@ -1041,7 +1197,7 @@
     kv_grad.last(kv_sum)
     gkv[:, 0:width] = turn(kv_sum[:, 0:width], cosine, -sine).astype(BF)
     gkv[:, width : 2 * width] = kv_sum[:, width : 2 * width].astype(BF)
-    kv_w = Spread(spot, lambda w: gkv, lambda w: gkv4.at[w], sems)
+    kv_w = Gather(spot, gkv, lambda w: gkv4.at[w], sems)
     shared_w.finish()
     ring3 = Ring(spot, r3, ring_recv.at[2], ring_send.at[2], parts=2)
     ring3.start()
@@ -1057,19 +1213,22 @@
         grad_second + scale * weighted - inputs * (scale * scale * scale * mean)
     )
     gain_grad = jnp.sum(grad_normed * inputs * scale, axis=0, keepdims=True)
-    pk[...] = jnp.concatenate([gain_grad, pack_grad_ref[1:16]], axis=0)
-    pack_w = Spread(spot, lambda w: pk, lambda w: pk4.at[w], sems)
+    pk[...] = jnp.concatenate([gain_grad, pack_grad_ref[1:16]], axis=0).astype(BF)
+    pack_w = Gather(spot, pk, lambda w: pk4.at[w], sems)
+    send_across(give_ref.at[2], other_out.at[2])
     for number in (3, 2, 1, 0):
         first.meet(number)
     first.relay(3)
     first.relay(2)
+    kv_w.forward()
+    pack_w.forward()
     kv_w.finish()
     pack_w.finish()
     grad_kv = gkv4[...].reshape(4 * rows, 2 * width)
     both = nn(n_all[...], grad_kv)
     both = jnp.concatenate([both[:, 0:width], both[:, width : 2 * width]], axis=0).astype(BF)
     size = both.shape[0] // 8
-    extra = (pk4[0] + pk4[1] + pk4[2] + pk4[3]).astype(BF)
+    extra = sum(pk4[w].astype(F32) for w in range(4)).astype(BF)
     for r in range(8):
         a2[r, 0:size] = both[size * r : size * (r + 1)]
         a2[r, size : size + 16] = extra
@@ -1112,13 +1271,13 @@
         part_w.drain()
     for part_w in (shared, kv_grad, first, second, ring1, ring2, ring3):
         part_w.drain()
-    for copy in saves:
+    for copy in saves + loads[6:]:
         copy.wait()
 
 
 def run_backward(
     grad_second, tok, pack, pack_grad, normed, mixed, q, lse, cosr, sinr, kb, qb, dsh, kv, wfull,
-    give,
+    give, other,
 ):
     rows, width = tok.shape
     pairs = width // PAIR
@@ -1144,9 +1303,9 @@
             shape((ranks, size, width), BF),
             shape((ranks, size, width), BF),
             shape((ranks, tall, 128), BF),
-            shape((2, shard, hidden), BF),
+            shape((3, shard, hidden), BF),
         ),
-        in_specs=[vm] * 12 + [any_] * 4,
+        in_specs=[vm] * 12 + [any_] * 5,
         out_specs=(vm, vm, any_, any_, any_, any_),
         scratch_shapes=[
             low(4, width, width),
@@ -1169,8 +1328,8 @@
             low(width, rows),
             low(shard, 4 * rows),
             low(shard, 4 * rows),
-            full(16, width),
-            full(4, 16, width),
+            low(16, width),
+            low(4, 16, width),
             low(ranks, size, width),
             low(4, size, width),
             low(4, size, width),
@@ -1202,12 +1361,12 @@
         ),
     )(
         grad_second, tok, pack, pack_grad, normed, mixed, q, lse, cosr, sinr, kb, qb, dsh, kv,
-        wfull, give,
+        wfull, give, other,
     )
 
 
 def unpack_kernel(
-    result, grad_input, pack, att1, att2, sh, keep, other0, other,
+    result, grad_input, pack, att1, att2, sh, keep, other,
     result_out, grad_input_out, gain_one, gain_two, router,
     query, key, value, output, gate, up, down, eg, eu, ed,
 ):
@@ -1218,9 +1377,8 @@
     query[...] = att1[1, 0].astype(F32)
     key[...] = att2[0, 0].astype(F32)
     value[...] = att2[1, 0].astype(F32)
-    eg[...] = keep[0].astype(F32) + other0[...].astype(F32)
-    eu[...] = keep[1].astype(F32) + other[0].astype(F32)
-    ed[...] = keep[2].astype(F32) + other[1].astype(F32)
+    for a, ref in enumerate((eg, eu, ed)):
+        ref[...] = keep[a].astype(F32) + other[a].astype(F32)
     size = gate.shape[0]
     shard = 4 * size
     width = 4 * shard
@@ -1247,9 +1405,9 @@
         router[...] = mine.T[0:shard, 2 : 2 + router.shape[1]]
 
 
-def run_unpack(result, grad_input, pack, att1, att2, sh, keep, other0, other, experts):
+def run_unpack(result, grad_input, pack, att1, att2, sh, keep, other, experts):
     rows, width = result.shape
-    shard, hidden = other0.shape
+    shard, hidden = keep.shape[1:]
     steps = 4
     shape = jax.ShapeDtypeStruct
     size = shard // steps
@@ -1283,8 +1441,7 @@
             att,
             whole(*sh.shape),
             stack(3, size, hidden),
-            by_rows(size, hidden),
-            stack(2, size, hidden),
+            stack(3, size, hidden),
         ],
         out_specs=(
             by_rows(rows // steps, width),
@@ -1298,27 +1455,7 @@
             *[by_rows(size, hidden)] * 3,
         ),
         compiler_params=pltpu.CompilerParams(vmem_limit_bytes=VMEM_BYTES),
-    )(result, grad_input, pack, att1, att2, sh, keep, other0, other)
-
-
-def angles_of(block_deal, rows_dev):
-    here = places(lax.axis_index("ctx") * rows_dev, rows_dev, block_deal, rows_dev)
-    half_size = HD // 2
-    frequency = 10000.0 ** (-jnp.arange(half_size, dtype=F32) / half_size)
-    angles = here.astype(F32)[:, None] * frequency[None, :]
-    cosine, sine = jnp.cos(angles), jnp.sin(angles)
-    cosr = jnp.concatenate([cosine] * 4, axis=1)
-    sinr = jnp.concatenate([-sine, sine, -sine, sine], axis=1)
-    return here, cosr, sinr
-
-
-def pack_params(gain_one, gain_two, router):
-    width = 4 * gain_one.shape[0]
-    shard = jnp.concatenate(
-        [gain_one[None], gain_two[None], router.T, jnp.zeros((6, gain_one.shape[0]), BF)], axis=0
-    ).astype(F32)
-    start = lax.axis_index("wt") * gain_one.shape[0]
-    return lax.dynamic_update_slice(jnp.zeros((16, width), F32), shard, (0, start))
+    )(result, grad_input, pack, att1, att2, sh, keep, other)
 
 
 def contract_product(left, right, left_dim, right_dim):
@@ -1838,29 +1975,26 @@
     slot_order,
     block_deal,
 ):
-    rows_dev = tokens.shape[1]
-    ranks = lax.axis_size("ctx")
-    here, cosr, sinr = angles_of(block_deal, rows_dev)
-    kb = (places(0, ranks * rows_dev, block_deal, rows_dev) // BLK)[None, :]
-    qb = jnp.concatenate([here // BLK] * 2)[:, None]
-    pack = pack_params(gain_attention, gain_mixer, router_weight)
+    half_size = HD // 2
+    frequency = 10000.0 ** (-jnp.arange(half_size, dtype=F32) / half_size)
     (
-        q_st, mixed, lse, normed, pack_all, result, grad_second, pack_grad, dsh, kv_all, wfull,
-        keep, give, other0,
+        cosr, sinr, kb, qb, q_st, mixed, lse, normed, pack_all, result, grad_second, pack_grad, dsh,
+        kv_all, wfull, keep, give, other,
     ) = run_forward(
-        tokens[0], pack, cosr, sinr, kb, qb, cotangent[0], routes[0], slot_order[0], shared_down,
-        query_weight, key_weight, value_weight, output_weight, shared_gate, shared_up,
+        tokens[0], gain_attention[None], gain_mixer[None], router_weight,
+        jnp.concatenate([frequency] * 4)[None], block_deal, cotangent[0], routes[0], slot_order[0],
+        shared_down, query_weight, key_weight, value_weight, output_weight, shared_gate, shared_up,
         expert_gate, expert_up, expert_down,
     )
     grad_input, pack_sum, att1, att2, sh, other = run_backward(
         grad_second, tokens[0], pack_all, pack_grad, normed, mixed, q_st, lse, cosr, sinr, kb, qb,
-        dsh, kv_all, wfull, give,
+        dsh, kv_all, wfull, give, other,
     )
     (
         result, grad_input, gain_one, gain_two, router, query, key, value, output, gate, up, down,
         eg, eu, ed,
     ) = run_unpack(
-        result, grad_input, pack_sum, att1, att2, sh, keep, other0, other, router_weight.shape[1]
+        result, grad_input, pack_sum, att1, att2, sh, keep, other, router_weight.shape[1]
     )
     return (
         result[None], grad_input[None], gain_one.reshape(-1), query, key, value, output,

time: 306 us -> 271 us (0.89)
  Pallas kernels: 296 us -> 263 us
  other arithmetic: 4.05 us -> 0.6 us
    pallas_call x1, Pallas kernels: 130 us -> 112 us  [run_backward(): pl.pallas_call(backward_kernel, out_shape=(shape((rows, width), F32), sha...]
    pallas_call x1, Pallas kernels: 156 us -> 142 us  [run_forward(): pl.pallas_call(forward_kernel, out_shape=(shape((rows, PAIR), F32), shape...]
where the time goes in v5:
time: 271 us
  Pallas kernels  263 us (97%)
  local copies, waits for them, and re-layouts  6.83 us (3%)
    pallas_call x1, Pallas kernels, run_forward(): pl.pallas_call(forward_kernel, out_shape=(shape((rows, PAIR), F32), shape...  142 us
    pallas_call x1, Pallas kernels, run_backward(): pl.pallas_call(backward_kernel, out_shape=(shape((rows, width), F32), sha...  112 us
    pallas_call x1, Pallas kernels, run_unpack(): pl.pallas_call(unpack_kernel, grid=(steps,), out_shape=(shape((rows, widt...  9.05 us

profile of v5, /device:TPU:0, one launch (start us, length us, event | category | flops | bytes accessed | tf_op | source)
XLA Modules:
  0.0 270.6 jit_solution(5174455581748506426)
XLA Ops:
  0.7 0.6 maximum_bitcast_fusion.freq
  1.3 1.2 broadcast_in_dim.15.gain_one
  2.5 1.2 broadcast_in_dim.16.gain_two
  3.7 1.4 copy.34.router_ref
  5.1 1.4 copy.33
  6.5 141.8 %shard_map.289 = (f32[128,128]{1,0:T(8,128)}, f32[128,128]{1,0:T(8,128)}, s32[1,1024]{1,0:T(1,128)}, s32[256,1]{1,0:T(8,128)}, bf16[6,256,128]{2,1,0:T(8,128)(2,...) custom-call(bf16[128,768]{1,0:T(8,128)(2,1)} %bitcast.12, ...), custom_call_target="tpu_custom_call" | custom-call | tf_op jit(solution)/shard_map/pallas_call | solution.py:984
  148.4 111.6 %shard_map.290 = (f32[128,768]{1,0:T(8,128)}, f32[16,768]{1,0:T(8,128)}, bf16[8,48,768]{2,1,0:T(8,128)(2,1)}, bf16[8,48,768]{2,1,0:T(8,128)(2,1)}, bf16[8,1152,1...) custom-call(f32[128,768]{1,0:T(8,128)} %get-tuple-element.55.grad_second_ref, bf16[128,768]{1,0:T(8,128)(2,1)} %bitcast.13, ...), custom_call_target="tpu_custom_call" | custom-call | tf_op jit(solution)/shard_map/pallas_call | solution.py:1298
  260.0 9.1 %shard_map.291 = (bf16[128,768]{1,0:T(8,128)(2,1)}, f32[128,768]{1,0:T(8,128)}, f32[1,192]{1,0:T(1,128)}, f32[1,192]{1,0:T(1,128)}, f32[192,8]{1,0:T(8,128)}, /*...) custom-call(bf16[128,768]{1,0:T(8,128)(2,1)} %get-tuple-element.54.r, ...), custom_call_target="tpu_custom_call" | custom-call | tf_op jit(solution)/shard_map/pallas_call | solution.py:1422
  269.1 1.6 copy.35
  (1 shorter events, 0.0 us)

commit v6 on v5

--- a/solution.py
+++ b/solution.py
@@ -1,5 +1,6 @@
 import jax
 import jax.numpy as jnp
+import numpy as np
 from jax import lax
 from jax.experimental import pallas as pl
 from jax.experimental.pallas import tpu as pltpu
@@ -449,6 +450,15 @@
 
         self.sent_end.append(copy)
 
+    def absorb(self, number):
+        plane = self.spot.plane(number)
+
+        @pl.when(self.spot.mid == 1)
+        def _():
+            for h in range(self.parts):
+                self.wait(self.zo, self.zo_recv, plane, h)
+                self.add(self.own(plane, h), self.cut(self.zo, plane, h))
+
     def relay(self, number):
         plane = self.spot.plane(number)
         land, recv = (self.zi, self.zi_recv) if number == 1 else (self.zo, self.zo_recv)
@@ -468,8 +478,9 @@
         @pl.when(self.spot.mid == 1)
         def _():
             for h, copy in enumerate(copies):
-                self.wait(land, recv, plane, h)
-                self.add(self.own(plane, h), self.cut(land, plane, h))
+                if land is not None:
+                    self.wait(land, recv, plane, h)
+                    self.add(self.own(plane, h), self.cut(land, plane, h))
                 copy.start()
 
         self.sent_mid += copies
@@ -481,6 +492,9 @@
             rows = pl.ds(self.rows * h, self.rows)
             total = self.own(plane, h)[...].astype(F32)
             result[rows] = total + self.cut(self.zi, plane, h)[...].astype(F32)
+
+        if self.zo is None:
+            return
 
         @pl.when(self.spot.mid == 1)
         def _():
@@ -583,11 +597,11 @@
 
 
 def slot_maps(routes, order, slots, experts):
-    rows, top = routes.shape
+    top, rows = routes.shape
     pairs = rows * top
-    columns = [routes[:, j : j + 1] for j in range(top)]
-    e_col = jnp.concatenate(columns, axis=0)
-    e_row = jnp.concatenate([diagonal(column, 0) for column in columns], axis=1)
+    lines = [routes[j : j + 1] for j in range(top)]
+    e_row = jnp.concatenate(lines, axis=1)
+    e_col = jnp.concatenate([diagonal(line, 1) for line in lines], axis=0)
     o_row = lax.rem(order, top) * rows + lax.div(order, top)
     o_col = diagonal(o_row, 1)
     down = lax.broadcasted_iota(jnp.int32, (pairs, pairs), 0)
@@ -612,13 +626,13 @@
 
 
 def forward_kernel(
-    tok, gain_one, gain_two, router_ref, freq, deal, cot, routes, order, sd,
+    tok, gains, router_ref, freq, deal, cot, routes, order, sd,
     wq, wk, wv, wo, sg, su, eg, eu, ed,
     cosr, sinr, kb, qb, q_out, mixed_out, lse_out, normed_out, pack_out, result_out, grad_second_out, pack_grad_out,
     dsh_out, kv_out, wfull_out, keep_out, give_out, other_out,
-    wbuf, kv, pack, packs, top, low, acc, sg_all, su_all, wg, wu, wd, mix, m4, cot4,
+    wbuf, kv, q_s, pack, packs, top, low, acc, sg_all, su_all, wg, wu, wd, mix, m4, cot4,
     sh_send, sh_recv, gm_send, gm_recv, xs, xr, gs, gr, os, orr, bs, br,
-    x_s, g_s, sum_s, gate_s, up_s, hid_s, dgate_s, dup_s, dsh, dsh_x, slot_s, pair_s, cb,
+    x_s, g_s, sum_s, gate_s, up_s, hid_s, dgate_s, dup_s, dsh, dsh_x, dsh_z, slot_s, pair_s, cb,
     sem, kv_recv, kv_send, a2a_send, a2a_recv, sem_sh,
 ):
     spot = Spot(4)
@@ -632,38 +646,46 @@
     part = sg_all.shape[1]
     peers = [(lax.rem(spot.k + o, ranks), spot.w) for o in range(1, ranks)]
     greet([spot.core, spot.across, spot.corner] + peers)
-    column = (spot.column, spot.x)
+    column, line = (spot.column, spot.x), (spot.line, spot.odd)
     key_w = Share(spot, wk, wbuf.at[1], sems, *column)
-    value_w = Share(spot, wv, wbuf.at[2], sems, *column)
     shards = jnp.concatenate(
-        [
-            jnp.concatenate([gain_one[...], gain_two[...]], axis=0).astype(F32),
-            router_ref[...].astype(F32).T,
-            jnp.zeros((16 - 2 - router_ref.shape[1], shard), F32),
-        ],
-        axis=0,
-    )
+        [gains[...], router_ref[...], jnp.zeros((16 - 2 - router_ref.shape[0], shard), BF)], axis=0
+    ).astype(F32)
     shards = jnp.concatenate([shards, jnp.zeros((16, width - shard), F32)], axis=1)
     pack[...] = pltpu.roll(shards, shard * spot.w, 1).astype(BF)
     params = Gather(spot, pack, lambda w: packs.at[w], sems)
+    value_w = Share(spot, wv, wbuf.at[2], sems, *column)
     query_w = Share(spot, wq, wbuf.at[0], sems, *column)
+
+    def stripe(ref):
+        return lambda w: ref.at[pl.ds(pl.multiple_of(shard * w, 64), shard)]
+
+    out_w = Share(spot, wo, wbuf.at[3], sems, *line)
+    sg_w = ShareColumns(spot, sg, sg_all, sems, *line)
+    su_w = ShareColumns(spot, su, su_all, sems, *line)
+    cot_w = Gather(spot, cot, lambda w: cot4.at[w], sems)
+    gate_w = Gather(spot, eg, stripe(wg), sems)
+    up_w = Gather(spot, eu, stripe(wu), sems)
     inputs = tok[...].astype(F32)
     scale = lax.rsqrt(jnp.mean(inputs * inputs, axis=-1, keepdims=True) + EPS)
     scaled = inputs * scale
     piece = rows // 2
     inner = lax.broadcasted_iota(jnp.int32, (rows, 1), 0)
-    paired = deal[spot.k]
-    unit = jnp.where(inner < piece, paired, 2 * ranks - 1 - paired)
-    place = unit * piece + lax.rem(inner, piece)
-    qb[...] = jnp.concatenate([lax.div(place, BLK)] * 2, axis=0)
+    lane = lax.broadcasted_iota(jnp.int32, (rows, PAIR), 1)
+    sign = jnp.where(lax.rem(lane, HD) < HD // 2, -1.0, 1.0)
+    for r in range(2):
+        paired = deal[2 * spot.z + r]
+        unit = jnp.where(inner < piece, paired, 2 * ranks - 1 - paired)
+        place = unit * piece + lax.rem(inner, piece)
+        qb[r] = jnp.concatenate([lax.div(place, BLK)] * 2, axis=0)
+        angles = place.astype(F32) * freq[...]
+        cosr[r] = jnp.cos(angles)
+        sinr[r] = jnp.sin(angles) * sign
     along = lax.broadcasted_iota(jnp.int32, (1, rows), 1)
     for r in range(ranks):
         unit = jnp.where(along < piece, deal[r], 2 * ranks - 1 - deal[r])
         kb[:, rows * r : rows * (r + 1)] = lax.div(unit * piece + lax.rem(along, piece), BLK)
-    angles = place.astype(F32) * freq[...]
-    cosr[...] = jnp.cos(angles)
-    lane = lax.broadcasted_iota(jnp.int32, angles.shape, 1)
-    sinr[...] = jnp.sin(angles) * jnp.where(lax.rem(lane, HD) < HD // 2, -1.0, 1.0)
+    key_w.forward()
     params.forward()
     params.finish()
     pack_all = (packs[0].astype(F32) + packs[1].astype(F32)) + (
@@ -672,9 +694,9 @@
     pack_out[...] = pack_all
     normed = (scaled * pack_all[0:1]).astype(BF)
     normed_out[...] = normed
-    cosine, sine = cosr[...], sinr[...]
-    key_w.forward()
+    cosine, sine = cosr[spot.x], sinr[spot.x]
     to_slots, to_pairs = slot_maps(routes[...], order[...], slots, ranks)
+    route = [diagonal(routes[j : j + 1], 1) for j in range(2)]
     slot_s[...] = to_slots
     pair_s[...] = to_pairs
     value_w.forward()
@@ -689,24 +711,16 @@
     ring.start()
     query_w.second()
 
-    def stripe(ref):
-        return lambda w: ref.at[pl.ds(pl.multiple_of(shard * w, 64), shard)]
-
-    line = (spot.line, spot.odd)
-    gate_w = Gather(spot, eg, stripe(wg), sems)
-    out_w = Share(spot, wo, wbuf.at[3], sems, *line)
-    cot_w = Gather(spot, cot, lambda w: cot4.at[w], sems)
-    sg_w = ShareColumns(spot, sg, sg_all, sems, *line)
-    su_w = ShareColumns(spot, su, su_all, sems, *line)
-    up_w = Gather(spot, eu, stripe(wu), sems)
     query_w.finish()
     query = turn(nn(normed, wbuf[0]), cosine, sine).astype(BF) * jnp.asarray(HD**-0.5, BF)
     for j in range(pairs):
-        q_out[j] = stack_pair(query[:, PAIR * j : PAIR * (j + 1)])
+        q_s[j] = stack_pair(query[:, PAIR * j : PAIR * (j + 1)])
+    for x in range(2):
+        q_out[x] = query[:, width // 2 * x : width // 2 * (x + 1)]
     top[...] = jnp.full_like(top, MASKED)
     low[...] = jnp.zeros_like(low)
     acc[...] = jnp.zeros_like(acc)
-    q_block = qb[...]
+    q_block = qb[spot.x]
 
     def chunk(plane):
         k_block = kb[:, pl.ds(pl.multiple_of(2 * rows * plane, 2 * rows), 2 * rows)]
@@ -716,7 +730,7 @@
             lane = pl.multiple_of(PAIR * j, PAIR)
             key = kv[pl.ds(2 * plane, 2), :, pl.ds(lane, PAIR)].reshape(2 * rows, PAIR)
             value = kv[pl.ds(2 * plane, 2), :, pl.ds(width + lane, PAIR)].reshape(2 * rows, PAIR)
-            scores = jnp.where(allowed, nt(q_out[j], key), MASKED)
+            scores = jnp.where(allowed, nt(q_s[j], key), MASKED)
             old = top[j]
             new = jnp.maximum(old, jnp.max(scores, axis=1, keepdims=True))
             raised = jnp.where(allowed, jnp.exp(scores - new[:, 0:1]), 0.0)
@@ -738,6 +752,8 @@
     chunk(spot.plane(1))
     ring.step(3, only=0)
     out_w.forward()
+    sg_w.forward()
+    su_w.forward()
     ring.other(2)
     chunk(spot.plane(2))
     out_w.second()
@@ -766,7 +782,7 @@
     router = jnp.concatenate([router, jnp.zeros((2, width), BF)], axis=0)
     logits = nt(mixer, router)
     lane = lax.broadcasted_iota(jnp.int32, logits.shape, 1)
-    matches = [lane == routes[:, j : j + 1] for j in range(2)]
+    matches = [lane == route[j] for j in range(2)]
     chosen = [jnp.sum(jnp.where(m, logits, 0.0), axis=1, keepdims=True) for m in matches]
     largest = jnp.maximum(chosen[0], chosen[1])
     raised = [jnp.exp(c - largest) for c in chosen]
@@ -776,8 +792,6 @@
     fold_rows(nn(slot_s[...], pair_grad), gs)
     grads_out = Exchange(spot, gs, gr, a2a_send.at[1], a2a_recv.at[1])
     grads_out.start()
-    sg_w.forward()
-    su_w.forward()
     gate_w.forward()
     up_w.forward()
     mixers.forward()
@@ -815,7 +829,7 @@
                 deep * r : deep * (r + 1), 128 * t : 128 * (t + 1)
             ]
     shared_back.forward()
-    shared_grad = Reduce(spot, dsh, dsh_x, None, None, sem_sh)
+    shared_grad = Reduce(spot, dsh, dsh_x, dsh_z, None, sem_sh)
     for number in (3, 2, 1, 0):
         shared_grad.side(number)
 
@@ -839,10 +853,15 @@
         return carry
 
     lax.fori_loop(0, hidden // block, up_step, 0)
+    down_w.forward()
+    down_w.finish()
+    shared_grad.meet(3)
+    sum_s[...] = nt(hid_s[...], wd[...])
+    fold_rows(sum_s[...], os)
+    outs = Exchange(spot, os, orr, a2a_send.at[2], a2a_recv.at[2])
+    outs.start()
     grads_out.finish()
     g_s[...] = unfold_rows(gr, slots)
-    down_w.forward()
-    down_w.finish()
 
     def down_step(i, carry):
         at = parts(i)
@@ -856,10 +875,6 @@
     fold_rows(sum_s[...], bs)
     backs = Exchange(spot, bs, br, a2a_send.at[3], a2a_recv.at[3])
     backs.start()
-    sum_s[...] = nt(hid_s[...], wd[...])
-    fold_rows(sum_s[...], os)
-    outs = Exchange(spot, os, orr, a2a_send.at[2], a2a_recv.at[2])
-    outs.start()
 
     for part_w in (gate_w, up_w, down_w):
         part_w.drain()
@@ -912,17 +927,15 @@
         for copy in saves[-2:]:
             copy.start()
 
+    shared_grad.meet(2)
     grads_of(0)
     grads_of(1)
     add_mate(0)
+    shared_grad.meet(1)
     grads_of(2)
     add_mate(1)
     add_mate(2)
-    for number in (3, 2, 1, 0):
-        shared_grad.meet(number)
-        plane = spot.plane(number)
-        dsh_out[plane] = dsh[2 * plane + spot.x]
-
+    shared_grad.meet(0)
     total = second + shared_out.finish()
     grad_mixer = shared_back.finish()
     outs.finish()
@@ -946,20 +959,24 @@
     pack_grad_out[...] = jnp.concatenate(
         [jnp.zeros_like(gain_grad), gain_grad, router_grad[:14]], axis=0
     )
+    for number in (3, 2, 0):
+        shared_grad.absorb(number)
+    for plane in range(4):
+        dsh_out[plane] = dsh[2 * plane + spot.x]
     for copy in across:
         copy.wait_recv()
     for part_w in (params, key_w, value_w, query_w, out_w, sg_w, su_w, cot_w, ring, mixers):
         part_w.drain()
-    for part_w in (rows_out, grads_out, outs, backs, shared_out, shared_back):
+    for part_w in (rows_out, grads_out, outs, backs, shared_out, shared_back, shared_grad):
         part_w.drain()
-    for copy in shared_grad.sent + swaps + across:
+    for copy in swaps + across:
         copy.wait_send()
     for copy in saves:
         copy.wait()
 
 
 def run_forward(
-    tok, gain_one, gain_two, router, freq, deal, cot, routes, order, sd,
+    tok, gains, router, freq, deal, cot, routes, order, sd,
     wq, wk, wv, wo, sg, su, eg, eu, ed,
 ):
     rows, width = tok.shape
@@ -984,11 +1001,11 @@
     return pl.pallas_call(
         forward_kernel,
         out_shape=(
-            shape((rows, PAIR), F32),
-            shape((rows, PAIR), F32),
+            shape((2, rows, PAIR), F32),
+            shape((2, rows, PAIR), F32),
             shape((1, ranks * rows), jnp.int32),
-            shape((2 * rows, 1), jnp.int32),
-            shape((pairs, 2 * rows, PAIR), BF),
+            shape((2, 2 * rows, 1), jnp.int32),
+            shape((2, rows, width // 2), BF),
             shape((rows, width), F32),
             shape((pairs, 2 * rows, PAIR), F32),
             shape((rows, width), BF),
@@ -1003,11 +1020,12 @@
             shape((3, shard, hidden), BF),
             shape((2 * shard // 3, hidden), BF),
         ),
-        in_specs=[vm] * 5 + [pl.BlockSpec(memory_space=pltpu.SMEM)] + [vm] * 4 + [any_] * 9,
+        in_specs=[vm] * 4 + [pl.BlockSpec(memory_space=pltpu.SMEM)] + [vm] * 4 + [any_] * 9,
         out_specs=tuple([vm] * 13 + [any_] * 5),
         scratch_shapes=[
             low(4, width, width),
             low(ranks, rows, 2 * width),
+            low(pairs, 2 * rows, PAIR),
             low(16, width),
             low(4, 16, width),
             full(pairs, 2 * rows, PAIR),
@@ -1036,6 +1054,7 @@
             low(total, hidden),
             low(ranks, tall, 128),
             low(4, tall, 128),
+            low(4, tall, 128),
             low(total, 2 * rows),
             low(2 * rows, total),
             low(3, 2, shard, hidden),
@@ -1050,29 +1069,43 @@
             collective_id=1, has_side_effects=True, vmem_limit_bytes=VMEM_BYTES
         ),
     )(
-        tok, gain_one, gain_two, router, freq, deal, cot, routes, order, sd,
+        tok, gains, router, freq, deal, cot, routes, order, sd,
         wq, wk, wv, wo, sg, su, eg, eu, ed,
     )
 
 
 def backward_kernel(
-    grad_second_ref, tok, pack_ref, pack_grad_ref, normed_ref, mixed_ref, q_ref, lse_ref,
+    grad_second_ref, tok, pack_ref, pack_grad_ref, normed_ref, mixed_ref, qc_ref, lse_ref,
     cosr, sinr, kb, qb, dsh_ref, kv_ref, wfull_ref, give_ref, other_ref,
     grad_input_out, pack_out, att1_out, att2_out, sh_out, other_out,
-    wbuf, kv, kvb, kv_x, kv_zo, kv_zi, kv_sum, gst, delta_s, dq,
-    ga, ga4, gq, gq4, gkv, gkv4, n_t, m_t, n_all, m_all, pk, pk4,
-    a1, a1_x, a1_zo, a1_zi, a1_sum, a2, a2_x, a2_zo, a2_zi, a2_sum, r1, r2,
-    sh, sh_zo, sh_zi, sh_sum, sh_chunk, r3,
+    wo, w_half, kv, kvb, kv_zo, kv_zi, kv_sum, q_land, gm, gm_land, qx, gx, lse_x, delta_s, delta_x,
+    stat, stat_land, dq, ga, ga4, gq, gq4, gkv, gkv4, n_t, m_t, n_all, m_all, pk, pk4, pk_sum, pk_land,
+    o_send, o_land, gn_send, gn_land, a1, a1_zo, a1_zi, a1_sum, a2, a2_zo, a2_zi, a2_sum, r1, r2,
+    sh, sh_zi, sh_sum, sh_chunk, r3,
     sem, sem_kv, sem_a1, sem_a2, sem_sh, ring_recv, ring_send,
 ):
     spot = Spot(4)
     sems = Sems(sem)
     rows, width = tok.shape
-    pairs = width // PAIR
+    half = width // 2
+    group = half // PAIR
     shard = width // 4
-    loads = [pltpu.make_async_copy(wfull_ref.at[i], wbuf.at[i], sems.new()) for i in (3, 0, 1, 2)]
-    loads.insert(1, pltpu.make_async_copy(kv_ref, kv, sems.new()))
-    loads.append(pltpu.make_async_copy(dsh_ref, sh, sems.new()))
+    mine = pl.ds(pl.multiple_of(half * spot.x, half), half)
+    values = pl.ds(pl.multiple_of(width + half * spot.x, half), half)
+    ranks = kv.shape[0]
+    dsh_load = pltpu.make_async_copy(dsh_ref, sh, sems.new())
+    dsh_load.start()
+    loads = [
+        pltpu.make_async_copy(wfull_ref.at[3], wo, sems.new()),
+        pltpu.make_async_copy(kv_ref.at[:, :, mine], kv.at[:, :, pl.ds(0, half)], sems.new()),
+        pltpu.make_async_copy(kv_ref.at[:, :, values], kv.at[:, :, pl.ds(half, half)], sems.new()),
+        *[
+            pltpu.make_async_copy(wfull_ref.at[i, :, mine], w_half.at[i], sems.new())
+            for i in range(3)
+        ],
+    ]
+    done = other_ref.shape[0]
+    loads.append(pltpu.make_async_copy(other_ref, other_out.at[0, pl.ds(0, done)], sems.new()))
     for copy in loads:
         copy.start()
 
@@ -1080,21 +1113,54 @@
         return ref.at[pl.ds(pl.multiple_of(shard * w, 64), shard)]
 
     greet((spot.core, spot.across, spot.corner, spot.column, spot.inner), (spot.mid, spot.outer))
+    asides = []
+
+    def aside(src, dst):
+        asides.append(remote(src, dst, sems.new(), sems.new(), spot.column))
+        asides[-1].start()
+        return asides[-1]
+
+    query_x = aside(qc_ref.at[1 - spot.x], q_land)
     grad_second = grad_second_ref[...]
     ga[...] = grad_second.astype(BF)
     grads_w = Gather(spot, ga, lambda w: ga4.at[w], sems)
-    loads[-1].wait()
-    shared = Reduce(spot, sh, None, sh_zo, sh_zi, sem_sh, folded=True)
-    for number in (3, 2, 1):
-        shared.launch(number)
     mixed = mixed_ref[...]
+    dsh_load.wait()
+    shared = Reduce(spot, sh, None, None, sh_zi, sem_sh, folded=True, parts=2)
+    shared.relay(3)
+    shared.relay(2)
+
+    loads[0].wait()
+    grad_mixed = nt(ga[...], wo[...]).astype(BF)
+    for x in range(2):
+        gm[x] = grad_mixed[:, half * x : half * (x + 1)]
+    grads_x = aside(gm.at[1 - spot.x], gm_land)
+    product = grad_mixed.astype(F32) * mixed
+    for j in range(2 * group):
+        delta_s[j] = jnp.broadcast_to(
+            jnp.sum(stack_pair(product[:, PAIR * j : PAIR * (j + 1)]), axis=1, keepdims=True),
+            (2 * rows, PAIR),
+        )
+    lane = lax.broadcasted_iota(jnp.int32, (2 * rows, PAIR), 1)
+    table = jnp.zeros((2 * rows, PAIR), F32)
+    for i in range(group):
+        theirs = group * (1 - spot.x) + i
+        table = jnp.where(lane == i, lse_ref[theirs], table)
+        table = jnp.where(lane == group + i, delta_s[theirs], table)
+    stat[...] = table.T[0:8]
+    stat_x = aside(stat, stat_land)
+    for i in range(group):
+        qx[i] = stack_pair(qc_ref[spot.x, :, PAIR * i : PAIR * (i + 1)])
+        gx[i] = stack_pair(gm[spot.x, :, PAIR * i : PAIR * (i + 1)])
+        lse_x[i] = lse_ref[group * spot.x + i]
+        delta_x[i] = delta_s[group * spot.x + i]
     n_t[...] = normed_ref[...].T
     m_t[...] = mixed.astype(BF).T
 
     def columns(ref):
         return lambda w: ref.at[:, pl.ds(pl.multiple_of(rows * w, 128), rows)]
 
-    normed_w = Spread(spot, lambda w: block(n_t, w), columns(n_all), sems)
+    normed_w = Spread(spot, lambda w: block(n_t, w), columns(n_all.at[spot.x]), sems)
     mixed_w = Spread(spot, lambda w: block(m_t, w), columns(m_all), sems)
     across = []
 
@@ -1102,73 +1168,60 @@
         across.append(remote(src, dst, sems.new(), sems.new(), spot.across))
         across[-1].start()
 
-    done = other_ref.shape[0]
-    loads.append(pltpu.make_async_copy(other_ref, other_out.at[0, pl.ds(0, done)], sems.new()))
-    loads[-1].start()
     left = pl.ds(done, shard - done)
     send_across(give_ref.at[0, left], other_out.at[0, left])
-    send_across(give_ref.at[1], other_out.at[1])
-    loads[0].wait()
-    grad_mixed = nt(ga[...], wbuf[3]).astype(BF)
-    product = grad_mixed.astype(F32) * mixed
-    for j in range(pairs):
-        lanes = slice(PAIR * j, PAIR * (j + 1))
-        gst[j] = stack_pair(grad_mixed[:, lanes])
-        delta_s[j] = jnp.broadcast_to(
-            jnp.sum(stack_pair(product[:, lanes]), axis=1, keepdims=True), (2 * rows, PAIR)
+    dq[...] = jnp.zeros_like(dq)
+    query_x.wait_recv()
+    grads_x.wait_recv()
+    for i in range(group):
+        qx[group + i] = stack_pair(q_land[:, PAIR * i : PAIR * (i + 1)])
+        gx[group + i] = stack_pair(gm_land[:, PAIR * i : PAIR * (i + 1)])
+    stat_x.wait_recv()
+    table = jnp.concatenate([stat_land[...], jnp.zeros((PAIR - 8, 2 * rows), F32)], axis=0).T
+    for i in range(group):
+        lse_x[group + i] = jnp.broadcast_to(table[:, i : i + 1], (2 * rows, PAIR))
+        delta_x[group + i] = jnp.broadcast_to(
+            table[:, group + i : group + i + 1], (2 * rows, PAIR)
         )
-    dq[...] = jnp.zeros_like(dq)
     loads[1].wait()
-    q_block = qb[...]
+    loads[2].wait()
 
     def chunk(number):
         plane = spot.plane(number)
         k_block = kb[:, pl.ds(pl.multiple_of(2 * rows * plane, 2 * rows), 2 * rows)]
-        allowed = k_block <= q_block
-
-        def one_pair(j, carry):
-            lane = pl.multiple_of(PAIR * j, PAIR)
+        allowed = [k_block <= qb[spot.x], k_block <= qb[1 - spot.x]]
+
+        def one_pair(i, carry):
+            lane = pl.multiple_of(PAIR * i, PAIR)
             both = pl.ds(2 * plane, 2)
             key = kv[both, :, pl.ds(lane, PAIR)].reshape(2 * rows, PAIR)
-            value = kv[both, :, pl.ds(width + lane, PAIR)].reshape(2 * rows, PAIR)
-            query, grad = q_ref[j], gst[j]
-            scores = nt(query, key)
-            probs = jnp.where(allowed, jnp.exp(scores - lse_ref[j][:, 0:1]), 0.0)
-            inner = nt(grad, value) - delta_s[j][:, 0:1]
-            grad_scores = (probs * inner * HD**-0.5).astype(BF)
-            dq[j] += nn(grad_scores, key)
-            grad_key = tn(grad_scores, query) * HD**0.5
-            grad_value = tn(probs.astype(BF), grad)
-            kvb[both, :, pl.ds(lane, PAIR)] = grad_key.astype(BF).reshape(2, rows, PAIR)
-            kvb[both, :, pl.ds(width + lane, PAIR)] = grad_value.astype(BF).reshape(2, rows, PAIR)
+            value = kv[both, :, pl.ds(half + lane, PAIR)].reshape(2 * rows, PAIR)
+            grad_key = jnp.zeros((2 * rows, PAIR), F32)
+            grad_value = jnp.zeros((2 * rows, PAIR), F32)
+            for owner in range(2):
+                j = group * owner + i
+                query, grad = qx[j], gx[j]
+                raised = jnp.exp(nt(query, key) - lse_x[j][:, 0:1])
+                probs = jnp.where(allowed[owner], raised, 0.0)
+                inner = nt(grad, value) - delta_x[j][:, 0:1]
+                grad_scores = (probs * inner * HD**-0.5).astype(BF)
+                dq[j] += nn(grad_scores, key)
+                grad_key += tn(grad_scores, query)
+                grad_value += tn(probs.astype(BF), grad)
+            kvb[plane, :, pl.ds(lane, PAIR)] = (grad_key * HD**0.5).astype(BF)
+            kvb[plane, :, pl.ds(half + lane, PAIR)] = grad_value.astype(BF)
             return carry
 
-        lax.fori_loop(0, pairs, one_pair, 0)
-
-    kv_grad = Reduce(spot, kvb, kv_x, kv_zo, kv_zi, sem_kv, parts=2)
+        lax.fori_loop(0, group, one_pair, 0)
+
+    kv_grad = Reduce(spot, kvb, None, kv_zo, kv_zi, sem_kv, folded=True, parts=2)
     chunk(3)
-    kv_grad.side(3)
+    kv_grad.launch(3)
     chunk(2)
-    kv_grad.side(2)
-    shared.relay(3)
+    kv_grad.launch(2)
+    shared.relay(1)
     chunk(1)
-    kv_grad.side(1)
-    shared.relay(2)
-    kv_grad.meet(3)
-    chunk(0)
-    kv_grad.side(0)
-    cosine, sine = cosr[...], sinr[...]
-    gq[...] = turn(
-        jnp.concatenate([unstack_pair(dq[j]) for j in range(pairs)], axis=1), cosine, -sine
-    ).astype(BF)
-    query_w = Gather(spot, gq, lambda w: gq4.at[w], sems)
-    shared.relay(1)
-    kv_grad.meet(2)
-    kv_grad.relay(3)
-    grads_w.forward()
-    for part_w in (grads_w, normed_w, mixed_w):
-        part_w.finish()
-    out_grad = nn(m_all[...], ga4[...].reshape(4 * rows, width))
+    kv_grad.launch(1)
     shared.last(sh_sum)
     sh_chunk[...] = sh_sum[...].astype(BF)
     part = 2 * shard // 2
@@ -1182,29 +1235,71 @@
     shared_w = Spread(spot, piece, place, sems)
     rest = sh_chunk.shape[0] - 4 * part
     r3[spot.k, pl.ds(4 * part, rest)] = sh_chunk[pl.ds(4 * part, rest)]
-    kv_grad.meet(1)
-    kv_grad.relay(2)
-    kv_grad.relay(1)
-    query_w.forward()
-    query_w.finish()
-    query_grad = nn(n_all[...], gq4[...].reshape(4 * rows, width))
-    half = jnp.concatenate([out_grad, query_grad], axis=0).astype(BF)
-    a1[...] = half.reshape(a1.shape)
-    first = Reduce(spot, a1, a1_x, a1_zo, a1_zi, sem_a1)
-    for number in (3, 2, 1, 0):
-        first.side(number)
-    kv_grad.meet(0)
-    kv_grad.last(kv_sum)
-    gkv[:, 0:width] = turn(kv_sum[:, 0:width], cosine, -sine).astype(BF)
-    gkv[:, width : 2 * width] = kv_sum[:, width : 2 * width].astype(BF)
-    kv_w = Gather(spot, gkv, lambda w: gkv4.at[w], sems)
+    kv_grad.relay(3)
+    chunk(0)
+    cosine, sine = cosr[...].reshape(2 * rows, PAIR), sinr[...].reshape(2 * rows, PAIR)
+    for owner in range(2):
+        at = spot.x if owner == 0 else 1 - spot.x
+        parts = [unstack_pair(dq[group * owner + i]) for i in range(group)]
+        gq[at] = turn(jnp.concatenate(parts, axis=1), cosr[at], -sinr[at]).astype(BF)
+    query_w = Gather(spot, gq, lambda w: gq4.at[w], sems)
+    send_across(give_ref.at[1], other_out.at[1])
     shared_w.finish()
     ring3 = Ring(spot, r3, ring_recv.at[2], ring_send.at[2], parts=2)
     ring3.start()
-    for copy in loads[2:5]:
+    normed_w.finish()
+    normed_x = aside(n_all.at[spot.x], n_all.at[spot.x])
+    grads_w.forward()
+    mixed_w.finish()
+    grads_w.finish()
+    kv_grad.relay(2)
+    out_grad = nn(m_all[...], ga4[...].reshape(4 * rows, width)).astype(BF)
+    for x in range(2):
+        o_send[x] = out_grad[:, half * x : half * (x + 1)]
+    out_x = aside(o_send.at[1 - spot.x], o_land)
+    kv_grad.relay(1)
+    ring3.step(1)
+    ring3.step(2, only=1)
+    for copy in loads[3:6]:
         copy.wait()
-    grad_normed = nt(gq[...], wbuf[0]) + nt(gkv[:, 0:width], wbuf[1])
-    grad_normed = grad_normed + nt(gkv[:, width : 2 * width], wbuf[2])
+    flat = gq[...].reshape(2 * rows, half)
+    grad_normed = nt(flat, w_half[0])
+    query_w.forward()
+    query_w.finish()
+    normed_x.wait_recv()
+
+    def weight_grad(grads4):
+        total = nn(n_all[0], grads4[:, 0].reshape(4 * rows, grads4.shape[3]))
+        return total + nn(n_all[1], grads4[:, 1].reshape(4 * rows, grads4.shape[3]))
+
+    query_grad = weight_grad(gq4).astype(BF)
+    out_x.wait_recv()
+    out_half = (o_send[spot.x].astype(F32) + o_land[...].astype(F32)).astype(BF)
+    size = shard // 4
+    for plane in range(4):
+        at = slice(size * plane, size * (plane + 1))
+        a1[plane, :, 0:half] = out_half[at]
+        a1[plane, :, half:width] = query_grad[at]
+    first = Reduce(spot, a1, None, a1_zo, a1_zi, sem_a1, folded=True)
+    for number in (3, 2, 1):
+        first.launch(number)
+    kv_grad.last(kv_sum)
+    gkv[:, :, 0:half] = (
+        turn(kv_sum[:, 0:half], cosine, -sine).astype(BF).reshape(2, rows, half)
+    )
+    gkv[:, :, half:width] = kv_sum[:, half:width].astype(BF).reshape(2, rows, half)
+    kv_w = Gather(spot, gkv, lambda w: gkv4.at[w], sems)
+    flat = gkv[...].reshape(2 * rows, width)
+    grad_normed = grad_normed + nt(flat[:, 0:half], w_half[1]) + nt(flat[:, half:width], w_half[2])
+    gn_send[...] = grad_normed.astype(BF).reshape(2, rows, width)
+    normed_grad_x = aside(gn_send.at[1 - spot.x], gn_land)
+    ring3.step(3, only=1)
+    first.relay(3)
+    first.relay(2)
+    first.relay(1)
+    ring3.step(2, only=0)
+    normed_grad_x.wait_recv()
+    grad_normed = gn_send[spot.x].astype(F32) + gn_land[...].astype(F32)
     inputs = tok[...].astype(F32)
     scale = lax.rsqrt(jnp.mean(inputs * inputs, axis=-1, keepdims=True) + EPS)
     weighted = grad_normed * pack_ref[0:1]
@@ -1216,46 +1311,39 @@
     pk[...] = jnp.concatenate([gain_grad, pack_grad_ref[1:16]], axis=0).astype(BF)
     pack_w = Gather(spot, pk, lambda w: pk4.at[w], sems)
     send_across(give_ref.at[2], other_out.at[2])
-    for number in (3, 2, 1, 0):
-        first.meet(number)
-    first.relay(3)
-    first.relay(2)
-    kv_w.forward()
-    pack_w.forward()
-    kv_w.finish()
-    pack_w.finish()
-    grad_kv = gkv4[...].reshape(4 * rows, 2 * width)
-    both = nn(n_all[...], grad_kv)
-    both = jnp.concatenate([both[:, 0:width], both[:, width : 2 * width]], axis=0).astype(BF)
-    size = both.shape[0] // 8
-    extra = sum(pk4[w].astype(F32) for w in range(4)).astype(BF)
-    for r in range(8):
-        a2[r, 0:size] = both[size * r : size * (r + 1)]
-        a2[r, size : size + 16] = extra
-    second = Reduce(spot, a2, a2_x, a2_zo, a2_zi, sem_a2)
-    for number in (3, 2, 1, 0):
-        second.side(number)
-    first.relay(1)
-    ring3.step(1)
     first.last(a1_sum)
     r1[spot.k] = a1_sum[...].astype(BF)
     ring1 = Ring(spot, r1, ring_recv.at[0], ring_send.at[0])
     ring1.start()
-    ring3.step(2)
-    for number in (3, 2, 1, 0):
-        second.meet(number)
+    kv_w.forward()
+    pack_w.forward()
+    pack_w.finish()
+    pk_sum[...] = sum(pk4[w].astype(F32) for w in range(4)).astype(BF)
+    pack_x = aside(pk_sum, pk_land)
+    kv_w.finish()
+    both = weight_grad(gkv4).astype(BF)
+    pack_x.wait_recv()
+    extra = (pk_sum[...].astype(F32) + pk_land[...].astype(F32)).astype(BF)
+    for plane in range(4):
+        a2[plane, 0:size] = both[size * plane : size * (plane + 1)]
+        a2[plane, size : size + 16] = extra
+    second = Reduce(spot, a2, None, a2_zo, a2_zi, sem_a2, folded=True)
+    for number in (3, 2, 1):
+        second.launch(number)
+    ring3.step(3, only=0)
     ring1.step(1)
-    ring3.step(3)
+    ring1.step(2, only=1)
     second.relay(3)
     second.relay(2)
     second.relay(1)
-    ring1.step(2)
+    ring1.step(3, only=1)
+    ring1.step(2, only=0)
     second.last(a2_sum)
     r2[spot.k] = a2_sum[0:size].astype(BF)
     ring2 = Ring(spot, r2, ring_recv.at[1], ring_send.at[1])
     ring2.start()
     pack_out[...] = a2_sum[size : size + 16]
-    ring1.step(3)
+    ring1.step(3, only=0)
     for number in (1, 2, 3):
         ring2.step(number)
     saves = []
@@ -1266,6 +1354,7 @@
         saves[-1].start()
     for copy in across:
         copy.wait_recv()
+    for copy in across + asides:
         copy.wait_send()
     for part_w in (grads_w, normed_w, mixed_w, query_w, shared_w, kv_w, pack_w):
         part_w.drain()
@@ -1276,14 +1365,15 @@
 
 
 def run_backward(
-    grad_second, tok, pack, pack_grad, normed, mixed, q, lse, cosr, sinr, kb, qb, dsh, kv, wfull,
+    grad_second, tok, pack, pack_grad, normed, mixed, qc, lse, cosr, sinr, kb, qb, dsh, kv, wfull,
     give, other,
 ):
     rows, width = tok.shape
     pairs = width // PAIR
+    half = width // 2
     ranks = 8
     shard, hidden = width // 4, give.shape[2]
-    size = 2 * shard // ranks
+    size = shard // 4
     tall = dsh.shape[1]
     any_, vm = pl.BlockSpec(memory_space=pl.ANY), pl.BlockSpec(memory_space=VMEM)
     shape = jax.ShapeDtypeStruct
@@ -1308,34 +1398,46 @@
         in_specs=[vm] * 12 + [any_] * 5,
         out_specs=(vm, vm, any_, any_, any_, any_),
         scratch_shapes=[
-            low(4, width, width),
-            low(ranks, rows, 2 * width),
-            low(ranks, rows, 2 * width),
-            low(4, rows, 2 * width),
-            low(4, rows, 2 * width),
-            low(4, rows, 2 * width),
-            full(rows, 2 * width),
+            low(width, width),
+            low(3, width, half),
+            low(ranks, rows, width),
+            low(4, 2 * rows, width),
+            low(4, 2 * rows, width),
+            low(4, 2 * rows, width),
+            full(2 * rows, width),
+            low(rows, half),
+            low(2, rows, half),
+            low(rows, half),
+            low(pairs, 2 * rows, PAIR),
             low(pairs, 2 * rows, PAIR),
             full(pairs, 2 * rows, PAIR),
             full(pairs, 2 * rows, PAIR),
+            full(pairs, 2 * rows, PAIR),
+            full(8, 2 * rows),
+            full(8, 2 * rows),
+            full(pairs, 2 * rows, PAIR),
             low(rows, width),
             low(4, rows, width),
-            low(rows, width),
-            low(4, rows, width),
-            low(rows, 2 * width),
-            low(4, rows, 2 * width),
+            low(2, rows, half),
+            low(4, 2, rows, half),
+            low(2, rows, width),
+            low(4, 2, rows, width),
             low(width, rows),
             low(width, rows),
-            low(shard, 4 * rows),
+            low(2, shard, 4 * rows),
             low(shard, 4 * rows),
             low(16, width),
             low(4, 16, width),
-            low(ranks, size, width),
+            low(16, width),
+            low(16, width),
+            low(2, shard, half),
+            low(shard, half),
+            low(2, rows, width),
+            low(rows, width),
             low(4, size, width),
             low(4, size, width),
             low(4, size, width),
             full(size, width),
-            low(ranks, size + 16, width),
             low(4, size + 16, width),
             low(4, size + 16, width),
             low(4, size + 16, width),
@@ -1344,11 +1446,10 @@
             low(ranks, size, width),
             low(4, tall, 128),
             low(4, tall, 128),
-            low(4, tall, 128),
             full(tall, 128),
             low(tall, 128),
             low(ranks, tall, 128),
-            dma((112,)),
+            dma((128,)),
             dma((5, 8)),
             dma((5, 8)),
             dma((5, 8)),
@@ -1360,7 +1461,7 @@
             collective_id=3, has_side_effects=True, vmem_limit_bytes=VMEM_BYTES
         ),
     )(
-        grad_second, tok, pack, pack_grad, normed, mixed, q, lse, cosr, sinr, kb, qb, dsh, kv,
+        grad_second, tok, pack, pack_grad, normed, mixed, qc, lse, cosr, sinr, kb, qb, dsh, kv,
         wfull, give, other,
     )
 
@@ -1373,10 +1474,11 @@
     i = pl.program_id(0)
     result_out[...] = result[...]
     grad_input_out[...] = grad_input[...]
-    output[...] = att1[0, 0].astype(F32)
-    query[...] = att1[1, 0].astype(F32)
-    key[...] = att2[0, 0].astype(F32)
-    value[...] = att2[1, 0].astype(F32)
+    half = query.shape[1] // 2
+    for x in range(2):
+        lanes = slice(half * x, half * (x + 1))
+        for ref, src, low in ((output, att1, 0), (query, att1, 1), (key, att2, 0), (value, att2, 1)):
+            ref[:, lanes] = src[0, x, :, half * low : half * (low + 1)].astype(F32)
     for a, ref in enumerate((eg, eu, ed)):
         ref[...] = keep[a].astype(F32) + other[a].astype(F32)
     size = gate.shape[0]
@@ -1402,7 +1504,7 @@
         mine = pltpu.roll(pack[...], back, 1)[:, 0:256]
         gain_one[...] = mine[0:1, 0:shard]
         gain_two[...] = mine[1:2, 0:shard]
-        router[...] = mine.T[0:shard, 2 : 2 + router.shape[1]]
+        router[...] = mine[2 : 2 + router.shape[0], 0:shard]
 
 
 def run_unpack(result, grad_input, pack, att1, att2, sh, keep, other, experts):
@@ -1411,14 +1513,14 @@
     steps = 4
     shape = jax.ShapeDtypeStruct
     size = shard // steps
-    att1 = att1.reshape(2, 4, size, width)
-    att2 = att2.reshape(2, 4, size, width)
+    att1 = att1.reshape(4, 2, size, width)
+    att2 = att2.reshape(4, 2, size, width)
     shared_hidden = sh.shape[0] * (sh.shape[1] - width) * 128 // width
     shared = 4 * shared_hidden
     by_rows = lambda r, c: pl.BlockSpec((r, c), lambda i: (i, 0))
     whole = lambda *dims: pl.BlockSpec(dims, lambda i: (0,) * len(dims))
     stack = lambda n, r, c: pl.BlockSpec((n, r, c), lambda i: (0, i, 0))
-    att = pl.BlockSpec((2, 1, size, width), lambda i: (0, i, 0, 0))
+    att = pl.BlockSpec((1, 2, size, width), lambda i: (i, 0, 0, 0))
     return pl.pallas_call(
         unpack_kernel,
         grid=(steps,),
@@ -1427,7 +1529,7 @@
             shape((rows, width), F32),
             shape((1, shard), F32),
             shape((1, shard), F32),
-            shape((shard, experts), F32),
+            shape((experts, shard), F32),
             *[shape((shard, width), F32)] * 4,
             *[shape((shard, shared), F32)] * 2,
             shape((shared_hidden, width), F32),
@@ -1448,7 +1550,7 @@
             by_rows(rows // steps, width),
             whole(1, shard),
             whole(1, shard),
-            whole(shard, experts),
+            whole(experts, shard),
             *[by_rows(size, width)] * 4,
             *[by_rows(size, shared)] * 2,
             by_rows(shared_hidden // steps, width),
@@ -1976,13 +2078,14 @@
     block_deal,
 ):
     half_size = HD // 2
-    frequency = 10000.0 ** (-jnp.arange(half_size, dtype=F32) / half_size)
+    frequency = 10000.0 ** (-np.arange(half_size) / half_size)
+    frequency = jnp.asarray(np.tile(frequency, 4)[None].astype(np.float32))
     (
         cosr, sinr, kb, qb, q_st, mixed, lse, normed, pack_all, result, grad_second, pack_grad, dsh,
         kv_all, wfull, keep, give, other,
     ) = run_forward(
-        tokens[0], gain_attention[None], gain_mixer[None], router_weight,
-        jnp.concatenate([frequency] * 4)[None], block_deal, cotangent[0], routes[0], slot_order[0],
+        tokens[0], jnp.stack([gain_attention, gain_mixer]), router_weight.T, frequency, block_deal,
+        cotangent[0], routes[0].T, slot_order[0],
         shared_down, query_weight, key_weight, value_weight, output_weight, shared_gate, shared_up,
         expert_gate, expert_up, expert_down,
     )
@@ -1998,7 +2101,7 @@
     )
     return (
         result[None], grad_input[None], gain_one.reshape(-1), query, key, value, output,
-        gain_two.reshape(-1), router, gate, up, down, eg, eu, ed,
+        gain_two.reshape(-1), router.T, gate, up, down, eg, eu, ed,
     )
 
 

time: 271 us -> 243 us (0.90)
  Pallas kernels: 263 us -> 240 us
  local copies, waits for them, and re-layouts: 6.83 us -> 1.32 us
    pallas_call x1, Pallas kernels: 142 us -> 130 us  [run_forward(): pl.pallas_call(forward_kernel, out_shape=(shape((2, rows, PAIR), F32), sh...]
    pallas_call x1, Pallas kernels: 112 us -> 101 us  [run_backward(): pl.pallas_call(backward_kernel, out_shape=(shape((rows, width), F32), sha...]
    unnamed x3 -> x0, local copies, waits for them, and re-layouts: 4.4 us -> none
where the time goes in v6:
time: 243 us
  Pallas kernels  240 us (99%)
    pallas_call x1, Pallas kernels, run_forward(): pl.pallas_call(forward_kernel, out_shape=(shape((2, rows, PAIR), F32), sh...  130 us
    pallas_call x1, Pallas kernels, run_backward(): pl.pallas_call(backward_kernel, out_shape=(shape((rows, width), F32), sha...  101 us
    pallas_call x1, Pallas kernels, run_unpack(): pl.pallas_call(unpack_kernel, grid=(steps,), out_shape=(shape((rows, widt...  8.81 us

profile of v6, /device:TPU:0, one launch (start us, length us, event | category | flops | bytes accessed | tf_op | source)
XLA Modules:
  0.0 242.9 jit_solution(11463604515374670554)
XLA Ops:
  0.6 0.7 stack.9
  1.3 0.7 stack.10
  2.0 0.6 pad_maximum_fusion.gains
  2.5 130.3 %shard_map.298 = (f32[2,128,128]{2,1,0:T(8,128)}, f32[2,128,128]{2,1,0:T(8,128)}, s32[1,1024]{1,0:T(1,128)}, s32[2,256,1]{2,1,0:T(8,128)}, bf16[2,128,384]{2,1,0...) custom-call(bf16[128,768]{1,0:T(8,128)(2,1)} %bitcast.14, ...), custom_call_target="tpu_custom_call" | custom-call | tf_op jit(solution)/shard_map/pallas_call | solution.py:1001
  132.8 101.1 %shard_map.299 = (f32[128,768]{1,0:T(8,128)}, f32[16,768]{1,0:T(8,128)}, bf16[8,48,768]{2,1,0:T(8,128)(2,1)}, bf16[8,48,768]{2,1,0:T(8,128)(2,1)}, bf16[8,1152,1...) custom-call(f32[128,768]{1,0:T(8,128)} %get-tuple-element.55.grad_second_ref, bf16[128,768]{1,0:T(8,128)(2,1)} %bitcast.15, ...), custom_call_target="tpu_custom_call" | custom-call | tf_op jit(solution)/shard_map/pallas_call | solution.py:1388
  233.9 8.8 %shard_map.300 = (bf16[128,768]{1,0:T(8,128)(2,1)}, f32[128,768]{1,0:T(8,128)}, f32[1,192]{1,0:T(1,128)}, f32[1,192]{1,0:T(1,128)}, f32[8,192]{1,0:T(8,128)}, /*...) custom-call(bf16[128,768]{1,0:T(8,128)(2,1)} %get-tuple-element.54.r, ...), custom_call_target="tpu_custom_call" | custom-call | tf_op jit(solution)/shard_map/pallas_call | solution.py:1524

commit v7 on v6

--- a/solution.py
+++ b/solution.py
@@ -21,7 +21,9 @@
 BF = jnp.bfloat16
 F32 = jnp.float32
 PAIR = 2 * HD
-VMEM_BYTES = 63 * 2**20
+VMEM_BYTES = 127 * 2**19
+SEMS_FORWARD = 148
+SEMS_BACKWARD = 73
 
 
 class Spot:
@@ -290,10 +292,10 @@
 
 
 class Ring:
-    def __init__(self, spot, blocks, recv, send, parts=1):
+    def __init__(self, spot, blocks, recv, send, parts=1, first=(0, 0)):
         self.spot, self.blocks, self.recv, self.send, self.parts = spot, blocks, recv, send, parts
         self.ranks = blocks.shape[0]
-        self.used = 0
+        self.first, self.used = first[0], first[1]
         self.sent, self.sent_mid, self.sent_end = [], [], []
 
     def piece(self, slot, part):
@@ -306,7 +308,7 @@
             self.piece(slot, part),
             self.piece(slot, part),
             self.send.at[self.used - 1],
-            self.recv.at[slot + self.ranks * part],
+            self.recv.at[self.first + slot + self.ranks * part],
             to,
         )
 
@@ -315,7 +317,7 @@
             self.piece(slot, part),
             self.piece(slot, part),
             self.send.at[0],
-            self.recv.at[slot + self.ranks * part],
+            self.recv.at[self.first + slot + self.ranks * part],
             self.spot.column,
         ).wait_recv()
 
@@ -385,9 +387,11 @@
 class Reduce:
     def __init__(self, spot, part, sides, zo, zi, sems, folded=False, parts=1):
         self.spot, self.part, self.sides, self.zo, self.zi = spot, part, sides, zo, zi
-        self.x_send, self.x_recv, self.z_send, self.zo_recv, self.zi_recv = (
-            sems.at[i] for i in range(5)
-        )
+        self.z_send, self.zo_recv = sems.at[0], sems.at[1]
+        if folded:
+            self.zi_recv = sems.at[2]
+        else:
+            self.x_send, self.x_recv = sems.at[2], sems.at[3]
         self.folded, self.parts = folded, parts
         self.rows = part.shape[1] // parts
         self.sent, self.sent_end, self.sent_mid = [], [], []
@@ -421,12 +425,12 @@
     def add(self, ref, land):
         ref[...] = (ref[...].astype(F32) + land[...].astype(F32)).astype(BF)
 
-    def meet(self, number):
+    def meet(self, number, launch):
         plane = self.spot.plane(number)
         for h in range(self.parts):
             self.wait(self.sides, self.x_recv, plane, h)
             self.add(self.own(plane, h), self.cut(self.sides, plane, h))
-            if number > 0 and self.zo is not None:
+            if launch:
                 self.launch_part(number, h)
 
     def launch(self, number):
@@ -459,7 +463,7 @@
                 self.wait(self.zo, self.zo_recv, plane, h)
                 self.add(self.own(plane, h), self.cut(self.zo, plane, h))
 
-    def relay(self, number):
+    def relay(self, number, settled=False):
         plane = self.spot.plane(number)
         land, recv = (self.zi, self.zi_recv) if number == 1 else (self.zo, self.zo_recv)
         copies = []
@@ -478,7 +482,7 @@
         @pl.when(self.spot.mid == 1)
         def _():
             for h, copy in enumerate(copies):
-                if land is not None:
+                if not settled:
                     self.wait(land, recv, plane, h)
                     self.add(self.own(plane, h), self.cut(land, plane, h))
                 copy.start()
@@ -492,9 +496,6 @@
             rows = pl.ds(self.rows * h, self.rows)
             total = self.own(plane, h)[...].astype(F32)
             result[rows] = total + self.cut(self.zi, plane, h)[...].astype(F32)
-
-        if self.zo is None:
-            return
 
         @pl.when(self.spot.mid == 1)
         def _():
@@ -628,10 +629,10 @@
 def forward_kernel(
     tok, gains, router_ref, freq, deal, cot, routes, order, sd,
     wq, wk, wv, wo, sg, su, eg, eu, ed,
-    cosr, sinr, kb, qb, q_out, mixed_out, lse_out, normed_out, pack_out, result_out, grad_second_out, pack_grad_out,
+    cosr, sinr, kb, qb, qx, gx, stats_out, normed_out, mixed_out, pack_out, result_out, grad_second_out, pack_grad_out,
     dsh_out, kv_out, wfull_out, keep_out, give_out, other_out,
-    wbuf, kv, q_s, pack, packs, top, low, acc, sg_all, su_all, wg, wu, wd, mix, m4, cot4,
-    sh_send, sh_recv, gm_send, gm_recv, xs, xr, gs, gr, os, orr, bs, br,
+    wbuf, kv, q_s, qc, q_land, gm, gm_land, stat, stat_land, mixed, pack, packs, top, low, acc, sg_all, su_all, wg, wu, wd, mix, m4, cot4,
+    sh_send, sh_recv, gm_send, gm_recv, xs, xr, gs, gr, orr, br,
     x_s, g_s, sum_s, gate_s, up_s, hid_s, dgate_s, dup_s, dsh, dsh_x, dsh_z, slot_s, pair_s, cb,
     sem, kv_recv, kv_send, a2a_send, a2a_recv, sem_sh,
 ):
@@ -693,7 +694,7 @@
     )
     pack_out[...] = pack_all
     normed = (scaled * pack_all[0:1]).astype(BF)
-    normed_out[...] = normed
+    normed_out[...] = normed.T
     cosine, sine = cosr[spot.x], sinr[spot.x]
     to_slots, to_pairs = slot_maps(routes[...], order[...], slots, ranks)
     route = [diagonal(routes[j : j + 1], 1) for j in range(2)]
@@ -716,7 +717,7 @@
     for j in range(pairs):
         q_s[j] = stack_pair(query[:, PAIR * j : PAIR * (j + 1)])
     for x in range(2):
-        q_out[x] = query[:, width // 2 * x : width // 2 * (x + 1)]
+        qc[x] = query[:, width // 2 * x : width // 2 * (x + 1)]
     top[...] = jnp.full_like(top, MASKED)
     low[...] = jnp.zeros_like(low)
     acc[...] = jnp.zeros_like(acc)
@@ -740,7 +741,7 @@
             acc[j] = acc[j] * factor + nn(raised.astype(BF), value)
             return carry
 
-        lax.fori_loop(0, pairs, one_pair, 0)
+        lax.fori_loop(0, pairs, one_pair, 0, unroll=3)
 
     ring.step(1)
     ring.step(2, only=1)
@@ -763,12 +764,19 @@
     saves = [pltpu.make_async_copy(kv, kv_out, sems.new())]
     saves[0].start()
     for j in range(pairs):
-        mixed_out[:, PAIR * j : PAIR * (j + 1)] = unstack_pair(acc[j] / low[j])
-        lse_out[j] = top[j] + jnp.log(low[j])
+        mixed[:, PAIR * j : PAIR * (j + 1)] = unstack_pair(acc[j] / low[j])
+        top[j] = top[j] + jnp.log(low[j])
+    asides = []
+
+    def aside(src, dst):
+        asides.append(remote(src, dst, sems.new(), sems.new(), spot.column))
+        asides[-1].start()
+        return asides[-1]
+
     out_w.finish()
     saves.append(pltpu.make_async_copy(wbuf, wfull_out, sems.new()))
     saves[1].start()
-    second = inputs + nn(mixed_out[...].astype(BF), wbuf[3])
+    second = inputs + nn(mixed[...].astype(BF), wbuf[3])
     scale = lax.rsqrt(jnp.mean(second * second, axis=-1, keepdims=True) + EPS)
     mixer = (second * scale * pack_all[1:2]).astype(BF)
     mix[...] = mixer
@@ -804,6 +812,8 @@
     act, slope = swish(gate_part)
     shared_hidden = (act * up_part).astype(BF)
     sh_send[...] = nn(shared_hidden, sd[...]).astype(BF).reshape(4, rows, width)
+    mixed_out[...] = mixed[...].astype(BF).T
+    query_x = aside(qc.at[1 - spot.x], q_land)
     shared_out = Merge(spot, sh_send, sh_recv, sems)
     hid_grad = nt(grad_all, sd[...])
     grad_gate = (hid_grad * up_part * slope).astype(BF)
@@ -855,10 +865,11 @@
     lax.fori_loop(0, hidden // block, up_step, 0)
     down_w.forward()
     down_w.finish()
-    shared_grad.meet(3)
+    shared_grad.meet(3, True)
     sum_s[...] = nt(hid_s[...], wd[...])
-    fold_rows(sum_s[...], os)
-    outs = Exchange(spot, os, orr, a2a_send.at[2], a2a_recv.at[2])
+    rows_out.drain()
+    fold_rows(sum_s[...], xs)
+    outs = Exchange(spot, xs, orr, a2a_send.at[2], a2a_recv.at[2])
     outs.start()
     grads_out.finish()
     g_s[...] = unfold_rows(gr, slots)
@@ -872,8 +883,9 @@
 
     lax.fori_loop(0, hidden // block, down_step, 0)
     sum_s[...] = nt(dgate_s[...], wg[...]) + nt(dup_s[...], wu[...])
-    fold_rows(sum_s[...], bs)
-    backs = Exchange(spot, bs, br, a2a_send.at[3], a2a_recv.at[3])
+    grads_out.drain()
+    fold_rows(sum_s[...], gs)
+    backs = Exchange(spot, gs, br, a2a_send.at[3], a2a_recv.at[3])
     backs.start()
 
     for part_w in (gate_w, up_w, down_w):
@@ -927,15 +939,15 @@
         for copy in saves[-2:]:
             copy.start()
 
-    shared_grad.meet(2)
+    shared_grad.meet(2, True)
     grads_of(0)
     grads_of(1)
     add_mate(0)
-    shared_grad.meet(1)
+    shared_grad.meet(1, False)
     grads_of(2)
     add_mate(1)
     add_mate(2)
-    shared_grad.meet(0)
+    shared_grad.meet(0, False)
     total = second + shared_out.finish()
     grad_mixer = shared_back.finish()
     outs.finish()
@@ -954,12 +966,48 @@
     grad_mixer = grad_mixer + nn(pair_s[:rows] + pair_s[rows:], unfold_rows(br, slots))
     weighted = grad_mixer * pack_all[1:2]
     mean = jnp.mean(weighted * second, axis=-1, keepdims=True)
-    grad_second_out[...] = grad + scale * weighted - second * (scale * scale * scale * mean)
+    grad_second = grad + scale * weighted - second * (scale * scale * scale * mean)
+    grad_second_out[...] = grad_second
+
+    grad_mixed = nt(grad_second.astype(BF), wbuf[3]).astype(BF)
+    half = width // 2
+    group = half // PAIR
+    for x in range(2):
+        gm[x] = grad_mixed[:, half * x : half * (x + 1)]
+    grads_x = aside(gm.at[1 - spot.x], gm_land)
+    product = grad_mixed.astype(F32) * mixed[...]
+    lane = lax.broadcasted_iota(jnp.int32, (2 * rows, PAIR), 1)
+    mine = jnp.zeros((2 * rows, PAIR), F32)
+    theirs = jnp.zeros((2 * rows, PAIR), F32)
+    for i in range(group):
+        delta = [
+            jnp.sum(stack_pair(product[:, PAIR * j : PAIR * (j + 1)]), axis=1, keepdims=True)
+            for j in (i, group + i)
+        ]
+        swap = spot.x == 1
+        mine = jnp.where(lane == i, top[group * spot.x + i], mine)
+        theirs = jnp.where(lane == i, top[group * (1 - spot.x) + i], theirs)
+        mine = jnp.where(lane == group + i, jnp.where(swap, delta[1], delta[0]), mine)
+        theirs = jnp.where(lane == group + i, jnp.where(swap, delta[0], delta[1]), theirs)
+        qx[i] = stack_pair(qc[spot.x, :, PAIR * i : PAIR * (i + 1)])
+        gx[i] = stack_pair(gm[spot.x, :, PAIR * i : PAIR * (i + 1)])
+    stat[...] = theirs.T[0:8]
+    stat_x = aside(stat, stat_land)
+    stats_out[0] = mine
     gain_grad = jnp.sum(grad_mixer * second * scale, axis=0, keepdims=True)
     pack_grad_out[...] = jnp.concatenate(
         [jnp.zeros_like(gain_grad), gain_grad, router_grad[:14]], axis=0
     )
-    for number in (3, 2, 0):
+    query_x.wait_recv()
+    grads_x.wait_recv()
+    for i in range(group):
+        qx[group + i] = stack_pair(q_land[:, PAIR * i : PAIR * (i + 1)])
+        gx[group + i] = stack_pair(gm_land[:, PAIR * i : PAIR * (i + 1)])
+    stat_x.wait_recv()
+    stats_out[1] = jnp.concatenate(
+        [stat_land[...], jnp.zeros((PAIR - 8, 2 * rows), F32)], axis=0
+    ).T
+    for number in (3, 2):
         shared_grad.absorb(number)
     for plane in range(4):
         dsh_out[plane] = dsh[2 * plane + spot.x]
@@ -967,9 +1015,9 @@
         copy.wait_recv()
     for part_w in (params, key_w, value_w, query_w, out_w, sg_w, su_w, cot_w, ring, mixers):
         part_w.drain()
-    for part_w in (rows_out, grads_out, outs, backs, shared_out, shared_back, shared_grad):
+    for part_w in (outs, backs, shared_out, shared_back, shared_grad):
         part_w.drain()
-    for copy in swaps + across:
+    for copy in swaps + across + asides:
         copy.wait_send()
     for copy in saves:
         copy.wait()
@@ -1005,10 +1053,11 @@
             shape((2, rows, PAIR), F32),
             shape((1, ranks * rows), jnp.int32),
             shape((2, 2 * rows, 1), jnp.int32),
-            shape((2, rows, width // 2), BF),
-            shape((rows, width), F32),
-            shape((pairs, 2 * rows, PAIR), F32),
-            shape((rows, width), BF),
+            shape((pairs, 2 * rows, PAIR), BF),
+            shape((pairs, 2 * rows, PAIR), BF),
+            shape((2, 2 * rows, PAIR), F32),
+            shape((width, rows), BF),
+            shape((width, rows), BF),
             shape((16, width), F32),
             shape((rows, width), BF),
             shape((rows, width), F32),
@@ -1021,11 +1070,18 @@
             shape((2 * shard // 3, hidden), BF),
         ),
         in_specs=[vm] * 4 + [pl.BlockSpec(memory_space=pltpu.SMEM)] + [vm] * 4 + [any_] * 9,
-        out_specs=tuple([vm] * 13 + [any_] * 5),
+        out_specs=tuple([vm] * 14 + [any_] * 5),
         scratch_shapes=[
             low(4, width, width),
             low(ranks, rows, 2 * width),
             low(pairs, 2 * rows, PAIR),
+            low(2, rows, width // 2),
+            low(rows, width // 2),
+            low(2, rows, width // 2),
+            low(rows, width // 2),
+            full(8, 2 * rows),
+            full(8, 2 * rows),
+            full(rows, width),
             low(16, width),
             low(4, 16, width),
             full(pairs, 2 * rows, PAIR),
@@ -1043,7 +1099,7 @@
             low(3, rows, width),
             low(4, rows, width),
             low(3, rows, width),
-            *[folded] * 8,
+            *[folded] * 6,
             low(total, width),
             low(total, width),
             full(total, width),
@@ -1058,12 +1114,12 @@
             low(total, 2 * rows),
             low(2 * rows, total),
             low(3, 2, shard, hidden),
-            dma((144,)),
+            dma((SEMS_FORWARD,)),
             dma((2 * ranks,)),
-            dma((32,)),
+            dma((22,)),
             dma((4, ranks)),
             dma((4, ranks)),
-            dma((5, 8)),
+            dma((4, 4)),
         ],
         compiler_params=pltpu.CompilerParams(
             collective_id=1, has_side_effects=True, vmem_limit_bytes=VMEM_BYTES
@@ -1075,13 +1131,12 @@
 
 
 def backward_kernel(
-    grad_second_ref, tok, pack_ref, pack_grad_ref, normed_ref, mixed_ref, qc_ref, lse_ref,
+    grad_second_ref, tok, pack_ref, pack_grad_ref, n_t, m_t, qx, gx, stats,
     cosr, sinr, kb, qb, dsh_ref, kv_ref, wfull_ref, give_ref, other_ref,
     grad_input_out, pack_out, att1_out, att2_out, sh_out, other_out,
-    wo, w_half, kv, kvb, kv_zo, kv_zi, kv_sum, q_land, gm, gm_land, qx, gx, lse_x, delta_s, delta_x,
-    stat, stat_land, dq, ga, ga4, gq, gq4, gkv, gkv4, n_t, m_t, n_all, m_all, pk, pk4, pk_sum, pk_land,
+    w_half, kv, kvb, kv_zo, kv_zi, kv_sum, dq, ga, ga4, gq, gq4, gkv, gkv4, n_all, m_all, pk, pk4,
     o_send, o_land, gn_send, gn_land, a1, a1_zo, a1_zi, a1_sum, a2, a2_zo, a2_zi, a2_sum, r1, r2,
-    sh, sh_zi, sh_sum, sh_chunk, r3,
+    sh, sh_zo, sh_zi, sh_sum, sh_chunk, r3,
     sem, sem_kv, sem_a1, sem_a2, sem_sh, ring_recv, ring_send,
 ):
     spot = Spot(4)
@@ -1096,7 +1151,6 @@
     dsh_load = pltpu.make_async_copy(dsh_ref, sh, sems.new())
     dsh_load.start()
     loads = [
-        pltpu.make_async_copy(wfull_ref.at[3], wo, sems.new()),
         pltpu.make_async_copy(kv_ref.at[:, :, mine], kv.at[:, :, pl.ds(0, half)], sems.new()),
         pltpu.make_async_copy(kv_ref.at[:, :, values], kv.at[:, :, pl.ds(half, half)], sems.new()),
         *[
@@ -1120,42 +1174,14 @@
         asides[-1].start()
         return asides[-1]
 
-    query_x = aside(qc_ref.at[1 - spot.x], q_land)
     grad_second = grad_second_ref[...]
     ga[...] = grad_second.astype(BF)
     grads_w = Gather(spot, ga, lambda w: ga4.at[w], sems)
-    mixed = mixed_ref[...]
     dsh_load.wait()
-    shared = Reduce(spot, sh, None, None, sh_zi, sem_sh, folded=True, parts=2)
-    shared.relay(3)
-    shared.relay(2)
-
-    loads[0].wait()
-    grad_mixed = nt(ga[...], wo[...]).astype(BF)
-    for x in range(2):
-        gm[x] = grad_mixed[:, half * x : half * (x + 1)]
-    grads_x = aside(gm.at[1 - spot.x], gm_land)
-    product = grad_mixed.astype(F32) * mixed
-    for j in range(2 * group):
-        delta_s[j] = jnp.broadcast_to(
-            jnp.sum(stack_pair(product[:, PAIR * j : PAIR * (j + 1)]), axis=1, keepdims=True),
-            (2 * rows, PAIR),
-        )
-    lane = lax.broadcasted_iota(jnp.int32, (2 * rows, PAIR), 1)
-    table = jnp.zeros((2 * rows, PAIR), F32)
-    for i in range(group):
-        theirs = group * (1 - spot.x) + i
-        table = jnp.where(lane == i, lse_ref[theirs], table)
-        table = jnp.where(lane == group + i, delta_s[theirs], table)
-    stat[...] = table.T[0:8]
-    stat_x = aside(stat, stat_land)
-    for i in range(group):
-        qx[i] = stack_pair(qc_ref[spot.x, :, PAIR * i : PAIR * (i + 1)])
-        gx[i] = stack_pair(gm[spot.x, :, PAIR * i : PAIR * (i + 1)])
-        lse_x[i] = lse_ref[group * spot.x + i]
-        delta_x[i] = delta_s[group * spot.x + i]
-    n_t[...] = normed_ref[...].T
-    m_t[...] = mixed.astype(BF).T
+    shared = Reduce(spot, sh, None, sh_zo, sh_zi, sem_sh, folded=True, parts=2)
+    shared.launch(1)
+    shared.relay(3, settled=True)
+    shared.relay(2, settled=True)
 
     def columns(ref):
         return lambda w: ref.at[:, pl.ds(pl.multiple_of(rows * w, 128), rows)]
@@ -1171,28 +1197,16 @@
     left = pl.ds(done, shard - done)
     send_across(give_ref.at[0, left], other_out.at[0, left])
     dq[...] = jnp.zeros_like(dq)
-    query_x.wait_recv()
-    grads_x.wait_recv()
-    for i in range(group):
-        qx[group + i] = stack_pair(q_land[:, PAIR * i : PAIR * (i + 1)])
-        gx[group + i] = stack_pair(gm_land[:, PAIR * i : PAIR * (i + 1)])
-    stat_x.wait_recv()
-    table = jnp.concatenate([stat_land[...], jnp.zeros((PAIR - 8, 2 * rows), F32)], axis=0).T
-    for i in range(group):
-        lse_x[group + i] = jnp.broadcast_to(table[:, i : i + 1], (2 * rows, PAIR))
-        delta_x[group + i] = jnp.broadcast_to(
-            table[:, group + i : group + i + 1], (2 * rows, PAIR)
-        )
+    loads[0].wait()
     loads[1].wait()
-    loads[2].wait()
 
     def chunk(number):
         plane = spot.plane(number)
         k_block = kb[:, pl.ds(pl.multiple_of(2 * rows * plane, 2 * rows), 2 * rows)]
         allowed = [k_block <= qb[spot.x], k_block <= qb[1 - spot.x]]
 
-        def one_pair(i, carry):
-            lane = pl.multiple_of(PAIR * i, PAIR)
+        for i in range(group):
+            lane = PAIR * i
             both = pl.ds(2 * plane, 2)
             key = kv[both, :, pl.ds(lane, PAIR)].reshape(2 * rows, PAIR)
             value = kv[both, :, pl.ds(half + lane, PAIR)].reshape(2 * rows, PAIR)
@@ -1200,19 +1214,17 @@
             grad_value = jnp.zeros((2 * rows, PAIR), F32)
             for owner in range(2):
                 j = group * owner + i
+                stat = stats[owner]
                 query, grad = qx[j], gx[j]
-                raised = jnp.exp(nt(query, key) - lse_x[j][:, 0:1])
+                raised = jnp.exp(nt(query, key) - stat[:, i : i + 1])
                 probs = jnp.where(allowed[owner], raised, 0.0)
-                inner = nt(grad, value) - delta_x[j][:, 0:1]
+                inner = nt(grad, value) - stat[:, group + i : group + i + 1]
                 grad_scores = (probs * inner * HD**-0.5).astype(BF)
                 dq[j] += nn(grad_scores, key)
                 grad_key += tn(grad_scores, query)
                 grad_value += tn(probs.astype(BF), grad)
             kvb[plane, :, pl.ds(lane, PAIR)] = (grad_key * HD**0.5).astype(BF)
             kvb[plane, :, pl.ds(half + lane, PAIR)] = grad_value.astype(BF)
-            return carry
-
-        lax.fori_loop(0, group, one_pair, 0)
 
     kv_grad = Reduce(spot, kvb, None, kv_zo, kv_zi, sem_kv, folded=True, parts=2)
     chunk(3)
@@ -1222,20 +1234,6 @@
     shared.relay(1)
     chunk(1)
     kv_grad.launch(1)
-    shared.last(sh_sum)
-    sh_chunk[...] = sh_sum[...].astype(BF)
-    part = 2 * shard // 2
-
-    def piece(w):
-        return sh_chunk.at[pl.ds(pl.multiple_of(part * w, 64), part)]
-
-    def place(w):
-        return r3.at[spot.k, pl.ds(pl.multiple_of(part * w, 64), part)]
-
-    shared_w = Spread(spot, piece, place, sems)
-    rest = sh_chunk.shape[0] - 4 * part
-    r3[spot.k, pl.ds(4 * part, rest)] = sh_chunk[pl.ds(4 * part, rest)]
-    kv_grad.relay(3)
     chunk(0)
     cosine, sine = cosr[...].reshape(2 * rows, PAIR), sinr[...].reshape(2 * rows, PAIR)
     for owner in range(2):
@@ -1243,9 +1241,23 @@
         parts = [unstack_pair(dq[group * owner + i]) for i in range(group)]
         gq[at] = turn(jnp.concatenate(parts, axis=1), cosr[at], -sinr[at]).astype(BF)
     query_w = Gather(spot, gq, lambda w: gq4.at[w], sems)
+    shared.last(sh_sum)
+    sh_chunk[...] = sh_sum[...].astype(BF)
+    part = 2 * shard // 2
+
+    def piece(w):
+        return sh_chunk.at[pl.ds(pl.multiple_of(part * w, 64), part)]
+
+    def place(w):
+        return r3.at[spot.k, pl.ds(pl.multiple_of(part * w, 64), part)]
+
+    shared_w = Spread(spot, piece, place, sems)
+    rest = sh_chunk.shape[0] - 4 * part
+    r3[spot.k, pl.ds(4 * part, rest)] = sh_chunk[pl.ds(4 * part, rest)]
     send_across(give_ref.at[1], other_out.at[1])
+    kv_grad.relay(3)
     shared_w.finish()
-    ring3 = Ring(spot, r3, ring_recv.at[2], ring_send.at[2], parts=2)
+    ring3 = Ring(spot, r3, ring_recv, ring_send, parts=2)
     ring3.start()
     normed_w.finish()
     normed_x = aside(n_all.at[spot.x], n_all.at[spot.x])
@@ -1258,9 +1270,9 @@
         o_send[x] = out_grad[:, half * x : half * (x + 1)]
     out_x = aside(o_send.at[1 - spot.x], o_land)
     kv_grad.relay(1)
-    ring3.step(1)
+    ring3.step(1, only=0)
     ring3.step(2, only=1)
-    for copy in loads[3:6]:
+    for copy in loads[2:5]:
         copy.wait()
     flat = gq[...].reshape(2 * rows, half)
     grad_normed = nt(flat, w_half[0])
@@ -1293,11 +1305,20 @@
     grad_normed = grad_normed + nt(flat[:, 0:half], w_half[1]) + nt(flat[:, half:width], w_half[2])
     gn_send[...] = grad_normed.astype(BF).reshape(2, rows, width)
     normed_grad_x = aside(gn_send.at[1 - spot.x], gn_land)
-    ring3.step(3, only=1)
+    ring3.step(1, only=1)
+    ring3.step(2, only=0)
     first.relay(3)
     first.relay(2)
     first.relay(1)
-    ring3.step(2, only=0)
+    ring3.step(3, only=1)
+    kv_w.forward()
+    kv_w.finish()
+    both = weight_grad(gkv4).astype(BF)
+    for plane in range(4):
+        a2[plane] = both[size * plane : size * (plane + 1)]
+    second = Reduce(spot, a2, None, a2_zo, a2_zi, sem_a2, folded=True)
+    for number in (3, 2, 1):
+        second.launch(number)
     normed_grad_x.wait_recv()
     grad_normed = gn_send[spot.x].astype(F32) + gn_land[...].astype(F32)
     inputs = tok[...].astype(F32)
@@ -1311,47 +1332,40 @@
     pk[...] = jnp.concatenate([gain_grad, pack_grad_ref[1:16]], axis=0).astype(BF)
     pack_w = Gather(spot, pk, lambda w: pk4.at[w], sems)
     send_across(give_ref.at[2], other_out.at[2])
+    second.relay(3)
     first.last(a1_sum)
     r1[spot.k] = a1_sum[...].astype(BF)
-    ring1 = Ring(spot, r1, ring_recv.at[0], ring_send.at[0])
+    ring1 = Ring(spot, r1, ring_recv, ring_send, first=(16, 22))
     ring1.start()
-    kv_w.forward()
+    second.relay(2)
+    second.relay(1)
+    ring3.step(3, only=0)
     pack_w.forward()
     pack_w.finish()
-    pk_sum[...] = sum(pk4[w].astype(F32) for w in range(4)).astype(BF)
-    pack_x = aside(pk_sum, pk_land)
-    kv_w.finish()
-    both = weight_grad(gkv4).astype(BF)
-    pack_x.wait_recv()
-    extra = (pk_sum[...].astype(F32) + pk_land[...].astype(F32)).astype(BF)
-    for plane in range(4):
-        a2[plane, 0:size] = both[size * plane : size * (plane + 1)]
-        a2[plane, size : size + 16] = extra
-    second = Reduce(spot, a2, None, a2_zo, a2_zi, sem_a2, folded=True)
-    for number in (3, 2, 1):
-        second.launch(number)
-    ring3.step(3, only=0)
+    extra = sum(pk4[w].astype(F32) for w in range(4)).astype(BF)
     ring1.step(1)
     ring1.step(2, only=1)
-    second.relay(3)
-    second.relay(2)
-    second.relay(1)
+    second.last(a2_sum)
+    r2[spot.k, 0:size] = a2_sum[...].astype(BF)
+    r2[spot.k, size : size + 16] = extra
+    ring2 = Ring(spot, r2, ring_recv, ring_send, first=(24, 33))
+    ring2.start()
     ring1.step(3, only=1)
     ring1.step(2, only=0)
-    second.last(a2_sum)
-    r2[spot.k] = a2_sum[0:size].astype(BF)
-    ring2 = Ring(spot, r2, ring_recv.at[1], ring_send.at[1])
-    ring2.start()
-    pack_out[...] = a2_sum[size : size + 16]
     ring1.step(3, only=0)
-    for number in (1, 2, 3):
-        ring2.step(number)
+    ring2.step(1)
+    ring2.step(2)
+    ring2.step(3)
     saves = []
     for ring, src, dst in ((ring3, r3, sh_out), (ring1, r1, att1_out), (ring2, r2, att2_out)):
         for number in range(4):
             ring.other(number)
         saves.append(pltpu.make_async_copy(src, dst, sems.new()))
         saves[-1].start()
+    total = jnp.zeros(pk.shape, F32)
+    for r in range(ranks):
+        total = total + r2[r, size : size + 16].astype(F32)
+    pack_out[...] = total
     for copy in across:
         copy.wait_recv()
     for copy in across + asides:
@@ -1360,12 +1374,12 @@
         part_w.drain()
     for part_w in (shared, kv_grad, first, second, ring1, ring2, ring3):
         part_w.drain()
-    for copy in saves + loads[6:]:
+    for copy in saves + loads[5:]:
         copy.wait()
 
 
 def run_backward(
-    grad_second, tok, pack, pack_grad, normed, mixed, qc, lse, cosr, sinr, kb, qb, dsh, kv, wfull,
+    grad_second, tok, pack, pack_grad, n_t, m_t, qx, gx, stats, cosr, sinr, kb, qb, dsh, kv, wfull,
     give, other,
 ):
     rows, width = tok.shape
@@ -1391,30 +1405,19 @@
             shape((rows, width), F32),
             shape(pack.shape, F32),
             shape((ranks, size, width), BF),
-            shape((ranks, size, width), BF),
+            shape((ranks, size + 16, width), BF),
             shape((ranks, tall, 128), BF),
             shape((3, shard, hidden), BF),
         ),
-        in_specs=[vm] * 12 + [any_] * 5,
+        in_specs=[vm] * 13 + [any_] * 5,
         out_specs=(vm, vm, any_, any_, any_, any_),
         scratch_shapes=[
-            low(width, width),
             low(3, width, half),
             low(ranks, rows, width),
             low(4, 2 * rows, width),
             low(4, 2 * rows, width),
             low(4, 2 * rows, width),
             full(2 * rows, width),
-            low(rows, half),
-            low(2, rows, half),
-            low(rows, half),
-            low(pairs, 2 * rows, PAIR),
-            low(pairs, 2 * rows, PAIR),
-            full(pairs, 2 * rows, PAIR),
-            full(pairs, 2 * rows, PAIR),
-            full(pairs, 2 * rows, PAIR),
-            full(8, 2 * rows),
-            full(8, 2 * rows),
             full(pairs, 2 * rows, PAIR),
             low(rows, width),
             low(4, rows, width),
@@ -1422,14 +1425,10 @@
             low(4, 2, rows, half),
             low(2, rows, width),
             low(4, 2, rows, width),
-            low(width, rows),
-            low(width, rows),
             low(2, shard, 4 * rows),
             low(shard, 4 * rows),
             low(16, width),
             low(4, 16, width),
-            low(16, width),
-            low(16, width),
             low(2, shard, half),
             low(shard, half),
             low(2, rows, width),
@@ -1438,30 +1437,31 @@
             low(4, size, width),
             low(4, size, width),
             full(size, width),
-            low(4, size + 16, width),
-            low(4, size + 16, width),
-            low(4, size + 16, width),
-            full(size + 16, width),
+            low(4, size, width),
+            low(4, size, width),
+            low(4, size, width),
+            full(size, width),
             low(ranks, size, width),
-            low(ranks, size, width),
+            low(ranks, size + 16, width),
+            low(4, tall, 128),
             low(4, tall, 128),
             low(4, tall, 128),
             full(tall, 128),
             low(tall, 128),
             low(ranks, tall, 128),
-            dma((128,)),
-            dma((5, 8)),
-            dma((5, 8)),
-            dma((5, 8)),
-            dma((5, 8)),
-            dma((3, 2 * ranks)),
-            dma((3, 32)),
+            dma((SEMS_BACKWARD,)),
+            dma((3, 8)),
+            dma((3, 4)),
+            dma((3, 4)),
+            dma((3, 8)),
+            dma((4 * ranks,)),
+            dma((44,)),
         ],
         compiler_params=pltpu.CompilerParams(
             collective_id=3, has_side_effects=True, vmem_limit_bytes=VMEM_BYTES
         ),
     )(
-        grad_second, tok, pack, pack_grad, normed, mixed, qc, lse, cosr, sinr, kb, qb, dsh, kv,
+        grad_second, tok, pack, pack_grad, n_t, m_t, qx, gx, stats, cosr, sinr, kb, qb, dsh, kv,
         wfull, give, other,
     )
 
@@ -1475,10 +1475,11 @@
     result_out[...] = result[...]
     grad_input_out[...] = grad_input[...]
     half = query.shape[1] // 2
+    size = query.shape[0]
     for x in range(2):
         lanes = slice(half * x, half * (x + 1))
         for ref, src, low in ((output, att1, 0), (query, att1, 1), (key, att2, 0), (value, att2, 1)):
-            ref[:, lanes] = src[0, x, :, half * low : half * (low + 1)].astype(F32)
+            ref[:, lanes] = src[0, x, 0:size, half * low : half * (low + 1)].astype(F32)
     for a, ref in enumerate((eg, eu, ed)):
         ref[...] = keep[a].astype(F32) + other[a].astype(F32)
     size = gate.shape[0]
@@ -1514,13 +1515,13 @@
     shape = jax.ShapeDtypeStruct
     size = shard // steps
     att1 = att1.reshape(4, 2, size, width)
-    att2 = att2.reshape(4, 2, size, width)
+    att2 = att2.reshape(4, 2, size + 16, width)
     shared_hidden = sh.shape[0] * (sh.shape[1] - width) * 128 // width
     shared = 4 * shared_hidden
     by_rows = lambda r, c: pl.BlockSpec((r, c), lambda i: (i, 0))
     whole = lambda *dims: pl.BlockSpec(dims, lambda i: (0,) * len(dims))
     stack = lambda n, r, c: pl.BlockSpec((n, r, c), lambda i: (0, i, 0))
-    att = pl.BlockSpec((1, 2, size, width), lambda i: (i, 0, 0, 0))
+    att = lambda r: pl.BlockSpec((1, 2, r, width), lambda i: (i, 0, 0, 0))
     return pl.pallas_call(
         unpack_kernel,
         grid=(steps,),
@@ -1539,8 +1540,8 @@
             by_rows(rows // steps, width),
             by_rows(rows // steps, width),
             whole(*pack.shape),
-            att,
-            att,
+            att(size),
+            att(size + 16),
             whole(*sh.shape),
             stack(3, size, hidden),
             stack(3, size, hidden),
@@ -2081,7 +2082,7 @@
     frequency = 10000.0 ** (-np.arange(half_size) / half_size)
     frequency = jnp.asarray(np.tile(frequency, 4)[None].astype(np.float32))
     (
-        cosr, sinr, kb, qb, q_st, mixed, lse, normed, pack_all, result, grad_second, pack_grad, dsh,
+        cosr, sinr, kb, qb, qx, gx, stats, n_t, m_t, pack_all, result, grad_second, pack_grad, dsh,
         kv_all, wfull, keep, give, other,
     ) = run_forward(
         tokens[0], jnp.stack([gain_attention, gain_mixer]), router_weight.T, frequency, block_deal,
@@ -2090,7 +2091,7 @@
         expert_gate, expert_up, expert_down,
     )
     grad_input, pack_sum, att1, att2, sh, other = run_backward(
-        grad_second, tokens[0], pack_all, pack_grad, normed, mixed, q_st, lse, cosr, sinr, kb, qb,
+        grad_second, tokens[0], pack_all, pack_grad, n_t, m_t, qx, gx, stats, cosr, sinr, kb, qb,
         dsh, kv_all, wfull, give, other,
     )
     (

time: 243 us -> 226 us (0.930)
  Pallas kernels: 240 us -> 223 us
    pallas_call x1, Pallas kernels: 101 us -> 85.3 us  [run_backward(): pl.pallas_call(backward_kernel, out_shape=(shape((rows, width), F32), sha...]
where the time goes in v7:
time: 226 us
  Pallas kernels  223 us (99%)
    pallas_call x1, Pallas kernels, run_forward(): pl.pallas_call(forward_kernel, out_shape=(shape((2, rows, PAIR), F32), sh...  129 us
    pallas_call x1, Pallas kernels, run_backward(): pl.pallas_call(backward_kernel, out_shape=(shape((rows, width), F32), sha...  85.3 us
    pallas_call x1, Pallas kernels, run_unpack(): pl.pallas_call(unpack_kernel, grid=(steps,), out_shape=(shape((rows, widt...  8.87 us

profile of v7, /device:TPU:0, one launch (start us, length us, event | category | flops | bytes accessed | tf_op | source)
XLA Modules:
  0.0 226.2 jit_solution(12064146929124500570)
XLA Ops:
  0.6 0.7 stack.9
  1.3 0.7 stack.10
  2.0 0.6 pad_maximum_fusion.gains
  2.5 129.3 %shard_map.298 = (f32[2,128,128]{2,1,0:T(8,128)}, f32[2,128,128]{2,1,0:T(8,128)}, s32[1,1024]{1,0:T(1,128)}, s32[2,256,1]{2,1,0:T(8,128)}, bf16[6,256,128]{2,1,0...) custom-call(bf16[128,768]{1,0:T(8,128)(2,1)} %bitcast.14, ...), custom_call_target="tpu_custom_call" | custom-call | tf_op jit(solution)/shard_map/pallas_call | solution.py:1049
  131.9 85.3 %shard_map.299 = (f32[128,768]{1,0:T(8,128)}, f32[16,768]{1,0:T(8,128)}, bf16[8,48,768]{2,1,0:T(8,128)(2,1)}, bf16[8,64,768]{2,1,0:T(8,128)(2,1)}, bf16[8,1152,1...) custom-call(f32[128,768]{1,0:T(8,128)} %get-tuple-element.56.grad_second_ref, bf16[128,768]{1,0:T(8,128)(2,1)} %bitcast.15, ...), custom_call_target="tpu_custom_call" | custom-call | tf_op jit(solution)/shard_map/pallas_call | solution.py:1402
  217.1 8.9 %shard_map.300 = (bf16[128,768]{1,0:T(8,128)(2,1)}, f32[128,768]{1,0:T(8,128)}, f32[1,192]{1,0:T(1,128)}, f32[1,192]{1,0:T(1,128)}, f32[8,192]{1,0:T(8,128)}, /*...) custom-call(bf16[128,768]{1,0:T(8,128)(2,1)} %get-tuple-element.55.r, ...), custom_call_target="tpu_custom_call" | custom-call | tf_op jit(solution)/shard_map/pallas_call | solution.py:1525

commit v8 on v7

--- a/solution.py
+++ b/solution.py
@@ -22,8 +22,9 @@
 F32 = jnp.float32
 PAIR = 2 * HD
 VMEM_BYTES = 127 * 2**19
-SEMS_FORWARD = 148
-SEMS_BACKWARD = 73
+SEMS_FORWARD = 207
+SEMS_BACKWARD = 95
+SEMS_RINGS = 48
 
 
 class Spot:
@@ -152,53 +153,73 @@
             copy.wait_send()
 
 
-class ShareColumns:
-    def __init__(self, spot, src, dst, sems, mate, bit):
-        self.spot, self.dst, self.sems, self.mate, self.bit = spot, dst, sems, mate, bit
-        self.rows, self.part_cols = src.shape[0], dst.shape[1]
-        self.half = self.rows // 2
-        half = pl.ds(pl.multiple_of(self.half * bit, 32), self.half)
-
-        def columns(to):
-            return pl.ds(pl.multiple_of(self.part_cols * to, self.part_cols), self.part_cols)
+class Quarters:
+    def __init__(self, spot, src, dst, sems, columns=False):
+        self.spot, self.dst, self.sems, self.columns = spot, dst, sems, columns
+        self.rows = src.shape[0]
+        self.size = self.rows // 4
+        self.q = 2 * spot.x + spot.odd
+        self.sources = (spot.across, spot.corner) if columns else (spot.across,)
+        cols = dst.shape[1]
+
+        def take(to, quarter):
+            at = pl.ds(pl.multiple_of(self.size * self.q, 16), self.size)
+            if not columns:
+                return src.at[at] if quarter else src
+            lanes = pl.ds(pl.multiple_of(cols * to, cols), cols)
+            return src.at[at, lanes] if quarter else src.at[:, lanes]
 
         here = dst.at[pl.ds(pl.multiple_of(self.rows * spot.w, 64), self.rows)]
-        self.halves = [
-            remote(
-                src.at[half, columns(to[1])],
-                self.part(spot.w, bit),
-                sems.new(),
-                sems.new(),
-                to,
-            )
-            for to in (spot.across, spot.corner)
+        self.far = [
+            remote(take(to[1], True), self.part(spot.w, self.q), sems.new(), sems.new(), to)
+            for to in self.sources
         ]
-        self.to_core = remote(
-            src.at[:, columns(spot.core[1])], here, sems.new(), sems.new(), spot.core
-        )
-        self.local = pltpu.make_async_copy(src.at[:, columns(spot.w)], here, sems.new())
-        for copy in self.halves + [self.to_core, self.local]:
+        self.to_core = remote(take(spot.core[1], False), here, sems.new(), sems.new(), spot.core)
+        self.local = pltpu.make_async_copy(take(spot.w, False), here, sems.new())
+        for copy in self.far + [self.to_core, self.local]:
             copy.start()
-
-    def part(self, w, bit):
-        return self.dst.at[pl.ds(pl.multiple_of(self.rows * w + self.half * bit, 32), self.half)]
+        self.lines, self.sides, self.cores = [], [], []
+
+    def part(self, w, q, count=1):
+        start = pl.multiple_of(self.rows * w + self.size * q, 16)
+        return self.dst.at[pl.ds(start, self.size * count)]
+
+    def send(self, copies, part, to):
+        copies.append(remote(part, part, self.sems.new(), self.sems.new(), to))
+        copies[-1].start()
 
     def forward(self):
-        self.aside = []
-        for copy, source in zip(self.halves, (self.spot.across, self.spot.corner)):
+        for copy, source in zip(self.far, self.sources):
             copy.wait_recv()
-            part = self.part(source[1], self.bit)
-            self.aside.append(remote(part, part, self.sems.new(), self.sems.new(), self.mate))
-            self.aside[-1].start()
+            part = self.part(source[1], self.q)
+            self.send(self.lines, part, self.spot.line)
+            self.send(self.sides, part, self.spot.column)
+            if not self.columns:
+                self.send(self.cores, part, self.spot.core)
+
+    def second(self):
+        for copy, source in zip(self.lines, self.sources):
+            copy.wait_recv()
+            part = self.part(source[1], 2 * self.spot.x + 1 - self.spot.odd)
+            self.send(self.sides, part, self.spot.column)
+            if not self.columns:
+                self.send(self.cores, part, self.spot.core)
+
+    def third(self):
+        for copy in self.sides:
+            copy.wait_recv()
+        if not self.columns:
+            part = self.part(self.spot.across[1], 2 * (1 - self.spot.x), 2)
+            self.send(self.cores, part, self.spot.core)
 
     def finish(self):
         self.local.wait()
         self.to_core.wait_recv()
-        for copy in self.aside:
+        for copy in self.cores:
             copy.wait_recv()
 
     def drain(self):
-        for copy in self.halves + self.aside + [self.to_core]:
+        for copy in self.far + self.lines + self.sides + self.cores + [self.to_core]:
             copy.wait_send()
 
 
@@ -292,15 +313,22 @@
 
 
 class Ring:
-    def __init__(self, spot, blocks, recv, send, parts=1, first=(0, 0)):
+    def __init__(self, spot, blocks, recv, send, parts=1, sides=1, first=(0, 0)):
         self.spot, self.blocks, self.recv, self.send, self.parts = spot, blocks, recv, send, parts
+        self.sides = sides
         self.ranks = blocks.shape[0]
         self.first, self.used = first[0], first[1]
         self.sent, self.sent_mid, self.sent_end = [], [], []
 
     def piece(self, slot, part):
-        rows = self.blocks.shape[1] // self.parts
-        return self.blocks.at[slot, pl.ds(rows * part, rows)]
+        if self.sides == 1:
+            rows = self.blocks.shape[1] // self.parts
+            return self.blocks.at[slot, pl.ds(rows * part, rows)]
+        high = self.parts // self.sides
+        rows, lanes = self.blocks.shape[1] // high, self.blocks.shape[2] // self.sides
+        return self.blocks.at[
+            slot, pl.ds(rows * (part % high), rows), pl.ds(lanes * (part // high), lanes)
+        ]
 
     def copy(self, slot, part, to):
         self.used += 1
@@ -321,17 +349,30 @@
             self.spot.column,
         ).wait_recv()
 
-    def start(self):
+    def start(self, parts=None, only=None):
         spot = self.spot
-        for part in range(self.parts):
+        for part in range(self.parts) if parts is None else parts:
             own = self.copy(spot.k, part, spot.inner)
             side = self.copy(spot.k, part, spot.column)
-            back = self.copy(spot.k, part, spot.outer)
-            own.start()
-            self.middle(back)
-            side.start()
-            self.sent += [own, side]
-            self.sent_mid += [back]
+            back = self.copy(spot.k, part, spot.outer) if only != 0 else None
+            if only is None:
+                own.start()
+                self.middle(back)
+                side.start()
+                self.sent += [own, side]
+                self.sent_mid += [back]
+                continue
+
+            @pl.when(spot.mid == only)
+            def _(copies=(own, back, side)):
+                for copy in copies:
+                    if copy is not None:
+                        copy.start()
+
+            if only == 1:
+                self.sent_mid += [own, back, side]
+            else:
+                self.sent_end += [own, side]
 
     def middle(self, copy):
         @pl.when(self.spot.mid == 1)
@@ -463,35 +504,35 @@
                 self.wait(self.zo, self.zo_recv, plane, h)
                 self.add(self.own(plane, h), self.cut(self.zo, plane, h))
 
-    def relay(self, number, settled=False):
+    def relay(self, number, settled=False, parts=None):
         plane = self.spot.plane(number)
         land, recv = (self.zi, self.zi_recv) if number == 1 else (self.zo, self.zo_recv)
         copies = []
-        for h in range(self.parts):
+        for h in range(self.parts) if parts is None else parts:
             at = plane + 4 * h
-            copies.append(
-                remote(
-                    self.own(plane, h),
-                    self.cut(self.zi, plane, h),
-                    self.z_send.at[at],
-                    self.zi_recv.at[at],
-                    self.spot.outer if number == 1 else self.spot.inner,
-                )
+            copy = remote(
+                self.own(plane, h),
+                self.cut(self.zi, plane, h),
+                self.z_send.at[at],
+                self.zi_recv.at[at],
+                self.spot.outer if number == 1 else self.spot.inner,
             )
+            copies.append((h, copy))
 
         @pl.when(self.spot.mid == 1)
         def _():
-            for h, copy in enumerate(copies):
+            for h, copy in copies:
                 if not settled:
                     self.wait(land, recv, plane, h)
                     self.add(self.own(plane, h), self.cut(land, plane, h))
                 copy.start()
 
-        self.sent_mid += copies
-
-    def last(self, result):
+        self.sent_mid += [copy for _, copy in copies]
+
+    def last(self, result, parts=None):
         plane = self.spot.plane(0)
-        for h in range(self.parts):
+        parts = range(self.parts) if parts is None else parts
+        for h in parts:
             self.wait(self.zi, self.zi_recv, plane, h)
             rows = pl.ds(self.rows * h, self.rows)
             total = self.own(plane, h)[...].astype(F32)
@@ -499,7 +540,7 @@
 
         @pl.when(self.spot.mid == 1)
         def _():
-            for h in range(self.parts):
+            for h in parts:
                 self.wait(self.zo, self.zo_recv, plane, h)
                 rows = pl.ds(self.rows * h, self.rows)
                 result[rows] += self.cut(self.zo, plane, h)[...].astype(F32)
@@ -627,11 +668,12 @@
 
 
 def forward_kernel(
-    tok, gains, router_ref, freq, deal, cot, routes, order, sd,
+    tok, gain_one, gain_two, router_ref, freq, deal, cot, routes, order, sd,
     wq, wk, wv, wo, sg, su, eg, eu, ed,
-    cosr, sinr, kb, qb, qx, gx, stats_out, normed_out, mixed_out, pack_out, result_out, grad_second_out, pack_grad_out,
-    dsh_out, kv_out, wfull_out, keep_out, give_out, other_out,
-    wbuf, kv, q_s, qc, q_land, gm, gm_land, stat, stat_land, mixed, pack, packs, top, low, acc, sg_all, su_all, wg, wu, wd, mix, m4, cot4,
+    cosr_out, sinr_out, kb_out, qb_out, qx_out, gx_out, stats_hbm, normed_hbm, mixed_hbm, pack_hbm,
+    result_hbm, grad_second_hbm, pack_grad_hbm, dsh_out, side_out, kv_out, wfull_out, keep_out, give_out, other_out,
+    cosr, sinr, kb, qb, qx, gx, stats_out, normed_out, mixed_out, pack_out, result_out,
+    grad_second_out, pack_grad_out, wbuf, kv, q_s, qc, q_land, gm, gm_land, stat, stat_land, mixed, pack, packs, top, low, acc, sg_all, su_all, wg, wu, wd, mix, m4, cot4,
     sh_send, sh_recv, gm_send, gm_recv, xs, xr, gs, gr, orr, br,
     x_s, g_s, sum_s, gate_s, up_s, hid_s, dgate_s, dup_s, dsh, dsh_x, dsh_z, slot_s, pair_s, cb,
     sem, kv_recv, kv_send, a2a_send, a2a_recv, sem_sh,
@@ -647,26 +689,40 @@
     part = sg_all.shape[1]
     peers = [(lax.rem(spot.k + o, ranks), spot.w) for o in range(1, ranks)]
     greet([spot.core, spot.across, spot.corner] + peers)
-    column, line = (spot.column, spot.x), (spot.line, spot.odd)
-    key_w = Share(spot, wk, wbuf.at[1], sems, *column)
+    line = (spot.line, spot.odd)
+    key_w = Quarters(spot, wk, wbuf.at[1], sems)
     shards = jnp.concatenate(
-        [gains[...], router_ref[...], jnp.zeros((16 - 2 - router_ref.shape[0], shard), BF)], axis=0
-    ).astype(F32)
+        [
+            gain_one[...].astype(F32).reshape(1, shard),
+            gain_two[...].astype(F32).reshape(1, shard),
+            router_ref[...].astype(F32),
+            jnp.zeros((16 - 2 - router_ref.shape[0], shard), F32),
+        ],
+        axis=0,
+    )
     shards = jnp.concatenate([shards, jnp.zeros((16, width - shard), F32)], axis=1)
     pack[...] = pltpu.roll(shards, shard * spot.w, 1).astype(BF)
     params = Gather(spot, pack, lambda w: packs.at[w], sems)
-    value_w = Share(spot, wv, wbuf.at[2], sems, *column)
-    query_w = Share(spot, wq, wbuf.at[0], sems, *column)
+    value_w = Quarters(spot, wv, wbuf.at[2], sems)
+    query_w = Quarters(spot, wq, wbuf.at[0], sems)
 
     def stripe(ref):
         return lambda w: ref.at[pl.ds(pl.multiple_of(shard * w, 64), shard)]
 
     out_w = Share(spot, wo, wbuf.at[3], sems, *line)
-    sg_w = ShareColumns(spot, sg, sg_all, sems, *line)
-    su_w = ShareColumns(spot, su, su_all, sems, *line)
+    sg_w = Quarters(spot, sg, sg_all, sems, columns=True)
+    su_w = Quarters(spot, su, su_all, sems, columns=True)
     cot_w = Gather(spot, cot, lambda w: cot4.at[w], sems)
     gate_w = Gather(spot, eg, stripe(wg), sems)
     up_w = Gather(spot, eu, stripe(wu), sems)
+    early = shard // 3
+
+    def down_part(start, count):
+        at = pl.ds(start, count)
+        place = lambda w: wd.at[pl.ds(pl.multiple_of(shard * w + start, 64), count)]
+        return Gather(spot, ed.at[at], place, sems)
+
+    down_w = [down_part(0, early)]
     inputs = tok[...].astype(F32)
     scale = lax.rsqrt(jnp.mean(inputs * inputs, axis=-1, keepdims=True) + EPS)
     scaled = inputs * scale
@@ -696,22 +752,25 @@
     normed = (scaled * pack_all[0:1]).astype(BF)
     normed_out[...] = normed.T
     cosine, sine = cosr[spot.x], sinr[spot.x]
+    value_w.forward()
     to_slots, to_pairs = slot_maps(routes[...], order[...], slots, ranks)
     route = [diagonal(routes[j : j + 1], 1) for j in range(2)]
     slot_s[...] = to_slots
     pair_s[...] = to_pairs
-    value_w.forward()
     key_w.second()
     query_w.forward()
+    value_w.second()
+    key_w.third()
     key_w.finish()
     kv[spot.k, :, 0:width] = turn(nn(normed, wbuf[1]), cosine, sine).astype(BF)
-    value_w.second()
+    ring = Ring(spot, kv, kv_recv, kv_send, parts=4, sides=2)
+    ring.start(parts=(0, 1))
+    query_w.second()
+    value_w.third()
     value_w.finish()
     kv[spot.k, :, width : 2 * width] = nn(normed, wbuf[2]).astype(BF)
-    ring = Ring(spot, kv, kv_recv, kv_send, parts=2)
-    ring.start()
-    query_w.second()
-
+    ring.start(parts=(2, 3))
+    query_w.third()
     query_w.finish()
     query = turn(nn(normed, wbuf[0]), cosine, sine).astype(BF) * jnp.asarray(HD**-0.5, BF)
     for j in range(pairs):
@@ -761,8 +820,19 @@
     cot_w.forward()
     ring.other(3)
     chunk(spot.plane(3))
-    saves = [pltpu.make_async_copy(kv, kv_out, sems.new())]
-    saves[0].start()
+    sg_w.second()
+    su_w.second()
+    saves = []
+
+    def save(src, dst):
+        saves.append(pltpu.make_async_copy(src, dst, sems.new()))
+        saves[-1].start()
+
+    save(kv, kv_out)
+    for src, dst in ((cosr, cosr_out), (sinr, sinr_out), (kb, kb_out), (qb, qb_out)):
+        save(src, dst)
+    save(normed_out, normed_hbm)
+    save(pack_out, pack_hbm)
     for j in range(pairs):
         mixed[:, PAIR * j : PAIR * (j + 1)] = unstack_pair(acc[j] / low[j])
         top[j] = top[j] + jnp.log(low[j])
@@ -774,15 +844,14 @@
         return asides[-1]
 
     out_w.finish()
-    saves.append(pltpu.make_async_copy(wbuf, wfull_out, sems.new()))
-    saves[1].start()
+    save(wbuf, wfull_out)
     second = inputs + nn(mixed[...].astype(BF), wbuf[3])
     scale = lax.rsqrt(jnp.mean(second * second, axis=-1, keepdims=True) + EPS)
     mixer = (second * scale * pack_all[1:2]).astype(BF)
     mix[...] = mixer
 
     mixers = Gather(spot, mix, lambda w: m4.at[w], sems)
-    down_w = Gather(spot, ed, stripe(wd), sems)
+    down_w.append(down_part(early, shard - early))
     fold_rows(nn(slot_s[:, :rows] + slot_s[:, rows:], mixer), xs)
     rows_out = Exchange(spot, xs, xr, a2a_send.at[0], a2a_recv.at[0])
     rows_out.start()
@@ -804,6 +873,8 @@
     up_w.forward()
     mixers.forward()
 
+    for part_w in (sg_w, su_w):
+        part_w.third()
     for part_w in (sg_w, su_w, cot_w, mixers):
         part_w.finish()
     rows_all = m4[...].reshape(4 * rows, width)
@@ -813,6 +884,7 @@
     shared_hidden = (act * up_part).astype(BF)
     sh_send[...] = nn(shared_hidden, sd[...]).astype(BF).reshape(4, rows, width)
     mixed_out[...] = mixed[...].astype(BF).T
+    save(mixed_out, mixed_hbm)
     query_x = aside(qc.at[1 - spot.x], q_land)
     shared_out = Merge(spot, sh_send, sh_recv, sems)
     hid_grad = nt(grad_all, sd[...])
@@ -840,7 +912,7 @@
             ]
     shared_back.forward()
     shared_grad = Reduce(spot, dsh, dsh_x, dsh_z, None, sem_sh)
-    for number in (3, 2, 1, 0):
+    for number in (3, 2):
         shared_grad.side(number)
 
     for part_w in (gate_w, up_w):
@@ -863,9 +935,10 @@
         return carry
 
     lax.fori_loop(0, hidden // block, up_step, 0)
-    down_w.forward()
-    down_w.finish()
-    shared_grad.meet(3, True)
+    for part_w in down_w:
+        part_w.forward()
+    for part_w in down_w:
+        part_w.finish()
     sum_s[...] = nt(hid_s[...], wd[...])
     rows_out.drain()
     fold_rows(sum_s[...], xs)
@@ -887,8 +960,9 @@
     fold_rows(sum_s[...], gs)
     backs = Exchange(spot, gs, br, a2a_send.at[3], a2a_recv.at[3])
     backs.start()
-
-    for part_w in (gate_w, up_w, down_w):
+    shared_grad.side(1)
+
+    for part_w in [gate_w, up_w] + down_w:
         part_w.drain()
     swaps, across = [], []
     first = 2 * shard // 3
@@ -924,36 +998,34 @@
         start = pl.multiple_of(shard * spot.across[1], 64)
         keep = ref.at[pl.ds(pl.multiple_of(shard * spot.w, 64), shard)]
         saves.append(pltpu.make_async_copy(keep, keep_out.at[a], sems.new()))
+        saves[-1].start()
         if a == 0:
             across.append(
                 remote(ref.at[pl.ds(start, first)], other_out, sems.new(), sems.new(), spot.across)
             )
             across[-1].start()
             give = ref.at[pl.ds(pl.multiple_of(start + first, 64), shard - first)]
-            saves.append(
-                pltpu.make_async_copy(give, give_out.at[0, pl.ds(first, shard - first)], sems.new())
-            )
+            there = give_out.at[0, pl.ds(first, shard - first)]
         else:
-            give = ref.at[pl.ds(start, shard)]
-            saves.append(pltpu.make_async_copy(give, give_out.at[a], sems.new()))
-        for copy in saves[-2:]:
-            copy.start()
-
-    shared_grad.meet(2, True)
+            give, there = ref.at[pl.ds(start, shard)], give_out.at[a]
+        saves.append(pltpu.make_async_copy(give, there, sems.new()))
+        saves[-1].start()
+
+    shared_grad.meet(3, True)
     grads_of(0)
     grads_of(1)
     add_mate(0)
-    shared_grad.meet(1, False)
+    shared_grad.meet(2, True)
     grads_of(2)
     add_mate(1)
     add_mate(2)
-    shared_grad.meet(0, False)
     total = second + shared_out.finish()
     grad_mixer = shared_back.finish()
     outs.finish()
     pair_out = nn(pair_s[...], unfold_rows(orr, slots))
     pair_out = [pair_out[:rows], pair_out[rows:]]
     result_out[...] = (total + gates[0] * pair_out[0] + gates[1] * pair_out[1]).astype(BF)
+    save(result_out, result_hbm)
     grad_gates = [jnp.sum(grad * p, axis=1, keepdims=True) for p in pair_out]
     inner = gates[0] * grad_gates[0] + gates[1] * grad_gates[1]
     grad_logits = jnp.zeros_like(logits)
@@ -962,12 +1034,14 @@
     pieces = split_three(grad_logits)
     router_grad = sum(tn(piece, mixer) for piece in pieces)
     grad_mixer = grad_mixer + sum(nn(piece, router) for piece in pieces)
+    shared_grad.meet(1, False)
     backs.finish()
     grad_mixer = grad_mixer + nn(pair_s[:rows] + pair_s[rows:], unfold_rows(br, slots))
     weighted = grad_mixer * pack_all[1:2]
     mean = jnp.mean(weighted * second, axis=-1, keepdims=True)
     grad_second = grad + scale * weighted - second * (scale * scale * scale * mean)
     grad_second_out[...] = grad_second
+    save(grad_second_out, grad_second_hbm)
 
     grad_mixed = nt(grad_second.astype(BF), wbuf[3]).astype(BF)
     half = width // 2
@@ -1010,7 +1084,15 @@
     for number in (3, 2):
         shared_grad.absorb(number)
     for plane in range(4):
-        dsh_out[plane] = dsh[2 * plane + spot.x]
+        save(dsh.at[2 * plane + spot.x], dsh_out.at[plane])
+    save(dsh.at[2 * spot.z + 1 - spot.x], side_out)
+    for src, dst in (
+        (qx, qx_out),
+        (gx, gx_out),
+        (stats_out, stats_hbm),
+        (pack_grad_out, pack_grad_hbm),
+    ):
+        save(src, dst)
     for copy in across:
         copy.wait_recv()
     for part_w in (params, key_w, value_w, query_w, out_w, sg_w, su_w, cot_w, ring, mixers):
@@ -1024,7 +1106,7 @@
 
 
 def run_forward(
-    tok, gains, router, freq, deal, cot, routes, order, sd,
+    tok, gain_one, gain_two, router, freq, deal, cot, routes, order, sd,
     wq, wk, wv, wo, sg, su, eg, eu, ed,
 ):
     rows, width = tok.shape
@@ -1063,15 +1145,29 @@
             shape((rows, width), F32),
             shape((16, width), F32),
             shape((4, tall, 128), BF),
+            shape((tall, 128), BF),
             shape((ranks, rows, 2 * width), BF),
             shape((4, width, width), BF),
             shape((3, shard, hidden), BF),
             shape((3, shard, hidden), BF),
             shape((2 * shard // 3, hidden), BF),
         ),
-        in_specs=[vm] * 4 + [pl.BlockSpec(memory_space=pltpu.SMEM)] + [vm] * 4 + [any_] * 9,
-        out_specs=tuple([vm] * 14 + [any_] * 5),
+        in_specs=[vm] * 5 + [pl.BlockSpec(memory_space=pltpu.SMEM)] + [vm] * 4 + [any_] * 9,
+        out_specs=tuple([any_] * 20),
         scratch_shapes=[
+            full(2, rows, PAIR),
+            full(2, rows, PAIR),
+            VMEM((1, ranks * rows), jnp.int32),
+            VMEM((2, 2 * rows, 1), jnp.int32),
+            low(pairs, 2 * rows, PAIR),
+            low(pairs, 2 * rows, PAIR),
+            full(2, 2 * rows, PAIR),
+            low(width, rows),
+            low(width, rows),
+            full(16, width),
+            low(rows, width),
+            full(rows, width),
+            full(16, width),
             low(4, width, width),
             low(ranks, rows, 2 * width),
             low(pairs, 2 * rows, PAIR),
@@ -1115,8 +1211,8 @@
             low(2 * rows, total),
             low(3, 2, shard, hidden),
             dma((SEMS_FORWARD,)),
-            dma((2 * ranks,)),
-            dma((22,)),
+            dma((4 * ranks,)),
+            dma((44,)),
             dma((4, ranks)),
             dma((4, ranks)),
             dma((4, 4)),
@@ -1125,18 +1221,19 @@
             collective_id=1, has_side_effects=True, vmem_limit_bytes=VMEM_BYTES
         ),
     )(
-        tok, gains, router, freq, deal, cot, routes, order, sd,
+        tok, gain_one, gain_two, router, freq, deal, cot, routes, order, sd,
         wq, wk, wv, wo, sg, su, eg, eu, ed,
     )
 
 
 def backward_kernel(
-    grad_second_ref, tok, pack_ref, pack_grad_ref, n_t, m_t, qx, gx, stats,
-    cosr, sinr, kb, qb, dsh_ref, kv_ref, wfull_ref, give_ref, other_ref,
+    grad_second_hbm, tok_hbm, pack_hbm, pack_grad_hbm, n_t_hbm, m_t_hbm, qx_hbm, gx_hbm, stats_hbm,
+    cosr_hbm, sinr_hbm, kb_hbm, qb_hbm, side_ref, dsh_ref, kv_ref, wfull_ref, give_ref, other_ref,
     grad_input_out, pack_out, att1_out, att2_out, sh_out, other_out,
+    grad_second_ref, tok, pack_ref, pack_grad_ref, n_t, m_t, qx, gx, stats, cosr, sinr, kb, qb,
     w_half, kv, kvb, kv_zo, kv_zi, kv_sum, dq, ga, ga4, gq, gq4, gkv, gkv4, n_all, m_all, pk, pk4,
     o_send, o_land, gn_send, gn_land, a1, a1_zo, a1_zi, a1_sum, a2, a2_zo, a2_zi, a2_sum, r1, r2,
-    sh, sh_zo, sh_zi, sh_sum, sh_chunk, r3,
+    sh, sh_land, sh_zo, sh_zi, sh_sum, sh_chunk, r3,
     sem, sem_kv, sem_a1, sem_a2, sem_sh, ring_recv, ring_send,
 ):
     spot = Spot(4)
@@ -1148,8 +1245,25 @@
     mine = pl.ds(pl.multiple_of(half * spot.x, half), half)
     values = pl.ds(pl.multiple_of(width + half * spot.x, half), half)
     ranks = kv.shape[0]
-    dsh_load = pltpu.make_async_copy(dsh_ref, sh, sems.new())
-    dsh_load.start()
+    inputs = []
+    for src, dst in (
+        (grad_second_hbm, grad_second_ref),
+        (dsh_ref, sh),
+        (qx_hbm, qx),
+        (gx_hbm, gx),
+        (stats_hbm, stats),
+        (kb_hbm, kb),
+        (qb_hbm, qb),
+        (n_t_hbm, n_t),
+        (m_t_hbm, m_t),
+        (cosr_hbm, cosr),
+        (sinr_hbm, sinr),
+        (tok_hbm, tok),
+        (pack_hbm, pack_ref),
+        (pack_grad_hbm, pack_grad_ref),
+    ):
+        inputs.append(pltpu.make_async_copy(src, dst, sems.new()))
+        inputs[-1].start()
     loads = [
         pltpu.make_async_copy(kv_ref.at[:, :, mine], kv.at[:, :, pl.ds(0, half)], sems.new()),
         pltpu.make_async_copy(kv_ref.at[:, :, values], kv.at[:, :, pl.ds(half, half)], sems.new()),
@@ -1174,10 +1288,13 @@
         asides[-1].start()
         return asides[-1]
 
+    shared_x = aside(side_ref, sh_land)
+    inputs[0].wait()
     grad_second = grad_second_ref[...]
     ga[...] = grad_second.astype(BF)
     grads_w = Gather(spot, ga, lambda w: ga4.at[w], sems)
-    dsh_load.wait()
+    for copy in inputs[1:]:
+        copy.wait()
     shared = Reduce(spot, sh, None, sh_zo, sh_zi, sem_sh, folded=True, parts=2)
     shared.launch(1)
     shared.relay(3, settled=True)
@@ -1194,8 +1311,12 @@
         across.append(remote(src, dst, sems.new(), sems.new(), spot.across))
         across[-1].start()
 
-    left = pl.ds(done, shard - done)
-    send_across(give_ref.at[0, left], other_out.at[0, left])
+    def send_give(a, start, count):
+        at = pl.ds(start, count)
+        send_across(give_ref.at[a, at], other_out.at[a, at])
+
+    third = shard // 3
+    send_give(1, 0, third)
     dq[...] = jnp.zeros_like(dq)
     loads[0].wait()
     loads[1].wait()
@@ -1231,47 +1352,50 @@
     kv_grad.launch(3)
     chunk(2)
     kv_grad.launch(2)
-    shared.relay(1)
     chunk(1)
     kv_grad.launch(1)
+    normed_w.finish()
+    normed_x = aside(n_all.at[spot.x], n_all.at[spot.x])
+    shared.relay(1)
+    kv_grad.relay(3, parts=(0,))
     chunk(0)
-    cosine, sine = cosr[...].reshape(2 * rows, PAIR), sinr[...].reshape(2 * rows, PAIR)
     for owner in range(2):
         at = spot.x if owner == 0 else 1 - spot.x
         parts = [unstack_pair(dq[group * owner + i]) for i in range(group)]
         gq[at] = turn(jnp.concatenate(parts, axis=1), cosr[at], -sinr[at]).astype(BF)
     query_w = Gather(spot, gq, lambda w: gq4.at[w], sems)
-    shared.last(sh_sum)
-    sh_chunk[...] = sh_sum[...].astype(BF)
-    part = 2 * shard // 2
-
-    def piece(w):
-        return sh_chunk.at[pl.ds(pl.multiple_of(part * w, 64), part)]
-
-    def place(w):
-        return r3.at[spot.k, pl.ds(pl.multiple_of(part * w, 64), part)]
-
-    shared_w = Spread(spot, piece, place, sems)
-    rest = sh_chunk.shape[0] - 4 * part
-    r3[spot.k, pl.ds(4 * part, rest)] = sh_chunk[pl.ds(4 * part, rest)]
-    send_across(give_ref.at[1], other_out.at[1])
-    kv_grad.relay(3)
-    shared_w.finish()
-    ring3 = Ring(spot, r3, ring_recv, ring_send, parts=2)
-    ring3.start()
-    normed_w.finish()
-    normed_x = aside(n_all.at[spot.x], n_all.at[spot.x])
     grads_w.forward()
     mixed_w.finish()
     grads_w.finish()
-    kv_grad.relay(2)
     out_grad = nn(m_all[...], ga4[...].reshape(4 * rows, width)).astype(BF)
     for x in range(2):
         o_send[x] = out_grad[:, half * x : half * (x + 1)]
     out_x = aside(o_send.at[1 - spot.x], o_land)
-    kv_grad.relay(1)
-    ring3.step(1, only=0)
-    ring3.step(2, only=1)
+    shared_x.wait_recv()
+    sh[spot.z] = (sh[spot.z].astype(F32) + sh_land[...].astype(F32)).astype(BF)
+    shared.last(sh_sum)
+    kv_grad.relay(3, parts=(1,))
+    sh_chunk[...] = sh_sum[...].astype(BF)
+    part = 2 * shard // 2
+
+    def piece(w):
+        return sh_chunk.at[pl.ds(pl.multiple_of(part * w, 64), part)]
+
+    def place(w):
+        return r3.at[spot.k, pl.ds(pl.multiple_of(part * w, 64), part)]
+
+    shared_w = Spread(spot, piece, place, sems)
+    rest = sh_chunk.shape[0] - 4 * part
+    r3[spot.k, pl.ds(4 * part, rest)] = sh_chunk[pl.ds(4 * part, rest)]
+    send_give(1, third, shard - third)
+    kv_grad.relay(2, parts=(0,))
+    kv_grad.relay(1, parts=(0,))
+    shared_w.finish()
+    ring3 = Ring(spot, r3, ring_recv, ring_send, parts=2)
+    ring3.start(only=0)
+    kv_grad.relay(2, parts=(1,))
+    kv_grad.relay(1, parts=(1,))
+    ring3.start(only=1)
     for copy in loads[2:5]:
         copy.wait()
     flat = gq[...].reshape(2 * rows, half)
@@ -1295,30 +1419,38 @@
     first = Reduce(spot, a1, None, a1_zo, a1_zi, sem_a1, folded=True)
     for number in (3, 2, 1):
         first.launch(number)
-    kv_grad.last(kv_sum)
-    gkv[:, :, 0:half] = (
-        turn(kv_sum[:, 0:half], cosine, -sine).astype(BF).reshape(2, rows, half)
-    )
-    gkv[:, :, half:width] = kv_sum[:, half:width].astype(BF).reshape(2, rows, half)
-    kv_w = Gather(spot, gkv, lambda w: gkv4.at[w], sems)
+    kv_w = []
+    for r in range(2):
+        at = slice(rows * r, rows * (r + 1))
+        kv_grad.last(kv_sum, parts=(r,))
+        gkv[r, :, 0:half] = turn(kv_sum[at, 0:half], cosr[r], -sinr[r]).astype(BF)
+        gkv[r, :, half:width] = kv_sum[at, half:width].astype(BF)
+        kv_w.append(Gather(spot, gkv.at[r], lambda w, r=r: gkv4.at[w, r], sems))
     flat = gkv[...].reshape(2 * rows, width)
     grad_normed = grad_normed + nt(flat[:, 0:half], w_half[1]) + nt(flat[:, half:width], w_half[2])
     gn_send[...] = grad_normed.astype(BF).reshape(2, rows, width)
     normed_grad_x = aside(gn_send.at[1 - spot.x], gn_land)
+    ring3.step(1, only=0)
+    ring3.step(2, only=1)
     ring3.step(1, only=1)
-    ring3.step(2, only=0)
     first.relay(3)
     first.relay(2)
-    first.relay(1)
-    ring3.step(3, only=1)
-    kv_w.forward()
-    kv_w.finish()
+    for part_w in kv_w:
+        part_w.forward()
+    for part_w in kv_w:
+        part_w.finish()
     both = weight_grad(gkv4).astype(BF)
     for plane in range(4):
         a2[plane] = both[size * plane : size * (plane + 1)]
     second = Reduce(spot, a2, None, a2_zo, a2_zi, sem_a2, folded=True)
     for number in (3, 2, 1):
         second.launch(number)
+    first.relay(1)
+    ring3.step(2, only=0)
+    second.relay(3)
+    second.relay(2)
+    second.relay(1)
+    ring3.step(3, only=1)
     normed_grad_x.wait_recv()
     grad_normed = gn_send[spot.x].astype(F32) + gn_land[...].astype(F32)
     inputs = tok[...].astype(F32)
@@ -1331,25 +1463,23 @@
     gain_grad = jnp.sum(grad_normed * inputs * scale, axis=0, keepdims=True)
     pk[...] = jnp.concatenate([gain_grad, pack_grad_ref[1:16]], axis=0).astype(BF)
     pack_w = Gather(spot, pk, lambda w: pk4.at[w], sems)
-    send_across(give_ref.at[2], other_out.at[2])
-    second.relay(3)
+    send_give(0, done, shard - done)
+    send_give(2, 0, shard)
     first.last(a1_sum)
     r1[spot.k] = a1_sum[...].astype(BF)
-    ring1 = Ring(spot, r1, ring_recv, ring_send, first=(16, 22))
+    ring1 = Ring(spot, r1, ring_recv, ring_send, first=(16, 28))
     ring1.start()
-    second.relay(2)
-    second.relay(1)
-    ring3.step(3, only=0)
     pack_w.forward()
     pack_w.finish()
     extra = sum(pk4[w].astype(F32) for w in range(4)).astype(BF)
-    ring1.step(1)
-    ring1.step(2, only=1)
     second.last(a2_sum)
     r2[spot.k, 0:size] = a2_sum[...].astype(BF)
     r2[spot.k, size : size + 16] = extra
-    ring2 = Ring(spot, r2, ring_recv, ring_send, first=(24, 33))
+    ring2 = Ring(spot, r2, ring_recv, ring_send, first=(24, 39))
     ring2.start()
+    ring3.step(3, only=0)
+    ring1.step(1)
+    ring1.step(2, only=1)
     ring1.step(3, only=1)
     ring1.step(2, only=0)
     ring1.step(3, only=0)
@@ -1370,7 +1500,7 @@
         copy.wait_recv()
     for copy in across + asides:
         copy.wait_send()
-    for part_w in (grads_w, normed_w, mixed_w, query_w, shared_w, kv_w, pack_w):
+    for part_w in [grads_w, normed_w, mixed_w, query_w, shared_w, pack_w] + kv_w:
         part_w.drain()
     for part_w in (shared, kv_grad, first, second, ring1, ring2, ring3):
         part_w.drain()
@@ -1379,7 +1509,8 @@
 
 
 def run_backward(
-    grad_second, tok, pack, pack_grad, n_t, m_t, qx, gx, stats, cosr, sinr, kb, qb, dsh, kv, wfull,
+    grad_second, tok, pack, pack_grad, n_t, m_t, qx, gx, stats, cosr, sinr, kb, qb, side, dsh, kv,
+    wfull,
     give, other,
 ):
     rows, width = tok.shape
@@ -1409,9 +1540,22 @@
             shape((ranks, tall, 128), BF),
             shape((3, shard, hidden), BF),
         ),
-        in_specs=[vm] * 13 + [any_] * 5,
+        in_specs=[any_] * 19,
         out_specs=(vm, vm, any_, any_, any_, any_),
         scratch_shapes=[
+            full(rows, width),
+            low(rows, width),
+            full(16, width),
+            full(16, width),
+            low(width, rows),
+            low(width, rows),
+            low(pairs, 2 * rows, PAIR),
+            low(pairs, 2 * rows, PAIR),
+            full(2, 2 * rows, PAIR),
+            full(2, rows, PAIR),
+            full(2, rows, PAIR),
+            VMEM((1, ranks * rows), jnp.int32),
+            VMEM((2, 2 * rows, 1), jnp.int32),
             low(3, width, half),
             low(ranks, rows, width),
             low(4, 2 * rows, width),
@@ -1444,6 +1588,7 @@
             low(ranks, size, width),
             low(ranks, size + 16, width),
             low(4, tall, 128),
+            low(tall, 128),
             low(4, tall, 128),
             low(4, tall, 128),
             full(tall, 128),
@@ -1455,13 +1600,13 @@
             dma((3, 4)),
             dma((3, 8)),
             dma((4 * ranks,)),
-            dma((44,)),
+            dma((SEMS_RINGS,)),
         ],
         compiler_params=pltpu.CompilerParams(
             collective_id=3, has_side_effects=True, vmem_limit_bytes=VMEM_BYTES
         ),
     )(
-        grad_second, tok, pack, pack_grad, n_t, m_t, qx, gx, stats, cosr, sinr, kb, qb, dsh, kv,
+        grad_second, tok, pack, pack_grad, n_t, m_t, qx, gx, stats, cosr, sinr, kb, qb, side, dsh, kv,
         wfull, give, other,
     )
 
@@ -1485,19 +1630,19 @@
     size = gate.shape[0]
     shard = 4 * size
     width = 4 * shard
-    row, within = lax.div(i, 2), lax.rem(i, 2) * size
+    within = lax.rem(i, 2) * size
     for c in range(4):
         for w in range(4):
             lanes = slice(512 * w + 128 * c, 512 * w + 128 * (c + 1))
             start = pl.multiple_of(shard * w + within, 16)
-            gate[:, lanes] = sh[4 * row + c, pl.ds(start, size)].astype(F32)
+            gate[:, lanes] = sh[c, pl.ds(start, size)].astype(F32)
             start = pl.multiple_of(shard * w + shard // 2 + within, 16)
-            up[:, lanes] = sh[4 * row + c, pl.ds(start, size)].astype(F32)
+            up[:, lanes] = sh[c, pl.ds(start, size)].astype(F32)
     deep = down.shape[0] // 2
     for r in range(2):
         for t in range(width // 128):
             at = slice(width + deep * t, width + deep * (t + 1))
-            down[deep * r : deep * (r + 1), 128 * t : 128 * (t + 1)] = sh[2 * i + r, at].astype(F32)
+            down[deep * r : deep * (r + 1), 128 * t : 128 * (t + 1)] = sh[2 * lax.rem(i, 2) + r, at].astype(F32)
 
     @pl.when(i == 0)
     def _():
@@ -1542,7 +1687,7 @@
             whole(*pack.shape),
             att(size),
             att(size + 16),
-            whole(*sh.shape),
+            pl.BlockSpec((4,) + sh.shape[1:], lambda i: (i // 2, 0, 0)),
             stack(3, size, hidden),
             stack(3, size, hidden),
         ],
@@ -2083,16 +2228,16 @@
     frequency = jnp.asarray(np.tile(frequency, 4)[None].astype(np.float32))
     (
         cosr, sinr, kb, qb, qx, gx, stats, n_t, m_t, pack_all, result, grad_second, pack_grad, dsh,
-        kv_all, wfull, keep, give, other,
+        side, kv_all, wfull, keep, give, other,
     ) = run_forward(
-        tokens[0], jnp.stack([gain_attention, gain_mixer]), router_weight.T, frequency, block_deal,
+        tokens[0], gain_attention, gain_mixer, router_weight.T, frequency, block_deal,
         cotangent[0], routes[0].T, slot_order[0],
         shared_down, query_weight, key_weight, value_weight, output_weight, shared_gate, shared_up,
         expert_gate, expert_up, expert_down,
     )
     grad_input, pack_sum, att1, att2, sh, other = run_backward(
         grad_second, tokens[0], pack_all, pack_grad, n_t, m_t, qx, gx, stats, cosr, sinr, kb, qb,
-        dsh, kv_all, wfull, give, other,
+        side, dsh, kv_all, wfull, give, other,
     )
     (
         result, grad_input, gain_one, gain_two, router, query, key, value, output, gate, up, down,

time: 226 us -> 214 us (0.947)
  Pallas kernels: 223 us -> 213 us
    pallas_call x1, Pallas kernels: 129 us -> 121 us  [run_forward(): pl.pallas_call(forward_kernel, out_shape=(shape((2, rows, PAIR), F32), sh...]
    pallas_call x1, Pallas kernels: 85.3 us -> 82.9 us  [run_backward(): pl.pallas_call(backward_kernel, out_shape=(shape((rows, width), F32), sha...]
where the time goes in v8:
time: 214 us
  Pallas kernels  213 us (100%)
    pallas_call x1, Pallas kernels, run_forward(): pl.pallas_call(forward_kernel, out_shape=(shape((2, rows, PAIR), F32), sh...  121 us
    pallas_call x1, Pallas kernels, run_backward(): pl.pallas_call(backward_kernel, out_shape=(shape((rows, width), F32), sha...  82.9 us
    pallas_call x1, Pallas kernels, run_unpack(): pl.pallas_call(unpack_kernel, grid=(steps,), out_shape=(shape((rows, widt...  9.12 us

profile of v8, /device:TPU:0, one launch (start us, length us, event | category | flops | bytes accessed | tf_op | source)
XLA Modules:
  0.0 213.5 jit_solution(5256968004175119716)
XLA Ops:
  0.7 120.6 %shard_map.298 = (f32[2,128,128]{2,1,0:T(8,128)}, f32[2,128,128]{2,1,0:T(8,128)}, s32[1,1024]{1,0:T(1,128)}, s32[2,256,1]{2,1,0:T(8,128)}, bf16[6,256,128]{2,1,0...) custom-call(bf16[128,768]{1,0:T(8,128)(2,1)} %bitcast.14, ...), custom_call_target="tpu_custom_call" | custom-call | tf_op jit(solution)/shard_map/pallas_call | solution.py:1131
  121.2 82.9 %shard_map.299 = (f32[128,768]{1,0:T(8,128)}, f32[16,768]{1,0:T(8,128)}, bf16[8,48,768]{2,1,0:T(8,128)(2,1)}, bf16[8,64,768]{2,1,0:T(8,128)(2,1)}, bf16[8,1152,1...) custom-call(f32[128,768]{1,0:T(8,128)} %get-tuple-element.57.grad_second_hbm, bf16[128,768]{1,0:T(8,128)(2,1)} %bitcast.15, ...), custom_call_target="tpu_custom_call" | custom-call | tf_op jit(solution)/shard_map/pallas_call | solution.py:1533
  204.2 9.1 %shard_map.300 = (bf16[128,768]{1,0:T(8,128)(2,1)}, f32[128,768]{1,0:T(8,128)}, f32[1,192]{1,0:T(1,128)}, f32[1,192]{1,0:T(1,128)}, f32[8,192]{1,0:T(8,128)}, /*...) custom-call(bf16[128,768]{1,0:T(8,128)(2,1)} %get-tuple-element.56.r, ...), custom_call_target="tpu_custom_call" | custom-call | tf_op jit(solution)/shard_map/pallas_call | solution.py:1670

commit v9 on v8

--- a/solution.py
+++ b/solution.py
@@ -22,9 +22,10 @@
 F32 = jnp.float32
 PAIR = 2 * HD
 VMEM_BYTES = 127 * 2**19
-SEMS_FORWARD = 207
-SEMS_BACKWARD = 95
+SEMS_FORWARD = 204
+SEMS_BACKWARD = 102
 SEMS_RINGS = 48
+SEMS_LAYOUT = 34
 
 
 class Spot:
@@ -670,10 +671,10 @@
 def forward_kernel(
     tok, gain_one, gain_two, router_ref, freq, deal, cot, routes, order, sd,
     wq, wk, wv, wo, sg, su, eg, eu, ed,
-    cosr_out, sinr_out, kb_out, qb_out, qx_out, gx_out, stats_hbm, normed_hbm, mixed_hbm, pack_hbm,
+    cosr_out, sinr_out, kb_out, qb_out, qx_out, gm_out, stats_hbm, stat_out, normed_hbm, mixed_hbm, pack_hbm,
     result_hbm, grad_second_hbm, pack_grad_hbm, dsh_out, side_out, kv_out, wfull_out, keep_out, give_out, other_out,
-    cosr, sinr, kb, qb, qx, gx, stats_out, normed_out, mixed_out, pack_out, result_out,
-    grad_second_out, pack_grad_out, wbuf, kv, q_s, qc, q_land, gm, gm_land, stat, stat_land, mixed, pack, packs, top, low, acc, sg_all, su_all, wg, wu, wd, mix, m4, cot4,
+    cosr, sinr, kb, qb, qx, stats_out, normed_out, mixed_out, pack_out, result_out,
+    grad_second_out, pack_grad_out, wbuf, kv, q_s, qc, q_land, gm, stat, mixed, pack, packs, top, low, acc, sg_all, su_all, wg, wu, wd, mix, m4, cot4,
     sh_send, sh_recv, gm_send, gm_recv, xs, xr, gs, gr, orr, br,
     x_s, g_s, sum_s, gate_s, up_s, hid_s, dgate_s, dup_s, dsh, dsh_x, dsh_z, slot_s, pair_s, cb,
     sem, kv_recv, kv_send, a2a_send, a2a_recv, sem_sh,
@@ -782,14 +783,15 @@
     acc[...] = jnp.zeros_like(acc)
     q_block = qb[spot.x]
 
-    def chunk(plane):
-        k_block = kb[:, pl.ds(pl.multiple_of(2 * rows * plane, 2 * rows), 2 * rows)]
+    def chunk(slot, count):
+        keys = count * rows
+        k_block = kb[:, pl.ds(pl.multiple_of(rows * slot, rows), keys)]
         allowed = k_block <= q_block
 
         def one_pair(j, carry):
             lane = pl.multiple_of(PAIR * j, PAIR)
-            key = kv[pl.ds(2 * plane, 2), :, pl.ds(lane, PAIR)].reshape(2 * rows, PAIR)
-            value = kv[pl.ds(2 * plane, 2), :, pl.ds(width + lane, PAIR)].reshape(2 * rows, PAIR)
+            key = kv[pl.ds(slot, count), :, pl.ds(lane, PAIR)].reshape(keys, PAIR)
+            value = kv[pl.ds(slot, count), :, pl.ds(width + lane, PAIR)].reshape(keys, PAIR)
             scores = jnp.where(allowed, nt(q_s[j], key), MASKED)
             old = top[j]
             new = jnp.maximum(old, jnp.max(scores, axis=1, keepdims=True))
@@ -805,21 +807,22 @@
     ring.step(1)
     ring.step(2, only=1)
     ring.other(0)
-    chunk(spot.plane(0))
+    chunk(2 * spot.plane(0), 2)
     ring.step(2, only=0)
     ring.step(3, only=1)
     ring.other(1)
-    chunk(spot.plane(1))
+    chunk(2 * spot.plane(1), 2)
     ring.step(3, only=0)
     out_w.forward()
     sg_w.forward()
     su_w.forward()
     ring.other(2)
-    chunk(spot.plane(2))
+    chunk(2 * spot.plane(2), 2)
     out_w.second()
     cot_w.forward()
+    chunk(2 * spot.plane(3) + spot.x, 1)
     ring.other(3)
-    chunk(spot.plane(3))
+    chunk(2 * spot.plane(3) + 1 - spot.x, 1)
     sg_w.second()
     su_w.second()
     saves = []
@@ -1048,7 +1051,6 @@
     group = half // PAIR
     for x in range(2):
         gm[x] = grad_mixed[:, half * x : half * (x + 1)]
-    grads_x = aside(gm.at[1 - spot.x], gm_land)
     product = grad_mixed.astype(F32) * mixed[...]
     lane = lax.broadcasted_iota(jnp.int32, (2 * rows, PAIR), 1)
     mine = jnp.zeros((2 * rows, PAIR), F32)
@@ -1064,23 +1066,15 @@
         mine = jnp.where(lane == group + i, jnp.where(swap, delta[1], delta[0]), mine)
         theirs = jnp.where(lane == group + i, jnp.where(swap, delta[0], delta[1]), theirs)
         qx[i] = stack_pair(qc[spot.x, :, PAIR * i : PAIR * (i + 1)])
-        gx[i] = stack_pair(gm[spot.x, :, PAIR * i : PAIR * (i + 1)])
     stat[...] = theirs.T[0:8]
-    stat_x = aside(stat, stat_land)
-    stats_out[0] = mine
+    stats_out[...] = mine
     gain_grad = jnp.sum(grad_mixer * second * scale, axis=0, keepdims=True)
     pack_grad_out[...] = jnp.concatenate(
         [jnp.zeros_like(gain_grad), gain_grad, router_grad[:14]], axis=0
     )
     query_x.wait_recv()
-    grads_x.wait_recv()
     for i in range(group):
         qx[group + i] = stack_pair(q_land[:, PAIR * i : PAIR * (i + 1)])
-        gx[group + i] = stack_pair(gm_land[:, PAIR * i : PAIR * (i + 1)])
-    stat_x.wait_recv()
-    stats_out[1] = jnp.concatenate(
-        [stat_land[...], jnp.zeros((PAIR - 8, 2 * rows), F32)], axis=0
-    ).T
     for number in (3, 2):
         shared_grad.absorb(number)
     for plane in range(4):
@@ -1088,8 +1082,9 @@
     save(dsh.at[2 * spot.z + 1 - spot.x], side_out)
     for src, dst in (
         (qx, qx_out),
-        (gx, gx_out),
+        (gm, gm_out),
         (stats_out, stats_hbm),
+        (stat, stat_out),
         (pack_grad_out, pack_grad_hbm),
     ):
         save(src, dst)
@@ -1136,8 +1131,9 @@
             shape((1, ranks * rows), jnp.int32),
             shape((2, 2 * rows, 1), jnp.int32),
             shape((pairs, 2 * rows, PAIR), BF),
-            shape((pairs, 2 * rows, PAIR), BF),
-            shape((2, 2 * rows, PAIR), F32),
+            shape((2, rows, width // 2), BF),
+            shape((2 * rows, PAIR), F32),
+            shape((8, 2 * rows), F32),
             shape((width, rows), BF),
             shape((width, rows), BF),
             shape((16, width), F32),
@@ -1153,15 +1149,14 @@
             shape((2 * shard // 3, hidden), BF),
         ),
         in_specs=[vm] * 5 + [pl.BlockSpec(memory_space=pltpu.SMEM)] + [vm] * 4 + [any_] * 9,
-        out_specs=tuple([any_] * 20),
+        out_specs=tuple([any_] * 21),
         scratch_shapes=[
             full(2, rows, PAIR),
             full(2, rows, PAIR),
             VMEM((1, ranks * rows), jnp.int32),
             VMEM((2, 2 * rows, 1), jnp.int32),
             low(pairs, 2 * rows, PAIR),
-            low(pairs, 2 * rows, PAIR),
-            full(2, 2 * rows, PAIR),
+            full(2 * rows, PAIR),
             low(width, rows),
             low(width, rows),
             full(16, width),
@@ -1174,8 +1169,6 @@
             low(2, rows, width // 2),
             low(rows, width // 2),
             low(2, rows, width // 2),
-            low(rows, width // 2),
-            full(8, 2 * rows),
             full(8, 2 * rows),
             full(rows, width),
             low(16, width),
@@ -1227,11 +1220,11 @@
 
 
 def backward_kernel(
-    grad_second_hbm, tok_hbm, pack_hbm, pack_grad_hbm, n_t_hbm, m_t_hbm, qx_hbm, gx_hbm, stats_hbm,
+    grad_second_hbm, tok_hbm, pack_hbm, pack_grad_hbm, n_t_hbm, m_t_hbm, qx_hbm, gm_hbm, stats_hbm, stat_hbm,
     cosr_hbm, sinr_hbm, kb_hbm, qb_hbm, side_ref, dsh_ref, kv_ref, wfull_ref, give_ref, other_ref,
     grad_input_out, pack_out, att1_out, att2_out, sh_out, other_out,
-    grad_second_ref, tok, pack_ref, pack_grad_ref, n_t, m_t, qx, gx, stats, cosr, sinr, kb, qb,
-    w_half, kv, kvb, kv_zo, kv_zi, kv_sum, dq, ga, ga4, gq, gq4, gkv, gkv4, n_all, m_all, pk, pk4,
+    grad_second_ref, tok, pack_ref, pack_grad_ref, n_t, m_t, qx, gm, stats, stat, cosr, sinr, kb, qb,
+    gx, gm_land, stat_land, w_half, kv, kvb, kv_zo, kv_zi, kv_sum, dq, ga, ga4, gq, gq4, gkv, gkv4, n_all, m_all, pk, pk4,
     o_send, o_land, gn_send, gn_land, a1, a1_zo, a1_zi, a1_sum, a2, a2_zo, a2_zi, a2_sum, r1, r2,
     sh, sh_land, sh_zo, sh_zi, sh_sum, sh_chunk, r3,
     sem, sem_kv, sem_a1, sem_a2, sem_sh, ring_recv, ring_send,
@@ -1245,25 +1238,28 @@
     mine = pl.ds(pl.multiple_of(half * spot.x, half), half)
     values = pl.ds(pl.multiple_of(width + half * spot.x, half), half)
     ranks = kv.shape[0]
-    inputs = []
-    for src, dst in (
-        (grad_second_hbm, grad_second_ref),
-        (dsh_ref, sh),
-        (qx_hbm, qx),
-        (gx_hbm, gx),
-        (stats_hbm, stats),
-        (kb_hbm, kb),
-        (qb_hbm, qb),
-        (n_t_hbm, n_t),
-        (m_t_hbm, m_t),
-        (cosr_hbm, cosr),
-        (sinr_hbm, sinr),
-        (tok_hbm, tok),
-        (pack_hbm, pack_ref),
-        (pack_grad_hbm, pack_grad_ref),
-    ):
-        inputs.append(pltpu.make_async_copy(src, dst, sems.new()))
-        inputs[-1].start()
+    sources = dict(
+        gm=(gm_hbm, gm),
+        stat=(stat_hbm, stat),
+        dsh=(dsh_ref, sh),
+        second=(grad_second_hbm, grad_second_ref),
+        n_t=(n_t_hbm, n_t),
+        m_t=(m_t_hbm, m_t),
+        qx=(qx_hbm, qx),
+        stats=(stats_hbm, stats.at[0]),
+        kb=(kb_hbm, kb),
+        qb=(qb_hbm, qb),
+        cosr=(cosr_hbm, cosr),
+        sinr=(sinr_hbm, sinr),
+        tok=(tok_hbm, tok),
+        pack=(pack_hbm, pack_ref),
+        pack_grad=(pack_grad_hbm, pack_grad_ref),
+    )
+    inputs = {
+        name: pltpu.make_async_copy(src, dst, sems.new()) for name, (src, dst) in sources.items()
+    }
+    for copy in inputs.values():
+        copy.start()
     loads = [
         pltpu.make_async_copy(kv_ref.at[:, :, mine], kv.at[:, :, pl.ds(0, half)], sems.new()),
         pltpu.make_async_copy(kv_ref.at[:, :, values], kv.at[:, :, pl.ds(half, half)], sems.new()),
@@ -1288,17 +1284,22 @@
         asides[-1].start()
         return asides[-1]
 
+    inputs["gm"].wait()
+    inputs["stat"].wait()
+    grads_x = aside(gm.at[1 - spot.x], gm_land)
+    stat_x = aside(stat, stat_land)
     shared_x = aside(side_ref, sh_land)
-    inputs[0].wait()
-    grad_second = grad_second_ref[...]
-    ga[...] = grad_second.astype(BF)
-    grads_w = Gather(spot, ga, lambda w: ga4.at[w], sems)
-    for copy in inputs[1:]:
-        copy.wait()
+    inputs["dsh"].wait()
     shared = Reduce(spot, sh, None, sh_zo, sh_zi, sem_sh, folded=True, parts=2)
     shared.launch(1)
     shared.relay(3, settled=True)
     shared.relay(2, settled=True)
+    inputs["second"].wait()
+    grad_second = grad_second_ref[...]
+    ga[...] = grad_second.astype(BF)
+    grads_w = Gather(spot, ga, lambda w: ga4.at[w], sems)
+    inputs["n_t"].wait()
+    inputs["m_t"].wait()
 
     def columns(ref):
         return lambda w: ref.at[:, pl.ds(pl.multiple_of(rows * w, 128), rows)]
@@ -1318,8 +1319,17 @@
     third = shard // 3
     send_give(1, 0, third)
     dq[...] = jnp.zeros_like(dq)
+    for name in ("qx", "stats", "kb", "qb", "cosr", "sinr", "tok", "pack", "pack_grad"):
+        inputs[name].wait()
     loads[0].wait()
     loads[1].wait()
+    for i in range(group):
+        gx[i] = stack_pair(gm[spot.x, :, PAIR * i : PAIR * (i + 1)])
+    grads_x.wait_recv()
+    for i in range(group):
+        gx[group + i] = stack_pair(gm_land[:, PAIR * i : PAIR * (i + 1)])
+    stat_x.wait_recv()
+    stats[1] = jnp.concatenate([stat_land[...], jnp.zeros((PAIR - 8, 2 * rows), F32)], axis=0).T
 
     def chunk(number):
         plane = spot.plane(number)
@@ -1363,7 +1373,6 @@
         at = spot.x if owner == 0 else 1 - spot.x
         parts = [unstack_pair(dq[group * owner + i]) for i in range(group)]
         gq[at] = turn(jnp.concatenate(parts, axis=1), cosr[at], -sinr[at]).astype(BF)
-    query_w = Gather(spot, gq, lambda w: gq4.at[w], sems)
     grads_w.forward()
     mixed_w.finish()
     grads_w.finish()
@@ -1387,7 +1396,8 @@
     shared_w = Spread(spot, piece, place, sems)
     rest = sh_chunk.shape[0] - 4 * part
     r3[spot.k, pl.ds(4 * part, rest)] = sh_chunk[pl.ds(4 * part, rest)]
-    send_give(1, third, shard - third)
+    query_w = Gather(spot, gq, lambda w: gq4.at[w], sems)
+    send_give(1, third, third)
     kv_grad.relay(2, parts=(0,))
     kv_grad.relay(1, parts=(0,))
     shared_w.finish()
@@ -1426,6 +1436,8 @@
         gkv[r, :, 0:half] = turn(kv_sum[at, 0:half], cosr[r], -sinr[r]).astype(BF)
         gkv[r, :, half:width] = kv_sum[at, half:width].astype(BF)
         kv_w.append(Gather(spot, gkv.at[r], lambda w, r=r: gkv4.at[w, r], sems))
+    send_give(1, 2 * third, third)
+    send_give(0, done, shard - done)
     flat = gkv[...].reshape(2 * rows, width)
     grad_normed = grad_normed + nt(flat[:, 0:half], w_half[1]) + nt(flat[:, half:width], w_half[2])
     gn_send[...] = grad_normed.astype(BF).reshape(2, rows, width)
@@ -1463,7 +1475,6 @@
     gain_grad = jnp.sum(grad_normed * inputs * scale, axis=0, keepdims=True)
     pk[...] = jnp.concatenate([gain_grad, pack_grad_ref[1:16]], axis=0).astype(BF)
     pack_w = Gather(spot, pk, lambda w: pk4.at[w], sems)
-    send_give(0, done, shard - done)
     send_give(2, 0, shard)
     first.last(a1_sum)
     r1[spot.k] = a1_sum[...].astype(BF)
@@ -1509,7 +1520,7 @@
 
 
 def run_backward(
-    grad_second, tok, pack, pack_grad, n_t, m_t, qx, gx, stats, cosr, sinr, kb, qb, side, dsh, kv,
+    grad_second, tok, pack, pack_grad, n_t, m_t, qx, gm, stats, stat, cosr, sinr, kb, qb, side, dsh, kv,
     wfull,
     give, other,
 ):
@@ -1540,7 +1551,7 @@
             shape((ranks, tall, 128), BF),
             shape((3, shard, hidden), BF),
         ),
-        in_specs=[any_] * 19,
+        in_specs=[any_] * 20,
         out_specs=(vm, vm, any_, any_, any_, any_),
         scratch_shapes=[
             full(rows, width),
@@ -1550,12 +1561,16 @@
             low(width, rows),
             low(width, rows),
             low(pairs, 2 * rows, PAIR),
-            low(pairs, 2 * rows, PAIR),
+            low(2, rows, half),
             full(2, 2 * rows, PAIR),
+            full(8, 2 * rows),
             full(2, rows, PAIR),
             full(2, rows, PAIR),
             VMEM((1, ranks * rows), jnp.int32),
             VMEM((2, 2 * rows, 1), jnp.int32),
+            low(pairs, 2 * rows, PAIR),
+            low(rows, half),
+            full(8, 2 * rows),
             low(3, width, half),
             low(ranks, rows, width),
             low(4, 2 * rows, width),
@@ -1606,70 +1621,95 @@
             collective_id=3, has_side_effects=True, vmem_limit_bytes=VMEM_BYTES
         ),
     )(
-        grad_second, tok, pack, pack_grad, n_t, m_t, qx, gx, stats, cosr, sinr, kb, qb, side, dsh, kv,
+        grad_second, tok, pack, pack_grad, n_t, m_t, qx, gm, stats, stat, cosr, sinr, kb, qb, side, dsh, kv,
         wfull, give, other,
     )
 
 
 def unpack_kernel(
-    result, grad_input, pack, att1, att2, sh, keep, other,
-    result_out, grad_input_out, gain_one, gain_two, router,
-    query, key, value, output, gate, up, down, eg, eu, ed,
+    result_hbm, grad_input_hbm, pack_hbm, att1_hbm, att2_hbm, sh_hbm, keep_hbm, other_hbm,
+    result_out, grad_input_out, gain_one_out, gain_two_out, router_out,
+    query_out, key_out, value_out, output_out, gate_out, up_out, down_out, eg_out, eu_out, ed_out,
+    result, grad_input, pack, att1, att2, sh, keep, other, experts_f, both_f, down, att_f,
+    gains, router, sem,
 ):
-    i = pl.program_id(0)
-    result_out[...] = result[...]
-    grad_input_out[...] = grad_input[...]
-    half = query.shape[1] // 2
-    size = query.shape[0]
-    for x in range(2):
-        lanes = slice(half * x, half * (x + 1))
-        for ref, src, low in ((output, att1, 0), (query, att1, 1), (key, att2, 0), (value, att2, 1)):
-            ref[:, lanes] = src[0, x, 0:size, half * low : half * (low + 1)].astype(F32)
-    for a, ref in enumerate((eg, eu, ed)):
-        ref[...] = keep[a].astype(F32) + other[a].astype(F32)
-    size = gate.shape[0]
-    shard = 4 * size
+    sems = Sems(sem)
+
+    def copy(src, dst):
+        made = pltpu.make_async_copy(src, dst, sems.new())
+        made.start()
+        return made
+
+    shard, hidden = keep.shape[1:]
     width = 4 * shard
-    within = lax.rem(i, 2) * size
-    for c in range(4):
-        for w in range(4):
-            lanes = slice(512 * w + 128 * c, 512 * w + 128 * (c + 1))
-            start = pl.multiple_of(shard * w + within, 16)
-            gate[:, lanes] = sh[c, pl.ds(start, size)].astype(F32)
-            start = pl.multiple_of(shard * w + shard // 2 + within, 16)
-            up[:, lanes] = sh[c, pl.ds(start, size)].astype(F32)
-    deep = down.shape[0] // 2
-    for r in range(2):
-        for t in range(width // 128):
-            at = slice(width + deep * t, width + deep * (t + 1))
-            down[deep * r : deep * (r + 1), 128 * t : 128 * (t + 1)] = sh[2 * lax.rem(i, 2) + r, at].astype(F32)
-
-    @pl.when(i == 0)
-    def _():
-        back = lax.rem(4 - lax.axis_index("wt"), 4) * shard
-        mine = pltpu.roll(pack[...], back, 1)[:, 0:256]
-        gain_one[...] = mine[0:1, 0:shard]
-        gain_two[...] = mine[1:2, 0:shard]
-        router[...] = mine[2 : 2 + router.shape[0], 0:shard]
+    half = width // 2
+    loads = []
+    for a in range(3):
+        loads.append([copy(keep_hbm.at[a], keep.at[a]), copy(other_hbm.at[a], other.at[a])])
+    shared_loads = [copy(sh_hbm.at[pl.ds(4 * r, 4)], sh.at[pl.ds(4 * r, 4)]) for r in range(2)]
+    att_loads = [copy(att1_hbm, att1), copy(att2_hbm, att2)]
+    small = [copy(pack_hbm, pack), copy(result_hbm, result), copy(grad_input_hbm, grad_input)]
+    saves = []
+    for a, out in enumerate((eg_out, eu_out, ed_out)):
+        for made in loads[a]:
+            made.wait()
+        for part in range(2):
+            at = slice(shard // 2 * part, shard // 2 * (part + 1))
+            experts_f[a, at] = keep[a, at].astype(F32) + other[a, at].astype(F32)
+            saves.append(copy(experts_f.at[a, at], out.at[at]))
+    size = shard // 2
+    deep = down.shape[0] // 8
+    for row in range(2):
+        shared_loads[row].wait()
+        rows = slice(size * row, size * (row + 1))
+        for c in range(4):
+            for w in range(4):
+                lanes = slice(512 * w + 128 * c, 512 * w + 128 * (c + 1))
+                for a in range(2):
+                    start = shard * w + size * a
+                    both_f[a, rows, lanes] = sh[4 * row + c, start : start + size].astype(F32)
+        for a, out in enumerate((gate_out, up_out)):
+            saves.append(copy(both_f.at[a, rows], out.at[rows]))
+        for r in range(4 * row, 4 * row + 4):
+            for t in range(width // 128):
+                at = slice(width + deep * t, width + deep * (t + 1))
+                lanes = slice(128 * t, 128 * (t + 1))
+                down[deep * r : deep * (r + 1), lanes] = sh[r, at].astype(F32)
+        rows = slice(4 * deep * row, 4 * deep * (row + 1))
+        saves.append(copy(down.at[rows], down_out.at[rows]))
+    for made in att_loads:
+        made.wait()
+    slots = att1.shape[1]
+    parts = ((output_out, att1, 0), (query_out, att1, 1), (key_out, att2, 0), (value_out, att2, 1))
+    for n, (out, src, low) in enumerate(parts):
+        for r in range(8):
+            plane, x = r // 2, r % 2
+            rows, lanes = slice(slots * plane, slots * (plane + 1)), slice(half * x, half * (x + 1))
+            att_f[n, rows, lanes] = src[r, 0:slots, half * low : half * (low + 1)].astype(F32)
+        saves.append(copy(att_f.at[n], out))
+    for made in small:
+        made.wait()
+    saves += [copy(result, result_out), copy(grad_input, grad_input_out)]
+    back = lax.rem(4 - lax.axis_index("wt"), 4) * shard
+    mine = pltpu.roll(pack[...], back, 1)
+    gains[0] = mine[0:1, 0:shard]
+    gains[1] = mine[1:2, 0:shard]
+    router[...] = mine[2 : 2 + router.shape[0], 0:shard]
+    saves += [copy(gains.at[0], gain_one_out), copy(gains.at[1], gain_two_out)]
+    saves.append(copy(router, router_out))
+    for made in saves:
+        made.wait()
 
 
 def run_unpack(result, grad_input, pack, att1, att2, sh, keep, other, experts):
     rows, width = result.shape
     shard, hidden = keep.shape[1:]
-    steps = 4
     shape = jax.ShapeDtypeStruct
-    size = shard // steps
-    att1 = att1.reshape(4, 2, size, width)
-    att2 = att2.reshape(4, 2, size + 16, width)
     shared_hidden = sh.shape[0] * (sh.shape[1] - width) * 128 // width
     shared = 4 * shared_hidden
-    by_rows = lambda r, c: pl.BlockSpec((r, c), lambda i: (i, 0))
-    whole = lambda *dims: pl.BlockSpec(dims, lambda i: (0,) * len(dims))
-    stack = lambda n, r, c: pl.BlockSpec((n, r, c), lambda i: (0, i, 0))
-    att = lambda r: pl.BlockSpec((1, 2, r, width), lambda i: (i, 0, 0, 0))
+    any_ = pl.BlockSpec(memory_space=pl.ANY)
     return pl.pallas_call(
         unpack_kernel,
-        grid=(steps,),
         out_shape=(
             shape((rows, width), BF),
             shape((rows, width), F32),
@@ -1681,27 +1721,25 @@
             shape((shared_hidden, width), F32),
             *[shape((shard, hidden), F32)] * 3,
         ),
-        in_specs=[
-            by_rows(rows // steps, width),
-            by_rows(rows // steps, width),
-            whole(*pack.shape),
-            att(size),
-            att(size + 16),
-            pl.BlockSpec((4,) + sh.shape[1:], lambda i: (i // 2, 0, 0)),
-            stack(3, size, hidden),
-            stack(3, size, hidden),
+        in_specs=[any_] * 8,
+        out_specs=tuple([any_] * 15),
+        scratch_shapes=[
+            VMEM((rows, width), BF),
+            VMEM((rows, width), F32),
+            VMEM(pack.shape, F32),
+            VMEM(att1.shape, BF),
+            VMEM(att2.shape, BF),
+            VMEM(sh.shape, BF),
+            VMEM(keep.shape, BF),
+            VMEM(other.shape, BF),
+            VMEM((3, shard, hidden), F32),
+            VMEM((2, shard, shared), F32),
+            VMEM((shared_hidden, width), F32),
+            VMEM((4, shard, width), F32),
+            VMEM((2, 1, shard), F32),
+            VMEM((experts, shard), F32),
+            pltpu.SemaphoreType.DMA((SEMS_LAYOUT,)),
         ],
-        out_specs=(
-            by_rows(rows // steps, width),
-            by_rows(rows // steps, width),
-            whole(1, shard),
-            whole(1, shard),
-            whole(experts, shard),
-            *[by_rows(size, width)] * 4,
-            *[by_rows(size, shared)] * 2,
-            by_rows(shared_hidden // steps, width),
-            *[by_rows(size, hidden)] * 3,
-        ),
         compiler_params=pltpu.CompilerParams(vmem_limit_bytes=VMEM_BYTES),
     )(result, grad_input, pack, att1, att2, sh, keep, other)
 
@@ -2227,7 +2265,7 @@
     frequency = 10000.0 ** (-np.arange(half_size) / half_size)
     frequency = jnp.asarray(np.tile(frequency, 4)[None].astype(np.float32))
     (
-        cosr, sinr, kb, qb, qx, gx, stats, n_t, m_t, pack_all, result, grad_second, pack_grad, dsh,
+        cosr, sinr, kb, qb, qx, gm, stats, stat, n_t, m_t, pack_all, result, grad_second, pack_grad, dsh,
         side, kv_all, wfull, keep, give, other,
     ) = run_forward(
         tokens[0], gain_attention, gain_mixer, router_weight.T, frequency, block_deal,
@@ -2236,7 +2274,7 @@
         expert_gate, expert_up, expert_down,
     )
     grad_input, pack_sum, att1, att2, sh, other = run_backward(
-        grad_second, tokens[0], pack_all, pack_grad, n_t, m_t, qx, gx, stats, cosr, sinr, kb, qb,
+        grad_second, tokens[0], pack_all, pack_grad, n_t, m_t, qx, gm, stats, stat, cosr, sinr, kb, qb,
         side, dsh, kv_all, wfull, give, other,
     )
     (

time: 214 us -> 211 us (0.986)
  Pallas kernels: 213 us -> 210 us
    pallas_call x1, Pallas kernels: 121 us -> 117 us  [run_forward(): pl.pallas_call(forward_kernel, out_shape=(shape((2, rows, PAIR), F32), sh...]
    pallas_call x1, Pallas kernels: 82.9 us -> 85.2 us  [run_backward(): pl.pallas_call(backward_kernel, out_shape=(shape((rows, width), F32), sha...]
where the time goes in v9:
time: 211 us
  Pallas kernels  210 us (100%)
    pallas_call x1, Pallas kernels, run_forward(): pl.pallas_call(forward_kernel, out_shape=(shape((2, rows, PAIR), F32), sh...  117 us
    pallas_call x1, Pallas kernels, run_backward(): pl.pallas_call(backward_kernel, out_shape=(shape((rows, width), F32), sha...  85.2 us
    pallas_call x1, Pallas kernels, run_unpack(): pl.pallas_call(unpack_kernel, out_shape=(shape((rows, width), BF), shape(...  7.78 us

profile of v9, /device:TPU:0, one launch (start us, length us, event | category | flops | bytes accessed | tf_op | source)
XLA Modules:
  0.0 211.1 jit_solution(7420729425538277822)
XLA Ops:
  0.7 117.3 %shard_map.298 = (f32[2,128,128]{2,1,0:T(8,128)}, f32[2,128,128]{2,1,0:T(8,128)}, s32[1,1024]{1,0:T(1,128)}, s32[2,256,1]{2,1,0:T(8,128)}, bf16[6,256,128]{2,1,0...) custom-call(bf16[128,768]{1,0:T(8,128)(2,1)} %bitcast.12, ...), custom_call_target="tpu_custom_call" | custom-call | tf_op jit(solution)/shard_map/pallas_call | solution.py:1126
  118.0 85.2 %shard_map.299 = (f32[128,768]{1,0:T(8,128)}, f32[16,768]{1,0:T(8,128)}, bf16[8,48,768]{2,1,0:T(8,128)(2,1)}, bf16[8,64,768]{2,1,0:T(8,128)(2,1)}, bf16[8,1152,1...) custom-call(f32[128,768]{1,0:T(8,128)} %get-tuple-element.58.grad_second_hbm, bf16[128,768]{1,0:T(8,128)(2,1)} %bitcast.13, ...), custom_call_target="tpu_custom_call" | custom-call | tf_op jit(solution)/shard_map/pallas_call | solution.py:1544
  203.2 7.8 %shard_map.300 = (bf16[128,768]{1,0:T(8,128)(2,1)}, f32[128,768]{1,0:T(8,128)}, f32[1,192]{1,0:T(1,128)}, f32[1,192]{1,0:T(1,128)}, f32[8,192]{1,0:T(8,128)}, /*...) custom-call(bf16[128,768]{1,0:T(8,128)(2,1)} %get-tuple-element.57.r, ...), custom_call_target="tpu_custom_call" | custom-call | tf_op jit(solution)/shard_map/pallas_call | solution.py:1711

commit v10 on v9

--- a/solution.py
+++ b/solution.py
@@ -25,7 +25,7 @@
 SEMS_FORWARD = 204
 SEMS_BACKWARD = 102
 SEMS_RINGS = 48
-SEMS_LAYOUT = 34
+SEMS_LAYOUT = 40
 
 
 class Spot:
@@ -1436,13 +1436,13 @@
         gkv[r, :, 0:half] = turn(kv_sum[at, 0:half], cosr[r], -sinr[r]).astype(BF)
         gkv[r, :, half:width] = kv_sum[at, half:width].astype(BF)
         kv_w.append(Gather(spot, gkv.at[r], lambda w, r=r: gkv4.at[w, r], sems))
+    ring3.step(1, only=0)
     send_give(1, 2 * third, third)
     send_give(0, done, shard - done)
     flat = gkv[...].reshape(2 * rows, width)
     grad_normed = grad_normed + nt(flat[:, 0:half], w_half[1]) + nt(flat[:, half:width], w_half[2])
     gn_send[...] = grad_normed.astype(BF).reshape(2, rows, width)
     normed_grad_x = aside(gn_send.at[1 - spot.x], gn_land)
-    ring3.step(1, only=0)
     ring3.step(2, only=1)
     ring3.step(1, only=1)
     first.relay(3)
@@ -1653,8 +1653,8 @@
     for a, out in enumerate((eg_out, eu_out, ed_out)):
         for made in loads[a]:
             made.wait()
-        for part in range(2):
-            at = slice(shard // 2 * part, shard // 2 * (part + 1))
+        for part in range(4):
+            at = slice(shard // 4 * part, shard // 4 * (part + 1))
             experts_f[a, at] = keep[a, at].astype(F32) + other[a, at].astype(F32)
             saves.append(copy(experts_f.at[a, at], out.at[at]))
     size = shard // 2

time: 211 us -> 211 us (level)
  no operation moved by 1% of the time
where the time goes in v10:
time: 211 us
  Pallas kernels  210 us (100%)
    pallas_call x1, Pallas kernels, run_forward(): pl.pallas_call(forward_kernel, out_shape=(shape((2, rows, PAIR), F32), sh...  117 us
    pallas_call x1, Pallas kernels, run_backward(): pl.pallas_call(backward_kernel, out_shape=(shape((rows, width), F32), sha...  85.2 us
    pallas_call x1, Pallas kernels, run_unpack(): pl.pallas_call(unpack_kernel, out_shape=(shape((rows, width), BF), shape(...  7.85 us

profile of v10, /device:TPU:0, one launch (start us, length us, event | category | flops | bytes accessed | tf_op | source)
XLA Modules:
  0.0 211.2 jit_solution(6322793365635100780)
XLA Ops:
  0.7 117.3 %shard_map.298 = (f32[2,128,128]{2,1,0:T(8,128)}, f32[2,128,128]{2,1,0:T(8,128)}, s32[1,1024]{1,0:T(1,128)}, s32[2,256,1]{2,1,0:T(8,128)}, bf16[6,256,128]{2,1,0...) custom-call(bf16[128,768]{1,0:T(8,128)(2,1)} %bitcast.12, ...), custom_call_target="tpu_custom_call" | custom-call | tf_op jit(solution)/shard_map/pallas_call | solution.py:1126
  118.0 85.2 %shard_map.299 = (f32[128,768]{1,0:T(8,128)}, f32[16,768]{1,0:T(8,128)}, bf16[8,48,768]{2,1,0:T(8,128)(2,1)}, bf16[8,64,768]{2,1,0:T(8,128)(2,1)}, bf16[8,1152,1...) custom-call(f32[128,768]{1,0:T(8,128)} %get-tuple-element.58.grad_second_hbm, bf16[128,768]{1,0:T(8,128)(2,1)} %bitcast.13, ...), custom_call_target="tpu_custom_call" | custom-call | tf_op jit(solution)/shard_map/pallas_call | solution.py:1544
  203.2 7.8 %shard_map.300 = (bf16[128,768]{1,0:T(8,128)(2,1)}, f32[128,768]{1,0:T(8,128)}, f32[1,192]{1,0:T(1,128)}, f32[1,192]{1,0:T(1,128)}, f32[8,192]{1,0:T(8,128)}, /*...) custom-call(bf16[128,768]{1,0:T(8,128)(2,1)} %get-tuple-element.57.r, ...), custom_call_target="tpu_custom_call" | custom-call | tf_op jit(solution)/shard_map/pallas_call | solution.py:1711
